TPU v7x, 128 devices: a whole 4x4x4 slice. The times are simulated.
128 devices in a mesh: layout: 4 (over z), gx: 4 (over y_hi, core), gy: 8 (over y_lo, x).
Axes of the slice: x: 4, y: 4 (y_hi: 2, y_lo: 2; y = y_hi * 2 + y_lo), z: 4, core: 2. Of those that a mesh axis runs over, the one named last changes fastest.
Arguments:
- state: float32 [4, 4, 64, 32, 1024], P('layout', None, 'gx', None, 'gy'), may hold values from -2 to 2
- planes: float32 [8, 4, 32, 1024], P('layout', None, None, 'gy'), may hold values from -2 to 2
- turbine_cell: int32 [4, 64, 32, 1024], P('layout', 'gx', None, 'gy'), may hold values from -1 to 63, as said below
- active: int32 [4, 64], P('layout'), may hold values 0 or 1
- yaw_sector: int32 [4, 64], P('layout'), may hold values from 0 to 7
- slot: int32 [4], replicated, may hold values from 0 to 7
Outputs:
- fields: float32 [4, 4, 64, 32, 1024], P('layout', None, 'gx', None, 'gy')
Inputs may be any that keep to these rules, and one draw needn't show every extreme that they name: `turbine_cell`: cells of value t form turbine t's actuator disk: one streamwise cell, 11 levels around level 16 and 11 spanwise cells (periodic). Every turbine has its disk and disks don't intersect; -1 elsewhere.
All inputs are finite; a program needn't handle non-finite values. No bound on the sum of `active` on one device may be relied on, other than what follows from the above.
Results may differ from a plain program's by a relative error of at most 0.00015.
Values sent between devices are 32-bit elements; how exact they have to be, the bound alone decides.
No kernel may reach another device: no remote copies, remote signals or barrier semaphores. Data moves between devices by JAX's collectives and lax.ppermute only.
A program may use at most 64 MiB of HBM per device.

v0:
```python
import jax
import jax.numpy as jnp
from jax import lax
from jax.sharding import PartitionSpec as P

STEPS = 4
SWEEPS = 4
RADIUS = 5


TIME_STEP = 0.25
VISCOSITY = 0.02
SMAGORINSKY = 0.0289
DIFFUSIVITY_RATIO = 1.0 / 0.7
BUOYANCY = 0.5
THRUST_COEFF = 1.33
YAW_INCREMENT = 0.1
BLOCKS = 4


def broadcast(array, axis, root):
    mine = lax.axis_index(axis) == root
    return lax.psum(jnp.where(mine, array, jnp.zeros_like(array)), axis)


def padded_2(array, sides, width):
    for axis, dim in sides:
        size, length = (lax.axis_size(axis), array.shape[dim])
        up = [(i, (i + 1) % size) for i in range(size)]
        down = [(j, i) for i, j in up]
        last = lax.slice_in_dim(array, length - width, length, axis=dim)
        leading = lax.slice_in_dim(array, 0, width, axis=dim)
        before = lax.ppermute(last, axis, up)
        after = lax.ppermute(leading, axis, down)
        array = jnp.concatenate([before, array, after], axis=dim)
    return array


def profiles(levels):
    height = (jnp.arange(levels).astype(jnp.float32) + 0.5) / levels
    wind_speed = height ** (1.0 / 7.0)
    warmth = 0.5 * height
    zeros = jnp.zeros((levels,), jnp.float32)
    return jnp.stack([wind_speed, zeros, zeros, warmth])


def pad_levels(values):
    keeping = jnp.array([1.0, 1.0, 0.0, 1.0], jnp.float32).reshape(4, 1, 1, 1)
    return jnp.concatenate(
        [values[:, :, :1] * keeping, values, values[:, :, -1:] * keeping], axis=2
    )


def stencil(padded):
    centre = padded[:, 1:-1, 1:-1, 1:-1]
    along_x = (padded[:, 2:, 1:-1, 1:-1] - padded[:, :-2, 1:-1, 1:-1]) * 0.5
    along_z = (padded[:, 1:-1, 2:, 1:-1] - padded[:, 1:-1, :-2, 1:-1]) * 0.5
    along_y = (padded[:, 1:-1, 1:-1, 2:] - padded[:, 1:-1, 1:-1, :-2]) * 0.5
    laplacian = (
        padded[:, 2:, 1:-1, 1:-1]
        + padded[:, :-2, 1:-1, 1:-1]
        + padded[:, 1:-1, 2:, 1:-1]
        + padded[:, 1:-1, :-2, 1:-1]
        + padded[:, 1:-1, 1:-1, 2:]
        + padded[:, 1:-1, 1:-1, :-2]
        - 6.0 * centre
    )
    return (centre, along_x, along_y, along_z, laplacian)


def tendency(padded, mean_theta, force_u, force_v):
    centre, along_x, along_y, along_z, laplacian = stencil(padded)
    advect = centre[0] * along_x + centre[1] * along_y + centre[2] * along_z
    shear_xy = 0.5 * (along_y[0] + along_x[1])
    shear_xz = 0.5 * (along_z[0] + along_x[2])
    shear_yz = 0.5 * (along_z[1] + along_y[2])
    strain = jnp.sqrt(
        2.0 * (along_x[0] ** 2 + along_y[1] ** 2 + along_z[2] ** 2)
        + 4.0 * (shear_xy**2 + shear_xz**2 + shear_yz**2)
    )
    viscous = VISCOSITY + SMAGORINSKY * strain
    scaling = jnp.array([1.0, 1.0, 1.0, DIFFUSIVITY_RATIO], jnp.float32).reshape(4, 1, 1, 1)
    extra = jnp.stack(
        [
            force_u,
            force_v,
            BUOYANCY * (centre[3] - mean_theta[None, :, None]),
            jnp.zeros_like(force_u),
        ]
    )
    return (centre, laplacian * viscous * scaling - advect + extra)


def band_start(levels):
    return levels // 2 - RADIUS


def band_blocks(values, levels):
    lowest = band_start(levels)
    band = values[:, lowest : lowest + 2 * RADIUS + 1]
    return band.reshape(BLOCKS, -1)


def one_hot(cell_ids, turbines):
    return (cell_ids[:, None] == jnp.arange(turbines, dtype=jnp.int32)[None, :]).astype(jnp.float32)


def disk_terms(values, disk_ids, yaw_angle):
    turbines = yaw_angle.shape[0]
    levels = disk_ids.shape[1]
    table = jnp.stack([jnp.cos(yaw_angle), jnp.sin(yaw_angle)])
    id_blocks = band_blocks(disk_ids, levels)
    u_blocks = band_blocks(values[0], levels)
    v_blocks = band_blocks(values[1], levels)

    def per_block(items):
        cell_ids, along_u, along_v = items
        marked = one_hot(cell_ids, turbines)
        angles = jnp.einsum("kt,ct->kc", table, marked, precision=lax.Precision.HIGHEST)
        normal = along_u * angles[0] + along_v * angles[1]
        sums = jnp.dot(normal, marked, precision=lax.Precision.HIGHEST)
        return (angles, sums)

    angles, sums = lax.map(per_block, (id_blocks, u_blocks, v_blocks))
    return (angles, jnp.sum(sums, axis=0))


def disk_force(disk_sums, running, disk_ids, angles):
    turbines = disk_sums.shape[0]
    rows, levels, cols = disk_ids.shape
    width = 2 * RADIUS + 1
    lowest = band_start(levels)
    disk_speed = disk_sums / float(width**2)
    thrust = -0.5 * THRUST_COEFF * disk_speed * jnp.abs(disk_speed) * running
    id_blocks = band_blocks(disk_ids, levels)

    def per_block(items):
        cell_ids, block_angles = items
        marked = one_hot(cell_ids, turbines)
        per_cell = jnp.dot(marked, thrust, precision=lax.Precision.HIGHEST)
        return per_cell[None, :] * block_angles

    forced = lax.map(per_block, (id_blocks, angles))
    forced = jnp.transpose(forced, (1, 0, 2)).reshape(2, rows, width, cols)
    forced = jnp.pad(forced, ((0, 0), (0, 0), (lowest, levels - lowest - width), (0, 0)))
    return (forced[0], forced[1])


def divergence(extended):
    vertical = extended[2][1:-1, :, 1:-1]
    zeros = jnp.zeros_like(vertical[:, :1])
    padded_w = jnp.concatenate([zeros, vertical, zeros], axis=1)
    return (
        (extended[0][2:, :, 1:-1] - extended[0][:-2, :, 1:-1]) * 0.5
        + (extended[1][1:-1, :, 2:] - extended[1][1:-1, :, :-2]) * 0.5
        + (padded_w[:, 2:] - padded_w[:, :-2]) * 0.5
    )


def vertical_pair(padded):
    centre = padded[1:-1, :, 1:-1]
    upward = jnp.concatenate([centre[:, 1:], centre[:, -1:]], axis=1)
    downward = jnp.concatenate([centre[:, :1], centre[:, :-1]], axis=1)
    return (upward, downward)


def jacobi(padded, source):
    upward, downward = vertical_pair(padded)
    beside_all = (
        padded[2:, :, 1:-1]
        + padded[:-2, :, 1:-1]
        + padded[1:-1, :, 2:]
        + padded[1:-1, :, :-2]
        + upward
        + downward
    )
    return (beside_all - source) / 6.0


def gradient(padded):
    upward, downward = vertical_pair(padded)
    return jnp.stack(
        [
            (padded[2:, :, 1:-1] - padded[:-2, :, 1:-1]) * 0.5,
            (padded[1:-1, :, 2:] - padded[1:-1, :, :-2]) * 0.5,
            (upward - downward) * 0.5,
        ]
    )


def clear_ends(padded, rim_width, inflow_side, outflow_side):
    padded = padded.at[:rim_width].multiply(jnp.where(inflow_side, 0.0, 1.0))
    return padded.at[-rim_width:].multiply(jnp.where(outflow_side, 0.0, 1.0))


def local(state, planes, turbine_cell, active, yaw_sector, slot):
    tile_levels = state.shape[3]
    tile_rows = state.shape[2]
    tile_cols = state.shape[4]
    mean_wind = profiles(tile_levels)
    fields = state[0] + mean_wind[:, None, :, None]
    disk_ids = turbine_cell[0]
    yaw_angle = (yaw_sector[0].astype(jnp.float32) - 3.5) * YAW_INCREMENT
    running = active[0].astype(jnp.float32)
    inflow_side = lax.axis_index("gx") == 0
    outflow_side = lax.axis_index("gx") == lax.axis_size("gx") - 1
    cell_count = tile_rows * lax.axis_size("gx") * tile_cols * lax.axis_size("gy")
    stored_count = planes.shape[0]
    rim_width = 1
    for step_index in range(STEPS):
        slot_now = slot[step_index]
        stored = lax.dynamic_index_in_dim(planes, slot_now % stored_count, 0, keepdims=False)
        inflow = broadcast(stored, "layout", slot_now // stored_count)
        inflow = inflow + mean_wind[:, :, None]
        theta_sum = jnp.sum(fields[3], axis=(0, 2))
        angles, disk_sums = disk_terms(fields, disk_ids, yaw_angle)
        theta_sum, disk_sums = lax.psum((theta_sum, disk_sums), ("gx", "gy"))
        extended = padded_2(fields, (("gx", 1), ("gy", 3)), 1)
        inflow_row = jnp.pad(inflow, ((0, 0), (0, 0), (1, 1)))[:, None]
        extended = extended.at[:, :1].set(jnp.where(inflow_side, inflow_row, extended[:, :1]))
        extended = extended.at[:, -1:].set(
            jnp.where(outflow_side, extended[:, -2:-1], extended[:, -1:])
        )
        force_u, force_v = disk_force(disk_sums, running, disk_ids, angles)
        current, tendencies = tendency(
            pad_levels(extended), theta_sum / cell_count, force_u, force_v
        )
        stepped = current + TIME_STEP * tendencies
        provisional = stepped[:3]
        star_ext = padded_2(provisional, (("gx", 1), ("gy", 3)), rim_width)
        plane_rim = jnp.pad(inflow[:3], ((0, 0), (0, 0), (1, 1)))
        star_ext = star_ext.at[:, :rim_width].set(
            jnp.where(inflow_side, plane_rim[:, None], star_ext[:, :rim_width])
        )
        star_ext = star_ext.at[:, -rim_width:].set(
            jnp.where(
                outflow_side, star_ext[:, -rim_width - 1 : -rim_width], star_ext[:, -rim_width:]
            )
        )
        source = divergence(star_ext)
        pressure = -source / 6.0
        for sweep_index in range(SWEEPS):
            bordered = padded_2(pressure, (("gx", 0), ("gy", 2)), 1)
            pressure = jacobi(clear_ends(bordered, 1, inflow_side, outflow_side), source)
        bordered = padded_2(pressure, (("gx", 0), ("gy", 2)), 1)
        gradients = gradient(clear_ends(bordered, 1, inflow_side, outflow_side))
        fields = jnp.concatenate([provisional - gradients, stepped[3:]], axis=0)
    return fields[None]


def solution(mesh):
    return jax.shard_map(
        local,
        mesh=mesh,
        in_specs=(
            P("layout", None, "gx", None, "gy"),
            P("layout", None, None, "gy"),
            P("layout", "gx", None, "gy"),
            P("layout", None),
            P("layout", None),
            P(),
        ),
        out_specs=P("layout", None, "gx", None, "gy"),
        check_vma=False,
    )
```

profile of v0, /device:TPU:1, one launch (start us, length us, event | category | flops | bytes accessed | tf_op | source)
XLA Modules:
  0.0 803.1 jit_solution(744561785181393031)
XLA Ops:
  9.7 3.0 collective-permute-start
  24.2 6.0 while.144
  30.3 59.6 %all-reduce.23 = (f32[64]{0:T(128)S(1)}, f32[32]{0:T(128)S(1)}) all-reduce(f32[64]{0:T(128)S(1)} %reduce_sum.72, f32[32]{0:T(128)S(1)} %get-tuple-element.1155), channel_id=1, replica_groups=mesh['layout'=4,'gx'=4,'gy'=8] {'gx','gy'}, use_global_device_ids=true, to_apply=%region_4.5 | all-reduce | flops 96 | bytes 768 | tf_op jit(solution)/shard_map/psum | solution.py:217
  89.9 2.8 while.145
  102.1 2.6 pad_maximum_fusion
  112.4 9.8 %collective-permute-start.5 = (f32[3,1,32,128]{3,2,1,0:T(8,128)S(1)}, f32[3,1,32,128]{3,2,1,0:T(8,128)S(1)}, u32[]{:S(2)}, u32[]{:S(2)}) collective-permute-start(f32[3,1,32,128]{3,2,1,0:T(8,128)S(1)} %get-tuple-element.1152), channel_id=1, source_target_pairs={{8,0},{16,8},{24,16},{0,24},{9,1},{17,9},{25,17},{1,25},{10,2},{18... | collective-permute-start | bytes 147464 | tf_op jit(solution)/shard_map/ppermute | solution.py:34
  127.5 3.3 collective-permute-done.6
  132.6 5.2 collective-permute-start.9
  141.9 4.6 collective-permute-done.11
  149.6 3.4 collective-permute-start.13
  158.5 5.1 collective-permute-done.15
  166.8 2.9 collective-permute-start.17
  174.6 5.4 collective-permute-done.19
  183.0 2.7 collective-permute-start.21
  190.5 5.2 collective-permute-done.23
  198.7 3.0 collective-permute-start.25
  206.7 5.3 collective-permute-done.27
  215.2 2.7 collective-permute-start.29
  219.7 6.0 while.146
  225.7 55.7 %all-reduce.22 = (f32[64]{0:T(128)S(1)}, f32[32]{0:T(128)S(1)}) all-reduce(f32[64]{0:T(128)S(1)} %reduce_sum.74, f32[32]{0:T(128)S(1)} %get-tuple-element.1150), channel_id=1, replica_groups=mesh['layout'=4,'gx'=4,'gy'=8] {'gx','gy'}, use_global_device_ids=true, to_apply=%region_13.14 | all-reduce | flops 96 | bytes 768 | tf_op jit(solution)/shard_map/psum | solution.py:217
  281.5 2.8 while.147
  302.9 9.3 %collective-permute-start.33 = (f32[3,1,32,128]{3,2,0,1:T(8,128)S(1)}, f32[3,1,32,128]{3,2,0,1:T(8,128)S(1)}, u32[]{:S(2)}, u32[]{:S(2)}) collective-permute-start(f32[3,1,32,128]{3,2,0,1:T(8,128)S(1)} %get-tuple-element.1146), channel_id=1, source_target_pairs={{8,0},{16,8},{24,16},{0,24},{9,1},{17,9},{25,17},{1,25},{10,2},{18... | collective-permute-start | bytes 147464 | tf_op jit(solution)/shard_map/ppermute | solution.py:34
  325.7 4.9 collective-permute-start.37
  334.8 3.7 collective-permute-done.39
  338.5 2.6 collective-permute-done.38
  342.0 3.9 collective-permute-start.41
  346.0 2.6 collective-permute-start.40
  351.7 4.9 collective-permute-done.43
  359.7 3.1 collective-permute-start.45
  367.6 5.3 collective-permute-done.47
  375.9 2.8 collective-permute-start.49
  383.5 5.3 collective-permute-done.51
  391.7 2.9 collective-permute-start.53
  399.5 5.2 collective-permute-done.55
  408.1 6.0 while.148
  414.2 58.9 %all-reduce.21 = (f32[64]{0:T(128)S(1)}, f32[32]{0:T(128)S(1)}) all-reduce(f32[64]{0:T(128)S(1)} %reduce_sum.76, f32[32]{0:T(128)S(1)} %get-tuple-element.1144), channel_id=1, replica_groups=mesh['layout'=4,'gx'=4,'gy'=8] {'gx','gy'}, use_global_device_ids=true, to_apply=%region_22.23 | all-reduce | flops 96 | bytes 768 | tf_op jit(solution)/shard_map/psum | solution.py:217
  473.1 6.8 collective-permute-start.57
  480.0 2.8 while.149
  500.6 5.2 collective-permute-start.61
  519.7 5.0 collective-permute-start.65
  528.6 4.5 collective-permute-done.67
  536.3 3.5 collective-permute-start.69
  545.2 5.3 collective-permute-done.71
  553.6 2.8 collective-permute-start.73
  561.1 5.3 collective-permute-done.75
  569.4 2.9 collective-permute-start.77
  577.0 5.3 collective-permute-done.79
  585.3 2.8 collective-permute-start.81
  593.0 5.0 collective-permute-done.83
  601.4 6.0 while.150
  607.4 60.1 %all-reduce.20 = (f32[64]{0:T(128)S(1)}, f32[32]{0:T(128)S(1)}) all-reduce(f32[64]{0:T(128)S(1)} %reduce_sum.78, f32[32]{0:T(128)S(1)} %get-tuple-element.1138), channel_id=1, replica_groups=mesh['layout'=4,'gx'=4,'gy'=8] {'gx','gy'}, use_global_device_ids=true, to_apply=%region_31.32 | all-reduce | flops 96 | bytes 768 | tf_op jit(solution)/shard_map/psum | solution.py:217
  667.6 5.7 collective-permute-start.85
  673.3 2.8 while.151
  694.0 5.2 collective-permute-start.89
  712.6 5.0 collective-permute-start.93
  721.8 4.3 collective-permute-done.95
  729.4 3.5 collective-permute-start.97
  738.6 5.0 collective-permute-done.99
  746.7 3.0 collective-permute-start.101
  754.5 5.4 collective-permute-done.103
  762.9 2.8 collective-permute-start.105
  770.4 5.3 collective-permute-done.107
  778.6 2.9 collective-permute-start.109
  786.3 5.3 collective-permute-done.111
  (724 shorter events, 312.8 us)
Async XLA Ops:
  6.5 98.2 %all-reduce.27.cloned.1.call-start = ((), (), s32[]{:S(2)}) async-start(), calls=%async_computation | async-start | bytes 524288 | tf_op jit(solution)/shard_map/psum | solution.py:23
  8.2 84.6 %collective-permute-start.1 = (f32[4,1,32,128]{3,2,1,0:T(8,128)S(1)}, f32[4,1,32,128]{3,2,1,0:T(8,128)S(1)}, u32[]{:S(2)}, u32[]{:S(2)}) collective-permute-start(f32[4,1,32,128]{3,2,1,0:T(8,128)S(1)} %get-tuple-element.1154), channel_id=1, source_target_pairs={{8,0},{16,8},{24,16},{0,24},{9,1},{17,9},{25,17},{1,25},{10,2},{18... | collective-permute-start | bytes 196616 | tf_op jit(solution)/shard_map/ppermute | solution.py:34
  9.7 83.1 %collective-permute-start = (f32[4,1,32,128]{3,2,1,0:T(8,128)S(1)}, f32[4,1,32,128]{3,2,1,0:T(8,128)S(1)}, u32[]{:S(2)}, u32[]{:S(2)}) collective-permute-start(f32[4,1,32,128]{3,2,1,0:T(8,128)S(1)} %get-tuple-element.1153), channel_id=1, source_target_pairs={{0,8},{8,16},{16,24},{24,0},{1,9},{9,17},{17,25},{25,1},{2,10},{10... | collective-permute-start | bytes 196616 | tf_op jit(solution)/shard_map/ppermute | solution.py:33
  112.4 10.7 %collective-permute-start.5 = (f32[3,1,32,128]{3,2,1,0:T(8,128)S(1)}, f32[3,1,32,128]{3,2,1,0:T(8,128)S(1)}, u32[]{:S(2)}, u32[]{:S(2)}) collective-permute-start(f32[3,1,32,128]{3,2,1,0:T(8,128)S(1)} %get-tuple-element.1152), channel_id=1, source_target_pairs={{8,0},{16,8},{24,16},{0,24},{9,1},{17,9},{25,17},{1,25},{10,2},{18... | collective-permute-start | bytes 147464 | tf_op jit(solution)/shard_map/ppermute | solution.py:34
  132.6 7.5 collective-permute-start.9
  140.3 6.1 collective-permute-start.11
  140.4 8.2 %collective-permute-start.10 = (f32[18,32,1]{2,1,0:T(8,128)S(1)}, f32[18,32,1]{2,1,0:T(8,128)S(1)}, u32[]{:S(2)}, u32[]{:S(2)}) collective-permute-start(f32[18,32,1]{2,1,0:T(8,128)S(1)} %get-tuple-element.1298), channel_id=1, source_target_pairs={{0,1},{1,2},{2,3},{3,4},{4,5},{5,6},{6,7},{7,0},{8,9},{9,10},{10,1... | collective-permute-start | bytes 6920 | tf_op jit(solution)/shard_map/ppermute | solution.py:33
  149.6 7.3 collective-permute-start.13
  157.0 6.7 collective-permute-start.15
  157.1 8.8 %collective-permute-start.14 = (f32[18,32,1]{2,1,0:T(8,128)S(1)}, f32[18,32,1]{2,1,0:T(8,128)S(1)}, u32[]{:S(2)}, u32[]{:S(2)}) collective-permute-start(f32[18,32,1]{2,1,0:T(8,128)S(1)} %get-tuple-element.1296), channel_id=1, source_target_pairs={{0,1},{1,2},{2,3},{3,4},{4,5},{5,6},{6,7},{7,0},{8,9},{9,10},{10,1... | collective-permute-start | bytes 6920 | tf_op jit(solution)/shard_map/ppermute | solution.py:33
  166.8 6.1 collective-permute-start.17
  173.0 7.0 collective-permute-start.19
  173.1 9.0 %collective-permute-start.18 = (f32[18,32,1]{2,1,0:T(8,128)S(1)}, f32[18,32,1]{2,1,0:T(8,128)S(1)}, u32[]{:S(2)}, u32[]{:S(2)}) collective-permute-start(f32[18,32,1]{2,1,0:T(8,128)S(1)} %get-tuple-element.1294), channel_id=1, source_target_pairs={{0,1},{1,2},{2,3},{3,4},{4,5},{5,6},{6,7},{7,0},{8,9},{9,10},{10,1... | collective-permute-start | bytes 6920 | tf_op jit(solution)/shard_map/ppermute | solution.py:33
  188.8 6.9 collective-permute-start.23
  189.0 8.7 %collective-permute-start.22 = (f32[18,32,1]{2,1,0:T(8,128)S(1)}, f32[18,32,1]{2,1,0:T(8,128)S(1)}, u32[]{:S(2)}, u32[]{:S(2)}) collective-permute-start(f32[18,32,1]{2,1,0:T(8,128)S(1)} %get-tuple-element.1292), channel_id=1, source_target_pairs={{0,1},{1,2},{2,3},{3,4},{4,5},{5,6},{6,7},{7,0},{8,9},{9,10},{10,1... | collective-permute-start | bytes 6920 | tf_op jit(solution)/shard_map/ppermute | solution.py:33
  198.7 6.1 collective-permute-start.25
  205.0 7.0 collective-permute-start.27
  205.1 9.0 %collective-permute-start.26 = (f32[18,32,1]{2,1,0:T(8,128)S(1)}, f32[18,32,1]{2,1,0:T(8,128)S(1)}, u32[]{:S(2)}, u32[]{:S(2)}) collective-permute-start(f32[18,32,1]{2,1,0:T(8,128)S(1)} %get-tuple-element.1290), channel_id=1, source_target_pairs={{0,1},{1,2},{2,3},{3,4},{4,5},{5,6},{6,7},{7,0},{8,9},{9,10},{10,1... | collective-permute-start | bytes 6920 | tf_op jit(solution)/shard_map/ppermute | solution.py:33
  215.2 69.1 %collective-permute-start.29 = (f32[4,1,32,128]{3,2,1,0:T(8,128)S(1)}, f32[4,1,32,128]{3,2,1,0:T(8,128)S(1)}, u32[]{:S(2)}, u32[]{:S(2)}) collective-permute-start(f32[4,1,32,128]{3,2,1,0:T(8,128)S(1)} %get-tuple-element.1148), channel_id=1, source_target_pairs={{8,0},{16,8},{24,16},{0,24},{9,1},{17,9},{25,17},{1,25},{10,2},{18... | collective-permute-start | bytes 196616 | tf_op jit(solution)/shard_map/ppermute | solution.py:34
  217.9 66.4 %collective-permute-start.28 = (f32[4,1,32,128]{3,2,1,0:T(8,128)S(1)}, f32[4,1,32,128]{3,2,1,0:T(8,128)S(1)}, u32[]{:S(2)}, u32[]{:S(2)}) collective-permute-start(f32[4,1,32,128]{3,2,1,0:T(8,128)S(1)} %get-tuple-element.1147), channel_id=1, source_target_pairs={{0,8},{8,16},{16,24},{24,0},{1,9},{9,17},{17,25},{25,1},{2,10},{10... | collective-permute-start | bytes 196616 | tf_op jit(solution)/shard_map/ppermute | solution.py:33
  302.9 10.2 %collective-permute-start.33 = (f32[3,1,32,128]{3,2,0,1:T(8,128)S(1)}, f32[3,1,32,128]{3,2,0,1:T(8,128)S(1)}, u32[]{:S(2)}, u32[]{:S(2)}) collective-permute-start(f32[3,1,32,128]{3,2,0,1:T(8,128)S(1)} %get-tuple-element.1146), channel_id=1, source_target_pairs={{8,0},{16,8},{24,16},{0,24},{9,1},{17,9},{25,17},{1,25},{10,2},{18... | collective-permute-start | bytes 147464 | tf_op jit(solution)/shard_map/ppermute | solution.py:34
  325.7 7.0 collective-permute-start.37
  333.0 8.2 %collective-permute-start.38 = (f32[18,32,1]{2,1,0:T(8,128)S(1)}, f32[18,32,1]{2,1,0:T(8,128)S(1)}, u32[]{:S(2)}, u32[]{:S(2)}) collective-permute-start(f32[18,32,1]{2,1,0:T(8,128)S(1)} %get-tuple-element.1288), channel_id=1, source_target_pairs={{0,1},{1,2},{2,3},{3,4},{4,5},{5,6},{6,7},{7,0},{8,9},{9,10},{10,1... | collective-permute-start | bytes 6920 | tf_op jit(solution)/shard_map/ppermute | solution.py:33
  342.0 7.9 collective-permute-start.41
  350.1 6.4 collective-permute-start.43
  350.2 8.6 %collective-permute-start.42 = (f32[18,32,1]{2,1,0:T(8,128)S(1)}, f32[18,32,1]{2,1,0:T(8,128)S(1)}, u32[]{:S(2)}, u32[]{:S(2)}) collective-permute-start(f32[18,32,1]{2,1,0:T(8,128)S(1)} %get-tuple-element.1286), channel_id=1, source_target_pairs={{0,1},{1,2},{2,3},{3,4},{4,5},{5,6},{6,7},{7,0},{8,9},{9,10},{10,1... | collective-permute-start | bytes 6920 | tf_op jit(solution)/shard_map/ppermute | solution.py:33
  359.7 6.2 collective-permute-start.45
  366.1 6.9 collective-permute-start.47
  366.1 8.8 %collective-permute-start.46 = (f32[18,32,1]{2,1,0:T(8,128)S(1)}, f32[18,32,1]{2,1,0:T(8,128)S(1)}, u32[]{:S(2)}, u32[]{:S(2)}) collective-permute-start(f32[18,32,1]{2,1,0:T(8,128)S(1)} %get-tuple-element.1284), channel_id=1, source_target_pairs={{0,1},{1,2},{2,3},{3,4},{4,5},{5,6},{6,7},{7,0},{8,9},{9,10},{10,1... | collective-permute-start | bytes 6920 | tf_op jit(solution)/shard_map/ppermute | solution.py:33
  381.9 6.8 collective-permute-start.51
  382.0 8.8 %collective-permute-start.50 = (f32[18,32,1]{2,1,0:T(8,128)S(1)}, f32[18,32,1]{2,1,0:T(8,128)S(1)}, u32[]{:S(2)}, u32[]{:S(2)}) collective-permute-start(f32[18,32,1]{2,1,0:T(8,128)S(1)} %get-tuple-element.1282), channel_id=1, source_target_pairs={{0,1},{1,2},{2,3},{3,4},{4,5},{5,6},{6,7},{7,0},{8,9},{9,10},{10,1... | collective-permute-start | bytes 6920 | tf_op jit(solution)/shard_map/ppermute | solution.py:33
  397.8 6.9 collective-permute-start.55
  397.9 8.8 %collective-permute-start.54 = (f32[18,32,1]{2,1,0:T(8,128)S(1)}, f32[18,32,1]{2,1,0:T(8,128)S(1)}, u32[]{:S(2)}, u32[]{:S(2)}) collective-permute-start(f32[18,32,1]{2,1,0:T(8,128)S(1)} %get-tuple-element.1280), channel_id=1, source_target_pairs={{0,1},{1,2},{2,3},{3,4},{4,5},{5,6},{6,7},{7,0},{8,9},{9,10},{10,1... | collective-permute-start | bytes 6920 | tf_op jit(solution)/shard_map/ppermute | solution.py:33
  473.1 9.6 %collective-permute-start.57 = (f32[4,1,32,128]{3,2,1,0:T(8,128)S(1)}, f32[4,1,32,128]{3,2,1,0:T(8,128)S(1)}, u32[]{:S(2)}, u32[]{:S(2)}) collective-permute-start(f32[4,1,32,128]{3,2,1,0:T(8,128)S(1)} %get-tuple-element.1142), channel_id=1, source_target_pairs={{8,0},{16,8},{24,16},{0,24},{9,1},{17,9},{25,17},{1,25},{10,2},{18... | collective-permute-start | bytes 196616 | tf_op jit(solution)/shard_map/ppermute | solution.py:34
  500.6 6.1 collective-permute-start.61
  519.7 7.3 collective-permute-start.65
  527.1 6.1 collective-permute-start.67
  527.2 8.2 %collective-permute-start.66 = (f32[18,32,1]{2,1,0:T(8,128)S(1)}, f32[18,32,1]{2,1,0:T(8,128)S(1)}, u32[]{:S(2)}, u32[]{:S(2)}) collective-permute-start(f32[18,32,1]{2,1,0:T(8,128)S(1)} %get-tuple-element.1278), channel_id=1, source_target_pairs={{0,1},{1,2},{2,3},{3,4},{4,5},{5,6},{6,7},{7,0},{8,9},{9,10},{10,1... | collective-permute-start | bytes 6920 | tf_op jit(solution)/shard_map/ppermute | solution.py:33
  536.3 7.2 collective-permute-start.69
  543.7 6.8 collective-permute-start.71
  543.7 8.9 %collective-permute-start.70 = (f32[18,32,1]{2,1,0:T(8,128)S(1)}, f32[18,32,1]{2,1,0:T(8,128)S(1)}, u32[]{:S(2)}, u32[]{:S(2)}) collective-permute-start(f32[18,32,1]{2,1,0:T(8,128)S(1)} %get-tuple-element.1276), channel_id=1, source_target_pairs={{0,1},{1,2},{2,3},{3,4},{4,5},{5,6},{6,7},{7,0},{8,9},{9,10},{10,1... | collective-permute-start | bytes 6920 | tf_op jit(solution)/shard_map/ppermute | solution.py:33
  559.5 6.8 collective-permute-start.75
  559.6 8.8 %collective-permute-start.74 = (f32[18,32,1]{2,1,0:T(8,128)S(1)}, f32[18,32,1]{2,1,0:T(8,128)S(1)}, u32[]{:S(2)}, u32[]{:S(2)}) collective-permute-start(f32[18,32,1]{2,1,0:T(8,128)S(1)} %get-tuple-element.1274), channel_id=1, source_target_pairs={{0,1},{1,2},{2,3},{3,4},{4,5},{5,6},{6,7},{7,0},{8,9},{9,10},{10,1... | collective-permute-start | bytes 6920 | tf_op jit(solution)/shard_map/ppermute | solution.py:33
  569.4 5.9 collective-permute-start.77
  575.4 6.9 collective-permute-start.79
  575.5 8.8 %collective-permute-start.78 = (f32[18,32,1]{2,1,0:T(8,128)S(1)}, f32[18,32,1]{2,1,0:T(8,128)S(1)}, u32[]{:S(2)}, u32[]{:S(2)}) collective-permute-start(f32[18,32,1]{2,1,0:T(8,128)S(1)} %get-tuple-element.1272), channel_id=1, source_target_pairs={{0,1},{1,2},{2,3},{3,4},{4,5},{5,6},{6,7},{7,0},{8,9},{9,10},{10,1... | collective-permute-start | bytes 6920 | tf_op jit(solution)/shard_map/ppermute | solution.py:33
  591.3 6.7 collective-permute-start.83
  591.4 8.6 %collective-permute-start.82 = (f32[18,32,1]{2,1,0:T(8,128)S(1)}, f32[18,32,1]{2,1,0:T(8,128)S(1)}, u32[]{:S(2)}, u32[]{:S(2)}) collective-permute-start(f32[18,32,1]{2,1,0:T(8,128)S(1)} %get-tuple-element.1270), channel_id=1, source_target_pairs={{0,1},{1,2},{2,3},{3,4},{4,5},{5,6},{6,7},{7,0},{8,9},{9,10},{10,1... | collective-permute-start | bytes 6920 | tf_op jit(solution)/shard_map/ppermute | solution.py:33
  667.6 8.5 %collective-permute-start.85 = (f32[4,1,32,128]{3,2,1,0:T(8,128)S(1)}, f32[4,1,32,128]{3,2,1,0:T(8,128)S(1)}, u32[]{:S(2)}, u32[]{:S(2)}) collective-permute-start(f32[4,1,32,128]{3,2,1,0:T(8,128)S(1)} %get-tuple-element.1136), channel_id=1, source_target_pairs={{8,0},{16,8},{24,16},{0,24},{9,1},{17,9},{25,17},{1,25},{10,2},{18... | collective-permute-start | bytes 196616 | tf_op jit(solution)/shard_map/ppermute | solution.py:34
  694.0 6.1 collective-permute-start.89
  712.6 7.3 collective-permute-start.93
  720.0 6.0 collective-permute-start.95
  720.1 8.4 %collective-permute-start.94 = (f32[18,32,1]{2,1,0:T(8,128)S(1)}, f32[18,32,1]{2,1,0:T(8,128)S(1)}, u32[]{:S(2)}, u32[]{:S(2)}) collective-permute-start(f32[18,32,1]{2,1,0:T(8,128)S(1)} %get-tuple-element.1268), channel_id=1, source_target_pairs={{0,1},{1,2},{2,3},{3,4},{4,5},{5,6},{6,7},{7,0},{8,9},{9,10},{10,1... | collective-permute-start | bytes 6920 | tf_op jit(solution)/shard_map/ppermute | solution.py:33
  729.4 7.5 collective-permute-start.97
  737.0 6.5 collective-permute-start.99
  737.1 8.6 %collective-permute-start.98 = (f32[18,32,1]{2,1,0:T(8,128)S(1)}, f32[18,32,1]{2,1,0:T(8,128)S(1)}, u32[]{:S(2)}, u32[]{:S(2)}) collective-permute-start(f32[18,32,1]{2,1,0:T(8,128)S(1)} %get-tuple-element.1266), channel_id=1, source_target_pairs={{0,1},{1,2},{2,3},{3,4},{4,5},{5,6},{6,7},{7,0},{8,9},{9,10},{10,1... | collective-permute-start | bytes 6920 | tf_op jit(solution)/shard_map/ppermute | solution.py:33
  746.7 6.1 collective-permute-start.101
  753.0 6.9 collective-permute-start.103
  753.1 8.9 %collective-permute-start.102 = (f32[18,32,1]{2,1,0:T(8,128)S(1)}, f32[18,32,1]{2,1,0:T(8,128)S(1)}, u32[]{:S(2)}, u32[]{:S(2)}) collective-permute-start(f32[18,32,1]{2,1,0:T(8,128)S(1)} %get-tuple-element.1264), channel_id=1, source_target_pairs={{0,1},{1,2},{2,3},{3,4},{4,5},{5,6},{6,7},{7,0},{8,9},{9,10},{10,1... | collective-permute-start | bytes 6920 | tf_op jit(solution)/shard_map/ppermute | solution.py:33
  768.8 6.8 collective-permute-start.107
  768.9 8.8 %collective-permute-start.106 = (f32[18,32,1]{2,1,0:T(8,128)S(1)}, f32[18,32,1]{2,1,0:T(8,128)S(1)}, u32[]{:S(2)}, u32[]{:S(2)}) collective-permute-start(f32[18,32,1]{2,1,0:T(8,128)S(1)} %get-tuple-element.1262), channel_id=1, source_target_pairs={{0,1},{1,2},{2,3},{3,4},{4,5},{5,6},{6,7},{7,0},{8,9},{9,10},{10,1... | collective-permute-start | bytes 6920 | tf_op jit(solution)/shard_map/ppermute | solution.py:33
  778.6 6.0 collective-permute-start.109
  784.8 6.9 collective-permute-start.111
  784.8 8.9 %collective-permute-start.110 = (f32[18,32,1]{2,1,0:T(8,128)S(1)}, f32[18,32,1]{2,1,0:T(8,128)S(1)}, u32[]{:S(2)}, u32[]{:S(2)}) collective-permute-start(f32[18,32,1]{2,1,0:T(8,128)S(1)} %get-tuple-element.1260), channel_id=1, source_target_pairs={{0,1},{1,2},{2,3},{3,4},{4,5},{5,6},{6,7},{7,0},{8,9},{9,10},{10,1... | collective-permute-start | bytes 6920 | tf_op jit(solution)/shard_map/ppermute | solution.py:33
  (73 other events, 409.9 us)
Sparse Core Ops, SparseCore 0:
  23.8 42.3 all-reduce.26
where the time goes:
time: 814 us; the launch traced here: 803 us
  blocking collectives  234 us (29%)
  starting transfers between devices  199 us (24%)
  waiting for transfers between devices  193 us (24%)
  local copies, waits for them, and re-layouts  62.5 us (8%)
  other arithmetic  55.8 us (7%)
  matrix products  30.7 us (4%)
  between operations  26.2 us (3%)
    psum x4, blocking collectives, local(): theta_sum, disk_sums = lax.psum((theta_sum, disk_sums), ('gx', 'gy'))  234 us
    ppermute x56, waiting for transfers between devices, padded_2(): after = lax.ppermute(leading, axis, down)  133 us
    ppermute x56, starting transfers between devices, padded_2(): after = lax.ppermute(leading, axis, down)  119 us
    ppermute x56, starting transfers between devices, padded_2(): before = lax.ppermute(last, axis, up)  80.8 us
    ppermute x56, waiting for transfers between devices, padded_2(): before = lax.ppermute(last, axis, up)  60.2 us
    concatenate x56, other arithmetic, padded_2(): array = jnp.concatenate([before, array, after], axis=dim)  22.8 us
  transfers between devices with their start and end apart: 113, of which 80 were waited for; matrix products, arithmetic and copies ran while one was open for 5% of the time, Pallas kernels for 0%

commit v1 on v0

v1 whole, which is shorter than its diff:
```python
import functools
import math

import jax
import jax.numpy as jnp
from jax import lax
from jax.experimental import pallas as pl
from jax.experimental.pallas import tpu as pltpu
from jax.sharding import PartitionSpec as P

STEPS = 4
SWEEPS = 4
RADIUS = 5
NZ = 32
XI = 16
GX = 4
OWN = 32
HALO = 8
EXT = OWN + 2 * HALO
PAD = EXT + 16
LANES = 128
WIDTH = 2 * RADIUS + 1
LOWEST = NZ // 2 - RADIUS
TILES = 4 * XI

TIME_STEP = 0.25
VISCOSITY = 0.02
SMAGORINSKY = 0.0289
DIFFUSIVITY_RATIO = 1.0 / 0.7
BUOYANCY = 0.5
THRUST_COEFF = 1.33
YAW_INCREMENT = 0.1
SIXTH = 1.0 / 6.0
F32 = jnp.float32
VLIMIT = 40 * 1024 * 1024

VMEM = pl.BlockSpec(memory_space=pltpu.VMEM)
SMEM = pl.BlockSpec(memory_space=pltpu.SMEM)


def shape(*dims):
    return jax.ShapeDtypeStruct(dims, F32)


def lanes(rows=8):
    return lax.broadcasted_iota(jnp.int32, (rows, LANES), 1)


def level_masks(rows=8):
    level = lanes(rows) & (NZ - 1)
    return level == 0, level == NZ - 1


def below(f, first):
    return jnp.where(first, f, pltpu.roll(f, 1, axis=1))


def above(f, last):
    return jnp.where(last, f, pltpu.roll(f, LANES - 1, axis=1))


def call(kernel, out_shape, in_specs, scratch=(), flops=10_000_000, **kwargs):
    return pl.pallas_call(
        kernel,
        out_shape=out_shape,
        in_specs=in_specs,
        out_specs=jax.tree.map(lambda _: VMEM, out_shape),
        scratch_shapes=list(scratch),
        compiler_params=pltpu.CompilerParams(vmem_limit_bytes=VLIMIT),
        cost_estimate=pl.CostEstimate(flops=flops, bytes_accessed=4_000_000, transcendentals=0),
        **kwargs,
    )


def block_transposed(sources, group, masks):
    out = None
    for c, value in enumerate(sources):
        moved = pltpu.roll(value, ((c - group) & 3) * 32, axis=1)
        out = moved if out is None else jnp.where(masks[c], moved, out)
    return out


def pack_kernel(scal, state, planes, s0, s1, s2, s3, pl_out):
    slab = scal[1]
    group = lanes() >> 5
    masks = [group == c for c in range(4)]

    def per_row(x, carry):
        for kt in range(4):
            sources = [state[c, x, kt * 8 : kt * 8 + 8, :] for c in range(4)]
            for s, out in enumerate((s0, s1, s2, s3)):
                out[x * 4 + kt] = block_transposed(sources, slab ^ s, masks)
        return carry

    lax.fori_loop(0, XI, per_row, 0)
    for plane in range(planes.shape[0]):
        for kt in range(4):
            sources = [planes[plane, c, kt * 8 : kt * 8 + 8, :] for c in range(4)]
            pl_out[plane * 4 + kt] = block_transposed(sources, slab, masks)


def maps_kernel(scal, active, yaw, ids, maps, counts, stage):
    own, slab = scal[0], scal[1]
    lane = lanes(XI)
    for g in range(GX):
        source = own ^ g
        left, mid, right = ids[source, 1], ids[source, 0], ids[source, 2]
        shift = (HALO - 32 * slab) & (LANES - 1)
        moved_mid = pltpu.roll(mid, shift, axis=1)
        moved_left = pltpu.roll(left, HALO, axis=1)
        moved_right = pltpu.roll(right, OWN + HALO, axis=1)
        here = jnp.where((lane < HALO) & (slab == 0), moved_left, moved_mid)
        here = jnp.where((lane >= OWN + HALO) & (slab == 3), moved_right, here)
        stage[0, g * XI : (g + 1) * XI, :] = here
    here = stage[0]

    def per_turbine(t, carry):
        sector, running = carry
        match = here == t.astype(F32)
        return (
            jnp.where(match, yaw[t].astype(F32), sector),
            jnp.where(match, active[t].astype(F32), running),
        )

    none = jnp.full((GX * XI, LANES), -1.0, F32)
    sector, running = lax.fori_loop(
        0, active.shape[0], per_turbine, (none, jnp.zeros((GX * XI, LANES), F32))
    )
    cosine = jnp.zeros((GX * XI, LANES), F32)
    sine = jnp.zeros((GX * XI, LANES), F32)
    for value in range(8):
        angle = (value - 3.5) * YAW_INCREMENT
        cosine = jnp.where(sector == value, F32(math.cos(angle)), cosine)
        sine = jnp.where(sector == value, F32(math.sin(angle)), sine)
    thrust = running * F32(-0.5 * THRUST_COEFF * TIME_STEP / float(WIDTH**2) ** 2)
    low = lanes(GX * XI) < 64
    stage[0] = jnp.where(low, here, pltpu.roll(thrust, 64, axis=1))
    stage[1] = jnp.where(low, cosine, pltpu.roll(sine, 64, axis=1))
    level = lanes(EXT) & (NZ - 1)
    band = (level >= LOWEST) & (level < LOWEST + WIDTH)
    row = lax.broadcasted_iota(jnp.int32, (EXT, LANES), 0)
    outside = jnp.full((8, LANES), -2.0, F32)
    for xi in range(XI):
        pair = []
        for which in range(2):
            rows = [
                jnp.broadcast_to(stage[which, g * XI + xi : g * XI + xi + 1, :], (NZ, LANES))
                for g in range(GX)
            ]
            pair.append(jnp.concatenate(rows, axis=0).T)
        ident = pair[0][:EXT]
        cos_u = jnp.where(band, pair[1][:EXT], 0.0)
        sin_v = jnp.where(band, pair[1][64 : 64 + EXT], 0.0)
        maps[0, xi, 0:8, :] = outside
        maps[0, xi, 8 : 8 + EXT, :] = ident
        maps[0, xi, 8 + EXT : PAD, :] = outside
        maps[1, xi, 8 : 8 + EXT, :] = cos_u
        maps[2, xi, 8 : 8 + EXT, :] = sin_v
        maps[3, xi, 8 : 8 + EXT, :] = pair[0][64 : 64 + EXT]
        for which in (1, 2, 3):
            maps[which, xi, 0:8, :] = jnp.zeros((8, LANES), F32)
            maps[which, xi, 8 + EXT : PAD, :] = jnp.zeros((8, LANES), F32)
        first, final = ident[:1], ident[EXT - 1 :]
        beyond = (ident == first) & (row > 0)
        before = (ident == final) & (row < EXT - 1)
        left_count = WIDTH - jnp.sum(jnp.where(beyond, 1.0, 0.0), axis=0, keepdims=True)
        right_count = WIDTH - jnp.sum(jnp.where(before, 1.0, 0.0), axis=0, keepdims=True)
        counts[0, xi : xi + 1, :] = jnp.where(first >= 0.0, left_count * cos_u[:1], 0.0)
        counts[1, xi : xi + 1, :] = jnp.where(final >= 0.0, right_count * cos_u[EXT - 1 :], 0.0)


def disk_edges(fields, maps, su, sd):
    row24 = lax.broadcasted_iota(jnp.int32, (24, LANES), 0)
    for xi in range(XI):
        base = 8 + HALO
        ident = maps[0, xi, base + 8 : base + 32, :]
        normal = (
            maps[1, xi, base + 8 : base + 32, :] * fields[0, xi, 8:32, :]
            + maps[2, xi, base + 8 : base + 32, :] * fields[1, xi, 8:32, :]
        )
        take = (ident == ident[16:17]) & (row24 <= 16)
        su[TILES + xi // 8, xi % 8 : xi % 8 + 1, :] = jnp.sum(
            jnp.where(take, normal, 0.0), axis=0, keepdims=True
        )
        ident = maps[0, xi, base : base + 24, :]
        normal = (
            maps[1, xi, base : base + 24, :] * fields[0, xi, 0:24, :]
            + maps[2, xi, base : base + 24, :] * fields[1, xi, 0:24, :]
        )
        take = (ident == ident[7:8]) & (row24 >= 7)
        sd[TILES + xi // 8, xi % 8 : xi % 8 + 1, :] = jnp.sum(
            jnp.where(take, normal, 0.0), axis=0, keepdims=True
        )


def over_groups(row):
    row = row + pltpu.roll(row, 64, axis=1)
    return row + pltpu.roll(row, 32, axis=1)


def unpack_kernel(
    scal, slot, profile, maps, s0, r1, r2, r3, p0, *rest, layouts, per_layout
):
    plane_refs = (p0,) + rest[: layouts - 1]
    fields, inflow, su, sd, sums, held, planes = rest[layouts - 1 :]
    own, here = scal[0], scal[2]
    for s, source in enumerate((s0, r1, r2, r3)):
        held[own ^ s] = source[...]
    for s, source in enumerate(plane_refs):
        planes[here ^ s] = source[...]

    def per_row(xi, total):
        rows = [held[g, pl.ds(xi * 4, 4)].reshape(NZ, LANES) for g in range(GX)]
        turned = jnp.concatenate(rows, axis=0).T
        for c in range(4):
            value = turned[c * 32 : c * 32 + 32] + profile[c : c + 1, :]
            fields[c, xi] = value
            sd[c * XI + xi] = value[:HALO]
            su[c * XI + xi] = value[OWN - HALO :]
            if c == 3:
                total = total + jnp.sum(value, axis=0, keepdims=True)
        return total

    total = lax.fori_loop(0, XI, per_row, jnp.zeros((1, LANES), F32))
    sums[...] = jnp.broadcast_to(over_groups(total), (8, LANES))
    rows = []
    for step in range(STEPS):
        plane = slot[step]
        rows.append(
            planes[plane // per_layout, pl.ds((plane % per_layout) * 4, 4)].reshape(NZ, LANES)
        )
    turned = jnp.concatenate(rows, axis=0).T
    for c in range(4):
        value = turned[c * 32 : c * 32 + 32] + profile[c : c + 1, :]
        inflow[c] = value
        sd[TILES + 2 + c] = value[:HALO]
        su[TILES + 2 + c] = value[OWN - HALO :]
    disk_edges(fields, maps, su, sd)


def mean_response(mean):
    lane = lanes(XI)
    row = lax.broadcasted_iota(jnp.int32, (XI, LANES), 0)
    level = lane & (NZ - 1)
    first, last = level == 0, level == NZ - 1

    def x_pair(p):
        lower = pltpu.roll(p, 1, axis=0)
        edge = jnp.where(lane < 32, 0.0, pltpu.roll(lower, 32, axis=1))
        lower = jnp.where(row == 0, edge, lower)
        upper = pltpu.roll(p, XI - 1, axis=0)
        edge = jnp.where(lane >= 96, 0.0, pltpu.roll(upper, 96, axis=1))
        upper = jnp.where(row == XI - 1, edge, upper)
        return lower, upper

    vertical = jnp.broadcast_to(mean, (XI, LANES)) * F32(-TIME_STEP * BUOYANCY)
    up = jnp.where(last, 0.0, pltpu.roll(vertical, LANES - 1, axis=1))
    down = jnp.where(first, 0.0, pltpu.roll(vertical, 1, axis=1))
    source = (up - down) * 0.5
    p = source * F32(-SIXTH)
    for sweep in range(SWEEPS):
        lower, upper = x_pair(p)
        p = (lower + upper + 2.0 * p + above(p, last) + below(p, first) - source) * F32(SIXTH)
    lower, upper = x_pair(p)
    return (upper - lower) * -0.5, vertical - (above(p, last) - below(p, first)) * 0.5


def step_kernel(*refs, step, cells):
    refs = list(refs)
    fields_in, lo, hi, maps, counts, inflow_in = refs[:6]
    del refs[:6]
    mean = None
    if step > 0:
        mean = refs.pop(0)
    out = refs.pop(0)
    su = sd = sums = inflow_out = None
    if step < STEPS - 1:
        su, sd, sums = refs[:3]
        del refs[:3]
    if step == 0:
        inflow_out = refs.pop(0)
    f, v, r, pa, pb, ns, change, inflow = refs
    first, last = level_masks()
    lane_ext = lanes(EXT)
    body = slice(8, 8 + EXT)

    if step > 0:
        du, dw = mean_response(mean[0:1, :] * F32(1.0 / cells))
        change[0] = du
        change[1] = dw
        inflow[...] = inflow_in[...]
    else:
        for c in range(4):
            inflow[c, 0:8] = lo[TILES + 2 + c]
            inflow[c, 8 : 8 + OWN] = inflow_in[c]
            inflow[c, 8 + OWN : EXT] = hi[TILES + 2 + c]
        inflow_out[...] = inflow[...]

    def fill(xi, carry):
        for c in range(4):
            low, mid, high = lo[c * XI + xi], fields_in[c, xi], hi[c * XI + xi]
            if step > 0 and c in (0, 2):
                d = change[c // 2, pl.ds(xi, 1), :]
                low, mid, high = low + d, mid + d, high + d
            f[c, xi + 1, 8:16] = low
            f[c, xi + 1, 16 : 16 + OWN] = mid
            f[c, xi + 1, 16 + OWN : 8 + EXT] = high
        return carry

    lax.fori_loop(0, XI, fill, 0)
    shift = (LANES - 32 * step) % LANES

    def entry(c):
        value = inflow[c]
        return pltpu.roll(value, shift, axis=1) if shift else value

    for c in range(4):
        f[c, 0, body] = jnp.where(
            lane_ext < 32, entry(c), pltpu.roll(f[c, XI, body], 32, axis=1)
        )
        f[c, XI + 1, body] = jnp.where(
            lane_ext >= 96, f[c, XI, body], pltpu.roll(f[c, 1, body], 96, axis=1)
        )

    def normal_speed(xi, carry):
        ns[xi] = maps[1, xi] * f[0, xi + 1] + maps[2, xi] * f[1, xi + 1]
        return carry

    for c in range(2):
        for xi in range(XI):
            f[c, xi + 1, 0:8] = jnp.zeros((8, LANES), F32)
            f[c, xi + 1, 8 + EXT : PAD] = jnp.zeros((8, LANES), F32)
    lax.fori_loop(0, XI, normal_speed, 0)
    for xi in range(XI):
        left = lo[TILES + xi // 8, xi % 8 : xi % 8 + 1, :]
        right = hi[TILES + xi // 8, xi % 8 : xi % 8 + 1, :]
        if step > 0:
            left = left + counts[0, xi : xi + 1, :] * change[0, xi : xi + 1, :]
            right = right + counts[1, xi : xi + 1, :] * change[0, xi : xi + 1, :]
        ns[xi, 8:9, :] = left
        ns[xi, 7 + EXT : 8 + EXT, :] = right
    row_group = lax.broadcasted_iota(jnp.int32, (LANES, LANES), 0)
    col_group = lax.broadcasted_iota(jnp.int32, (LANES, LANES), 1)
    gather = jnp.where((row_group >> 5) == (col_group >> 5), 1.0, 0.0).astype(F32)

    def thrusts(xi, carry):
        speed = jnp.dot(ns[xi], gather, precision=lax.Precision.HIGHEST, preferred_element_type=F32)
        ident = maps[0, xi]
        forward = speed
        backward = speed
        for d in (1, 2, 4, 8):
            same = ident == pltpu.roll(ident, d, axis=0)
            forward = forward + jnp.where(same, pltpu.roll(forward, d, axis=0), 0.0)
            same = ident == pltpu.roll(ident, PAD - d, axis=0)
            backward = backward + jnp.where(same, pltpu.roll(backward, PAD - d, axis=0), 0.0)
        total = forward + backward - speed
        ns[xi] = maps[3, xi] * total * jnp.abs(total)
        return carry

    lax.fori_loop(0, XI, thrusts, 0)

    def tendencies(xi, total):
        for tile in range(EXT // 8):
            base = 8 + tile * 8
            centre, gx, gy, gz, lap = [], [], [], [], []
            for c in range(4):
                mid = f[c, xi + 1, base : base + 8, :]
                xm = f[c, xi, base : base + 8, :]
                xp = f[c, xi + 2, base : base + 8, :]
                ym = f[c, xi + 1, base - 1 : base + 7, :]
                yp = f[c, xi + 1, base + 1 : base + 9, :]
                if c == 2:
                    zm = jnp.where(first, 0.0, pltpu.roll(mid, 1, axis=1))
                    zp = jnp.where(last, 0.0, pltpu.roll(mid, LANES - 1, axis=1))
                else:
                    zm, zp = below(mid, first), above(mid, last)
                centre.append(mid)
                gx.append(xp - xm)
                gy.append(yp - ym)
                gz.append(zp - zm)
                lap.append((xp + xm) + (yp + ym) + (zp + zm) - 6.0 * mid)
            s_xy = gy[0] + gx[1]
            s_xz = gz[0] + gx[2]
            s_yz = gz[1] + gy[2]
            strain = jnp.sqrt(
                2.0 * (gx[0] * gx[0] + gy[1] * gy[1] + gz[2] * gz[2])
                + (s_xy * s_xy + s_xz * s_xz + s_yz * s_yz)
            )
            nu = F32(TIME_STEP * VISCOSITY) + F32(0.5 * TIME_STEP * SMAGORINSKY) * strain
            half = F32(0.5 * TIME_STEP)
            au, av, aw = half * centre[0], half * centre[1], half * centre[2]
            h = ns[xi, base : base + 8, :]
            for c in range(4):
                scale = nu * F32(DIFFUSIVITY_RATIO) if c == 3 else nu
                new = centre[c] + (scale * lap[c] - (au * gx[c] + av * gy[c] + aw * gz[c]))
                if c < 2:
                    new = new + maps[1 + c, xi, base : base + 8, :] * h
                elif c == 2:
                    new = new + F32(TIME_STEP * BUOYANCY) * centre[3]
                if c < 3:
                    v[c, xi + 1, base : base + 8, :] = new
                elif 1 <= tile <= 4:
                    out[3, xi, tile * 8 - 8 : tile * 8, :] = new
                    if sums is not None:
                        total = total + new
                        if tile == 1:
                            sd[3 * XI + xi] = new
                        if tile == 4:
                            su[3 * XI + xi] = new
        return total

    total = lax.fori_loop(0, XI, tendencies, jnp.zeros((8, LANES), F32))
    if sums is not None:
        total = over_groups(jnp.sum(total, axis=0, keepdims=True))
        sums[...] = jnp.broadcast_to(total, (8, LANES))

    v[0, 0, body] = jnp.where(lane_ext < 32, entry(0), pltpu.roll(v[0, XI, body], 32, axis=1))
    v[0, XI + 1, body] = jnp.where(
        lane_ext >= 96, v[0, XI, body], pltpu.roll(v[0, 1, body], 96, axis=1)
    )

    def divergence(xi, carry):
        for tile in range(EXT // 8):
            base = 8 + tile * 8
            here = slice(base, base + 8)
            w = v[2, xi + 1, here, :]
            up = jnp.where(last, 0.0, pltpu.roll(w, LANES - 1, axis=1))
            down = jnp.where(first, 0.0, pltpu.roll(w, 1, axis=1))
            total = (v[0, xi + 2, here, :] - v[0, xi, here, :]) + (up - down)
            total = total + (
                v[1, xi + 1, base + 1 : base + 9, :] - v[1, xi + 1, base - 1 : base + 7, :]
            )
            source = total * F32(0.5 * SIXTH)
            r[xi, tile * 8 : tile * 8 + 8, :] = source
            pa[xi + 1, here, :] = -source
        return carry

    lax.fori_loop(0, XI, divergence, 0)

    def ends(p):
        p[0, body] = jnp.where(lane_ext < 32, 0.0, pltpu.roll(p[XI, body], 32, axis=1))
        p[XI + 1, body] = jnp.where(lane_ext >= 96, 0.0, pltpu.roll(p[1, body], 96, axis=1))

    for sweep in range(SWEEPS):
        p, q = (pa, pb) if sweep % 2 == 0 else (pb, pa)
        ends(p)

        def relax(xi, carry, p=p, q=q):
            for tile in range(EXT // 8):
                base = 8 + tile * 8
                here = slice(base, base + 8)
                mid = p[xi + 1, here, :]
                beside = (p[xi, here, :] + p[xi + 2, here, :]) + (
                    p[xi + 1, base - 1 : base + 7, :] + p[xi + 1, base + 1 : base + 9, :]
                )
                beside = beside + (below(mid, first) + above(mid, last))
                q[xi + 1, here, :] = beside * F32(SIXTH) - r[xi, tile * 8 : tile * 8 + 8, :]
            return carry

        lax.fori_loop(0, XI, relax, 0)
    p = pa if SWEEPS % 2 == 0 else pb
    ends(p)

    def correct(xi, carry):
        for tile in range(1, 5):
            base = 8 + tile * 8
            here = slice(base, base + 8)
            mid = p[xi + 1, here, :]
            slopes = (
                p[xi + 2, here, :] - p[xi, here, :],
                p[xi + 1, base + 1 : base + 9, :] - p[xi + 1, base - 1 : base + 7, :],
                above(mid, last) - below(mid, first),
            )
            for c in range(3):
                new = v[c, xi + 1, here, :] - 0.5 * slopes[c]
                out[c, xi, tile * 8 - 8 : tile * 8, :] = new
                if sums is not None:
                    if tile == 1:
                        sd[c * XI + xi] = new
                    if tile == 4:
                        su[c * XI + xi] = new
        return carry

    lax.fori_loop(0, XI, correct, 0)
    if sums is not None:
        disk_edges(out, maps, su, sd)


def send_kernel(scal, fields, s0, s1, s2, s3, turned):
    own = scal[0]

    def per_row(xi, carry):
        rows = jnp.concatenate([fields[c, xi] for c in range(4)], axis=0)
        turned[...] = rows.T.reshape(GX, 4, 8, LANES)
        for s, out in enumerate((s0, s1, s2, s3)):
            out[pl.ds(xi * 4, 4)] = turned[own ^ s]
        return carry

    lax.fori_loop(0, XI, per_row, 0)


def final_kernel(scal, mean, s0, r1, r2, r3, out, columns, *, cells):
    own, slab = scal[0], scal[1]
    du, dw = mean_response(mean[0:1, :] * F32(1.0 / cells))
    pad = jnp.zeros((LANES - 2 * XI, LANES), F32)
    columns[...] = jnp.concatenate([du, dw, pad], axis=0).T
    own_columns = columns[pl.ds(pl.multiple_of(own * NZ, NZ), NZ), :]
    group = lanes() >> 5
    masks = [group == (slab ^ s) for s in range(4)]
    for x in range(XI):
        for kt in range(4):
            sources = [ref[x * 4 + kt] for ref in (s0, r1, r2, r3)]
            for c in range(4):
                value = None
                for s, source in enumerate(sources):
                    moved = pltpu.roll(source, (((slab ^ s) - c) & 3) * 32, axis=1)
                    value = moved if value is None else jnp.where(masks[s], moved, value)
                if c in (0, 2):
                    column = (0 if c == 0 else XI) + x
                    value = value + own_columns[kt * 8 : kt * 8 + 8, column : column + 1]
                out[c, x, kt * 8 : kt * 8 + 8, :] = value


def ring(groups):
    place = []
    for j in range(groups):
        for b in range(GX):
            i = b ^ (3 * (j & 1))
            place.append(i * groups + j)
    size = len(place)
    up = [(place[s], place[(s + 1) % size]) for s in range(size)]
    return up, [(b, a) for a, b in up]


def swapped(value, axis, size, distance):
    return lax.ppermute(value, axis, [(i, i ^ distance) for i in range(size)])


def reduced(sums, groups):
    distance = 1
    while distance < GX:
        sums = sums + swapped(sums, "gx", GX, distance)
        distance *= 2
    distance = 1
    while distance < groups:
        sums = sums + swapped(sums, "gy", groups, distance)
        distance *= 2
    return sums


def local(state, planes, turbine_cell, active, yaw_sector, slot, *, layouts, groups):
    gx_index, gy_index = lax.axis_index("gx"), lax.axis_index("gy")
    slab = gx_index ^ (3 * (gy_index & 1))
    scal = jnp.stack([gx_index, slab, lax.axis_index("layout")]).astype(jnp.int32)
    cells = float(GX * XI * GX * OWN * groups)
    per_layout = planes.shape[0]
    height = (jnp.arange(NZ).astype(F32) + 0.5) / NZ
    zeros = jnp.zeros((NZ,), F32)
    profile = jnp.tile(jnp.stack([height ** (1.0 / 7.0), zeros, zeros, 0.5 * height]), (1, GX))
    profile = jnp.pad(profile, ((0, 4), (0, 0)))
    up, down = ring(groups)
    gy_up = [(j, (j + 1) % groups) for j in range(groups)]
    gy_down = [(b, a) for a, b in gy_up]

    ids = turbine_cell[0, :, NZ // 2, :].astype(F32)
    ids = jnp.stack([ids, lax.ppermute(ids, "gy", gy_up), lax.ppermute(ids, "gy", gy_down)])

    chunk = shape(TILES, 8, LANES)
    s0, s1, s2, s3, plane = call(
        pack_kernel,
        (chunk, chunk, chunk, chunk, shape(per_layout * 4, 8, LANES)),
        [SMEM, VMEM, VMEM],
        name="pack",
    )(scal, state[0], planes)
    ids = jnp.stack([ids] + [swapped(ids, "gx", GX, s) for s in (1, 2, 3)])
    received = [swapped(value, "gx", GX, s) for s, value in ((1, s1), (2, s2), (3, s3))]
    plane_received = [swapped(plane, "layout", layouts, s) for s in range(1, layouts)]
    maps, counts = call(
        maps_kernel,
        (shape(4, XI, PAD, LANES), shape(2, XI, LANES)),
        [SMEM, SMEM, SMEM, VMEM],
        [pltpu.VMEM((2, GX * XI, LANES), F32)],
        name="maps",
    )(scal, active[0], yaw_sector[0], ids)

    first_payload = shape(TILES + 6, 8, LANES)
    fields, inflow, su, sd, sums = call(
        functools.partial(unpack_kernel, layouts=layouts, per_layout=per_layout),
        (
            shape(4, XI, OWN, LANES),
            shape(4, OWN, LANES),
            first_payload,
            first_payload,
            shape(8, LANES),
        ),
        [SMEM, SMEM, VMEM, VMEM] + [VMEM] * (4 + layouts),
        [
            pltpu.VMEM((GX, TILES, 8, LANES), F32),
            pltpu.VMEM((layouts, per_layout * 4, 8, LANES), F32),
        ],
        name="unpack",
    )(scal, slot, profile, maps, s0, *received, plane, *plane_received)

    mean = None
    for step in range(STEPS):
        lo = lax.ppermute(su, ("gx", "gy"), up)
        hi = lax.ppermute(sd, ("gx", "gy"), down)
        next_mean = reduced(sums, groups)
        outs = [shape(4, XI, OWN, LANES)]
        if step < STEPS - 1:
            outs += [shape(TILES + 2, 8, LANES), shape(TILES + 2, 8, LANES), shape(8, LANES)]
        if step == 0:
            outs += [shape(4, EXT, LANES)]
        operands = [fields, lo, hi, maps, counts, inflow] + ([mean] if step > 0 else [])
        results = call(
            functools.partial(step_kernel, step=step, cells=cells),
            tuple(outs),
            [VMEM] * len(operands),
            [
                pltpu.VMEM((4, XI + 2, PAD, LANES), F32),
                pltpu.VMEM((3, XI + 2, PAD, LANES), F32),
                pltpu.VMEM((XI, EXT, LANES), F32),
                pltpu.VMEM((XI + 2, PAD, LANES), F32),
                pltpu.VMEM((XI + 2, PAD, LANES), F32),
                pltpu.VMEM((XI, PAD, LANES), F32),
                pltpu.VMEM((2, XI, LANES), F32),
                pltpu.VMEM((4, EXT, LANES), F32),
            ],
            flops=30_000_000,
            name="step%d" % step,
        )(*operands)
        results = list(results)
        fields = results.pop(0)
        if step < STEPS - 1:
            su, sd, sums = results[:3]
            del results[:3]
        if step == 0:
            inflow = results.pop(0)
        mean = next_mean

    s0, s1, s2, s3 = call(
        send_kernel,
        (chunk, chunk, chunk, chunk),
        [SMEM, VMEM],
        [pltpu.VMEM((GX, 4, 8, LANES), F32)],
        name="send",
    )(scal, fields)
    received = [swapped(value, "gx", GX, s) for s, value in ((1, s1), (2, s2), (3, s3))]
    fields = call(
        functools.partial(final_kernel, cells=cells),
        shape(4, XI, NZ, LANES),
        [SMEM, VMEM] + [VMEM] * 4,
        [pltpu.VMEM((LANES, LANES), F32)],
        name="final",
    )(scal, mean, s0, *received)
    return fields[None]


def solution(mesh):
    body = functools.partial(local, layouts=mesh.shape["layout"], groups=mesh.shape["gy"])
    return jax.shard_map(
        body,
        mesh=mesh,
        in_specs=(
            P("layout", None, "gx", None, "gy"),
            P("layout", None, None, "gy"),
            P("layout", "gx", None, "gy"),
            P("layout", None),
            P("layout", None),
            P(),
        ),
        out_specs=P("layout", None, "gx", None, "gy"),
        check_vma=False,
    )
```

time: 814 us -> 219 us (0.27)
  blocking collectives: 234 us -> 0 us
  starting transfers between devices: 199 us -> 58.8 us
  waiting for transfers between devices: 193 us -> 77.3 us
  Pallas kernels: 0 us -> 74.1 us
  local copies, waits for them, and re-layouts: 62.5 us -> 5.11 us
  other arithmetic: 55.8 us -> 0.24 us
  matrix products: 30.7 us -> 0 us
  between operations: 26.2 us -> 0.16 us
    psum x4 -> x0, blocking collectives: 234 us -> none  [local(): theta_sum, disk_sums = lax.psum((theta_sum, disk_sums), ('gx', 'gy'))]
    ppermute x112 -> x42, starting transfers between devices: 199 us -> 58.8 us  [the longest x32 34.6 us: swapped(): return lax.ppermute(value, axis, [(i, i ^ distance) for i in range(size)])]
    ppermute x112 -> x42, waiting for transfers between devices: 193 us -> 77.3 us  [the longest x32 69.7 us: swapped(): return lax.ppermute(value, axis, [(i, i ^ distance) for i in range(size)])]
    pallas_call x0 -> x9, Pallas kernels: none -> 74.1 us  [the longest x4 61.3 us: local(): call(functools.partial(step_kernel, step=step, cells=cells), tuple(outs),...]
    slice x129 -> x1, local copies, waits for them, and re-layouts: 32.2 us -> 0.84 us  [local(): ids = turbine_cell[0, :, NZ // 2, :].astype(F32)]
    dot_general x48 -> x0, matrix products: 30.7 us -> none  [the longest x16 12.9 us: per_block(): sums = jnp.dot(normal, marked, precision=lax.Precision.HIGHEST)]
    concatenate x56 -> x0, other arithmetic: 22.8 us -> none  [padded_2(): array = jnp.concatenate([before, array, after], axis=dim)]
    ppermute x16 -> x0, local copies, waits for them, and re-layouts: 15 us -> none  [the longest x8 10.4 us: padded_2(): before = lax.ppermute(last, axis, up)]
  transfers between devices with their start and end apart: 113 -> 42, of which waited for: 80 -> 25; matrix products, arithmetic and copies ran while one was open for 5% -> 0% of each run, Pallas kernels for 0% -> 2%
where the time goes in v1:
time: 219 us; the launch traced here: 216 us
  waiting for transfers between devices  77.3 us (35%)
  Pallas kernels  74.1 us (34%)
  starting transfers between devices  58.8 us (27%)
  local copies, waits for them, and re-layouts  5.11 us (2%)
    ppermute x32, waiting for transfers between devices, swapped(): return lax.ppermute(value, axis, [(i, i ^ distance) for i in range(size)])  69.7 us
    pallas_call x4, Pallas kernels, local(): call(functools.partial(step_kernel, step=step, cells=cells), tuple(outs),...  61.3 us
    ppermute x32, starting transfers between devices, swapped(): return lax.ppermute(value, axis, [(i, i ^ distance) for i in range(size)])  34.6 us
    ppermute x4, starting transfers between devices, local(): lo = lax.ppermute(su, ('gx', 'gy'), up)  19.9 us
    ppermute x4, waiting for transfers between devices, local(): lo = lax.ppermute(su, ('gx', 'gy'), up)  6.66 us
  transfers between devices with their start and end apart: 42, of which 25 were waited for; matrix products, arithmetic and copies ran while one was open for 0% of the time, Pallas kernels for 2%

profile of v1, /device:TPU:1, one launch (start us, length us, event | category | flops | bytes accessed | tf_op | source)
XLA Modules:
  0.0 215.7 jit_solution(16636255193077769952)
XLA Ops:
  0.0 0.8 slice.3
  0.9 4.3 %collective-permute-start.1 = (f32[16,128]{1,0:T(8,128)S(1)}, f32[16,128]{1,0:T(8,128)S(1)}, u32[]{:S(2)}, u32[]{:S(2)}) collective-permute-start(f32[16,128]{1,0:T(8,128)S(1)} %get-tuple-element.66), channel_id=1, source_target_pairs={{1,0},{2,1},{3,2},{4,3},{5,4},{6,5},{7,6},{0,7},{9,8},{10,9},{11,1... | collective-permute-start | bytes 24584 | tf_op jit(solution)/shard_map/ppermute | solution.py:566
  5.3 1.2 copy-done
  6.5 0.9 copy-done.1
  7.4 2.8 %pack.1 = (f32[64,8,128]{2,1,0:T(8,128)S(1)}, f32[64,8,128]{2,1,0:T(8,128)S(1)}, f32[64,8,128]{2,1,0:T(8,128)S(1)}, f32[64,8,128]{2,1,0:T(8,128)S(1)}, f32[8,8,128]{2,1,0:T(8,128)S(1)}) custom-call(s32[3]{0:T(128)S(1)} %pad_add_fusion.scal, f32[4,16,32,128]{3,2,1,0:T(8,128)S(1)} %bitcast.19, f32[2,4,32,128]{3,2,1,0:T(8,128)S(1)} %copy-done.1), custom_call_target="tpu_custom_call" | custom-call | flops 10000000 | bytes 4000000 | tf_op jit(solution)/shard_map/pack/pallas_call | solution.py:569
  10.2 3.8 %collective-permute-start.10 = (f32[8,8,128]{2,1,0:T(8,128)S(1)}, f32[8,8,128]{2,1,0:T(8,128)S(1)}, u32[]{:S(2)}, u32[]{:S(2)}) collective-permute-start(f32[8,8,128]{2,1,0:T(8,128)S(1)} %get-tuple-element.39.p0), channel_id=1, source_target_pairs={{0,96},{32,64},{64,32},{96,0},{1,97},{33,65},{65,33},{97,1},{2,98}... | collective-permute-start | bytes 98312 | tf_op jit(solution)/shard_map/ppermute | solution.py:536
  14.0 1.2 collective-permute-start.5
  15.2 2.6 %collective-permute-start.6 = (f32[64,8,128]{2,1,0:T(8,128)S(1)}, f32[64,8,128]{2,1,0:T(8,128)S(1)}, u32[]{:S(2)}, u32[]{:S(2)}) collective-permute-start(f32[64,8,128]{2,1,0:T(8,128)S(1)} %get-tuple-element.37), channel_id=1, source_target_pairs={{0,16},{8,24},{16,0},{24,8},{1,17},{9,25},{17,1},{25,9},{2,18},{10... | collective-permute-start | bytes 786440 | tf_op jit(solution)/shard_map/ppermute | solution.py:536
  17.9 0.4 collective-permute-start.3
  18.3 0.6 collective-permute-start.2
  19.0 6.2 %collective-permute-done.3 = f32[3,16,128]{2,1,0:T(8,128)S(1)} collective-permute-done((f32[3,16,128]{2,1,0:T(8,128)S(1)}, f32[3,16,128]{2,1,0:T(8,128)S(1)}, u32[]{:S(2)}, u32[]{:S(2)}) %collective-permute-start.3) | collective-permute-done | bytes 24608 | tf_op jit(solution)/shard_map/ppermute | solution.py:536
  25.2 3.3 %collective-permute-start.7 = (f32[64,8,128]{2,1,0:T(8,128)S(1)}, f32[64,8,128]{2,1,0:T(8,128)S(1)}, u32[]{:S(2)}, u32[]{:S(2)}) collective-permute-start(f32[64,8,128]{2,1,0:T(8,128)S(1)} %get-tuple-element.38), channel_id=1, source_target_pairs={{0,24},{8,16},{16,8},{24,0},{1,25},{9,17},{17,9},{25,1},{2,26},{10... | collective-permute-start | bytes 786440 | tf_op jit(solution)/shard_map/ppermute | solution.py:536
  28.6 0.1 tile.10
  28.7 7.4 %collective-permute-done.4 = f32[3,16,128]{2,1,0:T(8,128)S(1)} collective-permute-done((f32[3,16,128]{2,1,0:T(8,128)S(1)}, f32[3,16,128]{2,1,0:T(8,128)S(1)}, u32[]{:S(2)}, u32[]{:S(2)}) %collective-permute-start.4) | collective-permute-done | bytes 24608 | tf_op jit(solution)/shard_map/ppermute | solution.py:536
  36.1 0.4 collective-permute-start.8
  36.5 0.6 copy-done.2
  37.2 0.7 copy-done.3
  37.8 2.1 maps.1
  39.9 0.5 collective-permute-done.9.rest_1_
  40.4 0.6 copy-done.4
  41.1 2.6 %unpack.1 = (f32[4,16,32,128]{3,2,1,0:T(8,128)S(1)}, f32[4,32,128]{2,1,0:T(8,128)S(1)}, f32[70,8,128]{2,1,0:T(8,128)S(1)}, f32[70,8,128]{2,1,0:T(8,128)S(1)}, f32[8,128]{1,0:T(8,128)S(1)}) custom-call(s32[3]{0:T(128)S(1)} %pad_add_fusion.scal, s32[4]{0:T(128)S(1)} %copy-done.4, f32[8,128]{1,0:T(8,128)S(1)} %pad.4.profile, ...), custom_call_target="tpu_custom_call" | custom-call | flops 10000000 | bytes 4000000 | tf_op jit(solution)/shard_map/unpack/pallas_call | solution.py:587
  43.6 4.1 %collective-permute-start.11 = (f32[70,8,128]{2,1,0:T(8,128)S(1)}, f32[70,8,128]{2,1,0:T(8,128)S(1)}, u32[]{:S(2)}, u32[]{:S(2)}) collective-permute-start(f32[70,8,128]{2,1,0:T(8,128)S(1)} %get-tuple-element.41), channel_id=1, source_target_pairs={{0,8},{8,16},{16,24},{24,25},{25,17},{17,9},{9,1},{1,2},{2,10},{10... | collective-permute-start | bytes 860168 | tf_op jit(solution)/shard_map/ppermute | solution.py:606
  47.8 6.6 %collective-permute-done.11.refs_1_ = f32[70,8,128]{2,1,0:T(8,128)S(1)} collective-permute-done((f32[70,8,128]{2,1,0:T(8,128)S(1)}, f32[70,8,128]{2,1,0:T(8,128)S(1)}, u32[]{:S(2)}, u32[]{:S(2)}) %collective-permute-start.11) | collective-permute-done | bytes 286752 | tf_op jit(solution)/shard_map/ppermute | solution.py:606
  54.4 0.9 collective-permute-done.12.refs_2_
  55.3 15.0 %step0.1 = (f32[4,16,32,128]{3,2,1,0:T(8,128)S(1)}, f32[66,8,128]{2,1,0:T(8,128)S(1)}, f32[66,8,128]{2,1,0:T(8,128)S(1)}, f32[8,128]{1,0:T(8,128)S(1)}, f32[4,48,128]{2,1,0:T(8,128)S(1)}) custom-call(f32[4,16,32,128]{3,2,1,0:T(8,128)S(1)} %get-tuple-element.40.refs_0_, f32[70,8,128]{2,1,0:T(8,128)S(1)} %collective-permute-done.11.refs_1_, ...), custom_call_target="tpu_custom_call" | custom-call | flops 30000000 | bytes 4000000 | tf_op jit(solution)/shard_map/step0/pallas_call | solution.py:615
  70.3 3.2 %collective-permute-start.13 = (f32[66,8,128]{2,1,0:T(8,128)S(1)}, f32[66,8,128]{2,1,0:T(8,128)S(1)}, u32[]{:S(2)}, u32[]{:S(2)}) collective-permute-start(f32[66,8,128]{2,1,0:T(8,128)S(1)} %get-tuple-element.46), channel_id=1, source_target_pairs={{0,8},{8,16},{16,24},{24,25},{25,17},{17,9},{9,1},{1,2},{2,10},{10... | collective-permute-start | bytes 811016 | tf_op jit(solution)/shard_map/ppermute | solution.py:606
  73.5 1.2 collective-permute-done.15
  74.7 3.0 %collective-permute-start.16 = (f32[8,128]{1,0:T(8,128)S(1)}, f32[8,128]{1,0:T(8,128)S(1)}, u32[]{:S(2)}, u32[]{:S(2)}) collective-permute-start(f32[8,128]{1,0:T(8,128)S(1)} %add.79), channel_id=1, source_target_pairs={{0,16},{8,24},{16,0},{24,8},{1,17},{9,25},{17,1},{25,9},{2,18},{10... | collective-permute-start | bytes 12296 | tf_op jit(solution)/shard_map/ppermute | solution.py:536
  77.7 1.0 collective-permute-done.16
  78.7 2.6 %collective-permute-done.17 = f32[8,128]{1,0:T(8,128)S(1)} collective-permute-done((f32[8,128]{1,0:T(8,128)S(1)}, f32[8,128]{1,0:T(8,128)S(1)}, u32[]{:S(2)}, u32[]{:S(2)}) %collective-permute-start.17) | collective-permute-done | bytes 4128 | tf_op jit(solution)/shard_map/ppermute | solution.py:536
  81.3 3.4 %collective-permute-start.18 = (f32[8,128]{1,0:T(8,128)S(1)}, f32[8,128]{1,0:T(8,128)S(1)}, u32[]{:S(2)}, u32[]{:S(2)}) collective-permute-start(f32[8,128]{1,0:T(8,128)S(1)} %add.81), channel_id=1, source_target_pairs={{0,2},{1,3},{2,0},{3,1},{4,6},{5,7},{6,4},{7,5},{8,10},{9,11},{10,... | collective-permute-start | bytes 12296 | tf_op jit(solution)/shard_map/ppermute | solution.py:536
  84.7 1.0 collective-permute-done.18
  85.7 0.5 collective-permute-start.19
  86.1 2.0 collective-permute-done.19
  88.1 15.5 %step1.1 = (f32[4,16,32,128]{3,2,1,0:T(8,128)S(1)}, f32[66,8,128]{2,1,0:T(8,128)S(1)}, f32[66,8,128]{2,1,0:T(8,128)S(1)}, f32[8,128]{1,0:T(8,128)S(1)}) custom-call(f32[4,16,32,128]{3,2,1,0:T(8,128)S(1)} %get-tuple-element.45.refs_0_, f32[66,8,128]{2,1,0:T(8,128)S(1)} %collective-permute-done.13.refs_1_, f32[66,8,128]{2,1,0:T(8,128)S(1)} %collective-permute-done.14.refs_2_, ...), custom_call_target="tpu_custom_call" | custom-call | flops 30000000 | bytes 4000000 | tf_op jit(solution)/shard_map/step1/pallas_call | solution.py:615
  103.6 7.3 %collective-permute-start.20 = (f32[66,8,128]{2,1,0:T(8,128)S(1)}, f32[66,8,128]{2,1,0:T(8,128)S(1)}, u32[]{:S(2)}, u32[]{:S(2)}) collective-permute-start(f32[66,8,128]{2,1,0:T(8,128)S(1)} %get-tuple-element.51), channel_id=1, source_target_pairs={{0,8},{8,16},{16,24},{24,25},{25,17},{17,9},{9,1},{1,2},{2,10},{10... | collective-permute-start | bytes 811016 | tf_op jit(solution)/shard_map/ppermute | solution.py:606
  111.0 2.8 %collective-permute-start.22 = (f32[8,128]{1,0:T(8,128)S(1)}, f32[8,128]{1,0:T(8,128)S(1)}, u32[]{:S(2)}, u32[]{:S(2)}) collective-permute-start(f32[8,128]{1,0:T(8,128)S(1)} %get-tuple-element.53), channel_id=1, source_target_pairs={{0,8},{8,0},{16,24},{24,16},{1,9},{9,1},{17,25},{25,17},{2,10},{10... | collective-permute-start | bytes 12296 | tf_op jit(solution)/shard_map/ppermute | solution.py:536
  113.7 0.8 collective-permute-done.22
  114.6 0.6 collective-permute-start.23
  115.2 3.4 %collective-permute-done.23 = f32[8,128]{1,0:T(8,128)S(1)} collective-permute-done((f32[8,128]{1,0:T(8,128)S(1)}, f32[8,128]{1,0:T(8,128)S(1)}, u32[]{:S(2)}, u32[]{:S(2)}) %collective-permute-start.23) | collective-permute-done | bytes 4128 | tf_op jit(solution)/shard_map/ppermute | solution.py:536
  118.5 2.5 %collective-permute-done.24 = f32[8,128]{1,0:T(8,128)S(1)} collective-permute-done((f32[8,128]{1,0:T(8,128)S(1)}, f32[8,128]{1,0:T(8,128)S(1)}, u32[]{:S(2)}, u32[]{:S(2)}) %collective-permute-start.24) | collective-permute-done | bytes 4128 | tf_op jit(solution)/shard_map/ppermute | solution.py:536
  121.0 4.0 %collective-permute-done.25 = f32[8,128]{1,0:T(8,128)S(1)} collective-permute-done((f32[8,128]{1,0:T(8,128)S(1)}, f32[8,128]{1,0:T(8,128)S(1)}, u32[]{:S(2)}, u32[]{:S(2)}) %collective-permute-start.25) | collective-permute-done | bytes 4128 | tf_op jit(solution)/shard_map/ppermute | solution.py:536
  125.0 2.7 %collective-permute-done.26 = f32[8,128]{1,0:T(8,128)S(1)} collective-permute-done((f32[8,128]{1,0:T(8,128)S(1)}, f32[8,128]{1,0:T(8,128)S(1)}, u32[]{:S(2)}, u32[]{:S(2)}) %collective-permute-start.26) | collective-permute-done | bytes 4128 | tf_op jit(solution)/shard_map/ppermute | solution.py:536
  127.7 15.5 %step2.1 = (f32[4,16,32,128]{3,2,1,0:T(8,128)S(1)}, f32[66,8,128]{2,1,0:T(8,128)S(1)}, f32[66,8,128]{2,1,0:T(8,128)S(1)}, f32[8,128]{1,0:T(8,128)S(1)}) custom-call(f32[4,16,32,128]{3,2,1,0:T(8,128)S(1)} %get-tuple-element.50.refs_0_, f32[66,8,128]{2,1,0:T(8,128)S(1)} %collective-permute-done.20.refs_1_, f32[66,8,128]{2,1,0:T(8,128)S(1)} %collective-permute-done.21.refs_2_, ...), custom_call_target="tpu_custom_call" | custom-call | flops 30000000 | bytes 4000000 | tf_op jit(solution)/shard_map/step2/pallas_call | solution.py:615
  143.2 5.3 %collective-permute-start.32 = (f32[66,8,128]{2,1,0:T(8,128)S(1)}, f32[66,8,128]{2,1,0:T(8,128)S(1)}, u32[]{:S(2)}, u32[]{:S(2)}) collective-permute-start(f32[66,8,128]{2,1,0:T(8,128)S(1)} %get-tuple-element.56), channel_id=1, source_target_pairs={{0,8},{8,16},{16,24},{24,25},{25,17},{17,9},{9,1},{1,2},{2,10},{10... | collective-permute-start | bytes 811016 | tf_op jit(solution)/shard_map/ppermute | solution.py:606
  148.6 3.5 %collective-permute-start.34 = (f32[8,128]{1,0:T(8,128)S(1)}, f32[8,128]{1,0:T(8,128)S(1)}, u32[]{:S(2)}, u32[]{:S(2)}) collective-permute-start(f32[8,128]{1,0:T(8,128)S(1)} %get-tuple-element.58), channel_id=1, source_target_pairs={{0,8},{8,0},{16,24},{24,16},{1,9},{9,1},{17,25},{25,17},{2,10},{10... | collective-permute-start | bytes 12296 | tf_op jit(solution)/shard_map/ppermute | solution.py:536
  152.1 0.8 collective-permute-done.34
  152.9 4.0 %collective-permute-done.35 = f32[8,128]{1,0:T(8,128)S(1)} collective-permute-done((f32[8,128]{1,0:T(8,128)S(1)}, f32[8,128]{1,0:T(8,128)S(1)}, u32[]{:S(2)}, u32[]{:S(2)}) %collective-permute-start.35) | collective-permute-done | bytes 4128 | tf_op jit(solution)/shard_map/ppermute | solution.py:536
  156.9 2.5 %collective-permute-done.36 = f32[8,128]{1,0:T(8,128)S(1)} collective-permute-done((f32[8,128]{1,0:T(8,128)S(1)}, f32[8,128]{1,0:T(8,128)S(1)}, u32[]{:S(2)}, u32[]{:S(2)}) %collective-permute-start.36) | collective-permute-done | bytes 4128 | tf_op jit(solution)/shard_map/ppermute | solution.py:536
  159.4 4.0 %collective-permute-done.37 = f32[8,128]{1,0:T(8,128)S(1)} collective-permute-done((f32[8,128]{1,0:T(8,128)S(1)}, f32[8,128]{1,0:T(8,128)S(1)}, u32[]{:S(2)}, u32[]{:S(2)}) %collective-permute-start.37) | collective-permute-done | bytes 4128 | tf_op jit(solution)/shard_map/ppermute | solution.py:536
  163.3 2.7 %collective-permute-done.38 = f32[8,128]{1,0:T(8,128)S(1)} collective-permute-done((f32[8,128]{1,0:T(8,128)S(1)}, f32[8,128]{1,0:T(8,128)S(1)}, u32[]{:S(2)}, u32[]{:S(2)}) %collective-permute-start.38) | collective-permute-done | bytes 4128 | tf_op jit(solution)/shard_map/ppermute | solution.py:536
  166.1 15.3 %step3.1.fields = f32[4,16,32,128]{3,2,1,0:T(8,128)S(1)} custom-call(f32[4,16,32,128]{3,2,1,0:T(8,128)S(1)} %get-tuple-element.55.refs_0_, f32[66,8,128]{2,1,0:T(8,128)S(1)} %collective-permute-done.32.refs_1_, f32[66,8,128]{2,1,0:T(8,128)S(1)} %collective-permute-done.33.refs_2_, f32[4,16,64,128]{3,2,1,0:T(8,128)S(1)} %get-tuple-element.34.maps.refs_3_, ...), custom_call_target="tpu_custom_call" | custom-call | flops 30000000 | bytes 4000000 | tf_op jit(solution)/shard_map/step3/pallas_call | solution.py:615
  181.4 2.2 %send.1 = (f32[64,8,128]{2,1,0:T(8,128)S(1)}, f32[64,8,128]{2,1,0:T(8,128)S(1)}, f32[64,8,128]{2,1,0:T(8,128)S(1)}, f32[64,8,128]{2,1,0:T(8,128)S(1)}) custom-call(s32[3]{0:T(128)S(1)} %pad_add_fusion.scal, f32[4,16,32,128]{3,2,1,0:T(8,128)S(1)} %step3.1.fields), custom_call_target="tpu_custom_call" | custom-call | flops 10000000 | bytes 4000000 | tf_op jit(solution)/shard_map/send/pallas_call | solution.py:641
  183.7 4.7 %collective-permute-start.39 = (f32[64,8,128]{2,1,0:T(8,128)S(1)}, f32[64,8,128]{2,1,0:T(8,128)S(1)}, u32[]{:S(2)}, u32[]{:S(2)}) collective-permute-start(f32[64,8,128]{2,1,0:T(8,128)S(1)} %get-tuple-element.60), channel_id=1, source_target_pairs={{0,8},{8,0},{16,24},{24,16},{1,9},{9,1},{17,25},{25,17},{2,10},{10... | collective-permute-start | bytes 786440 | tf_op jit(solution)/shard_map/ppermute | solution.py:536
  188.4 0.2 collective-permute-start.40
  188.6 3.0 %collective-permute-start.41 = (f32[64,8,128]{2,1,0:T(8,128)S(1)}, f32[64,8,128]{2,1,0:T(8,128)S(1)}, u32[]{:S(2)}, u32[]{:S(2)}) collective-permute-start(f32[64,8,128]{2,1,0:T(8,128)S(1)} %get-tuple-element.62), channel_id=1, source_target_pairs={{0,24},{8,16},{16,8},{24,0},{1,25},{9,17},{17,9},{25,1},{2,26},{10... | collective-permute-start | bytes 786440 | tf_op jit(solution)/shard_map/ppermute | solution.py:536
  191.6 0.2 collective-permute-start.27
  191.7 1.0 collective-permute-done.27
  192.8 0.2 collective-permute-start.28
  193.0 10.4 %collective-permute-done.28 = f32[8,128]{1,0:T(8,128)S(1)} collective-permute-done((f32[8,128]{1,0:T(8,128)S(1)}, f32[8,128]{1,0:T(8,128)S(1)}, u32[]{:S(2)}, u32[]{:S(2)}) %collective-permute-start.28) | collective-permute-done | bytes 4128 | tf_op jit(solution)/shard_map/ppermute | solution.py:536
  203.4 2.5 %collective-permute-done.29 = f32[8,128]{1,0:T(8,128)S(1)} collective-permute-done((f32[8,128]{1,0:T(8,128)S(1)}, f32[8,128]{1,0:T(8,128)S(1)}, u32[]{:S(2)}, u32[]{:S(2)}) %collective-permute-start.29) | collective-permute-done | bytes 4128 | tf_op jit(solution)/shard_map/ppermute | solution.py:536
  205.8 4.0 %collective-permute-done.30 = f32[8,128]{1,0:T(8,128)S(1)} collective-permute-done((f32[8,128]{1,0:T(8,128)S(1)}, f32[8,128]{1,0:T(8,128)S(1)}, u32[]{:S(2)}, u32[]{:S(2)}) %collective-permute-start.30) | collective-permute-done | bytes 4128 | tf_op jit(solution)/shard_map/ppermute | solution.py:536
  209.8 2.7 %collective-permute-done.31 = f32[8,128]{1,0:T(8,128)S(1)} collective-permute-done((f32[8,128]{1,0:T(8,128)S(1)}, f32[8,128]{1,0:T(8,128)S(1)}, u32[]{:S(2)}, u32[]{:S(2)}) %collective-permute-start.31) | collective-permute-done | bytes 4128 | tf_op jit(solution)/shard_map/ppermute | solution.py:536
  212.6 3.1 %final.1 = f32[4,16,32,128]{3,2,1,0:T(8,128)} custom-call(s32[3]{0:T(128)S(1)} %pad_add_fusion.scal, f32[8,128]{1,0:T(8,128)S(1)} %add.93.mean, f32[64,8,128]{2,1,0:T(8,128)S(1)} %get-tuple-element.59.s0, f32[64,8,128]{2,1,0:T(8,128)S(1)} %collective-permute-done.39.r1, f32[64,8,128]{2,1,0:T(8,128)S(1)} %collective-permute-done.40.r2, ...), custom_call_target="tpu_custom_call" | custom-call | flops 10000000 | bytes 4000000 | tf_op jit(solution)/shard_map/final/pallas_call | solution.py:649
  (71 shorter events, 0.5 us)
Async XLA Ops:
  0.9 17.0 %collective-permute-start.1 = (f32[16,128]{1,0:T(8,128)S(1)}, f32[16,128]{1,0:T(8,128)S(1)}, u32[]{:S(2)}, u32[]{:S(2)}) collective-permute-start(f32[16,128]{1,0:T(8,128)S(1)} %get-tuple-element.66), channel_id=1, source_target_pairs={{1,0},{2,1},{3,2},{4,3},{5,4},{6,5},{7,6},{0,7},{9,8},{10,9},{11,1... | collective-permute-start | bytes 24584 | tf_op jit(solution)/shard_map/ppermute | solution.py:566
  5.2 12.7 %collective-permute-start = (f32[16,128]{1,0:T(8,128)S(1)}, f32[16,128]{1,0:T(8,128)S(1)}, u32[]{:S(2)}, u32[]{:S(2)}) collective-permute-start(f32[16,128]{1,0:T(8,128)S(1)} %get-tuple-element.66), channel_id=1, source_target_pairs={{0,1},{1,2},{2,3},{3,4},{4,5},{5,6},{6,7},{7,0},{8,9},{9,10},{10,1... | collective-permute-start | bytes 24584 | tf_op jit(solution)/shard_map/ppermute | solution.py:566
  5.3 1.2 copy-start
  6.5 0.9 copy-start.1
  10.2 26.0 %collective-permute-start.10 = (f32[8,8,128]{2,1,0:T(8,128)S(1)}, f32[8,8,128]{2,1,0:T(8,128)S(1)}, u32[]{:S(2)}, u32[]{:S(2)}) collective-permute-start(f32[8,8,128]{2,1,0:T(8,128)S(1)} %get-tuple-element.39.p0), channel_id=1, source_target_pairs={{0,96},{32,64},{64,32},{96,0},{1,97},{33,65},{65,33},{97,1},{2,98}... | collective-permute-start | bytes 98312 | tf_op jit(solution)/shard_map/ppermute | solution.py:536
  14.0 26.4 %collective-permute-start.5 = (f32[64,8,128]{2,1,0:T(8,128)S(1)}, f32[64,8,128]{2,1,0:T(8,128)S(1)}, u32[]{:S(2)}, u32[]{:S(2)}) collective-permute-start(f32[64,8,128]{2,1,0:T(8,128)S(1)} %get-tuple-element.36), channel_id=1, source_target_pairs={{0,8},{8,0},{16,24},{24,16},{1,9},{9,1},{17,25},{25,17},{2,10},{10... | collective-permute-start | bytes 786440 | tf_op jit(solution)/shard_map/ppermute | solution.py:536
  15.2 25.2 %collective-permute-start.6 = (f32[64,8,128]{2,1,0:T(8,128)S(1)}, f32[64,8,128]{2,1,0:T(8,128)S(1)}, u32[]{:S(2)}, u32[]{:S(2)}) collective-permute-start(f32[64,8,128]{2,1,0:T(8,128)S(1)} %get-tuple-element.37), channel_id=1, source_target_pairs={{0,16},{8,24},{16,0},{24,8},{1,17},{9,25},{17,1},{25,9},{2,18},{10... | collective-permute-start | bytes 786440 | tf_op jit(solution)/shard_map/ppermute | solution.py:536
  17.9 7.3 %collective-permute-start.3 = (f32[3,16,128]{2,1,0:T(8,128)S(1)}, f32[3,16,128]{2,1,0:T(8,128)S(1)}, u32[]{:S(2)}, u32[]{:S(2)}) collective-permute-start(f32[3,16,128]{2,1,0:T(8,128)S(1)} %get-tuple-element.64), channel_id=1, source_target_pairs={{0,16},{8,24},{16,0},{24,8},{1,17},{9,25},{17,1},{25,9},{2,18},{10... | collective-permute-start | bytes 73736 | tf_op jit(solution)/shard_map/ppermute | solution.py:536
  18.3 10.2 %collective-permute-start.2 = (f32[3,16,128]{2,1,0:T(8,128)S(1)}, f32[3,16,128]{2,1,0:T(8,128)S(1)}, u32[]{:S(2)}, u32[]{:S(2)}) collective-permute-start(f32[3,16,128]{2,1,0:T(8,128)S(1)} %get-tuple-element.64), channel_id=1, source_target_pairs={{0,8},{8,0},{16,24},{24,16},{1,9},{9,1},{17,25},{25,17},{2,10},{10... | collective-permute-start | bytes 73736 | tf_op jit(solution)/shard_map/ppermute | solution.py:536
  25.2 15.2 %collective-permute-start.7 = (f32[64,8,128]{2,1,0:T(8,128)S(1)}, f32[64,8,128]{2,1,0:T(8,128)S(1)}, u32[]{:S(2)}, u32[]{:S(2)}) collective-permute-start(f32[64,8,128]{2,1,0:T(8,128)S(1)} %get-tuple-element.38), channel_id=1, source_target_pairs={{0,24},{8,16},{16,8},{24,0},{1,25},{9,17},{17,9},{25,1},{2,26},{10... | collective-permute-start | bytes 786440 | tf_op jit(solution)/shard_map/ppermute | solution.py:536
  28.5 7.6 %collective-permute-start.4 = (f32[3,16,128]{2,1,0:T(8,128)S(1)}, f32[3,16,128]{2,1,0:T(8,128)S(1)}, u32[]{:S(2)}, u32[]{:S(2)}) collective-permute-start(f32[3,16,128]{2,1,0:T(8,128)S(1)} %get-tuple-element.64), channel_id=1, source_target_pairs={{0,24},{8,16},{16,8},{24,0},{1,25},{9,17},{17,9},{25,1},{2,26},{10... | collective-permute-start | bytes 73736 | tf_op jit(solution)/shard_map/ppermute | solution.py:536
  36.1 4.3 %collective-permute-start.9 = (f32[8,8,128]{2,1,0:T(8,128)S(1)}, f32[8,8,128]{2,1,0:T(8,128)S(1)}, u32[]{:S(2)}, u32[]{:S(2)}) collective-permute-start(f32[8,8,128]{2,1,0:T(8,128)S(1)} %get-tuple-element.39.p0), channel_id=1, source_target_pairs={{0,64},{32,96},{64,0},{96,32},{1,65},{33,97},{65,1},{97,33},{2,66}... | collective-permute-start | bytes 98312 | tf_op jit(solution)/shard_map/ppermute | solution.py:536
  36.1 4.3 %collective-permute-start.8 = (f32[8,8,128]{2,1,0:T(8,128)S(1)}, f32[8,8,128]{2,1,0:T(8,128)S(1)}, u32[]{:S(2)}, u32[]{:S(2)}) collective-permute-start(f32[8,8,128]{2,1,0:T(8,128)S(1)} %get-tuple-element.39.p0), channel_id=1, source_target_pairs={{0,32},{32,0},{64,96},{96,64},{1,33},{33,1},{65,97},{97,65},{2,34}... | collective-permute-start | bytes 98312 | tf_op jit(solution)/shard_map/ppermute | solution.py:536
  36.5 0.7 copy-start.2
  37.2 0.7 copy-start.3
  40.4 0.7 copy-start.4
  43.6 10.8 %collective-permute-start.11 = (f32[70,8,128]{2,1,0:T(8,128)S(1)}, f32[70,8,128]{2,1,0:T(8,128)S(1)}, u32[]{:S(2)}, u32[]{:S(2)}) collective-permute-start(f32[70,8,128]{2,1,0:T(8,128)S(1)} %get-tuple-element.41), channel_id=1, source_target_pairs={{0,8},{8,16},{16,24},{24,25},{25,17},{17,9},{9,1},{1,2},{2,10},{10... | collective-permute-start | bytes 860168 | tf_op jit(solution)/shard_map/ppermute | solution.py:606
  47.8 7.6 %collective-permute-start.12 = (f32[70,8,128]{2,1,0:T(8,128)S(1)}, f32[70,8,128]{2,1,0:T(8,128)S(1)}, u32[]{:S(2)}, u32[]{:S(2)}) collective-permute-start(f32[70,8,128]{2,1,0:T(8,128)S(1)} %get-tuple-element.42), channel_id=1, source_target_pairs={{8,0},{16,8},{24,16},{25,24},{17,25},{9,17},{1,9},{2,1},{10,2},{18... | collective-permute-start | bytes 860168 | tf_op jit(solution)/shard_map/ppermute | solution.py:607
  70.3 17.8 %collective-permute-start.13 = (f32[66,8,128]{2,1,0:T(8,128)S(1)}, f32[66,8,128]{2,1,0:T(8,128)S(1)}, u32[]{:S(2)}, u32[]{:S(2)}) collective-permute-start(f32[66,8,128]{2,1,0:T(8,128)S(1)} %get-tuple-element.46), channel_id=1, source_target_pairs={{0,8},{8,16},{16,24},{24,25},{25,17},{17,9},{9,1},{1,2},{2,10},{10... | collective-permute-start | bytes 811016 | tf_op jit(solution)/shard_map/ppermute | solution.py:606
  73.5 14.6 %collective-permute-start.14 = (f32[66,8,128]{2,1,0:T(8,128)S(1)}, f32[66,8,128]{2,1,0:T(8,128)S(1)}, u32[]{:S(2)}, u32[]{:S(2)}) collective-permute-start(f32[66,8,128]{2,1,0:T(8,128)S(1)} %get-tuple-element.47), channel_id=1, source_target_pairs={{8,0},{16,8},{24,16},{25,24},{17,25},{9,17},{1,9},{2,1},{10,2},{18... | collective-permute-start | bytes 811016 | tf_op jit(solution)/shard_map/ppermute | solution.py:607
  73.5 1.2 collective-permute-start.15
  74.7 4.0 %collective-permute-start.16 = (f32[8,128]{1,0:T(8,128)S(1)}, f32[8,128]{1,0:T(8,128)S(1)}, u32[]{:S(2)}, u32[]{:S(2)}) collective-permute-start(f32[8,128]{1,0:T(8,128)S(1)} %add.79), channel_id=1, source_target_pairs={{0,16},{8,24},{16,0},{24,8},{1,17},{9,25},{17,1},{25,9},{2,18},{10... | collective-permute-start | bytes 12296 | tf_op jit(solution)/shard_map/ppermute | solution.py:536
  78.7 2.6 %collective-permute-start.17 = (f32[8,128]{1,0:T(8,128)S(1)}, f32[8,128]{1,0:T(8,128)S(1)}, u32[]{:S(2)}, u32[]{:S(2)}) collective-permute-start(f32[8,128]{1,0:T(8,128)S(1)} %add.80), channel_id=1, source_target_pairs={{0,1},{1,0},{2,3},{3,2},{4,5},{5,4},{6,7},{7,6},{8,9},{9,8},{10,11... | collective-permute-start | bytes 12296 | tf_op jit(solution)/shard_map/ppermute | solution.py:536
  81.3 4.4 %collective-permute-start.18 = (f32[8,128]{1,0:T(8,128)S(1)}, f32[8,128]{1,0:T(8,128)S(1)}, u32[]{:S(2)}, u32[]{:S(2)}) collective-permute-start(f32[8,128]{1,0:T(8,128)S(1)} %add.81), channel_id=1, source_target_pairs={{0,2},{1,3},{2,0},{3,1},{4,6},{5,7},{6,4},{7,5},{8,10},{9,11},{10,... | collective-permute-start | bytes 12296 | tf_op jit(solution)/shard_map/ppermute | solution.py:536
  85.7 2.5 %collective-permute-start.19 = (f32[8,128]{1,0:T(8,128)S(1)}, f32[8,128]{1,0:T(8,128)S(1)}, u32[]{:S(2)}, u32[]{:S(2)}) collective-permute-start(f32[8,128]{1,0:T(8,128)S(1)} %add.82), channel_id=1, source_target_pairs={{0,4},{1,5},{2,6},{3,7},{4,0},{5,1},{6,2},{7,3},{8,12},{9,13},{10,... | collective-permute-start | bytes 12296 | tf_op jit(solution)/shard_map/ppermute | solution.py:536
  103.6 24.1 %collective-permute-start.20 = (f32[66,8,128]{2,1,0:T(8,128)S(1)}, f32[66,8,128]{2,1,0:T(8,128)S(1)}, u32[]{:S(2)}, u32[]{:S(2)}) collective-permute-start(f32[66,8,128]{2,1,0:T(8,128)S(1)} %get-tuple-element.51), channel_id=1, source_target_pairs={{0,8},{8,16},{16,24},{24,25},{25,17},{17,9},{9,1},{1,2},{2,10},{10... | collective-permute-start | bytes 811016 | tf_op jit(solution)/shard_map/ppermute | solution.py:606
  111.0 16.8 %collective-permute-start.21 = (f32[66,8,128]{2,1,0:T(8,128)S(1)}, f32[66,8,128]{2,1,0:T(8,128)S(1)}, u32[]{:S(2)}, u32[]{:S(2)}) collective-permute-start(f32[66,8,128]{2,1,0:T(8,128)S(1)} %get-tuple-element.52), channel_id=1, source_target_pairs={{8,0},{16,8},{24,16},{25,24},{17,25},{9,17},{1,9},{2,1},{10,2},{18... | collective-permute-start | bytes 811016 | tf_op jit(solution)/shard_map/ppermute | solution.py:607
  111.0 3.6 %collective-permute-start.22 = (f32[8,128]{1,0:T(8,128)S(1)}, f32[8,128]{1,0:T(8,128)S(1)}, u32[]{:S(2)}, u32[]{:S(2)}) collective-permute-start(f32[8,128]{1,0:T(8,128)S(1)} %get-tuple-element.53), channel_id=1, source_target_pairs={{0,8},{8,0},{16,24},{24,16},{1,9},{9,1},{17,25},{25,17},{2,10},{10... | collective-permute-start | bytes 12296 | tf_op jit(solution)/shard_map/ppermute | solution.py:536
  114.6 4.0 %collective-permute-start.23 = (f32[8,128]{1,0:T(8,128)S(1)}, f32[8,128]{1,0:T(8,128)S(1)}, u32[]{:S(2)}, u32[]{:S(2)}) collective-permute-start(f32[8,128]{1,0:T(8,128)S(1)} %add.84), channel_id=1, source_target_pairs={{0,16},{8,24},{16,0},{24,8},{1,17},{9,25},{17,1},{25,9},{2,18},{10... | collective-permute-start | bytes 12296 | tf_op jit(solution)/shard_map/ppermute | solution.py:536
  118.5 2.5 %collective-permute-start.24 = (f32[8,128]{1,0:T(8,128)S(1)}, f32[8,128]{1,0:T(8,128)S(1)}, u32[]{:S(2)}, u32[]{:S(2)}) collective-permute-start(f32[8,128]{1,0:T(8,128)S(1)} %add.85), channel_id=1, source_target_pairs={{0,1},{1,0},{2,3},{3,2},{4,5},{5,4},{6,7},{7,6},{8,9},{9,8},{10,11... | collective-permute-start | bytes 12296 | tf_op jit(solution)/shard_map/ppermute | solution.py:536
  121.0 4.0 %collective-permute-start.25 = (f32[8,128]{1,0:T(8,128)S(1)}, f32[8,128]{1,0:T(8,128)S(1)}, u32[]{:S(2)}, u32[]{:S(2)}) collective-permute-start(f32[8,128]{1,0:T(8,128)S(1)} %add.86), channel_id=1, source_target_pairs={{0,2},{1,3},{2,0},{3,1},{4,6},{5,7},{6,4},{7,5},{8,10},{9,11},{10,... | collective-permute-start | bytes 12296 | tf_op jit(solution)/shard_map/ppermute | solution.py:536
  125.0 2.8 %collective-permute-start.26 = (f32[8,128]{1,0:T(8,128)S(1)}, f32[8,128]{1,0:T(8,128)S(1)}, u32[]{:S(2)}, u32[]{:S(2)}) collective-permute-start(f32[8,128]{1,0:T(8,128)S(1)} %add.87), channel_id=1, source_target_pairs={{0,4},{1,5},{2,6},{3,7},{4,0},{5,1},{6,2},{7,3},{8,12},{9,13},{10,... | collective-permute-start | bytes 12296 | tf_op jit(solution)/shard_map/ppermute | solution.py:536
  143.2 22.8 %collective-permute-start.32 = (f32[66,8,128]{2,1,0:T(8,128)S(1)}, f32[66,8,128]{2,1,0:T(8,128)S(1)}, u32[]{:S(2)}, u32[]{:S(2)}) collective-permute-start(f32[66,8,128]{2,1,0:T(8,128)S(1)} %get-tuple-element.56), channel_id=1, source_target_pairs={{0,8},{8,16},{16,24},{24,25},{25,17},{17,9},{9,1},{1,2},{2,10},{10... | collective-permute-start | bytes 811016 | tf_op jit(solution)/shard_map/ppermute | solution.py:606
  148.5 17.5 %collective-permute-start.33 = (f32[66,8,128]{2,1,0:T(8,128)S(1)}, f32[66,8,128]{2,1,0:T(8,128)S(1)}, u32[]{:S(2)}, u32[]{:S(2)}) collective-permute-start(f32[66,8,128]{2,1,0:T(8,128)S(1)} %get-tuple-element.57), channel_id=1, source_target_pairs={{8,0},{16,8},{24,16},{25,24},{17,25},{9,17},{1,9},{2,1},{10,2},{18... | collective-permute-start | bytes 811016 | tf_op jit(solution)/shard_map/ppermute | solution.py:607
  148.6 4.4 %collective-permute-start.34 = (f32[8,128]{1,0:T(8,128)S(1)}, f32[8,128]{1,0:T(8,128)S(1)}, u32[]{:S(2)}, u32[]{:S(2)}) collective-permute-start(f32[8,128]{1,0:T(8,128)S(1)} %get-tuple-element.58), channel_id=1, source_target_pairs={{0,8},{8,0},{16,24},{24,16},{1,9},{9,1},{17,25},{25,17},{2,10},{10... | collective-permute-start | bytes 12296 | tf_op jit(solution)/shard_map/ppermute | solution.py:536
  152.9 4.0 %collective-permute-start.35 = (f32[8,128]{1,0:T(8,128)S(1)}, f32[8,128]{1,0:T(8,128)S(1)}, u32[]{:S(2)}, u32[]{:S(2)}) collective-permute-start(f32[8,128]{1,0:T(8,128)S(1)} %add.94), channel_id=1, source_target_pairs={{0,16},{8,24},{16,0},{24,8},{1,17},{9,25},{17,1},{25,9},{2,18},{10... | collective-permute-start | bytes 12296 | tf_op jit(solution)/shard_map/ppermute | solution.py:536
  156.9 2.5 %collective-permute-start.36 = (f32[8,128]{1,0:T(8,128)S(1)}, f32[8,128]{1,0:T(8,128)S(1)}, u32[]{:S(2)}, u32[]{:S(2)}) collective-permute-start(f32[8,128]{1,0:T(8,128)S(1)} %add.95), channel_id=1, source_target_pairs={{0,1},{1,0},{2,3},{3,2},{4,5},{5,4},{6,7},{7,6},{8,9},{9,8},{10,11... | collective-permute-start | bytes 12296 | tf_op jit(solution)/shard_map/ppermute | solution.py:536
  159.4 4.0 %collective-permute-start.37 = (f32[8,128]{1,0:T(8,128)S(1)}, f32[8,128]{1,0:T(8,128)S(1)}, u32[]{:S(2)}, u32[]{:S(2)}) collective-permute-start(f32[8,128]{1,0:T(8,128)S(1)} %add.96), channel_id=1, source_target_pairs={{0,2},{1,3},{2,0},{3,1},{4,6},{5,7},{6,4},{7,5},{8,10},{9,11},{10,... | collective-permute-start | bytes 12296 | tf_op jit(solution)/shard_map/ppermute | solution.py:536
  163.3 2.8 %collective-permute-start.38 = (f32[8,128]{1,0:T(8,128)S(1)}, f32[8,128]{1,0:T(8,128)S(1)}, u32[]{:S(2)}, u32[]{:S(2)}) collective-permute-start(f32[8,128]{1,0:T(8,128)S(1)} %add.97), channel_id=1, source_target_pairs={{0,4},{1,5},{2,6},{3,7},{4,0},{5,1},{6,2},{7,3},{8,12},{9,13},{10,... | collective-permute-start | bytes 12296 | tf_op jit(solution)/shard_map/ppermute | solution.py:536
  183.7 28.9 %collective-permute-start.39 = (f32[64,8,128]{2,1,0:T(8,128)S(1)}, f32[64,8,128]{2,1,0:T(8,128)S(1)}, u32[]{:S(2)}, u32[]{:S(2)}) collective-permute-start(f32[64,8,128]{2,1,0:T(8,128)S(1)} %get-tuple-element.60), channel_id=1, source_target_pairs={{0,8},{8,0},{16,24},{24,16},{1,9},{9,1},{17,25},{25,17},{2,10},{10... | collective-permute-start | bytes 786440 | tf_op jit(solution)/shard_map/ppermute | solution.py:536
  188.4 24.2 %collective-permute-start.40 = (f32[64,8,128]{2,1,0:T(8,128)S(1)}, f32[64,8,128]{2,1,0:T(8,128)S(1)}, u32[]{:S(2)}, u32[]{:S(2)}) collective-permute-start(f32[64,8,128]{2,1,0:T(8,128)S(1)} %get-tuple-element.61), channel_id=1, source_target_pairs={{0,16},{8,24},{16,0},{24,8},{1,17},{9,25},{17,1},{25,9},{2,18},{10... | collective-permute-start | bytes 786440 | tf_op jit(solution)/shard_map/ppermute | solution.py:536
  188.6 23.9 %collective-permute-start.41 = (f32[64,8,128]{2,1,0:T(8,128)S(1)}, f32[64,8,128]{2,1,0:T(8,128)S(1)}, u32[]{:S(2)}, u32[]{:S(2)}) collective-permute-start(f32[64,8,128]{2,1,0:T(8,128)S(1)} %get-tuple-element.62), channel_id=1, source_target_pairs={{0,24},{8,16},{16,8},{24,0},{1,25},{9,17},{17,9},{25,1},{2,26},{10... | collective-permute-start | bytes 786440 | tf_op jit(solution)/shard_map/ppermute | solution.py:536
  191.6 1.2 collective-permute-start.27
  192.8 10.6 %collective-permute-start.28 = (f32[8,128]{1,0:T(8,128)S(1)}, f32[8,128]{1,0:T(8,128)S(1)}, u32[]{:S(2)}, u32[]{:S(2)}) collective-permute-start(f32[8,128]{1,0:T(8,128)S(1)} %add.89), channel_id=1, source_target_pairs={{0,16},{8,24},{16,0},{24,8},{1,17},{9,25},{17,1},{25,9},{2,18},{10... | collective-permute-start | bytes 12296 | tf_op jit(solution)/shard_map/ppermute | solution.py:536
  203.4 2.5 %collective-permute-start.29 = (f32[8,128]{1,0:T(8,128)S(1)}, f32[8,128]{1,0:T(8,128)S(1)}, u32[]{:S(2)}, u32[]{:S(2)}) collective-permute-start(f32[8,128]{1,0:T(8,128)S(1)} %add.90), channel_id=1, source_target_pairs={{0,1},{1,0},{2,3},{3,2},{4,5},{5,4},{6,7},{7,6},{8,9},{9,8},{10,11... | collective-permute-start | bytes 12296 | tf_op jit(solution)/shard_map/ppermute | solution.py:536
  205.8 4.0 %collective-permute-start.30 = (f32[8,128]{1,0:T(8,128)S(1)}, f32[8,128]{1,0:T(8,128)S(1)}, u32[]{:S(2)}, u32[]{:S(2)}) collective-permute-start(f32[8,128]{1,0:T(8,128)S(1)} %add.91), channel_id=1, source_target_pairs={{0,2},{1,3},{2,0},{3,1},{4,6},{5,7},{6,4},{7,5},{8,10},{9,11},{10,... | collective-permute-start | bytes 12296 | tf_op jit(solution)/shard_map/ppermute | solution.py:536
  209.8 2.8 %collective-permute-start.31 = (f32[8,128]{1,0:T(8,128)S(1)}, f32[8,128]{1,0:T(8,128)S(1)}, u32[]{:S(2)}, u32[]{:S(2)}) collective-permute-start(f32[8,128]{1,0:T(8,128)S(1)} %add.92), channel_id=1, source_target_pairs={{0,4},{1,5},{2,6},{3,7},{4,0},{5,1},{6,2},{7,3},{8,12},{9,13},{10,... | collective-permute-start | bytes 12296 | tf_op jit(solution)/shard_map/ppermute | solution.py:536

commit v2 on v1

--- a/solution.py
+++ b/solution.py
@@ -22,6 +22,8 @@
 WIDTH = 2 * RADIUS + 1
 LOWEST = NZ // 2 - RADIUS
 TILES = 4 * XI
+MORE = 4
+UNROLL = {"fill": 4, "tend": 4, "div": 16, "relax": 16, "correct": 16}
 
 TIME_STEP = 0.25
 VISCOSITY = 0.02
@@ -32,6 +34,7 @@
 YAW_INCREMENT = 0.1
 SIXTH = 1.0 / 6.0
 F32 = jnp.float32
+INTS = 7
 VLIMIT = 40 * 1024 * 1024
 
 VMEM = pl.BlockSpec(memory_space=pltpu.VMEM)
@@ -72,6 +75,43 @@
     )
 
 
+def rows(name, body, carry=0):
+    count = UNROLL[name]
+
+    def some(index, carry):
+        for offset in range(count):
+            carry = body(index * count + offset, carry)
+        return carry
+
+    return lax.fori_loop(0, XI // count, some, carry)
+
+
+def group_matrix(banded):
+    row = lax.broadcasted_iota(jnp.int32, (LANES, LANES), 0)
+    column = lax.broadcasted_iota(jnp.int32, (LANES, LANES), 1)
+    level = (row if banded == "row" else column) & (NZ - 1)
+    inside = (level >= LOWEST) & (level < LOWEST + WIDTH)
+    return jnp.where(((row >> 5) == (column >> 5)) & inside, 1.0, 0.0).astype(F32)
+
+
+def exact_dot(a, b):
+    return jnp.dot(a, b, precision=lax.Precision.HIGHEST, preferred_element_type=F32)
+
+
+def band_sums(fields, su, sd, sums):
+    matrix = group_matrix("row")
+    level = lanes(OWN) & (NZ - 1)
+    for c in range(2):
+        total = exact_dot(fields[c].reshape(XI * OWN, LANES), matrix)
+        packed = jnp.zeros((OWN, LANES), F32)
+        for xi in range(XI):
+            packed = jnp.where(level == xi, total[xi * OWN : (xi + 1) * OWN], packed)
+        sums[c] = packed
+        for t in range(2):
+            sd[TILES + 2 * c + t] = packed[t * 8 : t * 8 + 8]
+            su[TILES + 2 * c + t] = packed[16 + t * 8 : 24 + t * 8]
+
+
 def block_transposed(sources, group, masks):
     out = None
     for c, value in enumerate(sources):
@@ -99,98 +139,44 @@
             pl_out[plane * 4 + kt] = block_transposed(sources, slab, masks)
 
 
-def maps_kernel(scal, active, yaw, ids, maps, counts, stage):
-    own, slab = scal[0], scal[1]
-    lane = lanes(XI)
+def maps_kernel(ints, ids, maps):
+    own, slab = ints[0], ints[1]
+    lane = lanes(NZ)
+    pieces = []
     for g in range(GX):
         source = own ^ g
-        left, mid, right = ids[source, 1], ids[source, 0], ids[source, 2]
-        shift = (HALO - 32 * slab) & (LANES - 1)
-        moved_mid = pltpu.roll(mid, shift, axis=1)
-        moved_left = pltpu.roll(left, HALO, axis=1)
-        moved_right = pltpu.roll(right, OWN + HALO, axis=1)
-        here = jnp.where((lane < HALO) & (slab == 0), moved_left, moved_mid)
-        here = jnp.where((lane >= OWN + HALO) & (slab == 3), moved_right, here)
-        stage[0, g * XI : (g + 1) * XI, :] = here
-    here = stage[0]
+        moved_mid = pltpu.roll(ids[source, 0], (16 - 32 * slab) & (LANES - 1), axis=1)
+        moved_left = pltpu.roll(ids[source, 1], 16, axis=1)
+        moved_right = pltpu.roll(ids[source, 2], OWN + 16, axis=1)
+        here = jnp.where((lane[:XI] < 16) & (slab == 0), moved_left, moved_mid)
+        here = jnp.where((lane[:XI] >= OWN + 16) & (slab == 3), moved_right, here)
+        pieces += [here, jnp.full((XI, LANES), -1.0, F32)]
+    here = jnp.concatenate(pieces, axis=0)
+    turbines = (ints.shape[0] - INTS) // 2
 
     def per_turbine(t, carry):
         sector, running = carry
         match = here == t.astype(F32)
         return (
-            jnp.where(match, yaw[t].astype(F32), sector),
-            jnp.where(match, active[t].astype(F32), running),
+            jnp.where(match, ints[INTS + turbines + t].astype(F32), sector),
+            jnp.where(match, ints[INTS + t].astype(F32), running),
         )
 
-    none = jnp.full((GX * XI, LANES), -1.0, F32)
     sector, running = lax.fori_loop(
-        0, active.shape[0], per_turbine, (none, jnp.zeros((GX * XI, LANES), F32))
+        0, turbines, per_turbine, (jnp.full((LANES, LANES), -1.0, F32), jnp.zeros((LANES, LANES), F32))
     )
-    cosine = jnp.zeros((GX * XI, LANES), F32)
-    sine = jnp.zeros((GX * XI, LANES), F32)
+    cosine = jnp.zeros((LANES, LANES), F32)
+    sine = jnp.zeros((LANES, LANES), F32)
     for value in range(8):
         angle = (value - 3.5) * YAW_INCREMENT
         cosine = jnp.where(sector == value, F32(math.cos(angle)), cosine)
         sine = jnp.where(sector == value, F32(math.sin(angle)), sine)
     thrust = running * F32(-0.5 * THRUST_COEFF * TIME_STEP / float(WIDTH**2) ** 2)
-    low = lanes(GX * XI) < 64
-    stage[0] = jnp.where(low, here, pltpu.roll(thrust, 64, axis=1))
-    stage[1] = jnp.where(low, cosine, pltpu.roll(sine, 64, axis=1))
-    level = lanes(EXT) & (NZ - 1)
-    band = (level >= LOWEST) & (level < LOWEST + WIDTH)
-    row = lax.broadcasted_iota(jnp.int32, (EXT, LANES), 0)
-    outside = jnp.full((8, LANES), -2.0, F32)
-    for xi in range(XI):
-        pair = []
-        for which in range(2):
-            rows = [
-                jnp.broadcast_to(stage[which, g * XI + xi : g * XI + xi + 1, :], (NZ, LANES))
-                for g in range(GX)
-            ]
-            pair.append(jnp.concatenate(rows, axis=0).T)
-        ident = pair[0][:EXT]
-        cos_u = jnp.where(band, pair[1][:EXT], 0.0)
-        sin_v = jnp.where(band, pair[1][64 : 64 + EXT], 0.0)
-        maps[0, xi, 0:8, :] = outside
-        maps[0, xi, 8 : 8 + EXT, :] = ident
-        maps[0, xi, 8 + EXT : PAD, :] = outside
-        maps[1, xi, 8 : 8 + EXT, :] = cos_u
-        maps[2, xi, 8 : 8 + EXT, :] = sin_v
-        maps[3, xi, 8 : 8 + EXT, :] = pair[0][64 : 64 + EXT]
-        for which in (1, 2, 3):
-            maps[which, xi, 0:8, :] = jnp.zeros((8, LANES), F32)
-            maps[which, xi, 8 + EXT : PAD, :] = jnp.zeros((8, LANES), F32)
-        first, final = ident[:1], ident[EXT - 1 :]
-        beyond = (ident == first) & (row > 0)
-        before = (ident == final) & (row < EXT - 1)
-        left_count = WIDTH - jnp.sum(jnp.where(beyond, 1.0, 0.0), axis=0, keepdims=True)
-        right_count = WIDTH - jnp.sum(jnp.where(before, 1.0, 0.0), axis=0, keepdims=True)
-        counts[0, xi : xi + 1, :] = jnp.where(first >= 0.0, left_count * cos_u[:1], 0.0)
-        counts[1, xi : xi + 1, :] = jnp.where(final >= 0.0, right_count * cos_u[EXT - 1 :], 0.0)
-
-
-def disk_edges(fields, maps, su, sd):
-    row24 = lax.broadcasted_iota(jnp.int32, (24, LANES), 0)
-    for xi in range(XI):
-        base = 8 + HALO
-        ident = maps[0, xi, base + 8 : base + 32, :]
-        normal = (
-            maps[1, xi, base + 8 : base + 32, :] * fields[0, xi, 8:32, :]
-            + maps[2, xi, base + 8 : base + 32, :] * fields[1, xi, 8:32, :]
-        )
-        take = (ident == ident[16:17]) & (row24 <= 16)
-        su[TILES + xi // 8, xi % 8 : xi % 8 + 1, :] = jnp.sum(
-            jnp.where(take, normal, 0.0), axis=0, keepdims=True
-        )
-        ident = maps[0, xi, base : base + 24, :]
-        normal = (
-            maps[1, xi, base : base + 24, :] * fields[0, xi, 0:24, :]
-            + maps[2, xi, base : base + 24, :] * fields[1, xi, 0:24, :]
-        )
-        take = (ident == ident[7:8]) & (row24 >= 7)
-        sd[TILES + xi // 8, xi % 8 : xi % 8 + 1, :] = jnp.sum(
-            jnp.where(take, normal, 0.0), axis=0, keepdims=True
-        )
+    low = lanes(LANES) < 64
+    first = jnp.where(low, here, pltpu.roll(thrust, 64, axis=1)).T
+    second = jnp.where(low, cosine, pltpu.roll(sine, 64, axis=1)).T
+    maps[0], maps[3] = first[:64], first[64:]
+    maps[1], maps[2] = second[:64], second[64:]
 
 
 def over_groups(row):
@@ -199,10 +185,10 @@
 
 
 def unpack_kernel(
-    scal, slot, profile, maps, s0, r1, r2, r3, p0, *rest, layouts, per_layout
+    scal, profile, s0, r1, r2, r3, p0, *rest, layouts, per_layout
 ):
     plane_refs = (p0,) + rest[: layouts - 1]
-    fields, inflow, su, sd, sums, held, planes = rest[layouts - 1 :]
+    fields, inflow, su, sd, bands, sums, held, planes = rest[layouts - 1 :]
     own, here = scal[0], scal[2]
     for s, source in enumerate((s0, r1, r2, r3)):
         held[own ^ s] = source[...]
@@ -210,8 +196,8 @@
         planes[here ^ s] = source[...]
 
     def per_row(xi, total):
-        rows = [held[g, pl.ds(xi * 4, 4)].reshape(NZ, LANES) for g in range(GX)]
-        turned = jnp.concatenate(rows, axis=0).T
+        parts = [held[g, pl.ds(xi * 4, 4)].reshape(NZ, LANES) for g in range(GX)]
+        turned = jnp.concatenate(parts, axis=0).T
         for c in range(4):
             value = turned[c * 32 : c * 32 + 32] + profile[c : c + 1, :]
             fields[c, xi] = value
@@ -221,21 +207,21 @@
                 total = total + jnp.sum(value, axis=0, keepdims=True)
         return total
 
-    total = lax.fori_loop(0, XI, per_row, jnp.zeros((1, LANES), F32))
+    total = rows("fill", per_row, jnp.zeros((1, LANES), F32))
     sums[...] = jnp.broadcast_to(over_groups(total), (8, LANES))
-    rows = []
+    parts = []
     for step in range(STEPS):
-        plane = slot[step]
-        rows.append(
+        plane = scal[3 + step]
+        parts.append(
             planes[plane // per_layout, pl.ds((plane % per_layout) * 4, 4)].reshape(NZ, LANES)
         )
-    turned = jnp.concatenate(rows, axis=0).T
+    turned = jnp.concatenate(parts, axis=0).T
     for c in range(4):
         value = turned[c * 32 : c * 32 + 32] + profile[c : c + 1, :]
         inflow[c] = value
-        sd[TILES + 2 + c] = value[:HALO]
-        su[TILES + 2 + c] = value[OWN - HALO :]
-    disk_edges(fields, maps, su, sd)
+        sd[TILES + MORE + c] = value[:HALO]
+        su[TILES + MORE + c] = value[OWN - HALO :]
+    band_sums(fields, su, sd, bands)
 
 
 def mean_response(mean):
@@ -267,16 +253,16 @@
 
 def step_kernel(*refs, step, cells):
     refs = list(refs)
-    fields_in, lo, hi, maps, counts, inflow_in = refs[:6]
+    fields_in, lo, hi, maps, bands_in, inflow_in = refs[:6]
     del refs[:6]
     mean = None
     if step > 0:
         mean = refs.pop(0)
     out = refs.pop(0)
-    su = sd = sums = inflow_out = None
+    su = sd = bands = sums = inflow_out = None
     if step < STEPS - 1:
-        su, sd, sums = refs[:3]
-        del refs[:3]
+        su, sd, bands, sums = refs[:4]
+        del refs[:4]
     if step == 0:
         inflow_out = refs.pop(0)
     f, v, r, pa, pb, ns, change, inflow = refs
@@ -291,9 +277,9 @@
         inflow[...] = inflow_in[...]
     else:
         for c in range(4):
-            inflow[c, 0:8] = lo[TILES + 2 + c]
+            inflow[c, 0:8] = lo[TILES + MORE + c]
             inflow[c, 8 : 8 + OWN] = inflow_in[c]
-            inflow[c, 8 + OWN : EXT] = hi[TILES + 2 + c]
+            inflow[c, 8 + OWN : EXT] = hi[TILES + MORE + c]
         inflow_out[...] = inflow[...]
 
     def fill(xi, carry):
@@ -307,7 +293,7 @@
             f[c, xi + 1, 16 + OWN : 8 + EXT] = high
         return carry
 
-    lax.fori_loop(0, XI, fill, 0)
+    rows("fill", fill)
     shift = (LANES - 32 * step) % LANES
 
     def entry(c):
@@ -322,42 +308,36 @@
             lane_ext >= 96, f[c, XI, body], pltpu.roll(f[c, 1, body], 96, axis=1)
         )
 
-    def normal_speed(xi, carry):
-        ns[xi] = maps[1, xi] * f[0, xi + 1] + maps[2, xi] * f[1, xi + 1]
-        return carry
-
+    packed = []
     for c in range(2):
-        for xi in range(XI):
-            f[c, xi + 1, 0:8] = jnp.zeros((8, LANES), F32)
-            f[c, xi + 1, 8 + EXT : PAD] = jnp.zeros((8, LANES), F32)
-    lax.fori_loop(0, XI, normal_speed, 0)
-    for xi in range(XI):
-        left = lo[TILES + xi // 8, xi % 8 : xi % 8 + 1, :]
-        right = hi[TILES + xi // 8, xi % 8 : xi % 8 + 1, :]
-        if step > 0:
-            left = left + counts[0, xi : xi + 1, :] * change[0, xi : xi + 1, :]
-            right = right + counts[1, xi : xi + 1, :] * change[0, xi : xi + 1, :]
-        ns[xi, 8:9, :] = left
-        ns[xi, 7 + EXT : 8 + EXT, :] = right
-    row_group = lax.broadcasted_iota(jnp.int32, (LANES, LANES), 0)
-    col_group = lax.broadcasted_iota(jnp.int32, (LANES, LANES), 1)
-    gather = jnp.where((row_group >> 5) == (col_group >> 5), 1.0, 0.0).astype(F32)
-
-    def thrusts(xi, carry):
-        speed = jnp.dot(ns[xi], gather, precision=lax.Precision.HIGHEST, preferred_element_type=F32)
-        ident = maps[0, xi]
-        forward = speed
-        backward = speed
-        for d in (1, 2, 4, 8):
-            same = ident == pltpu.roll(ident, d, axis=0)
-            forward = forward + jnp.where(same, pltpu.roll(forward, d, axis=0), 0.0)
-            same = ident == pltpu.roll(ident, PAD - d, axis=0)
-            backward = backward + jnp.where(same, pltpu.roll(backward, PAD - d, axis=0), 0.0)
-        total = forward + backward - speed
-        ns[xi] = maps[3, xi] * total * jnp.abs(total)
-        return carry
-
-    lax.fori_loop(0, XI, thrusts, 0)
+        parts = [lo[TILES + 2 * c + t] for t in range(2)] + [bands_in[c]]
+        parts += [hi[TILES + 2 * c + t] for t in range(2)]
+        packed.append(jnp.concatenate(parts, axis=0))
+    if step > 0:
+        level = lanes(XI) & (NZ - 1)
+        row = lax.broadcasted_iota(jnp.int32, (XI, LANES), 0)
+        shift_u = jnp.where(level == row, exact_dot(change[0], group_matrix("row")), 0.0)
+        packed[0] = packed[0] + jnp.sum(shift_u, axis=0, keepdims=True)
+    ident, cosine, sine = maps[0], maps[1], maps[2]
+    speed = cosine * packed[0] + sine * packed[1]
+    forward = backward = speed
+    size = ident.shape[0]
+    row = lax.broadcasted_iota(jnp.int32, ident.shape, 0)
+    for d in (1, 2, 4, 8):
+        same = (ident == pltpu.roll(ident, d, axis=0)) & (row >= d)
+        forward = forward + jnp.where(same, pltpu.roll(forward, d, axis=0), 0.0)
+        same = (ident == pltpu.roll(ident, size - d, axis=0)) & (row < size - d)
+        backward = backward + jnp.where(same, pltpu.roll(backward, size - d, axis=0), 0.0)
+    total = forward + backward - speed
+    thrust = maps[3] * total * jnp.abs(total)
+    level = lanes(EXT) & (NZ - 1)
+    matrix = group_matrix("column")
+    for c, direction in enumerate((cosine, sine)):
+        pushed = (thrust * direction)[8 : 8 + EXT]
+        for part in range(0, XI, 4):
+            spread = [jnp.where(level == xi, pushed, 0.0) for xi in range(part, part + 4)]
+            result = exact_dot(jnp.concatenate(spread, axis=0), matrix)
+            ns[c, part : part + 4] = result.reshape(4, EXT, LANES)
 
     def tendencies(xi, total):
         for tile in range(EXT // 8):
@@ -389,12 +369,11 @@
             nu = F32(TIME_STEP * VISCOSITY) + F32(0.5 * TIME_STEP * SMAGORINSKY) * strain
             half = F32(0.5 * TIME_STEP)
             au, av, aw = half * centre[0], half * centre[1], half * centre[2]
-            h = ns[xi, base : base + 8, :]
             for c in range(4):
                 scale = nu * F32(DIFFUSIVITY_RATIO) if c == 3 else nu
                 new = centre[c] + (scale * lap[c] - (au * gx[c] + av * gy[c] + aw * gz[c]))
                 if c < 2:
-                    new = new + maps[1 + c, xi, base : base + 8, :] * h
+                    new = new + ns[c, xi, tile * 8 : tile * 8 + 8, :]
                 elif c == 2:
                     new = new + F32(TIME_STEP * BUOYANCY) * centre[3]
                 if c < 3:
@@ -409,7 +388,7 @@
                             su[3 * XI + xi] = new
         return total
 
-    total = lax.fori_loop(0, XI, tendencies, jnp.zeros((8, LANES), F32))
+    total = rows("tend", tendencies, jnp.zeros((8, LANES), F32))
     if sums is not None:
         total = over_groups(jnp.sum(total, axis=0, keepdims=True))
         sums[...] = jnp.broadcast_to(total, (8, LANES))
@@ -435,7 +414,7 @@
             pa[xi + 1, here, :] = -source
         return carry
 
-    lax.fori_loop(0, XI, divergence, 0)
+    rows("div", divergence)
 
     def ends(p):
         p[0, body] = jnp.where(lane_ext < 32, 0.0, pltpu.roll(p[XI, body], 32, axis=1))
@@ -457,7 +436,7 @@
                 q[xi + 1, here, :] = beside * F32(SIXTH) - r[xi, tile * 8 : tile * 8 + 8, :]
             return carry
 
-        lax.fori_loop(0, XI, relax, 0)
+        rows("relax", relax)
     p = pa if SWEEPS % 2 == 0 else pb
     ends(p)
 
@@ -481,17 +460,30 @@
                         su[c * XI + xi] = new
         return carry
 
-    lax.fori_loop(0, XI, correct, 0)
+    rows("correct", correct)
     if sums is not None:
-        disk_edges(out, maps, su, sd)
+        band_sums(out, su, sd, bands)
+
+
+def step_scratch():
+    return [
+        pltpu.VMEM((4, XI + 2, PAD, LANES), F32),
+        pltpu.VMEM((3, XI + 2, PAD, LANES), F32),
+        pltpu.VMEM((XI, EXT, LANES), F32),
+        pltpu.VMEM((XI + 2, PAD, LANES), F32),
+        pltpu.VMEM((XI + 2, PAD, LANES), F32),
+        pltpu.VMEM((2, XI, EXT, LANES), F32),
+        pltpu.VMEM((2, XI, LANES), F32),
+        pltpu.VMEM((4, EXT, LANES), F32),
+    ]
 
 
 def send_kernel(scal, fields, s0, s1, s2, s3, turned):
     own = scal[0]
 
     def per_row(xi, carry):
-        rows = jnp.concatenate([fields[c, xi] for c in range(4)], axis=0)
-        turned[...] = rows.T.reshape(GX, 4, 8, LANES)
+        stacked = jnp.concatenate([fields[c, xi] for c in range(4)], axis=0)
+        turned[...] = stacked.T.reshape(GX, 4, 8, LANES)
         for s, out in enumerate((s0, s1, s2, s3)):
             out[pl.ds(xi * 4, 4)] = turned[own ^ s]
         return carry
@@ -536,22 +528,11 @@
     return lax.ppermute(value, axis, [(i, i ^ distance) for i in range(size)])
 
 
-def reduced(sums, groups):
-    distance = 1
-    while distance < GX:
-        sums = sums + swapped(sums, "gx", GX, distance)
-        distance *= 2
-    distance = 1
-    while distance < groups:
-        sums = sums + swapped(sums, "gy", groups, distance)
-        distance *= 2
-    return sums
-
-
 def local(state, planes, turbine_cell, active, yaw_sector, slot, *, layouts, groups):
     gx_index, gy_index = lax.axis_index("gx"), lax.axis_index("gy")
     slab = gx_index ^ (3 * (gy_index & 1))
     scal = jnp.stack([gx_index, slab, lax.axis_index("layout")]).astype(jnp.int32)
+    scal = jnp.concatenate([scal, slot, active[0], yaw_sector[0]])
     cells = float(GX * XI * GX * OWN * groups)
     per_layout = planes.shape[0]
     height = (jnp.arange(NZ).astype(F32) + 0.5) / NZ
@@ -575,68 +556,71 @@
     ids = jnp.stack([ids] + [swapped(ids, "gx", GX, s) for s in (1, 2, 3)])
     received = [swapped(value, "gx", GX, s) for s, value in ((1, s1), (2, s2), (3, s3))]
     plane_received = [swapped(plane, "layout", layouts, s) for s in range(1, layouts)]
-    maps, counts = call(
-        maps_kernel,
-        (shape(4, XI, PAD, LANES), shape(2, XI, LANES)),
-        [SMEM, SMEM, SMEM, VMEM],
-        [pltpu.VMEM((2, GX * XI, LANES), F32)],
-        name="maps",
-    )(scal, active[0], yaw_sector[0], ids)
-
-    first_payload = shape(TILES + 6, 8, LANES)
-    fields, inflow, su, sd, sums = call(
+    maps = call(maps_kernel, shape(4, 2 * OWN, LANES), [SMEM, VMEM], name="maps")(scal, ids)
+
+    first_payload = shape(TILES + MORE + 4, 8, LANES)
+    fields, inflow, su, sd, bands, sums = call(
         functools.partial(unpack_kernel, layouts=layouts, per_layout=per_layout),
         (
             shape(4, XI, OWN, LANES),
             shape(4, OWN, LANES),
             first_payload,
             first_payload,
+            shape(2, OWN, LANES),
             shape(8, LANES),
         ),
-        [SMEM, SMEM, VMEM, VMEM] + [VMEM] * (4 + layouts),
+        [SMEM, VMEM] + [VMEM] * (4 + layouts),
         [
             pltpu.VMEM((GX, TILES, 8, LANES), F32),
             pltpu.VMEM((layouts, per_layout * 4, 8, LANES), F32),
         ],
         name="unpack",
-    )(scal, slot, profile, maps, s0, *received, plane, *plane_received)
-
-    mean = None
+    )(scal, profile, s0, *received, plane, *plane_received)
+
+    half = groups // 2
+    mean = pending = None
     for step in range(STEPS):
         lo = lax.ppermute(su, ("gx", "gy"), up)
         hi = lax.ppermute(sd, ("gx", "gy"), down)
-        next_mean = reduced(sums, groups)
+        if pending is not None:
+            mean = pending
+            distance = 1
+            while distance < half:
+                mean = mean + swapped(mean, "gy", groups, distance)
+                distance *= 2
+        partial = sums + swapped(sums, "gx", GX, 1)
+        partial = partial + swapped(partial, "gy", groups, half)
+        fields, partial = lax.optimization_barrier((fields, partial))
+        arriving = swapped(partial, "gx", GX, 2)
         outs = [shape(4, XI, OWN, LANES)]
         if step < STEPS - 1:
-            outs += [shape(TILES + 2, 8, LANES), shape(TILES + 2, 8, LANES), shape(8, LANES)]
+            payload = shape(TILES + MORE, 8, LANES)
+            outs += [payload, payload, shape(2, OWN, LANES), shape(8, LANES)]
         if step == 0:
             outs += [shape(4, EXT, LANES)]
-        operands = [fields, lo, hi, maps, counts, inflow] + ([mean] if step > 0 else [])
+        operands = [fields, lo, hi, maps, bands, inflow] + ([mean] if step > 0 else [])
         results = call(
             functools.partial(step_kernel, step=step, cells=cells),
             tuple(outs),
             [VMEM] * len(operands),
-            [
-                pltpu.VMEM((4, XI + 2, PAD, LANES), F32),
-                pltpu.VMEM((3, XI + 2, PAD, LANES), F32),
-                pltpu.VMEM((XI, EXT, LANES), F32),
-                pltpu.VMEM((XI + 2, PAD, LANES), F32),
-                pltpu.VMEM((XI + 2, PAD, LANES), F32),
-                pltpu.VMEM((XI, PAD, LANES), F32),
-                pltpu.VMEM((2, XI, LANES), F32),
-                pltpu.VMEM((4, EXT, LANES), F32),
-            ],
+            step_scratch(),
             flops=30_000_000,
             name="step%d" % step,
         )(*operands)
         results = list(results)
         fields = results.pop(0)
         if step < STEPS - 1:
-            su, sd, sums = results[:3]
-            del results[:3]
+            su, sd, bands, sums = results[:4]
+            del results[:4]
         if step == 0:
             inflow = results.pop(0)
-        mean = next_mean
+        fields, arriving = lax.optimization_barrier((fields, arriving))
+        pending = partial + arriving
+    mean = pending
+    distance = 1
+    while distance < half:
+        mean = mean + swapped(mean, "gy", groups, distance)
+        distance *= 2
 
     s0, s1, s2, s3 = call(
         send_kernel,

time: 219 us -> 144 us (0.66); the launches traced: 216 us -> 144 us
  Pallas kernels: 74.1 us -> 30.8 us
  waiting for transfers between devices: 77.3 us -> 39.2 us
  starting transfers between devices: 58.8 us -> 69.9 us
    pallas_call x4, Pallas kernels: 61.3 us -> 19.3 us  [local(): call(functools.partial(step_kernel, step=step, cells=cells), tuple(outs),...]
    ppermute x32, waiting for transfers between devices: 69.7 us -> 39.2 us  [swapped(): return lax.ppermute(value, axis, [(i, i ^ distance) for i in range(size)])]
    ppermute x32, starting transfers between devices: 34.6 us -> 52.9 us  [swapped(): return lax.ppermute(value, axis, [(i, i ^ distance) for i in range(size)])]
    ppermute x4, waiting for transfers between devices: 6.66 us -> 0.01 us  [local(): lo = lax.ppermute(su, ('gx', 'gy'), up)]
    ppermute x4, starting transfers between devices: 19.9 us -> 13.4 us  [local(): lo = lax.ppermute(su, ('gx', 'gy'), up)]
  transfers between devices with their start and end apart: 42 -> 42, of which waited for: 25 -> 16; matrix products, arithmetic and copies ran while one was open for 0% -> 1% of each run, Pallas kernels for 2% -> 5%
where the time goes in v2:
time: 144 us
  starting transfers between devices  69.9 us (49%)
  waiting for transfers between devices  39.2 us (27%)
  Pallas kernels  30.8 us (21%)
  local copies, waits for them, and re-layouts  3.92 us (3%)
    ppermute x32, starting transfers between devices, swapped(): return lax.ppermute(value, axis, [(i, i ^ distance) for i in range(size)])  52.9 us
    ppermute x32, waiting for transfers between devices, swapped(): return lax.ppermute(value, axis, [(i, i ^ distance) for i in range(size)])  39.2 us
    pallas_call x4, Pallas kernels, local(): call(functools.partial(step_kernel, step=step, cells=cells), tuple(outs),...  19.3 us
    ppermute x4, starting transfers between devices, local(): lo = lax.ppermute(su, ('gx', 'gy'), up)  13.4 us
    pallas_call x1, Pallas kernels, local(): call(functools.partial(final_kernel, cells=cells), shape(4, XI, NZ, LANES...  3.11 us
  transfers between devices with their start and end apart: 42, of which 16 were waited for; matrix products, arithmetic and copies ran while one was open for 1% of the time, Pallas kernels for 5%

profile of v2, /device:TPU:1, one launch (start us, length us, event | category | flops | bytes accessed | tf_op | source)
XLA Modules:
  0.0 144.3 jit_solution(9157394172338670674)
XLA Ops:
  0.0 0.6 copy-done.2
  0.7 0.1 concatenate.3.scal.ints
  0.8 1.2 copy-done
  2.0 0.9 copy-done.1
  2.9 2.8 %pack.1 = (f32[64,8,128]{2,1,0:T(8,128)S(1)}, f32[64,8,128]{2,1,0:T(8,128)S(1)}, f32[64,8,128]{2,1,0:T(8,128)S(1)}, f32[64,8,128]{2,1,0:T(8,128)S(1)}, f32[8,8,128]{2,1,0:T(8,128)S(1)}) custom-call(s32[135]{0:T(256)S(1)} %concatenate.3.scal.ints, f32[4,16,32,128]{3,2,1,0:T(8,128)S(1)} %bitcast.19, f32[2,4,32,128]{3,2,1,0:T(8,128)S(1)} %copy-done.1), custom_call_target="tpu_custom_call" | custom-call | flops 10000000 | bytes 4000000 | tf_op jit(solution)/shard_map/pack/pallas_call | solution.py:550
  5.7 2.5 %collective-permute-start.3 = (f32[8,8,128]{2,1,0:T(8,128)S(1)}, f32[8,8,128]{2,1,0:T(8,128)S(1)}, u32[]{:S(2)}, u32[]{:S(2)}) collective-permute-start(f32[8,8,128]{2,1,0:T(8,128)S(1)} %get-tuple-element.56.p0), channel_id=1, source_target_pairs={{0,32},{32,0},{64,96},{96,64},{1,33},{33,1},{65,97},{97,65},{2,34}... | collective-permute-start | bytes 98312 | tf_op jit(solution)/shard_map/ppermute | solution.py:528
  8.2 3.3 %collective-permute-start.4 = (f32[8,8,128]{2,1,0:T(8,128)S(1)}, f32[8,8,128]{2,1,0:T(8,128)S(1)}, u32[]{:S(2)}, u32[]{:S(2)}) collective-permute-start(f32[8,8,128]{2,1,0:T(8,128)S(1)} %get-tuple-element.56.p0), channel_id=1, source_target_pairs={{0,64},{32,96},{64,0},{96,32},{1,65},{33,97},{65,1},{97,33},{2,66}... | collective-permute-start | bytes 98312 | tf_op jit(solution)/shard_map/ppermute | solution.py:528
  11.5 1.2 collective-permute-start
  12.8 2.9 %collective-permute-start.1 = (f32[64,8,128]{2,1,0:T(8,128)S(1)}, f32[64,8,128]{2,1,0:T(8,128)S(1)}, u32[]{:S(2)}, u32[]{:S(2)}) collective-permute-start(f32[64,8,128]{2,1,0:T(8,128)S(1)} %get-tuple-element.54), channel_id=1, source_target_pairs={{0,16},{8,24},{16,0},{24,8},{1,17},{9,25},{17,1},{25,9},{2,18},{10... | collective-permute-start | bytes 786440 | tf_op jit(solution)/shard_map/ppermute | solution.py:528
  15.7 0.2 collective-permute-start.2
  15.9 0.1 pad.13.clone
  16.1 0.1 tile.10
  16.2 0.8 slice.3
  17.1 3.2 %collective-permute-done.5.rest_2_ = f32[8,8,128]{2,1,0:T(8,128)S(1)} collective-permute-done((f32[8,8,128]{2,1,0:T(8,128)S(1)}, f32[8,8,128]{2,1,0:T(8,128)S(1)}, u32[]{:S(2)}, u32[]{:S(2)}) %collective-permute-start.5) | collective-permute-done | bytes 32800 | tf_op jit(solution)/shard_map/ppermute | solution.py:528
  20.3 1.9 %collective-permute-done.1.r2 = f32[64,8,128]{2,1,0:T(8,128)S(1)} collective-permute-done((f32[64,8,128]{2,1,0:T(8,128)S(1)}, f32[64,8,128]{2,1,0:T(8,128)S(1)}, u32[]{:S(2)}, u32[]{:S(2)}) %collective-permute-start.1) | collective-permute-done | bytes 262176 | tf_op jit(solution)/shard_map/ppermute | solution.py:528
  22.2 5.7 %collective-permute-done.2.r3 = f32[64,8,128]{2,1,0:T(8,128)S(1)} collective-permute-done((f32[64,8,128]{2,1,0:T(8,128)S(1)}, f32[64,8,128]{2,1,0:T(8,128)S(1)}, u32[]{:S(2)}, u32[]{:S(2)}) %collective-permute-start.2) | collective-permute-done | bytes 262176 | tf_op jit(solution)/shard_map/ppermute | solution.py:528
  27.9 1.8 %unpack.1 = (f32[4,16,32,128]{3,2,1,0:T(8,128)S(1)}, f32[4,32,128]{2,1,0:T(8,128)S(1)}, f32[72,8,128]{2,1,0:T(8,128)S(1)}, f32[72,8,128]{2,1,0:T(8,128)S(1)}, f3...) custom-call(s32[135]{0:T(256)S(1)} %concatenate.3.scal.ints, f32[8,128]{1,0:T(8,128)S(1)} %pad.4.profile, ...), custom_call_target="tpu_custom_call" | custom-call | flops 10000000 | bytes 4000000 | tf_op jit(solution)/shard_map/unpack/pallas_call | solution.py:562
  29.7 3.2 %collective-permute-start.8 = (f32[72,8,128]{2,1,0:T(8,128)S(1)}, f32[72,8,128]{2,1,0:T(8,128)S(1)}, u32[]{:S(2)}, u32[]{:S(2)}) collective-permute-start(f32[72,8,128]{2,1,0:T(8,128)S(1)} %get-tuple-element.60), channel_id=1, source_target_pairs={{0,8},{8,16},{16,24},{24,25},{25,17},{17,9},{9,1},{1,2},{2,10},{10... | collective-permute-start | bytes 884744 | tf_op jit(solution)/shard_map/ppermute | solution.py:583
  32.9 1.4 collective-permute-start.10
  34.2 2.3 %collective-permute-start.11 = (f32[16,128]{1,0:T(8,128)S(1)}, f32[16,128]{1,0:T(8,128)S(1)}, u32[]{:S(2)}, u32[]{:S(2)}) collective-permute-start(f32[16,128]{1,0:T(8,128)S(1)} %get-tuple-element.102), channel_id=1, source_target_pairs={{1,0},{2,1},{3,2},{4,3},{5,4},{6,5},{7,6},{0,7},{9,8},{10,9},{11,1... | collective-permute-start | bytes 24584 | tf_op jit(solution)/shard_map/ppermute | solution.py:547
  36.5 1.8 %collective-permute-start.6 = (f32[8,128]{1,0:T(8,128)S(1)}, f32[8,128]{1,0:T(8,128)S(1)}, u32[]{:S(2)}, u32[]{:S(2)}) collective-permute-start(f32[8,128]{1,0:T(8,128)S(1)} %get-tuple-element.58), channel_id=1, source_target_pairs={{0,8},{8,0},{16,24},{24,16},{1,9},{9,1},{17,25},{25,17},{2,10},{10... | collective-permute-start | bytes 12296 | tf_op jit(solution)/shard_map/ppermute | solution.py:528
  38.4 1.8 %collective-permute-start.12 = (f32[3,16,128]{2,1,0:T(8,128)S(1)}, f32[3,16,128]{2,1,0:T(8,128)S(1)}, u32[]{:S(2)}, u32[]{:S(2)}) collective-permute-start(f32[3,16,128]{2,1,0:T(8,128)S(1)} %get-tuple-element.100), channel_id=1, source_target_pairs={{0,8},{8,0},{16,24},{24,16},{1,9},{9,1},{17,25},{25,17},{2,10},{10... | collective-permute-start | bytes 73736 | tf_op jit(solution)/shard_map/ppermute | solution.py:528
  40.2 2.0 %collective-permute-start.13 = (f32[3,16,128]{2,1,0:T(8,128)S(1)}, f32[3,16,128]{2,1,0:T(8,128)S(1)}, u32[]{:S(2)}, u32[]{:S(2)}) collective-permute-start(f32[3,16,128]{2,1,0:T(8,128)S(1)} %get-tuple-element.100), channel_id=1, source_target_pairs={{0,16},{8,24},{16,0},{24,8},{1,17},{9,25},{17,1},{25,9},{2,18},{10... | collective-permute-start | bytes 73736 | tf_op jit(solution)/shard_map/ppermute | solution.py:528
  42.2 1.2 collective-permute-start.14
  43.4 1.3 collective-permute-start.7
  44.7 2.3 %collective-permute-done.14 = f32[3,16,128]{2,1,0:T(8,128)S(1)} collective-permute-done((f32[3,16,128]{2,1,0:T(8,128)S(1)}, f32[3,16,128]{2,1,0:T(8,128)S(1)}, u32[]{:S(2)}, u32[]{:S(2)}) %collective-permute-start.14) | collective-permute-done | bytes 24608 | tf_op jit(solution)/shard_map/ppermute | solution.py:528
  47.0 1.7 %maps.1.refs_3_ = f32[4,64,128]{2,1,0:T(8,128)S(1)} custom-call(s32[135]{0:T(256)S(1)} %concatenate.3.scal.ints, f32[4,3,16,128]{3,2,1,0:T(8,128)S(1)} %pad_maximum_fusion.ids), custom_call_target="tpu_custom_call" | custom-call | flops 10000000 | bytes 4000000 | tf_op jit(solution)/shard_map/maps/pallas_call | solution.py:559
  48.7 4.4 %step0.1 = (f32[4,16,32,128]{3,2,1,0:T(8,128)S(1)}, f32[68,8,128]{2,1,0:T(8,128)S(1)}, f32[68,8,128]{2,1,0:T(8,128)S(1)}, f32[2,32,128]{2,1,0:T(8,128)S(1)}, f32...) custom-call(f32[4,16,32,128]{3,2,1,0:T(8,128)S(1)} %get-tuple-element.59.refs_0_, ...), custom_call_target="tpu_custom_call" | custom-call | flops 30000000 | bytes 4000000 | tf_op jit(solution)/shard_map/step0/pallas_call | solution.py:602
  53.1 1.3 collective-permute-start.18
  54.3 0.3 collective-permute-start.15
  54.6 3.4 %collective-permute-start.16 = (f32[8,128]{1,0:T(8,128)S(1)}, f32[8,128]{1,0:T(8,128)S(1)}, u32[]{:S(2)}, u32[]{:S(2)}) collective-permute-start(f32[8,128]{1,0:T(8,128)S(1)} %get-tuple-element.67), channel_id=1, source_target_pairs={{0,8},{8,0},{16,24},{24,16},{1,9},{9,1},{17,25},{25,17},{2,10},{10... | collective-permute-start | bytes 12296 | tf_op jit(solution)/shard_map/ppermute | solution.py:528
  58.0 3.0 %collective-permute-done.15 = f32[8,128]{1,0:T(8,128)S(1)} collective-permute-done((f32[8,128]{1,0:T(8,128)S(1)}, f32[8,128]{1,0:T(8,128)S(1)}, u32[]{:S(2)}, u32[]{:S(2)}) %collective-permute-start.15) | collective-permute-done | bytes 4128 | tf_op jit(solution)/shard_map/ppermute | solution.py:528
  61.0 1.3 collective-permute-start.17
  62.3 1.1 collective-permute-done.20
  63.4 5.3 %collective-permute-start.21 = (f32[8,128]{1,0:T(8,128)S(1)}, f32[8,128]{1,0:T(8,128)S(1)}, u32[]{:S(2)}, u32[]{:S(2)}) collective-permute-start(f32[8,128]{1,0:T(8,128)S(1)} %add.84), channel_id=1, source_target_pairs={{0,2},{1,3},{2,0},{3,1},{4,6},{5,7},{6,4},{7,5},{8,10},{9,11},{10,... | collective-permute-start | bytes 12296 | tf_op jit(solution)/shard_map/ppermute | solution.py:528
  68.7 1.0 collective-permute-done.21
  69.7 5.0 %step1.1 = (f32[4,16,32,128]{3,2,1,0:T(8,128)S(1)}, f32[68,8,128]{2,1,0:T(8,128)S(1)}, f32[68,8,128]{2,1,0:T(8,128)S(1)}, f32[2,32,128]{2,1,0:T(8,128)S(1)}, f32[8,128]{1,0:T(8,128)S(1)}) custom-call(f32[4,16,32,128]{3,2,1,0:T(8,128)S(1)} %get-tuple-element.68.refs_0_, f32[68,8,128]{2,1,0:T(8,128)S(1)} %collective-permute-done.18.refs_1_, ...), custom_call_target="tpu_custom_call" | custom-call | flops 30000000 | bytes 4000000 | tf_op jit(solution)/shard_map/step1/pallas_call | solution.py:602
  74.8 3.7 %collective-permute-start.25 = (f32[68,8,128]{2,1,0:T(8,128)S(1)}, f32[68,8,128]{2,1,0:T(8,128)S(1)}, u32[]{:S(2)}, u32[]{:S(2)}) collective-permute-start(f32[68,8,128]{2,1,0:T(8,128)S(1)} %get-tuple-element.79), channel_id=1, source_target_pairs={{0,8},{8,16},{16,24},{24,25},{25,17},{17,9},{9,1},{1,2},{2,10},{10... | collective-permute-start | bytes 835592 | tf_op jit(solution)/shard_map/ppermute | solution.py:583
  78.5 0.9 collective-permute-start.22
  79.4 2.7 %collective-permute-start.23 = (f32[8,128]{1,0:T(8,128)S(1)}, f32[8,128]{1,0:T(8,128)S(1)}, u32[]{:S(2)}, u32[]{:S(2)}) collective-permute-start(f32[8,128]{1,0:T(8,128)S(1)} %get-tuple-element.77), channel_id=1, source_target_pairs={{0,8},{8,0},{16,24},{24,16},{1,9},{9,1},{17,25},{25,17},{2,10},{10... | collective-permute-start | bytes 12296 | tf_op jit(solution)/shard_map/ppermute | solution.py:528
  82.1 2.9 %collective-permute-done.22 = f32[8,128]{1,0:T(8,128)S(1)} collective-permute-done((f32[8,128]{1,0:T(8,128)S(1)}, f32[8,128]{1,0:T(8,128)S(1)}, u32[]{:S(2)}, u32[]{:S(2)}) %collective-permute-start.22) | collective-permute-done | bytes 4128 | tf_op jit(solution)/shard_map/ppermute | solution.py:528
  85.0 0.8 collective-permute-start.24
  85.8 1.7 %collective-permute-done.27 = f32[8,128]{1,0:T(8,128)S(1)} collective-permute-done((f32[8,128]{1,0:T(8,128)S(1)}, f32[8,128]{1,0:T(8,128)S(1)}, u32[]{:S(2)}, u32[]{:S(2)}) %collective-permute-start.27) | collective-permute-done | bytes 4128 | tf_op jit(solution)/shard_map/ppermute | solution.py:528
  87.5 3.0 %collective-permute-start.28 = (f32[8,128]{1,0:T(8,128)S(1)}, f32[8,128]{1,0:T(8,128)S(1)}, u32[]{:S(2)}, u32[]{:S(2)}) collective-permute-start(f32[8,128]{1,0:T(8,128)S(1)} %add.89), channel_id=1, source_target_pairs={{0,2},{1,3},{2,0},{3,1},{4,6},{5,7},{6,4},{7,5},{8,10},{9,11},{10,... | collective-permute-start | bytes 12296 | tf_op jit(solution)/shard_map/ppermute | solution.py:528
  90.5 1.0 collective-permute-done.28
  91.5 5.0 %step2.1 = (f32[4,16,32,128]{3,2,1,0:T(8,128)S(1)}, f32[68,8,128]{2,1,0:T(8,128)S(1)}, f32[68,8,128]{2,1,0:T(8,128)S(1)}, f32[2,32,128]{2,1,0:T(8,128)S(1)}, f32[8,128]{1,0:T(8,128)S(1)}) custom-call(f32[4,16,32,128]{3,2,1,0:T(8,128)S(1)} %get-tuple-element.78.refs_0_, f32[68,8,128]{2,1,0:T(8,128)S(1)} %collective-permute-done.25.refs_1_, ...), custom_call_target="tpu_custom_call" | custom-call | flops 30000000 | bytes 4000000 | tf_op jit(solution)/shard_map/step2/pallas_call | solution.py:602
  96.5 5.3 %collective-permute-start.32 = (f32[68,8,128]{2,1,0:T(8,128)S(1)}, f32[68,8,128]{2,1,0:T(8,128)S(1)}, u32[]{:S(2)}, u32[]{:S(2)}) collective-permute-start(f32[68,8,128]{2,1,0:T(8,128)S(1)} %get-tuple-element.89), channel_id=1, source_target_pairs={{0,8},{8,16},{16,24},{24,25},{25,17},{17,9},{9,1},{1,2},{2,10},{10... | collective-permute-start | bytes 835592 | tf_op jit(solution)/shard_map/ppermute | solution.py:583
  101.8 0.2 collective-permute-start.29
  102.0 3.4 %collective-permute-start.30 = (f32[8,128]{1,0:T(8,128)S(1)}, f32[8,128]{1,0:T(8,128)S(1)}, u32[]{:S(2)}, u32[]{:S(2)}) collective-permute-start(f32[8,128]{1,0:T(8,128)S(1)} %get-tuple-element.86), channel_id=1, source_target_pairs={{0,8},{8,0},{16,24},{24,16},{1,9},{9,1},{17,25},{25,17},{2,10},{10... | collective-permute-start | bytes 12296 | tf_op jit(solution)/shard_map/ppermute | solution.py:528
  105.5 2.9 %collective-permute-done.29 = f32[8,128]{1,0:T(8,128)S(1)} collective-permute-done((f32[8,128]{1,0:T(8,128)S(1)}, f32[8,128]{1,0:T(8,128)S(1)}, u32[]{:S(2)}, u32[]{:S(2)}) %collective-permute-start.29) | collective-permute-done | bytes 4128 | tf_op jit(solution)/shard_map/ppermute | solution.py:528
  108.4 0.5 collective-permute-start.31
  108.9 2.0 %collective-permute-done.34 = f32[8,128]{1,0:T(8,128)S(1)} collective-permute-done((f32[8,128]{1,0:T(8,128)S(1)}, f32[8,128]{1,0:T(8,128)S(1)}, u32[]{:S(2)}, u32[]{:S(2)}) %collective-permute-start.34) | collective-permute-done | bytes 4128 | tf_op jit(solution)/shard_map/ppermute | solution.py:528
  110.8 0.1 collective-permute-done.31
  110.9 4.2 %collective-permute-start.36 = (f32[8,128]{1,0:T(8,128)S(1)}, f32[8,128]{1,0:T(8,128)S(1)}, u32[]{:S(2)}, u32[]{:S(2)}) collective-permute-start(f32[8,128]{1,0:T(8,128)S(1)} %add.92), channel_id=1, source_target_pairs={{0,16},{8,24},{16,0},{24,8},{1,17},{9,25},{17,1},{25,9},{2,18},{10... | collective-permute-start | bytes 12296 | tf_op jit(solution)/shard_map/ppermute | solution.py:528
  115.2 4.9 %step3.1.fields = f32[4,16,32,128]{3,2,1,0:T(8,128)S(1)} custom-call(f32[4,16,32,128]{3,2,1,0:T(8,128)S(1)} %get-tuple-element.88.refs_0_, f32[68,8,128]{2,1,0:T(8,128)S(1)} %collective-permute-done.32.refs_1_, f32[68,8,128]{2,1,0:T(8,128)S(1)} %collective-permute-done.33.refs_2_, f32[4,64,128]{2,1,0:T(8,128)S(1)} %maps.1.refs_3_, ...), custom_call_target="tpu_custom_call" | custom-call | flops 30000000 | bytes 4000000 | tf_op jit(solution)/shard_map/step3/pallas_call | solution.py:602
  120.1 2.3 %send.1 = (f32[64,8,128]{2,1,0:T(8,128)S(1)}, f32[64,8,128]{2,1,0:T(8,128)S(1)}, f32[64,8,128]{2,1,0:T(8,128)S(1)}, f32[64,8,128]{2,1,0:T(8,128)S(1)}) custom-call(s32[135]{0:T(256)S(1)} %concatenate.3.scal.ints, f32[4,16,32,128]{3,2,1,0:T(8,128)S(1)} %step3.1.fields), custom_call_target="tpu_custom_call" | custom-call | flops 10000000 | bytes 4000000 | tf_op jit(solution)/shard_map/send/pallas_call | solution.py:625
  122.3 3.7 %collective-permute-start.39 = (f32[64,8,128]{2,1,0:T(8,128)S(1)}, f32[64,8,128]{2,1,0:T(8,128)S(1)}, u32[]{:S(2)}, u32[]{:S(2)}) collective-permute-start(f32[64,8,128]{2,1,0:T(8,128)S(1)} %get-tuple-element.96), channel_id=1, source_target_pairs={{0,8},{8,0},{16,24},{24,16},{1,9},{9,1},{17,25},{25,17},{2,10},{10... | collective-permute-start | bytes 786440 | tf_op jit(solution)/shard_map/ppermute | solution.py:528
  126.0 1.6 %collective-permute-start.40 = (f32[64,8,128]{2,1,0:T(8,128)S(1)}, f32[64,8,128]{2,1,0:T(8,128)S(1)}, u32[]{:S(2)}, u32[]{:S(2)}) collective-permute-start(f32[64,8,128]{2,1,0:T(8,128)S(1)} %get-tuple-element.97), channel_id=1, source_target_pairs={{0,16},{8,24},{16,0},{24,8},{1,17},{9,25},{17,1},{25,9},{2,18},{10... | collective-permute-start | bytes 786440 | tf_op jit(solution)/shard_map/ppermute | solution.py:528
  127.6 1.6 %collective-permute-start.41 = (f32[64,8,128]{2,1,0:T(8,128)S(1)}, f32[64,8,128]{2,1,0:T(8,128)S(1)}, u32[]{:S(2)}, u32[]{:S(2)}) collective-permute-start(f32[64,8,128]{2,1,0:T(8,128)S(1)} %get-tuple-element.98), channel_id=1, source_target_pairs={{0,24},{8,16},{16,8},{24,0},{1,25},{9,17},{17,9},{25,1},{2,26},{10... | collective-permute-start | bytes 786440 | tf_op jit(solution)/shard_map/ppermute | solution.py:528
  129.2 2.7 %collective-permute-done.37 = f32[8,128]{1,0:T(8,128)S(1)} collective-permute-done((f32[8,128]{1,0:T(8,128)S(1)}, f32[8,128]{1,0:T(8,128)S(1)}, u32[]{:S(2)}, u32[]{:S(2)}) %collective-permute-start.37) | collective-permute-done | bytes 4128 | tf_op jit(solution)/shard_map/ppermute | solution.py:528
  132.0 1.5 %collective-permute-start.38 = (f32[8,128]{1,0:T(8,128)S(1)}, f32[8,128]{1,0:T(8,128)S(1)}, u32[]{:S(2)}, u32[]{:S(2)}) collective-permute-start(f32[8,128]{1,0:T(8,128)S(1)} %add.97), channel_id=1, source_target_pairs={{0,2},{1,3},{2,0},{3,1},{4,6},{5,7},{6,4},{7,5},{8,10},{9,11},{10,... | collective-permute-start | bytes 12296 | tf_op jit(solution)/shard_map/ppermute | solution.py:528
  133.5 2.8 %collective-permute-done.38 = f32[8,128]{1,0:T(8,128)S(1)} collective-permute-done((f32[8,128]{1,0:T(8,128)S(1)}, f32[8,128]{1,0:T(8,128)S(1)}, u32[]{:S(2)}, u32[]{:S(2)}) %collective-permute-start.38) | collective-permute-done | bytes 4128 | tf_op jit(solution)/shard_map/ppermute | solution.py:528
  136.3 4.9 %collective-permute-done.41.r3 = f32[64,8,128]{2,1,0:T(8,128)S(1)} collective-permute-done((f32[64,8,128]{2,1,0:T(8,128)S(1)}, f32[64,8,128]{2,1,0:T(8,128)S(1)}, u32[]{:S(2)}, u32[]{:S(2)}) %collective-permute-start.41) | collective-permute-done | bytes 262176 | tf_op jit(solution)/shard_map/ppermute | solution.py:528
  141.2 3.1 %final.1 = f32[4,16,32,128]{3,2,1,0:T(8,128)} custom-call(s32[135]{0:T(256)S(1)} %concatenate.3.scal.ints, f32[8,128]{1,0:T(8,128)S(1)} %add.98.mean, f32[64,8,128]{2,1,0:T(8,128)S(1)} %get-tuple-element.95.s0, f32[64,8,128]{2,1,0:T(8,128)S(1)} %collective-permute-done.39.r1, f32[64,8,128]{2,1,0:T(8,128)S(1)} %collective-permute-done.40.r2, ...), custom_call_target="tpu_custom_call" | custom-call | flops 10000000 | bytes 4000000 | tf_op jit(solution)/shard_map/final/pallas_call | solution.py:633
  (71 shorter events, 0.4 us)
Async XLA Ops:
  0.0 0.7 copy-start.2
  0.0 0.7 copy-start.3
  0.0 0.7 copy-start.4
  0.8 1.2 copy-start
  2.0 0.9 copy-start.1
  5.7 10.3 %collective-permute-start.3 = (f32[8,8,128]{2,1,0:T(8,128)S(1)}, f32[8,8,128]{2,1,0:T(8,128)S(1)}, u32[]{:S(2)}, u32[]{:S(2)}) collective-permute-start(f32[8,8,128]{2,1,0:T(8,128)S(1)} %get-tuple-element.56.p0), channel_id=1, source_target_pairs={{0,32},{32,0},{64,96},{96,64},{1,33},{33,1},{65,97},{97,65},{2,34}... | collective-permute-start | bytes 98312 | tf_op jit(solution)/shard_map/ppermute | solution.py:528
  8.2 8.8 %collective-permute-start.4 = (f32[8,8,128]{2,1,0:T(8,128)S(1)}, f32[8,8,128]{2,1,0:T(8,128)S(1)}, u32[]{:S(2)}, u32[]{:S(2)}) collective-permute-start(f32[8,8,128]{2,1,0:T(8,128)S(1)} %get-tuple-element.56.p0), channel_id=1, source_target_pairs={{0,64},{32,96},{64,0},{96,32},{1,65},{33,97},{65,1},{97,33},{2,66}... | collective-permute-start | bytes 98312 | tf_op jit(solution)/shard_map/ppermute | solution.py:528
  11.5 8.8 %collective-permute-start = (f32[64,8,128]{2,1,0:T(8,128)S(1)}, f32[64,8,128]{2,1,0:T(8,128)S(1)}, u32[]{:S(2)}, u32[]{:S(2)}) collective-permute-start(f32[64,8,128]{2,1,0:T(8,128)S(1)} %get-tuple-element.53), channel_id=1, source_target_pairs={{0,8},{8,0},{16,24},{24,16},{1,9},{9,1},{17,25},{25,17},{2,10},{10... | collective-permute-start | bytes 786440 | tf_op jit(solution)/shard_map/ppermute | solution.py:528
  12.8 9.4 %collective-permute-start.1 = (f32[64,8,128]{2,1,0:T(8,128)S(1)}, f32[64,8,128]{2,1,0:T(8,128)S(1)}, u32[]{:S(2)}, u32[]{:S(2)}) collective-permute-start(f32[64,8,128]{2,1,0:T(8,128)S(1)} %get-tuple-element.54), channel_id=1, source_target_pairs={{0,16},{8,24},{16,0},{24,8},{1,17},{9,25},{17,1},{25,9},{2,18},{10... | collective-permute-start | bytes 786440 | tf_op jit(solution)/shard_map/ppermute | solution.py:528
  15.7 12.2 %collective-permute-start.2 = (f32[64,8,128]{2,1,0:T(8,128)S(1)}, f32[64,8,128]{2,1,0:T(8,128)S(1)}, u32[]{:S(2)}, u32[]{:S(2)}) collective-permute-start(f32[64,8,128]{2,1,0:T(8,128)S(1)} %get-tuple-element.55), channel_id=1, source_target_pairs={{0,24},{8,16},{16,8},{24,0},{1,25},{9,17},{17,9},{25,1},{2,26},{10... | collective-permute-start | bytes 786440 | tf_op jit(solution)/shard_map/ppermute | solution.py:528
  16.0 4.3 %collective-permute-start.5 = (f32[8,8,128]{2,1,0:T(8,128)S(1)}, f32[8,8,128]{2,1,0:T(8,128)S(1)}, u32[]{:S(2)}, u32[]{:S(2)}) collective-permute-start(f32[8,8,128]{2,1,0:T(8,128)S(1)} %get-tuple-element.56.p0), channel_id=1, source_target_pairs={{0,96},{32,64},{64,32},{96,0},{1,97},{33,65},{65,33},{97,1},{2,98}... | collective-permute-start | bytes 98312 | tf_op jit(solution)/shard_map/ppermute | solution.py:528
  29.7 19.0 %collective-permute-start.8 = (f32[72,8,128]{2,1,0:T(8,128)S(1)}, f32[72,8,128]{2,1,0:T(8,128)S(1)}, u32[]{:S(2)}, u32[]{:S(2)}) collective-permute-start(f32[72,8,128]{2,1,0:T(8,128)S(1)} %get-tuple-element.60), channel_id=1, source_target_pairs={{0,8},{8,16},{16,24},{24,25},{25,17},{17,9},{9,1},{1,2},{2,10},{10... | collective-permute-start | bytes 884744 | tf_op jit(solution)/shard_map/ppermute | solution.py:583
  32.9 15.8 %collective-permute-start.9 = (f32[72,8,128]{2,1,0:T(8,128)S(1)}, f32[72,8,128]{2,1,0:T(8,128)S(1)}, u32[]{:S(2)}, u32[]{:S(2)}) collective-permute-start(f32[72,8,128]{2,1,0:T(8,128)S(1)} %get-tuple-element.61), channel_id=1, source_target_pairs={{8,0},{16,8},{24,16},{25,24},{17,25},{9,17},{1,9},{2,1},{10,2},{18... | collective-permute-start | bytes 884744 | tf_op jit(solution)/shard_map/ppermute | solution.py:584
  32.9 5.5 %collective-permute-start.10 = (f32[16,128]{1,0:T(8,128)S(1)}, f32[16,128]{1,0:T(8,128)S(1)}, u32[]{:S(2)}, u32[]{:S(2)}) collective-permute-start(f32[16,128]{1,0:T(8,128)S(1)} %get-tuple-element.102), channel_id=1, source_target_pairs={{0,1},{1,2},{2,3},{3,4},{4,5},{5,6},{6,7},{7,0},{8,9},{9,10},{10,1... | collective-permute-start | bytes 24584 | tf_op jit(solution)/shard_map/ppermute | solution.py:547
  34.2 4.1 %collective-permute-start.11 = (f32[16,128]{1,0:T(8,128)S(1)}, f32[16,128]{1,0:T(8,128)S(1)}, u32[]{:S(2)}, u32[]{:S(2)}) collective-permute-start(f32[16,128]{1,0:T(8,128)S(1)} %get-tuple-element.102), channel_id=1, source_target_pairs={{1,0},{2,1},{3,2},{4,3},{5,4},{6,5},{7,6},{0,7},{9,8},{10,9},{11,1... | collective-permute-start | bytes 24584 | tf_op jit(solution)/shard_map/ppermute | solution.py:547
  36.5 5.7 %collective-permute-start.6 = (f32[8,128]{1,0:T(8,128)S(1)}, f32[8,128]{1,0:T(8,128)S(1)}, u32[]{:S(2)}, u32[]{:S(2)}) collective-permute-start(f32[8,128]{1,0:T(8,128)S(1)} %get-tuple-element.58), channel_id=1, source_target_pairs={{0,8},{8,0},{16,24},{24,16},{1,9},{9,1},{17,25},{25,17},{2,10},{10... | collective-permute-start | bytes 12296 | tf_op jit(solution)/shard_map/ppermute | solution.py:528
  38.4 5.0 %collective-permute-start.12 = (f32[3,16,128]{2,1,0:T(8,128)S(1)}, f32[3,16,128]{2,1,0:T(8,128)S(1)}, u32[]{:S(2)}, u32[]{:S(2)}) collective-permute-start(f32[3,16,128]{2,1,0:T(8,128)S(1)} %get-tuple-element.100), channel_id=1, source_target_pairs={{0,8},{8,0},{16,24},{24,16},{1,9},{9,1},{17,25},{25,17},{2,10},{10... | collective-permute-start | bytes 73736 | tf_op jit(solution)/shard_map/ppermute | solution.py:528
  40.2 4.5 %collective-permute-start.13 = (f32[3,16,128]{2,1,0:T(8,128)S(1)}, f32[3,16,128]{2,1,0:T(8,128)S(1)}, u32[]{:S(2)}, u32[]{:S(2)}) collective-permute-start(f32[3,16,128]{2,1,0:T(8,128)S(1)} %get-tuple-element.100), channel_id=1, source_target_pairs={{0,16},{8,24},{16,0},{24,8},{1,17},{9,25},{17,1},{25,9},{2,18},{10... | collective-permute-start | bytes 73736 | tf_op jit(solution)/shard_map/ppermute | solution.py:528
  42.2 4.8 %collective-permute-start.14 = (f32[3,16,128]{2,1,0:T(8,128)S(1)}, f32[3,16,128]{2,1,0:T(8,128)S(1)}, u32[]{:S(2)}, u32[]{:S(2)}) collective-permute-start(f32[3,16,128]{2,1,0:T(8,128)S(1)} %get-tuple-element.100), channel_id=1, source_target_pairs={{0,24},{8,16},{16,8},{24,0},{1,25},{9,17},{17,9},{25,1},{2,26},{10... | collective-permute-start | bytes 73736 | tf_op jit(solution)/shard_map/ppermute | solution.py:528
  43.4 5.2 %collective-permute-start.7 = (f32[8,128]{1,0:T(8,128)S(1)}, f32[8,128]{1,0:T(8,128)S(1)}, u32[]{:S(2)}, u32[]{:S(2)}) collective-permute-start(f32[8,128]{1,0:T(8,128)S(1)} %add.79), channel_id=1, source_target_pairs={{0,4},{1,5},{2,6},{3,7},{4,0},{5,1},{6,2},{7,3},{8,12},{9,13},{10,... | collective-permute-start | bytes 12296 | tf_op jit(solution)/shard_map/ppermute | solution.py:528
  53.1 16.7 %collective-permute-start.18 = (f32[68,8,128]{2,1,0:T(8,128)S(1)}, f32[68,8,128]{2,1,0:T(8,128)S(1)}, u32[]{:S(2)}, u32[]{:S(2)}) collective-permute-start(f32[68,8,128]{2,1,0:T(8,128)S(1)} %get-tuple-element.69), channel_id=1, source_target_pairs={{0,8},{8,16},{16,24},{24,25},{25,17},{17,9},{9,1},{1,2},{2,10},{10... | collective-permute-start | bytes 835592 | tf_op jit(solution)/shard_map/ppermute | solution.py:583
  54.3 15.4 %collective-permute-start.19 = (f32[68,8,128]{2,1,0:T(8,128)S(1)}, f32[68,8,128]{2,1,0:T(8,128)S(1)}, u32[]{:S(2)}, u32[]{:S(2)}) collective-permute-start(f32[68,8,128]{2,1,0:T(8,128)S(1)} %get-tuple-element.70), channel_id=1, source_target_pairs={{8,0},{16,8},{24,16},{25,24},{17,25},{9,17},{1,9},{2,1},{10,2},{18... | collective-permute-start | bytes 835592 | tf_op jit(solution)/shard_map/ppermute | solution.py:584
  54.3 6.6 %collective-permute-start.15 = (f32[8,128]{1,0:T(8,128)S(1)}, f32[8,128]{1,0:T(8,128)S(1)}, u32[]{:S(2)}, u32[]{:S(2)}) collective-permute-start(f32[8,128]{1,0:T(8,128)S(1)} %add.80), channel_id=1, source_target_pairs={{0,16},{8,24},{16,0},{24,8},{1,17},{9,25},{17,1},{25,9},{2,18},{10... | collective-permute-start | bytes 12296 | tf_op jit(solution)/shard_map/ppermute | solution.py:528
  54.6 6.3 %collective-permute-start.16 = (f32[8,128]{1,0:T(8,128)S(1)}, f32[8,128]{1,0:T(8,128)S(1)}, u32[]{:S(2)}, u32[]{:S(2)}) collective-permute-start(f32[8,128]{1,0:T(8,128)S(1)} %get-tuple-element.67), channel_id=1, source_target_pairs={{0,8},{8,0},{16,24},{24,16},{1,9},{9,1},{17,25},{25,17},{2,10},{10... | collective-permute-start | bytes 12296 | tf_op jit(solution)/shard_map/ppermute | solution.py:528
  60.9 2.5 %collective-permute-start.20 = (f32[8,128]{1,0:T(8,128)S(1)}, f32[8,128]{1,0:T(8,128)S(1)}, u32[]{:S(2)}, u32[]{:S(2)}) collective-permute-start(f32[8,128]{1,0:T(8,128)S(1)} %add.83), channel_id=1, source_target_pairs={{0,1},{1,0},{2,3},{3,2},{4,5},{5,4},{6,7},{7,6},{8,9},{9,8},{10,11... | collective-permute-start | bytes 12296 | tf_op jit(solution)/shard_map/ppermute | solution.py:528
  61.0 7.8 %collective-permute-start.17 = (f32[8,128]{1,0:T(8,128)S(1)}, f32[8,128]{1,0:T(8,128)S(1)}, u32[]{:S(2)}, u32[]{:S(2)}) collective-permute-start(f32[8,128]{1,0:T(8,128)S(1)} %add.81), channel_id=1, source_target_pairs={{0,4},{1,5},{2,6},{3,7},{4,0},{5,1},{6,2},{7,3},{8,12},{9,13},{10,... | collective-permute-start | bytes 12296 | tf_op jit(solution)/shard_map/ppermute | solution.py:528
  63.4 6.3 %collective-permute-start.21 = (f32[8,128]{1,0:T(8,128)S(1)}, f32[8,128]{1,0:T(8,128)S(1)}, u32[]{:S(2)}, u32[]{:S(2)}) collective-permute-start(f32[8,128]{1,0:T(8,128)S(1)} %add.84), channel_id=1, source_target_pairs={{0,2},{1,3},{2,0},{3,1},{4,6},{5,7},{6,4},{7,5},{8,10},{9,11},{10,... | collective-permute-start | bytes 12296 | tf_op jit(solution)/shard_map/ppermute | solution.py:528
  74.8 16.8 %collective-permute-start.25 = (f32[68,8,128]{2,1,0:T(8,128)S(1)}, f32[68,8,128]{2,1,0:T(8,128)S(1)}, u32[]{:S(2)}, u32[]{:S(2)}) collective-permute-start(f32[68,8,128]{2,1,0:T(8,128)S(1)} %get-tuple-element.79), channel_id=1, source_target_pairs={{0,8},{8,16},{16,24},{24,25},{25,17},{17,9},{9,1},{1,2},{2,10},{10... | collective-permute-start | bytes 835592 | tf_op jit(solution)/shard_map/ppermute | solution.py:583
  78.5 13.1 %collective-permute-start.26 = (f32[68,8,128]{2,1,0:T(8,128)S(1)}, f32[68,8,128]{2,1,0:T(8,128)S(1)}, u32[]{:S(2)}, u32[]{:S(2)}) collective-permute-start(f32[68,8,128]{2,1,0:T(8,128)S(1)} %get-tuple-element.80), channel_id=1, source_target_pairs={{8,0},{16,8},{24,16},{25,24},{17,25},{9,17},{1,9},{2,1},{10,2},{18... | collective-permute-start | bytes 835592 | tf_op jit(solution)/shard_map/ppermute | solution.py:584
  78.5 6.6 %collective-permute-start.22 = (f32[8,128]{1,0:T(8,128)S(1)}, f32[8,128]{1,0:T(8,128)S(1)}, u32[]{:S(2)}, u32[]{:S(2)}) collective-permute-start(f32[8,128]{1,0:T(8,128)S(1)} %add.82), channel_id=1, source_target_pairs={{0,16},{8,24},{16,0},{24,8},{1,17},{9,25},{17,1},{25,9},{2,18},{10... | collective-permute-start | bytes 12296 | tf_op jit(solution)/shard_map/ppermute | solution.py:528
  79.4 5.7 %collective-permute-start.23 = (f32[8,128]{1,0:T(8,128)S(1)}, f32[8,128]{1,0:T(8,128)S(1)}, u32[]{:S(2)}, u32[]{:S(2)}) collective-permute-start(f32[8,128]{1,0:T(8,128)S(1)} %get-tuple-element.77), channel_id=1, source_target_pairs={{0,8},{8,0},{16,24},{24,16},{1,9},{9,1},{17,25},{25,17},{2,10},{10... | collective-permute-start | bytes 12296 | tf_op jit(solution)/shard_map/ppermute | solution.py:528
  85.0 2.5 %collective-permute-start.27 = (f32[8,128]{1,0:T(8,128)S(1)}, f32[8,128]{1,0:T(8,128)S(1)}, u32[]{:S(2)}, u32[]{:S(2)}) collective-permute-start(f32[8,128]{1,0:T(8,128)S(1)} %add.88), channel_id=1, source_target_pairs={{0,1},{1,0},{2,3},{3,2},{4,5},{5,4},{6,7},{7,6},{8,9},{9,8},{10,11... | collective-permute-start | bytes 12296 | tf_op jit(solution)/shard_map/ppermute | solution.py:528
  85.0 5.5 %collective-permute-start.24 = (f32[8,128]{1,0:T(8,128)S(1)}, f32[8,128]{1,0:T(8,128)S(1)}, u32[]{:S(2)}, u32[]{:S(2)}) collective-permute-start(f32[8,128]{1,0:T(8,128)S(1)} %add.86), channel_id=1, source_target_pairs={{0,4},{1,5},{2,6},{3,7},{4,0},{5,1},{6,2},{7,3},{8,12},{9,13},{10,... | collective-permute-start | bytes 12296 | tf_op jit(solution)/shard_map/ppermute | solution.py:528
  87.5 4.0 %collective-permute-start.28 = (f32[8,128]{1,0:T(8,128)S(1)}, f32[8,128]{1,0:T(8,128)S(1)}, u32[]{:S(2)}, u32[]{:S(2)}) collective-permute-start(f32[8,128]{1,0:T(8,128)S(1)} %add.89), channel_id=1, source_target_pairs={{0,2},{1,3},{2,0},{3,1},{4,6},{5,7},{6,4},{7,5},{8,10},{9,11},{10,... | collective-permute-start | bytes 12296 | tf_op jit(solution)/shard_map/ppermute | solution.py:528
  96.5 18.6 %collective-permute-start.32 = (f32[68,8,128]{2,1,0:T(8,128)S(1)}, f32[68,8,128]{2,1,0:T(8,128)S(1)}, u32[]{:S(2)}, u32[]{:S(2)}) collective-permute-start(f32[68,8,128]{2,1,0:T(8,128)S(1)} %get-tuple-element.89), channel_id=1, source_target_pairs={{0,8},{8,16},{16,24},{24,25},{25,17},{17,9},{9,1},{1,2},{2,10},{10... | collective-permute-start | bytes 835592 | tf_op jit(solution)/shard_map/ppermute | solution.py:583
  101.8 13.3 %collective-permute-start.33 = (f32[68,8,128]{2,1,0:T(8,128)S(1)}, f32[68,8,128]{2,1,0:T(8,128)S(1)}, u32[]{:S(2)}, u32[]{:S(2)}) collective-permute-start(f32[68,8,128]{2,1,0:T(8,128)S(1)} %get-tuple-element.90), channel_id=1, source_target_pairs={{8,0},{16,8},{24,16},{25,24},{17,25},{9,17},{1,9},{2,1},{10,2},{18... | collective-permute-start | bytes 835592 | tf_op jit(solution)/shard_map/ppermute | solution.py:584
  101.8 6.6 %collective-permute-start.29 = (f32[8,128]{1,0:T(8,128)S(1)}, f32[8,128]{1,0:T(8,128)S(1)}, u32[]{:S(2)}, u32[]{:S(2)}) collective-permute-start(f32[8,128]{1,0:T(8,128)S(1)} %add.87), channel_id=1, source_target_pairs={{0,16},{8,24},{16,0},{24,8},{1,17},{9,25},{17,1},{25,9},{2,18},{10... | collective-permute-start | bytes 12296 | tf_op jit(solution)/shard_map/ppermute | solution.py:528
  102.0 6.4 %collective-permute-start.30 = (f32[8,128]{1,0:T(8,128)S(1)}, f32[8,128]{1,0:T(8,128)S(1)}, u32[]{:S(2)}, u32[]{:S(2)}) collective-permute-start(f32[8,128]{1,0:T(8,128)S(1)} %get-tuple-element.86), channel_id=1, source_target_pairs={{0,8},{8,0},{16,24},{24,16},{1,9},{9,1},{17,25},{25,17},{2,10},{10... | collective-permute-start | bytes 12296 | tf_op jit(solution)/shard_map/ppermute | solution.py:528
  108.4 2.5 %collective-permute-start.34 = (f32[8,128]{1,0:T(8,128)S(1)}, f32[8,128]{1,0:T(8,128)S(1)}, u32[]{:S(2)}, u32[]{:S(2)}) collective-permute-start(f32[8,128]{1,0:T(8,128)S(1)} %add.93), channel_id=1, source_target_pairs={{0,1},{1,0},{2,3},{3,2},{4,5},{5,4},{6,7},{7,6},{8,9},{9,8},{10,11... | collective-permute-start | bytes 12296 | tf_op jit(solution)/shard_map/ppermute | solution.py:528
  108.4 2.5 %collective-permute-start.31 = (f32[8,128]{1,0:T(8,128)S(1)}, f32[8,128]{1,0:T(8,128)S(1)}, u32[]{:S(2)}, u32[]{:S(2)}) collective-permute-start(f32[8,128]{1,0:T(8,128)S(1)} %add.91), channel_id=1, source_target_pairs={{0,4},{1,5},{2,6},{3,7},{4,0},{5,1},{6,2},{7,3},{8,12},{9,13},{10,... | collective-permute-start | bytes 12296 | tf_op jit(solution)/shard_map/ppermute | solution.py:528
  110.8 4.3 %collective-permute-start.35 = (f32[8,128]{1,0:T(8,128)S(1)}, f32[8,128]{1,0:T(8,128)S(1)}, u32[]{:S(2)}, u32[]{:S(2)}) collective-permute-start(f32[8,128]{1,0:T(8,128)S(1)} %add.94), channel_id=1, source_target_pairs={{0,2},{1,3},{2,0},{3,1},{4,6},{5,7},{6,4},{7,5},{8,10},{9,11},{10,... | collective-permute-start | bytes 12296 | tf_op jit(solution)/shard_map/ppermute | solution.py:528
  110.9 9.1 %collective-permute-start.36 = (f32[8,128]{1,0:T(8,128)S(1)}, f32[8,128]{1,0:T(8,128)S(1)}, u32[]{:S(2)}, u32[]{:S(2)}) collective-permute-start(f32[8,128]{1,0:T(8,128)S(1)} %add.92), channel_id=1, source_target_pairs={{0,16},{8,24},{16,0},{24,8},{1,17},{9,25},{17,1},{25,9},{2,18},{10... | collective-permute-start | bytes 12296 | tf_op jit(solution)/shard_map/ppermute | solution.py:528
  122.3 13.9 %collective-permute-start.39 = (f32[64,8,128]{2,1,0:T(8,128)S(1)}, f32[64,8,128]{2,1,0:T(8,128)S(1)}, u32[]{:S(2)}, u32[]{:S(2)}) collective-permute-start(f32[64,8,128]{2,1,0:T(8,128)S(1)} %get-tuple-element.96), channel_id=1, source_target_pairs={{0,8},{8,0},{16,24},{24,16},{1,9},{9,1},{17,25},{25,17},{2,10},{10... | collective-permute-start | bytes 786440 | tf_op jit(solution)/shard_map/ppermute | solution.py:528
  126.0 10.3 %collective-permute-start.40 = (f32[64,8,128]{2,1,0:T(8,128)S(1)}, f32[64,8,128]{2,1,0:T(8,128)S(1)}, u32[]{:S(2)}, u32[]{:S(2)}) collective-permute-start(f32[64,8,128]{2,1,0:T(8,128)S(1)} %get-tuple-element.97), channel_id=1, source_target_pairs={{0,16},{8,24},{16,0},{24,8},{1,17},{9,25},{17,1},{25,9},{2,18},{10... | collective-permute-start | bytes 786440 | tf_op jit(solution)/shard_map/ppermute | solution.py:528
  127.6 13.5 %collective-permute-start.41 = (f32[64,8,128]{2,1,0:T(8,128)S(1)}, f32[64,8,128]{2,1,0:T(8,128)S(1)}, u32[]{:S(2)}, u32[]{:S(2)}) collective-permute-start(f32[64,8,128]{2,1,0:T(8,128)S(1)} %get-tuple-element.98), channel_id=1, source_target_pairs={{0,24},{8,16},{16,8},{24,0},{1,25},{9,17},{17,9},{25,1},{2,26},{10... | collective-permute-start | bytes 786440 | tf_op jit(solution)/shard_map/ppermute | solution.py:528
  129.2 2.8 %collective-permute-start.37 = (f32[8,128]{1,0:T(8,128)S(1)}, f32[8,128]{1,0:T(8,128)S(1)}, u32[]{:S(2)}, u32[]{:S(2)}) collective-permute-start(f32[8,128]{1,0:T(8,128)S(1)} %add.96), channel_id=1, source_target_pairs={{0,1},{1,0},{2,3},{3,2},{4,5},{5,4},{6,7},{7,6},{8,9},{9,8},{10,11... | collective-permute-start | bytes 12296 | tf_op jit(solution)/shard_map/ppermute | solution.py:528
  132.0 4.3 %collective-permute-start.38 = (f32[8,128]{1,0:T(8,128)S(1)}, f32[8,128]{1,0:T(8,128)S(1)}, u32[]{:S(2)}, u32[]{:S(2)}) collective-permute-start(f32[8,128]{1,0:T(8,128)S(1)} %add.97), channel_id=1, source_target_pairs={{0,2},{1,3},{2,0},{3,1},{4,6},{5,7},{6,4},{7,5},{8,10},{9,11},{10,... | collective-permute-start | bytes 12296 | tf_op jit(solution)/shard_map/ppermute | solution.py:528

commit v3 on v2

--- a/solution.py
+++ b/solution.py
@@ -62,7 +62,7 @@
     return jnp.where(last, f, pltpu.roll(f, LANES - 1, axis=1))
 
 
-def call(kernel, out_shape, in_specs, scratch=(), flops=10_000_000, **kwargs):
+def call(kernel, out_shape, in_specs, scratch=(), flops=2_000_000_000, **kwargs):
     return pl.pallas_call(
         kernel,
         out_shape=out_shape,
@@ -120,7 +120,7 @@
     return out
 
 
-def pack_kernel(scal, state, planes, s0, s1, s2, s3, pl_out):
+def pack_kernel(scal, state, planes, ids, s0, s1, s2, s3, pl_out):
     slab = scal[1]
     group = lanes() >> 5
     masks = [group == c for c in range(4)]
@@ -132,22 +132,24 @@
                 out[x * 4 + kt] = block_transposed(sources, slab ^ s, masks)
         return carry
 
-    lax.fori_loop(0, XI, per_row, 0)
+    rows("fill", per_row)
+    for half in range(2):
+        for out in (s0, s1, s2, s3):
+            out[TILES + half] = ids[half * 8 : half * 8 + 8].astype(F32)
     for plane in range(planes.shape[0]):
         for kt in range(4):
             sources = [planes[plane, c, kt * 8 : kt * 8 + 8, :] for c in range(4)]
             pl_out[plane * 4 + kt] = block_transposed(sources, slab, masks)
 
 
-def maps_kernel(ints, ids, maps):
-    own, slab = ints[0], ints[1]
+def maps_kernel(ints, mid, left, right, maps):
+    slab = ints[1]
     lane = lanes(NZ)
     pieces = []
     for g in range(GX):
-        source = own ^ g
-        moved_mid = pltpu.roll(ids[source, 0], (16 - 32 * slab) & (LANES - 1), axis=1)
-        moved_left = pltpu.roll(ids[source, 1], 16, axis=1)
-        moved_right = pltpu.roll(ids[source, 2], OWN + 16, axis=1)
+        moved_mid = pltpu.roll(mid[g], (16 - 32 * slab) & (LANES - 1), axis=1)
+        moved_left = pltpu.roll(left[g], 16, axis=1)
+        moved_right = pltpu.roll(right[g], OWN + 16, axis=1)
         here = jnp.where((lane[:XI] < 16) & (slab == 0), moved_left, moved_mid)
         here = jnp.where((lane[:XI] >= OWN + 16) & (slab == 3), moved_right, here)
         pieces += [here, jnp.full((XI, LANES), -1.0, F32)]
@@ -188,10 +190,12 @@
     scal, profile, s0, r1, r2, r3, p0, *rest, layouts, per_layout
 ):
     plane_refs = (p0,) + rest[: layouts - 1]
-    fields, inflow, su, sd, bands, sums, held, planes = rest[layouts - 1 :]
+    fields, inflow, su, sd, bands, sums, ids, held, planes = rest[layouts - 1 :]
     own, here = scal[0], scal[2]
     for s, source in enumerate((s0, r1, r2, r3)):
-        held[own ^ s] = source[...]
+        held[own ^ s] = source[:TILES]
+        for half in range(2):
+            ids[own ^ s, half * 8 : half * 8 + 8, :] = source[TILES + half]
     for s, source in enumerate(plane_refs):
         planes[here ^ s] = source[...]
 
@@ -543,23 +547,19 @@
     gy_up = [(j, (j + 1) % groups) for j in range(groups)]
     gy_down = [(b, a) for a, b in gy_up]
 
-    ids = turbine_cell[0, :, NZ // 2, :].astype(F32)
-    ids = jnp.stack([ids, lax.ppermute(ids, "gy", gy_up), lax.ppermute(ids, "gy", gy_down)])
-
-    chunk = shape(TILES, 8, LANES)
+    chunk = shape(TILES + 2, 8, LANES)
     s0, s1, s2, s3, plane = call(
         pack_kernel,
         (chunk, chunk, chunk, chunk, shape(per_layout * 4, 8, LANES)),
-        [SMEM, VMEM, VMEM],
+        [SMEM, VMEM, VMEM, VMEM],
         name="pack",
-    )(scal, state[0], planes)
-    ids = jnp.stack([ids] + [swapped(ids, "gx", GX, s) for s in (1, 2, 3)])
+    )(scal, state[0], planes, turbine_cell[0, :, NZ // 2, :])
     received = [swapped(value, "gx", GX, s) for s, value in ((1, s1), (2, s2), (3, s3))]
+    received[0], plane = lax.optimization_barrier((received[0], plane))
     plane_received = [swapped(plane, "layout", layouts, s) for s in range(1, layouts)]
-    maps = call(maps_kernel, shape(4, 2 * OWN, LANES), [SMEM, VMEM], name="maps")(scal, ids)
 
     first_payload = shape(TILES + MORE + 4, 8, LANES)
-    fields, inflow, su, sd, bands, sums = call(
+    fields, inflow, su, sd, bands, sums, ids = call(
         functools.partial(unpack_kernel, layouts=layouts, per_layout=per_layout),
         (
             shape(4, XI, OWN, LANES),
@@ -568,6 +568,7 @@
             first_payload,
             shape(2, OWN, LANES),
             shape(8, LANES),
+            shape(GX, XI, LANES),
         ),
         [SMEM, VMEM] + [VMEM] * (4 + layouts),
         [
@@ -577,18 +578,23 @@
         name="unpack",
     )(scal, profile, s0, *received, plane, *plane_received)
 
+    maps = call(maps_kernel, shape(4, 2 * OWN, LANES), [SMEM, VMEM, VMEM, VMEM], name="maps")(
+        scal, ids, lax.ppermute(ids, "gy", gy_up), lax.ppermute(ids, "gy", gy_down)
+    )
+
     half = groups // 2
+
+    def last_round(value):
+        return sum([swapped(value, "gy", groups, d) for d in range(1, half)], value)
+
     mean = pending = None
     for step in range(STEPS):
+        partial = sums + swapped(sums, "gx", GX, 1)
+        su, sd, partial = lax.optimization_barrier((su, sd, partial))
         lo = lax.ppermute(su, ("gx", "gy"), up)
         hi = lax.ppermute(sd, ("gx", "gy"), down)
         if pending is not None:
-            mean = pending
-            distance = 1
-            while distance < half:
-                mean = mean + swapped(mean, "gy", groups, distance)
-                distance *= 2
-        partial = sums + swapped(sums, "gx", GX, 1)
+            mean = last_round(pending)
         partial = partial + swapped(partial, "gy", groups, half)
         fields, partial = lax.optimization_barrier((fields, partial))
         arriving = swapped(partial, "gx", GX, 2)
@@ -604,7 +610,7 @@
             tuple(outs),
             [VMEM] * len(operands),
             step_scratch(),
-            flops=30_000_000,
+            flops=6_000_000_000,
             name="step%d" % step,
         )(*operands)
         results = list(results)
@@ -616,12 +622,9 @@
             inflow = results.pop(0)
         fields, arriving = lax.optimization_barrier((fields, arriving))
         pending = partial + arriving
-    mean = pending
-    distance = 1
-    while distance < half:
-        mean = mean + swapped(mean, "gy", groups, distance)
-        distance *= 2
-
+    mean = last_round(pending)
+
+    chunk = shape(TILES, 8, LANES)
     s0, s1, s2, s3 = call(
         send_kernel,
         (chunk, chunk, chunk, chunk),

time: 144 us -> 141 us (0.979)
  starting transfers between devices: 69.9 us -> 55.8 us
  waiting for transfers between devices: 39.2 us -> 50.5 us
    ppermute x32 -> x33, waiting for transfers between devices: 39.2 us -> 50.5 us  [swapped(): return lax.ppermute(value, axis, [(i, i ^ distance) for i in range(size)])]
    ppermute x32 -> x33, starting transfers between devices: 52.9 us -> 42.9 us  [swapped(): return lax.ppermute(value, axis, [(i, i ^ distance) for i in range(size)])]
    ppermute x4, starting transfers between devices: 13.4 us -> 9.18 us  [local(): lo = lax.ppermute(su, ('gx', 'gy'), up)]
  transfers between devices with their start and end apart: 42 -> 43, of which waited for: 16 -> 20; matrix products, arithmetic and copies ran while one was open for 1% -> 0% of each run, Pallas kernels for 5% -> 5%
where the time goes in v3:
time: 141 us
  starting transfers between devices  55.8 us (40%)
  waiting for transfers between devices  50.5 us (36%)
  Pallas kernels  30.1 us (21%)
  local copies, waits for them, and re-layouts  3.91 us (3%)
    ppermute x33, waiting for transfers between devices, swapped(): return lax.ppermute(value, axis, [(i, i ^ distance) for i in range(size)])  50.5 us
    ppermute x33, starting transfers between devices, swapped(): return lax.ppermute(value, axis, [(i, i ^ distance) for i in range(size)])  42.9 us
    pallas_call x4, Pallas kernels, local(): call(functools.partial(step_kernel, step=step, cells=cells), tuple(outs),...  19.3 us
    ppermute x4, starting transfers between devices, local(): lo = lax.ppermute(su, ('gx', 'gy'), up)  9.18 us
    pallas_call x1, Pallas kernels, local(): call(functools.partial(final_kernel, cells=cells), shape(4, XI, NZ, LANES...  3.11 us
  transfers between devices with their start and end apart: 43, of which 20 were waited for; matrix products, arithmetic and copies ran while one was open for 0% of the time, Pallas kernels for 5%

profile of v3, /device:TPU:1, one launch (start us, length us, event | category | flops | bytes accessed | tf_op | source)
XLA Modules:
  0.0 140.7 jit_solution(5891562563865874718)
XLA Ops:
  0.0 0.8 slice.3
  0.9 0.6 copy-done.2
  1.6 1.2 copy-done
  2.8 0.9 copy-done.1
  3.7 2.0 %pack.1 = (f32[66,8,128]{2,1,0:T(8,128)S(1)}, f32[66,8,128]{2,1,0:T(8,128)S(1)}, f32[66,8,128]{2,1,0:T(8,128)S(1)}, f32[66,8,128]{2,1,0:T(8,128)S(1)}, f32[8,8,128]{2,1,0:T(8,128)S(1)}) custom-call(s32[135]{0:T(256)S(1)} %concatenate.3.scal.ints, f32[4,16,32,128]{3,2,1,0:T(8,128)S(1)} %bitcast.11, f32[2,4,32,128]{3,2,1,0:T(8,128)S(1)} %copy-done.1, ...), custom_call_target="tpu_custom_call" | custom-call | flops 2000000000 | bytes 4000000 | tf_op jit(solution)/shard_map/pack/pallas_call | solution.py:551
  5.7 1.5 %collective-permute-start = (f32[66,8,128]{2,1,0:T(8,128)S(1)}, f32[66,8,128]{2,1,0:T(8,128)S(1)}, u32[]{:S(2)}, u32[]{:S(2)}) collective-permute-start(f32[66,8,128]{2,1,0:T(8,128)S(1)} %get-tuple-element.68), channel_id=1, source_target_pairs={{0,8},{8,0},{16,24},{24,16},{1,9},{9,1},{17,25},{25,17},{2,10},{10... | collective-permute-start | bytes 811016 | tf_op jit(solution)/shard_map/ppermute | solution.py:532
  7.2 3.0 %collective-permute-start.1 = (f32[66,8,128]{2,1,0:T(8,128)S(1)}, f32[66,8,128]{2,1,0:T(8,128)S(1)}, u32[]{:S(2)}, u32[]{:S(2)}) collective-permute-start(f32[66,8,128]{2,1,0:T(8,128)S(1)} %get-tuple-element.71), channel_id=1, source_target_pairs={{0,16},{8,24},{16,0},{24,8},{1,17},{9,25},{17,1},{25,9},{2,18},{10... | collective-permute-start | bytes 811016 | tf_op jit(solution)/shard_map/ppermute | solution.py:532
  10.2 0.2 collective-permute-start.2
  10.6 1.7 %collective-permute-start.3 = (f32[8,8,128]{2,1,0:T(8,128)S(1)}, f32[8,8,128]{2,1,0:T(8,128)S(1)}, u32[]{:S(2)}, u32[]{:S(2)}) collective-permute-start(f32[8,8,128]{2,1,0:T(8,128)S(1)} %get-tuple-element.73.p0), channel_id=1, source_target_pairs={{0,32},{32,0},{64,96},{96,64},{1,33},{33,1},{65,97},{97,65},{2,34}... | collective-permute-start | bytes 98312 | tf_op jit(solution)/shard_map/ppermute | solution.py:532
  12.3 3.3 %collective-permute-start.4 = (f32[8,8,128]{2,1,0:T(8,128)S(1)}, f32[8,8,128]{2,1,0:T(8,128)S(1)}, u32[]{:S(2)}, u32[]{:S(2)}) collective-permute-start(f32[8,8,128]{2,1,0:T(8,128)S(1)} %get-tuple-element.73.p0), channel_id=1, source_target_pairs={{0,64},{32,96},{64,0},{96,32},{1,65},{33,97},{65,1},{97,33},{2,66}... | collective-permute-start | bytes 98312 | tf_op jit(solution)/shard_map/ppermute | solution.py:532
  15.8 1.0 collective-permute-done.1.r2
  16.8 6.0 %collective-permute-done.2.r3 = f32[66,8,128]{2,1,0:T(8,128)S(1)} collective-permute-done((f32[66,8,128]{2,1,0:T(8,128)S(1)}, f32[66,8,128]{2,1,0:T(8,128)S(1)}, u32[]{:S(2)}, u32[]{:S(2)}) %collective-permute-start.2) | collective-permute-done | bytes 270368 | tf_op jit(solution)/shard_map/ppermute | solution.py:532
  22.8 1.8 %unpack.1 = (f32[4,16,32,128]{3,2,1,0:T(8,128)S(1)}, f32[4,32,128]{2,1,0:T(8,128)S(1)}, f32[72,8,128]{2,1,0:T(8,128)S(1)}, f32[72,8,128]{2,1,0:T(8,128)S(1)}, f3...) custom-call(s32[135]{0:T(256)S(1)} %concatenate.3.scal.ints, f32[8,128]{1,0:T(8,128)S(1)} %pad.4.profile, ...), custom_call_target="tpu_custom_call" | custom-call | flops 2000000000 | bytes 4000000 | tf_op jit(solution)/shard_map/unpack/pallas_call | solution.py:562
  24.6 0.3 collective-permute-start.6
  24.9 0.9 collective-permute-done.6
  25.8 3.1 %collective-permute-start.8 = (f32[72,8,128]{2,1,0:T(8,128)S(1)}, f32[72,8,128]{2,1,0:T(8,128)S(1)}, u32[]{:S(2)}, u32[]{:S(2)}) collective-permute-start(f32[72,8,128]{2,1,0:T(8,128)S(1)} %get-tuple-element.80), channel_id=1, source_target_pairs={{0,8},{8,16},{16,24},{24,25},{25,17},{17,9},{9,1},{1,2},{2,10},{10... | collective-permute-start | bytes 884744 | tf_op jit(solution)/shard_map/ppermute | solution.py:594
  28.9 1.4 %collective-permute-start.10 = (f32[4,16,128]{2,1,0:T(8,128)S(1)}, f32[4,16,128]{2,1,0:T(8,128)S(1)}, u32[]{:S(2)}, u32[]{:S(2)}) collective-permute-start(f32[4,16,128]{2,1,0:T(8,128)S(1)} %get-tuple-element.82.mid), channel_id=1, source_target_pairs={{0,1},{1,2},{2,3},{3,4},{4,5},{5,6},{6,7},{7,0},{8,9},{9,10},{10,1... | collective-permute-start | bytes 98312 | tf_op jit(solution)/shard_map/ppermute | solution.py:582
  30.3 2.3 %collective-permute-start.11 = (f32[4,16,128]{2,1,0:T(8,128)S(1)}, f32[4,16,128]{2,1,0:T(8,128)S(1)}, u32[]{:S(2)}, u32[]{:S(2)}) collective-permute-start(f32[4,16,128]{2,1,0:T(8,128)S(1)} %get-tuple-element.82.mid), channel_id=1, source_target_pairs={{1,0},{2,1},{3,2},{4,3},{5,4},{6,5},{7,6},{0,7},{9,8},{10,9},{11,1... | collective-permute-start | bytes 98312 | tf_op jit(solution)/shard_map/ppermute | solution.py:582
  32.6 0.2 collective-permute-start.7
  32.9 4.8 %collective-permute-done.7 = f32[8,128]{1,0:T(8,128)S(1)} collective-permute-done((f32[8,128]{1,0:T(8,128)S(1)}, f32[8,128]{1,0:T(8,128)S(1)}, u32[]{:S(2)}, u32[]{:S(2)}) %collective-permute-start.7) | collective-permute-done | bytes 4128 | tf_op jit(solution)/shard_map/ppermute | solution.py:532
  37.6 1.7 %maps.1.refs_3_ = f32[4,64,128]{2,1,0:T(8,128)S(1)} custom-call(s32[135]{0:T(256)S(1)} %concatenate.3.scal.ints, f32[4,16,128]{2,1,0:T(8,128)S(1)} %get-tuple-element.82.mid, f32[4,16,128]{2,1,0:T(8,128)S(1)} %collective-permute-done.10.left, f32[4,16,128]{2,1,0:T(8,128)S(1)} %collective-permute-done.11.right), custom_call_target="tpu_custom_call" | custom-call | flops 2000000000 | bytes 4000000 | tf_op jit(solution)/shard_map/maps/pallas_call | solution.py:581
  39.3 4.4 %step0.1 = (f32[4,16,32,128]{3,2,1,0:T(8,128)S(1)}, f32[68,8,128]{2,1,0:T(8,128)S(1)}, f32[68,8,128]{2,1,0:T(8,128)S(1)}, f32[2,32,128]{2,1,0:T(8,128)S(1)}, f32...) custom-call(f32[4,16,32,128]{3,2,1,0:T(8,128)S(1)} %get-tuple-element.79.refs_0_, ...), custom_call_target="tpu_custom_call" | custom-call | flops 6000000000 | bytes 4000000 | tf_op jit(solution)/shard_map/step0/pallas_call | solution.py:608
  43.7 0.5 collective-permute-start.13
  44.2 0.8 collective-permute-done.13
  45.0 2.2 %collective-permute-start.15 = (f32[68,8,128]{2,1,0:T(8,128)S(1)}, f32[68,8,128]{2,1,0:T(8,128)S(1)}, u32[]{:S(2)}, u32[]{:S(2)}) collective-permute-start(f32[68,8,128]{2,1,0:T(8,128)S(1)} %get-tuple-element.93), channel_id=1, source_target_pairs={{0,8},{8,16},{16,24},{24,25},{25,17},{17,9},{9,1},{1,2},{2,10},{10... | collective-permute-start | bytes 835592 | tf_op jit(solution)/shard_map/ppermute | solution.py:594
  47.2 0.3 collective-permute-start.12
  47.5 6.3 %collective-permute-done.12 = f32[8,128]{1,0:T(8,128)S(1)} collective-permute-done((f32[8,128]{1,0:T(8,128)S(1)}, f32[8,128]{1,0:T(8,128)S(1)}, u32[]{:S(2)}, u32[]{:S(2)}) %collective-permute-start.12) | collective-permute-done | bytes 4128 | tf_op jit(solution)/shard_map/ppermute | solution.py:532
  53.8 5.5 %collective-permute-start.18 = (f32[8,128]{1,0:T(8,128)S(1)}, f32[8,128]{1,0:T(8,128)S(1)}, u32[]{:S(2)}, u32[]{:S(2)}) collective-permute-start(f32[8,128]{1,0:T(8,128)S(1)} %add.95), channel_id=1, source_target_pairs={{0,2},{1,3},{2,0},{3,1},{4,6},{5,7},{6,4},{7,5},{8,10},{9,11},{10,... | collective-permute-start | bytes 12296 | tf_op jit(solution)/shard_map/ppermute | solution.py:532
  59.3 0.2 collective-permute-start.14
  59.5 0.9 collective-permute-done.18
  60.3 2.6 %collective-permute-done.19 = f32[8,128]{1,0:T(8,128)S(1)} collective-permute-done((f32[8,128]{1,0:T(8,128)S(1)}, f32[8,128]{1,0:T(8,128)S(1)}, u32[]{:S(2)}, u32[]{:S(2)}) %collective-permute-start.19) | collective-permute-done | bytes 4128 | tf_op jit(solution)/shard_map/ppermute | solution.py:532
  63.0 5.0 %step1.1 = (f32[4,16,32,128]{3,2,1,0:T(8,128)S(1)}, f32[68,8,128]{2,1,0:T(8,128)S(1)}, f32[68,8,128]{2,1,0:T(8,128)S(1)}, f32[2,32,128]{2,1,0:T(8,128)S(1)}, f32[8,128]{1,0:T(8,128)S(1)}) custom-call(f32[4,16,32,128]{3,2,1,0:T(8,128)S(1)} %get-tuple-element.92.refs_0_, f32[68,8,128]{2,1,0:T(8,128)S(1)} %collective-permute-done.15.refs_1_, ...), custom_call_target="tpu_custom_call" | custom-call | flops 6000000000 | bytes 4000000 | tf_op jit(solution)/shard_map/step1/pallas_call | solution.py:608
  68.0 0.8 collective-permute-start.21
  68.9 0.8 collective-permute-done.21
  69.7 3.3 %collective-permute-start.23 = (f32[68,8,128]{2,1,0:T(8,128)S(1)}, f32[68,8,128]{2,1,0:T(8,128)S(1)}, u32[]{:S(2)}, u32[]{:S(2)}) collective-permute-start(f32[68,8,128]{2,1,0:T(8,128)S(1)} %get-tuple-element.106), channel_id=1, source_target_pairs={{0,8},{8,16},{16,24},{24,25},{25,17},{17,9},{9,1},{1,2},{2,10},{10... | collective-permute-start | bytes 835592 | tf_op jit(solution)/shard_map/ppermute | solution.py:594
  73.0 0.5 collective-permute-start.20
  73.5 6.1 %collective-permute-done.20 = f32[8,128]{1,0:T(8,128)S(1)} collective-permute-done((f32[8,128]{1,0:T(8,128)S(1)}, f32[8,128]{1,0:T(8,128)S(1)}, u32[]{:S(2)}, u32[]{:S(2)}) %collective-permute-start.20) | collective-permute-done | bytes 4128 | tf_op jit(solution)/shard_map/ppermute | solution.py:532
  79.6 2.6 %collective-permute-start.26 = (f32[8,128]{1,0:T(8,128)S(1)}, f32[8,128]{1,0:T(8,128)S(1)}, u32[]{:S(2)}, u32[]{:S(2)}) collective-permute-start(f32[8,128]{1,0:T(8,128)S(1)} %add.101), channel_id=1, source_target_pairs={{0,2},{1,3},{2,0},{3,1},{4,6},{5,7},{6,4},{7,5},{8,10},{9,11},{10,... | collective-permute-start | bytes 12296 | tf_op jit(solution)/shard_map/ppermute | solution.py:532
  82.2 1.2 collective-permute-start.27
  83.4 0.2 collective-permute-start.22
  83.6 2.3 %collective-permute-done.27 = f32[8,128]{1,0:T(8,128)S(1)} collective-permute-done((f32[8,128]{1,0:T(8,128)S(1)}, f32[8,128]{1,0:T(8,128)S(1)}, u32[]{:S(2)}, u32[]{:S(2)}) %collective-permute-start.27) | collective-permute-done | bytes 4128 | tf_op jit(solution)/shard_map/ppermute | solution.py:532
  86.0 5.0 %step2.1 = (f32[4,16,32,128]{3,2,1,0:T(8,128)S(1)}, f32[68,8,128]{2,1,0:T(8,128)S(1)}, f32[68,8,128]{2,1,0:T(8,128)S(1)}, f32[2,32,128]{2,1,0:T(8,128)S(1)}, f32[8,128]{1,0:T(8,128)S(1)}) custom-call(f32[4,16,32,128]{3,2,1,0:T(8,128)S(1)} %get-tuple-element.105.refs_0_, f32[68,8,128]{2,1,0:T(8,128)S(1)} %collective-permute-done.23.refs_1_, ...), custom_call_target="tpu_custom_call" | custom-call | flops 6000000000 | bytes 4000000 | tf_op jit(solution)/shard_map/step2/pallas_call | solution.py:608
  91.0 3.6 %collective-permute-start.29 = (f32[8,128]{1,0:T(8,128)S(1)}, f32[8,128]{1,0:T(8,128)S(1)}, u32[]{:S(2)}, u32[]{:S(2)}) collective-permute-start(f32[8,128]{1,0:T(8,128)S(1)} %get-tuple-element.115), channel_id=1, source_target_pairs={{0,8},{8,0},{16,24},{24,16},{1,9},{9,1},{17,25},{25,17},{2,10},{10... | collective-permute-start | bytes 12296 | tf_op jit(solution)/shard_map/ppermute | solution.py:532
  94.6 0.8 collective-permute-done.29
  95.5 0.6 collective-permute-start.31
  96.1 0.3 collective-permute-start.28
  96.3 6.3 %collective-permute-done.28 = f32[8,128]{1,0:T(8,128)S(1)} collective-permute-done((f32[8,128]{1,0:T(8,128)S(1)}, f32[8,128]{1,0:T(8,128)S(1)}, u32[]{:S(2)}, u32[]{:S(2)}) %collective-permute-start.28) | collective-permute-done | bytes 4128 | tf_op jit(solution)/shard_map/ppermute | solution.py:532
  102.7 2.6 %collective-permute-start.34 = (f32[8,128]{1,0:T(8,128)S(1)}, f32[8,128]{1,0:T(8,128)S(1)}, u32[]{:S(2)}, u32[]{:S(2)}) collective-permute-start(f32[8,128]{1,0:T(8,128)S(1)} %add.107), channel_id=1, source_target_pairs={{0,2},{1,3},{2,0},{3,1},{4,6},{5,7},{6,4},{7,5},{8,10},{9,11},{10,... | collective-permute-start | bytes 12296 | tf_op jit(solution)/shard_map/ppermute | solution.py:532
  105.2 1.3 collective-permute-start.35
  106.5 0.1 collective-permute-done.34
  106.6 2.3 %collective-permute-done.35 = f32[8,128]{1,0:T(8,128)S(1)} collective-permute-done((f32[8,128]{1,0:T(8,128)S(1)}, f32[8,128]{1,0:T(8,128)S(1)}, u32[]{:S(2)}, u32[]{:S(2)}) %collective-permute-start.35) | collective-permute-done | bytes 4128 | tf_op jit(solution)/shard_map/ppermute | solution.py:532
  108.9 0.4 collective-permute-done.30
  109.3 5.8 %collective-permute-start.36 = (f32[8,128]{1,0:T(8,128)S(1)}, f32[8,128]{1,0:T(8,128)S(1)}, u32[]{:S(2)}, u32[]{:S(2)}) collective-permute-start(f32[8,128]{1,0:T(8,128)S(1)} %add.106), channel_id=1, source_target_pairs={{0,16},{8,24},{16,0},{24,8},{1,17},{9,25},{17,1},{25,9},{2,18},{10... | collective-permute-start | bytes 12296 | tf_op jit(solution)/shard_map/ppermute | solution.py:532
  115.1 4.9 %step3.1.fields = f32[4,16,32,128]{3,2,1,0:T(8,128)S(1)} custom-call(f32[4,16,32,128]{3,2,1,0:T(8,128)S(1)} %get-tuple-element.118.refs_0_, f32[68,8,128]{2,1,0:T(8,128)S(1)} %collective-permute-done.31.refs_1_, f32[68,8,128]{2,1,0:T(8,128)S(1)} %collective-permute-done.32.refs_2_, f32[4,64,128]{2,1,0:T(8,128)S(1)} %maps.1.refs_3_, ...), custom_call_target="tpu_custom_call" | custom-call | flops 6000000000 | bytes 4000000 | tf_op jit(solution)/shard_map/step3/pallas_call | solution.py:608
  120.0 2.3 %send.1 = (f32[64,8,128]{2,1,0:T(8,128)S(1)}, f32[64,8,128]{2,1,0:T(8,128)S(1)}, f32[64,8,128]{2,1,0:T(8,128)S(1)}, f32[64,8,128]{2,1,0:T(8,128)S(1)}) custom-call(s32[135]{0:T(256)S(1)} %concatenate.3.scal.ints, f32[4,16,32,128]{3,2,1,0:T(8,128)S(1)} %step3.1.fields), custom_call_target="tpu_custom_call" | custom-call | flops 2000000000 | bytes 4000000 | tf_op jit(solution)/shard_map/send/pallas_call | solution.py:628
  122.4 1.6 %collective-permute-start.41 = (f32[64,8,128]{2,1,0:T(8,128)S(1)}, f32[64,8,128]{2,1,0:T(8,128)S(1)}, u32[]{:S(2)}, u32[]{:S(2)}) collective-permute-start(f32[64,8,128]{2,1,0:T(8,128)S(1)} %get-tuple-element.127), channel_id=1, source_target_pairs={{0,16},{8,24},{16,0},{24,8},{1,17},{9,25},{17,1},{25,9},{2,18},{10... | collective-permute-start | bytes 786440 | tf_op jit(solution)/shard_map/ppermute | solution.py:532
  123.9 2.1 %collective-permute-start.42 = (f32[64,8,128]{2,1,0:T(8,128)S(1)}, f32[64,8,128]{2,1,0:T(8,128)S(1)}, u32[]{:S(2)}, u32[]{:S(2)}) collective-permute-start(f32[64,8,128]{2,1,0:T(8,128)S(1)} %get-tuple-element.128), channel_id=1, source_target_pairs={{0,24},{8,16},{16,8},{24,0},{1,25},{9,17},{17,9},{25,1},{2,26},{10... | collective-permute-start | bytes 786440 | tf_op jit(solution)/shard_map/ppermute | solution.py:532
  126.0 2.3 %collective-permute-start.38 = (f32[8,128]{1,0:T(8,128)S(1)}, f32[8,128]{1,0:T(8,128)S(1)}, u32[]{:S(2)}, u32[]{:S(2)}) collective-permute-start(f32[8,128]{1,0:T(8,128)S(1)} %add.111), channel_id=1, source_target_pairs={{0,2},{1,3},{2,0},{3,1},{4,6},{5,7},{6,4},{7,5},{8,10},{9,11},{10,... | collective-permute-start | bytes 12296 | tf_op jit(solution)/shard_map/ppermute | solution.py:532
  128.3 0.4 collective-permute-done.37
  128.7 1.1 collective-permute-start.39
  129.9 0.4 collective-permute-done.38
  130.2 2.5 %collective-permute-done.39 = f32[8,128]{1,0:T(8,128)S(1)} collective-permute-done((f32[8,128]{1,0:T(8,128)S(1)}, f32[8,128]{1,0:T(8,128)S(1)}, u32[]{:S(2)}, u32[]{:S(2)}) %collective-permute-start.39) | collective-permute-done | bytes 4128 | tf_op jit(solution)/shard_map/ppermute | solution.py:532
  132.7 4.9 %collective-permute-done.42.r3 = f32[64,8,128]{2,1,0:T(8,128)S(1)} collective-permute-done((f32[64,8,128]{2,1,0:T(8,128)S(1)}, f32[64,8,128]{2,1,0:T(8,128)S(1)}, u32[]{:S(2)}, u32[]{:S(2)}) %collective-permute-start.42) | collective-permute-done | bytes 262176 | tf_op jit(solution)/shard_map/ppermute | solution.py:532
  137.6 3.1 %final.1 = f32[4,16,32,128]{3,2,1,0:T(8,128)} custom-call(s32[135]{0:T(256)S(1)} %concatenate.3.scal.ints, f32[8,128]{1,0:T(8,128)S(1)} %add_add_fusion.mean, f32[64,8,128]{2,1,0:T(8,128)S(1)} %get-tuple-element.125.s0, f32[64,8,128]{2,1,0:T(8,128)S(1)} %collective-permute-done.40.r1, f32[64,8,128]{2,1,0:T(8,128)S(1)} %collective-permute-done.41.r2, ...), custom_call_target="tpu_custom_call" | custom-call | flops 2000000000 | bytes 4000000 | tf_op jit(solution)/shard_map/final/pallas_call | solution.py:636
  (66 shorter events, 0.6 us)
Async XLA Ops:
  0.8 0.7 copy-start.2
  0.8 0.7 copy-start.3
  0.9 0.7 copy-start.4
  1.6 1.2 copy-start
  2.8 0.9 copy-start.1
  5.7 4.8 %collective-permute-start = (f32[66,8,128]{2,1,0:T(8,128)S(1)}, f32[66,8,128]{2,1,0:T(8,128)S(1)}, u32[]{:S(2)}, u32[]{:S(2)}) collective-permute-start(f32[66,8,128]{2,1,0:T(8,128)S(1)} %get-tuple-element.68), channel_id=1, source_target_pairs={{0,8},{8,0},{16,24},{24,16},{1,9},{9,1},{17,25},{25,17},{2,10},{10... | collective-permute-start | bytes 811016 | tf_op jit(solution)/shard_map/ppermute | solution.py:532
  7.2 9.6 %collective-permute-start.1 = (f32[66,8,128]{2,1,0:T(8,128)S(1)}, f32[66,8,128]{2,1,0:T(8,128)S(1)}, u32[]{:S(2)}, u32[]{:S(2)}) collective-permute-start(f32[66,8,128]{2,1,0:T(8,128)S(1)} %get-tuple-element.71), channel_id=1, source_target_pairs={{0,16},{8,24},{16,0},{24,8},{1,17},{9,25},{17,1},{25,9},{2,18},{10... | collective-permute-start | bytes 811016 | tf_op jit(solution)/shard_map/ppermute | solution.py:532
  10.2 12.5 %collective-permute-start.2 = (f32[66,8,128]{2,1,0:T(8,128)S(1)}, f32[66,8,128]{2,1,0:T(8,128)S(1)}, u32[]{:S(2)}, u32[]{:S(2)}) collective-permute-start(f32[66,8,128]{2,1,0:T(8,128)S(1)} %get-tuple-element.72), channel_id=1, source_target_pairs={{0,24},{8,16},{16,8},{24,0},{1,25},{9,17},{17,9},{25,1},{2,26},{10... | collective-permute-start | bytes 811016 | tf_op jit(solution)/shard_map/ppermute | solution.py:532
  10.6 12.2 %collective-permute-start.3 = (f32[8,8,128]{2,1,0:T(8,128)S(1)}, f32[8,8,128]{2,1,0:T(8,128)S(1)}, u32[]{:S(2)}, u32[]{:S(2)}) collective-permute-start(f32[8,8,128]{2,1,0:T(8,128)S(1)} %get-tuple-element.73.p0), channel_id=1, source_target_pairs={{0,32},{32,0},{64,96},{96,64},{1,33},{33,1},{65,97},{97,65},{2,34}... | collective-permute-start | bytes 98312 | tf_op jit(solution)/shard_map/ppermute | solution.py:532
  12.3 10.5 %collective-permute-start.4 = (f32[8,8,128]{2,1,0:T(8,128)S(1)}, f32[8,8,128]{2,1,0:T(8,128)S(1)}, u32[]{:S(2)}, u32[]{:S(2)}) collective-permute-start(f32[8,8,128]{2,1,0:T(8,128)S(1)} %get-tuple-element.73.p0), channel_id=1, source_target_pairs={{0,64},{32,96},{64,0},{96,32},{1,65},{33,97},{65,1},{97,33},{2,66}... | collective-permute-start | bytes 98312 | tf_op jit(solution)/shard_map/ppermute | solution.py:532
  15.6 7.2 %collective-permute-start.5 = (f32[8,8,128]{2,1,0:T(8,128)S(1)}, f32[8,8,128]{2,1,0:T(8,128)S(1)}, u32[]{:S(2)}, u32[]{:S(2)}) collective-permute-start(f32[8,8,128]{2,1,0:T(8,128)S(1)} %get-tuple-element.73.p0), channel_id=1, source_target_pairs={{0,96},{32,64},{64,32},{96,0},{1,97},{33,65},{65,33},{97,1},{2,98}... | collective-permute-start | bytes 98312 | tf_op jit(solution)/shard_map/ppermute | solution.py:532
  24.6 1.2 collective-permute-start.6
  25.8 13.5 %collective-permute-start.8 = (f32[72,8,128]{2,1,0:T(8,128)S(1)}, f32[72,8,128]{2,1,0:T(8,128)S(1)}, u32[]{:S(2)}, u32[]{:S(2)}) collective-permute-start(f32[72,8,128]{2,1,0:T(8,128)S(1)} %get-tuple-element.80), channel_id=1, source_target_pairs={{0,8},{8,16},{16,24},{24,25},{25,17},{17,9},{9,1},{1,2},{2,10},{10... | collective-permute-start | bytes 884744 | tf_op jit(solution)/shard_map/ppermute | solution.py:594
  28.9 10.4 %collective-permute-start.9 = (f32[72,8,128]{2,1,0:T(8,128)S(1)}, f32[72,8,128]{2,1,0:T(8,128)S(1)}, u32[]{:S(2)}, u32[]{:S(2)}) collective-permute-start(f32[72,8,128]{2,1,0:T(8,128)S(1)} %get-tuple-element.81), channel_id=1, source_target_pairs={{8,0},{16,8},{24,16},{25,24},{17,25},{9,17},{1,9},{2,1},{10,2},{18... | collective-permute-start | bytes 884744 | tf_op jit(solution)/shard_map/ppermute | solution.py:595
  28.9 8.7 %collective-permute-start.10 = (f32[4,16,128]{2,1,0:T(8,128)S(1)}, f32[4,16,128]{2,1,0:T(8,128)S(1)}, u32[]{:S(2)}, u32[]{:S(2)}) collective-permute-start(f32[4,16,128]{2,1,0:T(8,128)S(1)} %get-tuple-element.82.mid), channel_id=1, source_target_pairs={{0,1},{1,2},{2,3},{3,4},{4,5},{5,6},{6,7},{7,0},{8,9},{9,10},{10,1... | collective-permute-start | bytes 98312 | tf_op jit(solution)/shard_map/ppermute | solution.py:582
  30.3 7.3 %collective-permute-start.11 = (f32[4,16,128]{2,1,0:T(8,128)S(1)}, f32[4,16,128]{2,1,0:T(8,128)S(1)}, u32[]{:S(2)}, u32[]{:S(2)}) collective-permute-start(f32[4,16,128]{2,1,0:T(8,128)S(1)} %get-tuple-element.82.mid), channel_id=1, source_target_pairs={{1,0},{2,1},{3,2},{4,3},{5,4},{6,5},{7,6},{0,7},{9,8},{10,9},{11,1... | collective-permute-start | bytes 98312 | tf_op jit(solution)/shard_map/ppermute | solution.py:582
  32.6 5.0 %collective-permute-start.7 = (f32[8,128]{1,0:T(8,128)S(1)}, f32[8,128]{1,0:T(8,128)S(1)}, u32[]{:S(2)}, u32[]{:S(2)}) collective-permute-start(f32[8,128]{1,0:T(8,128)S(1)} %add.91), channel_id=1, source_target_pairs={{0,4},{1,5},{2,6},{3,7},{4,0},{5,1},{6,2},{7,3},{8,12},{9,13},{10,... | collective-permute-start | bytes 12296 | tf_op jit(solution)/shard_map/ppermute | solution.py:532
  43.7 1.3 collective-permute-start.13
  45.0 18.0 %collective-permute-start.15 = (f32[68,8,128]{2,1,0:T(8,128)S(1)}, f32[68,8,128]{2,1,0:T(8,128)S(1)}, u32[]{:S(2)}, u32[]{:S(2)}) collective-permute-start(f32[68,8,128]{2,1,0:T(8,128)S(1)} %get-tuple-element.93), channel_id=1, source_target_pairs={{0,8},{8,16},{16,24},{24,25},{25,17},{17,9},{9,1},{1,2},{2,10},{10... | collective-permute-start | bytes 835592 | tf_op jit(solution)/shard_map/ppermute | solution.py:594
  47.2 15.8 %collective-permute-start.16 = (f32[68,8,128]{2,1,0:T(8,128)S(1)}, f32[68,8,128]{2,1,0:T(8,128)S(1)}, u32[]{:S(2)}, u32[]{:S(2)}) collective-permute-start(f32[68,8,128]{2,1,0:T(8,128)S(1)} %get-tuple-element.94), channel_id=1, source_target_pairs={{8,0},{16,8},{24,16},{25,24},{17,25},{9,17},{1,9},{2,1},{10,2},{18... | collective-permute-start | bytes 835592 | tf_op jit(solution)/shard_map/ppermute | solution.py:595
  47.2 6.6 %collective-permute-start.12 = (f32[8,128]{1,0:T(8,128)S(1)}, f32[8,128]{1,0:T(8,128)S(1)}, u32[]{:S(2)}, u32[]{:S(2)}) collective-permute-start(f32[8,128]{1,0:T(8,128)S(1)} %add.92), channel_id=1, source_target_pairs={{0,16},{8,24},{16,0},{24,8},{1,17},{9,25},{17,1},{25,9},{2,18},{10... | collective-permute-start | bytes 12296 | tf_op jit(solution)/shard_map/ppermute | solution.py:532
  53.8 5.5 %collective-permute-start.17 = (f32[8,128]{1,0:T(8,128)S(1)}, f32[8,128]{1,0:T(8,128)S(1)}, u32[]{:S(2)}, u32[]{:S(2)}) collective-permute-start(f32[8,128]{1,0:T(8,128)S(1)} %add.95), channel_id=1, source_target_pairs={{0,1},{1,0},{2,3},{3,2},{4,5},{5,4},{6,7},{7,6},{8,9},{9,8},{10,11... | collective-permute-start | bytes 12296 | tf_op jit(solution)/shard_map/ppermute | solution.py:532
  53.8 6.5 %collective-permute-start.18 = (f32[8,128]{1,0:T(8,128)S(1)}, f32[8,128]{1,0:T(8,128)S(1)}, u32[]{:S(2)}, u32[]{:S(2)}) collective-permute-start(f32[8,128]{1,0:T(8,128)S(1)} %add.95), channel_id=1, source_target_pairs={{0,2},{1,3},{2,0},{3,1},{4,6},{5,7},{6,4},{7,5},{8,10},{9,11},{10,... | collective-permute-start | bytes 12296 | tf_op jit(solution)/shard_map/ppermute | solution.py:532
  59.3 3.7 %collective-permute-start.19 = (f32[8,128]{1,0:T(8,128)S(1)}, f32[8,128]{1,0:T(8,128)S(1)}, u32[]{:S(2)}, u32[]{:S(2)}) collective-permute-start(f32[8,128]{1,0:T(8,128)S(1)} %add.95), channel_id=1, source_target_pairs={{0,3},{1,2},{2,1},{3,0},{4,7},{5,6},{6,5},{7,4},{8,11},{9,10},{10,... | collective-permute-start | bytes 12296 | tf_op jit(solution)/shard_map/ppermute | solution.py:532
  59.3 3.7 %collective-permute-start.14 = (f32[8,128]{1,0:T(8,128)S(1)}, f32[8,128]{1,0:T(8,128)S(1)}, u32[]{:S(2)}, u32[]{:S(2)}) collective-permute-start(f32[8,128]{1,0:T(8,128)S(1)} %add.93), channel_id=1, source_target_pairs={{0,4},{1,5},{2,6},{3,7},{4,0},{5,1},{6,2},{7,3},{8,12},{9,13},{10,... | collective-permute-start | bytes 12296 | tf_op jit(solution)/shard_map/ppermute | solution.py:532
  68.0 1.6 %collective-permute-start.21 = (f32[8,128]{1,0:T(8,128)S(1)}, f32[8,128]{1,0:T(8,128)S(1)}, u32[]{:S(2)}, u32[]{:S(2)}) collective-permute-start(f32[8,128]{1,0:T(8,128)S(1)} %get-tuple-element.103), channel_id=1, source_target_pairs={{0,8},{8,0},{16,24},{24,16},{1,9},{9,1},{17,25},{25,17},{2,10},{10... | collective-permute-start | bytes 12296 | tf_op jit(solution)/shard_map/ppermute | solution.py:532
  69.7 16.3 %collective-permute-start.23 = (f32[68,8,128]{2,1,0:T(8,128)S(1)}, f32[68,8,128]{2,1,0:T(8,128)S(1)}, u32[]{:S(2)}, u32[]{:S(2)}) collective-permute-start(f32[68,8,128]{2,1,0:T(8,128)S(1)} %get-tuple-element.106), channel_id=1, source_target_pairs={{0,8},{8,16},{16,24},{24,25},{25,17},{17,9},{9,1},{1,2},{2,10},{10... | collective-permute-start | bytes 835592 | tf_op jit(solution)/shard_map/ppermute | solution.py:594
  73.0 13.0 %collective-permute-start.24 = (f32[68,8,128]{2,1,0:T(8,128)S(1)}, f32[68,8,128]{2,1,0:T(8,128)S(1)}, u32[]{:S(2)}, u32[]{:S(2)}) collective-permute-start(f32[68,8,128]{2,1,0:T(8,128)S(1)} %get-tuple-element.107), channel_id=1, source_target_pairs={{8,0},{16,8},{24,16},{25,24},{17,25},{9,17},{1,9},{2,1},{10,2},{18... | collective-permute-start | bytes 835592 | tf_op jit(solution)/shard_map/ppermute | solution.py:595
  73.0 6.6 %collective-permute-start.20 = (f32[8,128]{1,0:T(8,128)S(1)}, f32[8,128]{1,0:T(8,128)S(1)}, u32[]{:S(2)}, u32[]{:S(2)}) collective-permute-start(f32[8,128]{1,0:T(8,128)S(1)} %add.94), channel_id=1, source_target_pairs={{0,16},{8,24},{16,0},{24,8},{1,17},{9,25},{17,1},{25,9},{2,18},{10... | collective-permute-start | bytes 12296 | tf_op jit(solution)/shard_map/ppermute | solution.py:532
  79.6 3.9 %collective-permute-start.25 = (f32[8,128]{1,0:T(8,128)S(1)}, f32[8,128]{1,0:T(8,128)S(1)}, u32[]{:S(2)}, u32[]{:S(2)}) collective-permute-start(f32[8,128]{1,0:T(8,128)S(1)} %add.101), channel_id=1, source_target_pairs={{0,1},{1,0},{2,3},{3,2},{4,5},{5,4},{6,7},{7,6},{8,9},{9,8},{10,11... | collective-permute-start | bytes 12296 | tf_op jit(solution)/shard_map/ppermute | solution.py:532
  79.6 4.0 %collective-permute-start.26 = (f32[8,128]{1,0:T(8,128)S(1)}, f32[8,128]{1,0:T(8,128)S(1)}, u32[]{:S(2)}, u32[]{:S(2)}) collective-permute-start(f32[8,128]{1,0:T(8,128)S(1)} %add.101), channel_id=1, source_target_pairs={{0,2},{1,3},{2,0},{3,1},{4,6},{5,7},{6,4},{7,5},{8,10},{9,11},{10,... | collective-permute-start | bytes 12296 | tf_op jit(solution)/shard_map/ppermute | solution.py:532
  82.2 3.7 %collective-permute-start.27 = (f32[8,128]{1,0:T(8,128)S(1)}, f32[8,128]{1,0:T(8,128)S(1)}, u32[]{:S(2)}, u32[]{:S(2)}) collective-permute-start(f32[8,128]{1,0:T(8,128)S(1)} %add.101), channel_id=1, source_target_pairs={{0,3},{1,2},{2,1},{3,0},{4,7},{5,6},{6,5},{7,4},{8,11},{9,10},{10,... | collective-permute-start | bytes 12296 | tf_op jit(solution)/shard_map/ppermute | solution.py:532
  83.4 2.5 %collective-permute-start.22 = (f32[8,128]{1,0:T(8,128)S(1)}, f32[8,128]{1,0:T(8,128)S(1)}, u32[]{:S(2)}, u32[]{:S(2)}) collective-permute-start(f32[8,128]{1,0:T(8,128)S(1)} %add.99), channel_id=1, source_target_pairs={{0,4},{1,5},{2,6},{3,7},{4,0},{5,1},{6,2},{7,3},{8,12},{9,13},{10,... | collective-permute-start | bytes 12296 | tf_op jit(solution)/shard_map/ppermute | solution.py:532
  91.0 4.5 %collective-permute-start.29 = (f32[8,128]{1,0:T(8,128)S(1)}, f32[8,128]{1,0:T(8,128)S(1)}, u32[]{:S(2)}, u32[]{:S(2)}) collective-permute-start(f32[8,128]{1,0:T(8,128)S(1)} %get-tuple-element.115), channel_id=1, source_target_pairs={{0,8},{8,0},{16,24},{24,16},{1,9},{9,1},{17,25},{25,17},{2,10},{10... | collective-permute-start | bytes 12296 | tf_op jit(solution)/shard_map/ppermute | solution.py:532
  95.5 19.6 %collective-permute-start.31 = (f32[68,8,128]{2,1,0:T(8,128)S(1)}, f32[68,8,128]{2,1,0:T(8,128)S(1)}, u32[]{:S(2)}, u32[]{:S(2)}) collective-permute-start(f32[68,8,128]{2,1,0:T(8,128)S(1)} %get-tuple-element.119), channel_id=1, source_target_pairs={{0,8},{8,16},{16,24},{24,25},{25,17},{17,9},{9,1},{1,2},{2,10},{10... | collective-permute-start | bytes 835592 | tf_op jit(solution)/shard_map/ppermute | solution.py:594
  96.1 19.0 %collective-permute-start.32 = (f32[68,8,128]{2,1,0:T(8,128)S(1)}, f32[68,8,128]{2,1,0:T(8,128)S(1)}, u32[]{:S(2)}, u32[]{:S(2)}) collective-permute-start(f32[68,8,128]{2,1,0:T(8,128)S(1)} %get-tuple-element.120), channel_id=1, source_target_pairs={{8,0},{16,8},{24,16},{25,24},{17,25},{9,17},{1,9},{2,1},{10,2},{18... | collective-permute-start | bytes 835592 | tf_op jit(solution)/shard_map/ppermute | solution.py:595
  96.1 6.6 %collective-permute-start.28 = (f32[8,128]{1,0:T(8,128)S(1)}, f32[8,128]{1,0:T(8,128)S(1)}, u32[]{:S(2)}, u32[]{:S(2)}) collective-permute-start(f32[8,128]{1,0:T(8,128)S(1)} %add.100), channel_id=1, source_target_pairs={{0,16},{8,24},{16,0},{24,8},{1,17},{9,25},{17,1},{25,9},{2,18},{10... | collective-permute-start | bytes 12296 | tf_op jit(solution)/shard_map/ppermute | solution.py:532
  102.7 3.9 %collective-permute-start.33 = (f32[8,128]{1,0:T(8,128)S(1)}, f32[8,128]{1,0:T(8,128)S(1)}, u32[]{:S(2)}, u32[]{:S(2)}) collective-permute-start(f32[8,128]{1,0:T(8,128)S(1)} %add.107), channel_id=1, source_target_pairs={{0,1},{1,0},{2,3},{3,2},{4,5},{5,4},{6,7},{7,6},{8,9},{9,8},{10,11... | collective-permute-start | bytes 12296 | tf_op jit(solution)/shard_map/ppermute | solution.py:532
  102.7 4.0 %collective-permute-start.34 = (f32[8,128]{1,0:T(8,128)S(1)}, f32[8,128]{1,0:T(8,128)S(1)}, u32[]{:S(2)}, u32[]{:S(2)}) collective-permute-start(f32[8,128]{1,0:T(8,128)S(1)} %add.107), channel_id=1, source_target_pairs={{0,2},{1,3},{2,0},{3,1},{4,6},{5,7},{6,4},{7,5},{8,10},{9,11},{10,... | collective-permute-start | bytes 12296 | tf_op jit(solution)/shard_map/ppermute | solution.py:532
  105.2 3.7 %collective-permute-start.35 = (f32[8,128]{1,0:T(8,128)S(1)}, f32[8,128]{1,0:T(8,128)S(1)}, u32[]{:S(2)}, u32[]{:S(2)}) collective-permute-start(f32[8,128]{1,0:T(8,128)S(1)} %add.107), channel_id=1, source_target_pairs={{0,3},{1,2},{2,1},{3,0},{4,7},{5,6},{6,5},{7,4},{8,11},{9,10},{10,... | collective-permute-start | bytes 12296 | tf_op jit(solution)/shard_map/ppermute | solution.py:532
  106.5 2.8 %collective-permute-start.30 = (f32[8,128]{1,0:T(8,128)S(1)}, f32[8,128]{1,0:T(8,128)S(1)}, u32[]{:S(2)}, u32[]{:S(2)}) collective-permute-start(f32[8,128]{1,0:T(8,128)S(1)} %add.105), channel_id=1, source_target_pairs={{0,4},{1,5},{2,6},{3,7},{4,0},{5,1},{6,2},{7,3},{8,12},{9,13},{10,... | collective-permute-start | bytes 12296 | tf_op jit(solution)/shard_map/ppermute | solution.py:532
  109.3 10.7 %collective-permute-start.36 = (f32[8,128]{1,0:T(8,128)S(1)}, f32[8,128]{1,0:T(8,128)S(1)}, u32[]{:S(2)}, u32[]{:S(2)}) collective-permute-start(f32[8,128]{1,0:T(8,128)S(1)} %add.106), channel_id=1, source_target_pairs={{0,16},{8,24},{16,0},{24,8},{1,17},{9,25},{17,1},{25,9},{2,18},{10... | collective-permute-start | bytes 12296 | tf_op jit(solution)/shard_map/ppermute | solution.py:532
  122.3 10.5 %collective-permute-start.40 = (f32[64,8,128]{2,1,0:T(8,128)S(1)}, f32[64,8,128]{2,1,0:T(8,128)S(1)}, u32[]{:S(2)}, u32[]{:S(2)}) collective-permute-start(f32[64,8,128]{2,1,0:T(8,128)S(1)} %get-tuple-element.126), channel_id=1, source_target_pairs={{0,8},{8,0},{16,24},{24,16},{1,9},{9,1},{17,25},{25,17},{2,10},{10... | collective-permute-start | bytes 786440 | tf_op jit(solution)/shard_map/ppermute | solution.py:532
  122.4 10.4 %collective-permute-start.41 = (f32[64,8,128]{2,1,0:T(8,128)S(1)}, f32[64,8,128]{2,1,0:T(8,128)S(1)}, u32[]{:S(2)}, u32[]{:S(2)}) collective-permute-start(f32[64,8,128]{2,1,0:T(8,128)S(1)} %get-tuple-element.127), channel_id=1, source_target_pairs={{0,16},{8,24},{16,0},{24,8},{1,17},{9,25},{17,1},{25,9},{2,18},{10... | collective-permute-start | bytes 786440 | tf_op jit(solution)/shard_map/ppermute | solution.py:532
  123.9 13.7 %collective-permute-start.42 = (f32[64,8,128]{2,1,0:T(8,128)S(1)}, f32[64,8,128]{2,1,0:T(8,128)S(1)}, u32[]{:S(2)}, u32[]{:S(2)}) collective-permute-start(f32[64,8,128]{2,1,0:T(8,128)S(1)} %get-tuple-element.128), channel_id=1, source_target_pairs={{0,24},{8,16},{16,8},{24,0},{1,25},{9,17},{17,9},{25,1},{2,26},{10... | collective-permute-start | bytes 786440 | tf_op jit(solution)/shard_map/ppermute | solution.py:532
  126.0 2.8 %collective-permute-start.37 = (f32[8,128]{1,0:T(8,128)S(1)}, f32[8,128]{1,0:T(8,128)S(1)}, u32[]{:S(2)}, u32[]{:S(2)}) collective-permute-start(f32[8,128]{1,0:T(8,128)S(1)} %add.111), channel_id=1, source_target_pairs={{0,1},{1,0},{2,3},{3,2},{4,5},{5,4},{6,7},{7,6},{8,9},{9,8},{10,11... | collective-permute-start | bytes 12296 | tf_op jit(solution)/shard_map/ppermute | solution.py:532
  126.0 4.3 %collective-permute-start.38 = (f32[8,128]{1,0:T(8,128)S(1)}, f32[8,128]{1,0:T(8,128)S(1)}, u32[]{:S(2)}, u32[]{:S(2)}) collective-permute-start(f32[8,128]{1,0:T(8,128)S(1)} %add.111), channel_id=1, source_target_pairs={{0,2},{1,3},{2,0},{3,1},{4,6},{5,7},{6,4},{7,5},{8,10},{9,11},{10,... | collective-permute-start | bytes 12296 | tf_op jit(solution)/shard_map/ppermute | solution.py:532
  128.7 4.0 %collective-permute-start.39 = (f32[8,128]{1,0:T(8,128)S(1)}, f32[8,128]{1,0:T(8,128)S(1)}, u32[]{:S(2)}, u32[]{:S(2)}) collective-permute-start(f32[8,128]{1,0:T(8,128)S(1)} %add.111), channel_id=1, source_target_pairs={{0,3},{1,2},{2,1},{3,0},{4,7},{5,6},{6,5},{7,4},{8,11},{9,10},{10,... | collective-permute-start | bytes 12296 | tf_op jit(solution)/shard_map/ppermute | solution.py:532

commit v4 on v3

--- a/solution.py
+++ b/solution.py
@@ -133,23 +133,23 @@
         return carry
 
     rows("fill", per_row)
-    for half in range(2):
+    for half in range(6):
         for out in (s0, s1, s2, s3):
-            out[TILES + half] = ids[half * 8 : half * 8 + 8].astype(F32)
+            out[TILES + half] = ids[half // 2, (half % 2) * 8 : (half % 2) * 8 + 8]
     for plane in range(planes.shape[0]):
         for kt in range(4):
             sources = [planes[plane, c, kt * 8 : kt * 8 + 8, :] for c in range(4)]
             pl_out[plane * 4 + kt] = block_transposed(sources, slab, masks)
 
 
-def maps_kernel(ints, mid, left, right, maps):
+def maps_kernel(ints, ids, maps):
     slab = ints[1]
     lane = lanes(NZ)
     pieces = []
     for g in range(GX):
-        moved_mid = pltpu.roll(mid[g], (16 - 32 * slab) & (LANES - 1), axis=1)
-        moved_left = pltpu.roll(left[g], 16, axis=1)
-        moved_right = pltpu.roll(right[g], OWN + 16, axis=1)
+        moved_mid = pltpu.roll(ids[0, g], (16 - 32 * slab) & (LANES - 1), axis=1)
+        moved_left = pltpu.roll(ids[1, g], 16, axis=1)
+        moved_right = pltpu.roll(ids[2, g], OWN + 16, axis=1)
         here = jnp.where((lane[:XI] < 16) & (slab == 0), moved_left, moved_mid)
         here = jnp.where((lane[:XI] >= OWN + 16) & (slab == 3), moved_right, here)
         pieces += [here, jnp.full((XI, LANES), -1.0, F32)]
@@ -194,8 +194,8 @@
     own, here = scal[0], scal[2]
     for s, source in enumerate((s0, r1, r2, r3)):
         held[own ^ s] = source[:TILES]
-        for half in range(2):
-            ids[own ^ s, half * 8 : half * 8 + 8, :] = source[TILES + half]
+        for half in range(6):
+            ids[half // 2, own ^ s, (half % 2) * 8 : (half % 2) * 8 + 8, :] = source[TILES + half]
     for s, source in enumerate(plane_refs):
         planes[here ^ s] = source[...]
 
@@ -547,13 +547,15 @@
     gy_up = [(j, (j + 1) % groups) for j in range(groups)]
     gy_down = [(b, a) for a, b in gy_up]
 
-    chunk = shape(TILES + 2, 8, LANES)
+    ids = turbine_cell[0, :, NZ // 2, :].astype(F32)
+    ids = jnp.stack([ids, lax.ppermute(ids, "gy", gy_up), lax.ppermute(ids, "gy", gy_down)])
+    chunk = shape(TILES + 6, 8, LANES)
     s0, s1, s2, s3, plane = call(
         pack_kernel,
         (chunk, chunk, chunk, chunk, shape(per_layout * 4, 8, LANES)),
         [SMEM, VMEM, VMEM, VMEM],
         name="pack",
-    )(scal, state[0], planes, turbine_cell[0, :, NZ // 2, :])
+    )(scal, state[0], planes, ids)
     received = [swapped(value, "gx", GX, s) for s, value in ((1, s1), (2, s2), (3, s3))]
     received[0], plane = lax.optimization_barrier((received[0], plane))
     plane_received = [swapped(plane, "layout", layouts, s) for s in range(1, layouts)]
@@ -568,7 +570,7 @@
             first_payload,
             shape(2, OWN, LANES),
             shape(8, LANES),
-            shape(GX, XI, LANES),
+            shape(3, GX, XI, LANES),
         ),
         [SMEM, VMEM] + [VMEM] * (4 + layouts),
         [
@@ -578,9 +580,7 @@
         name="unpack",
     )(scal, profile, s0, *received, plane, *plane_received)
 
-    maps = call(maps_kernel, shape(4, 2 * OWN, LANES), [SMEM, VMEM, VMEM, VMEM], name="maps")(
-        scal, ids, lax.ppermute(ids, "gy", gy_up), lax.ppermute(ids, "gy", gy_down)
-    )
+    maps = call(maps_kernel, shape(4, 2 * OWN, LANES), [SMEM, VMEM], name="maps")(scal, ids)
 
     half = groups // 2
 
@@ -620,7 +620,7 @@
             del results[:4]
         if step == 0:
             inflow = results.pop(0)
-        fields, arriving = lax.optimization_barrier((fields, arriving))
+        su, sd, fields, arriving = lax.optimization_barrier((su, sd, fields, arriving))
         pending = partial + arriving
     mean = last_round(pending)
 

time: 141 us -> 128 us (0.908)
  waiting for transfers between devices: 50.5 us -> 34.5 us
  starting transfers between devices: 55.8 us -> 60.1 us
    ppermute x33, waiting for transfers between devices: 50.5 us -> 34.2 us  [swapped(): return lax.ppermute(value, axis, [(i, i ^ distance) for i in range(size)])]
    ppermute x33, starting transfers between devices: 42.9 us -> 46.7 us  [swapped(): return lax.ppermute(value, axis, [(i, i ^ distance) for i in range(size)])]
    unnamed x10 -> x4, local copies, waits for them, and re-layouts: 2.81 us -> 1.22 us
  transfers between devices with their start and end apart: 43 -> 43, of which waited for: 20 -> 20; matrix products, arithmetic and copies ran while one was open for 0% -> 1% of each run, Pallas kernels for 5% -> 16%
where the time goes in v4:
time: 128 us
  starting transfers between devices  60.1 us (47%)
  waiting for transfers between devices  34.5 us (27%)
  Pallas kernels  30.1 us (24%)
  local copies, waits for them, and re-layouts  3.05 us (2%)
    ppermute x33, starting transfers between devices, swapped(): return lax.ppermute(value, axis, [(i, i ^ distance) for i in range(size)])  46.7 us
    ppermute x33, waiting for transfers between devices, swapped(): return lax.ppermute(value, axis, [(i, i ^ distance) for i in range(size)])  34.2 us
    pallas_call x4, Pallas kernels, local(): call(functools.partial(step_kernel, step=step, cells=cells), tuple(outs),...  19.3 us
    ppermute x4, starting transfers between devices, local(): lo = lax.ppermute(su, ('gx', 'gy'), up)  8.96 us
    pallas_call x1, Pallas kernels, local(): call(functools.partial(final_kernel, cells=cells), shape(4, XI, NZ, LANES...  3.11 us
  transfers between devices with their start and end apart: 43, of which 20 were waited for; matrix products, arithmetic and copies ran while one was open for 1% of the time, Pallas kernels for 16%

profile of v4, /device:TPU:1, one launch (start us, length us, event | category | flops | bytes accessed | tf_op | source)
XLA Modules:
  0.0 128.0 jit_solution(14249552574154544353)
XLA Ops:
  0.0 0.9 slice.3
  0.9 2.0 %collective-permute-start = (f32[16,128]{1,0:T(8,128)S(1)}, f32[16,128]{1,0:T(8,128)S(1)}, u32[]{:S(2)}, u32[]{:S(2)}) collective-permute-start(f32[16,128]{1,0:T(8,128)S(1)} %get-tuple-element.142), channel_id=1, source_target_pairs={{0,1},{1,2},{2,3},{3,4},{4,5},{5,6},{6,7},{7,0},{8,9},{9,10},{10,1... | collective-permute-start | bytes 24584 | tf_op jit(solution)/shard_map/ppermute | solution.py:551
  2.9 2.4 %collective-permute-start.1 = (f32[16,128]{1,0:T(8,128)S(1)}, f32[16,128]{1,0:T(8,128)S(1)}, u32[]{:S(2)}, u32[]{:S(2)}) collective-permute-start(f32[16,128]{1,0:T(8,128)S(1)} %get-tuple-element.142), channel_id=1, source_target_pairs={{1,0},{2,1},{3,2},{4,3},{5,4},{6,5},{7,6},{0,7},{9,8},{10,9},{11,1... | collective-permute-start | bytes 24584 | tf_op jit(solution)/shard_map/ppermute | solution.py:551
  5.3 0.8 concatenate.3.scal.ints
  6.0 0.2 collective-permute-done
  6.3 1.2 copy-done
  7.5 2.0 %pack.1 = (f32[70,8,128]{2,1,0:T(8,128)S(1)}, f32[70,8,128]{2,1,0:T(8,128)S(1)}, f32[70,8,128]{2,1,0:T(8,128)S(1)}, f32[70,8,128]{2,1,0:T(8,128)S(1)}, f32[8,8,128]{2,1,0:T(8,128)S(1)}) custom-call(s32[135]{0:T(256)S(1)} %concatenate.3.scal.ints, f32[4,16,32,128]{3,2,1,0:T(8,128)S(1)} %bitcast.14, f32[2,4,32,128]{3,2,1,0:T(8,128)S(1)} %copy-done.1, ...), custom_call_target="tpu_custom_call" | custom-call | flops 2000000000 | bytes 4000000 | tf_op jit(solution)/shard_map/pack/pallas_call | solution.py:553
  9.5 1.9 %collective-permute-start.2 = (f32[70,8,128]{2,1,0:T(8,128)S(1)}, f32[70,8,128]{2,1,0:T(8,128)S(1)}, u32[]{:S(2)}, u32[]{:S(2)}) collective-permute-start(f32[70,8,128]{2,1,0:T(8,128)S(1)} %get-tuple-element.74), channel_id=1, source_target_pairs={{0,8},{8,0},{16,24},{24,16},{1,9},{9,1},{17,25},{25,17},{2,10},{10... | collective-permute-start | bytes 860168 | tf_op jit(solution)/shard_map/ppermute | solution.py:532
  11.4 3.0 %collective-permute-start.3 = (f32[70,8,128]{2,1,0:T(8,128)S(1)}, f32[70,8,128]{2,1,0:T(8,128)S(1)}, u32[]{:S(2)}, u32[]{:S(2)}) collective-permute-start(f32[70,8,128]{2,1,0:T(8,128)S(1)} %get-tuple-element.77), channel_id=1, source_target_pairs={{0,16},{8,24},{16,0},{24,8},{1,17},{9,25},{17,1},{25,9},{2,18},{10... | collective-permute-start | bytes 860168 | tf_op jit(solution)/shard_map/ppermute | solution.py:532
  14.5 0.2 collective-permute-start.4
  14.6 1.8 %collective-permute-start.5 = (f32[8,8,128]{2,1,0:T(8,128)S(1)}, f32[8,8,128]{2,1,0:T(8,128)S(1)}, u32[]{:S(2)}, u32[]{:S(2)}) collective-permute-start(f32[8,8,128]{2,1,0:T(8,128)S(1)} %get-tuple-element.79.p0), channel_id=1, source_target_pairs={{0,32},{32,0},{64,96},{96,64},{1,33},{33,1},{65,97},{97,65},{2,34}... | collective-permute-start | bytes 98312 | tf_op jit(solution)/shard_map/ppermute | solution.py:532
  16.4 3.3 %collective-permute-start.6 = (f32[8,8,128]{2,1,0:T(8,128)S(1)}, f32[8,8,128]{2,1,0:T(8,128)S(1)}, u32[]{:S(2)}, u32[]{:S(2)}) collective-permute-start(f32[8,8,128]{2,1,0:T(8,128)S(1)} %get-tuple-element.79.p0), channel_id=1, source_target_pairs={{0,64},{32,96},{64,0},{96,32},{1,65},{33,97},{65,1},{97,33},{2,66}... | collective-permute-start | bytes 98312 | tf_op jit(solution)/shard_map/ppermute | solution.py:532
  19.9 1.5 %collective-permute-done.3.r2 = f32[70,8,128]{2,1,0:T(8,128)S(1)} collective-permute-done((f32[70,8,128]{2,1,0:T(8,128)S(1)}, f32[70,8,128]{2,1,0:T(8,128)S(1)}, u32[]{:S(2)}, u32[]{:S(2)}) %collective-permute-start.3) | collective-permute-done | bytes 286752 | tf_op jit(solution)/shard_map/ppermute | solution.py:532
  21.5 6.2 %collective-permute-done.4.r3 = f32[70,8,128]{2,1,0:T(8,128)S(1)} collective-permute-done((f32[70,8,128]{2,1,0:T(8,128)S(1)}, f32[70,8,128]{2,1,0:T(8,128)S(1)}, u32[]{:S(2)}, u32[]{:S(2)}) %collective-permute-start.4) | collective-permute-done | bytes 286752 | tf_op jit(solution)/shard_map/ppermute | solution.py:532
  27.7 1.8 %unpack.1 = (f32[4,16,32,128]{3,2,1,0:T(8,128)S(1)}, f32[4,32,128]{2,1,0:T(8,128)S(1)}, f32[72,8,128]{2,1,0:T(8,128)S(1)}, f32[72,8,128]{2,1,0:T(8,128)S(1)}, f3...) custom-call(s32[135]{0:T(256)S(1)} %concatenate.3.scal.ints, ...), custom_call_target="tpu_custom_call" | custom-call | flops 2000000000 | bytes 4000000 | tf_op jit(solution)/shard_map/unpack/pallas_call | solution.py:564
  29.5 0.4 collective-permute-start.8
  29.9 0.9 collective-permute-done.8
  30.8 3.1 %collective-permute-start.10 = (f32[72,8,128]{2,1,0:T(8,128)S(1)}, f32[72,8,128]{2,1,0:T(8,128)S(1)}, u32[]{:S(2)}, u32[]{:S(2)}) collective-permute-start(f32[72,8,128]{2,1,0:T(8,128)S(1)} %get-tuple-element.86), channel_id=1, source_target_pairs={{0,8},{8,16},{16,24},{24,25},{25,17},{17,9},{9,1},{1,2},{2,10},{10... | collective-permute-start | bytes 884744 | tf_op jit(solution)/shard_map/ppermute | solution.py:594
  33.9 0.4 collective-permute-start.9
  34.3 1.6 %maps.1.refs_3_ = f32[4,64,128]{2,1,0:T(8,128)S(1)} custom-call(s32[135]{0:T(256)S(1)} %concatenate.3.scal.ints, f32[3,4,16,128]{3,2,1,0:T(8,128)S(1)} %get-tuple-element.88.ids), custom_call_target="tpu_custom_call" | custom-call | flops 2000000000 | bytes 4000000 | tf_op jit(solution)/shard_map/maps/pallas_call | solution.py:583
  35.9 5.7 %collective-permute-done.9 = f32[8,128]{1,0:T(8,128)S(1)} collective-permute-done((f32[8,128]{1,0:T(8,128)S(1)}, f32[8,128]{1,0:T(8,128)S(1)}, u32[]{:S(2)}, u32[]{:S(2)}) %collective-permute-start.9) | collective-permute-done | bytes 4128 | tf_op jit(solution)/shard_map/ppermute | solution.py:532
  41.7 4.4 %step0.1 = (f32[4,16,32,128]{3,2,1,0:T(8,128)S(1)}, f32[68,8,128]{2,1,0:T(8,128)S(1)}, f32[68,8,128]{2,1,0:T(8,128)S(1)}, f32[2,32,128]{2,1,0:T(8,128)S(1)}, f32...) custom-call(f32[4,16,32,128]{3,2,1,0:T(8,128)S(1)} %get-tuple-element.85.refs_0_, ...), custom_call_target="tpu_custom_call" | custom-call | flops 6000000000 | bytes 4000000 | tf_op jit(solution)/shard_map/step0/pallas_call | solution.py:608
  46.0 2.0 %collective-permute-start.13 = (f32[8,128]{1,0:T(8,128)S(1)}, f32[8,128]{1,0:T(8,128)S(1)}, u32[]{:S(2)}, u32[]{:S(2)}) collective-permute-start(f32[8,128]{1,0:T(8,128)S(1)} %get-tuple-element.98), channel_id=1, source_target_pairs={{0,8},{8,0},{16,24},{24,16},{1,9},{9,1},{17,25},{25,17},{2,10},{10... | collective-permute-start | bytes 12296 | tf_op jit(solution)/shard_map/ppermute | solution.py:532
  48.0 0.8 collective-permute-done.13
  48.9 1.5 %collective-permute-start.15 = (f32[68,8,128]{2,1,0:T(8,128)S(1)}, f32[68,8,128]{2,1,0:T(8,128)S(1)}, u32[]{:S(2)}, u32[]{:S(2)}) collective-permute-start(f32[68,8,128]{2,1,0:T(8,128)S(1)} %get-tuple-element.101), channel_id=1, source_target_pairs={{0,8},{8,16},{16,24},{24,25},{25,17},{17,9},{9,1},{1,2},{2,10},{10... | collective-permute-start | bytes 835592 | tf_op jit(solution)/shard_map/ppermute | solution.py:594
  50.4 0.2 collective-permute-start.17
  50.6 5.0 %collective-permute-start.18 = (f32[8,128]{1,0:T(8,128)S(1)}, f32[8,128]{1,0:T(8,128)S(1)}, u32[]{:S(2)}, u32[]{:S(2)}) collective-permute-start(f32[8,128]{1,0:T(8,128)S(1)} %add.95), channel_id=1, source_target_pairs={{0,2},{1,3},{2,0},{3,1},{4,6},{5,7},{6,4},{7,5},{8,10},{9,11},{10,... | collective-permute-start | bytes 12296 | tf_op jit(solution)/shard_map/ppermute | solution.py:532
  55.5 1.1 collective-permute-start.14
  56.7 0.2 collective-permute-done.18
  56.8 2.4 %collective-permute-done.19 = f32[8,128]{1,0:T(8,128)S(1)} collective-permute-done((f32[8,128]{1,0:T(8,128)S(1)}, f32[8,128]{1,0:T(8,128)S(1)}, u32[]{:S(2)}, u32[]{:S(2)}) %collective-permute-start.19) | collective-permute-done | bytes 4128 | tf_op jit(solution)/shard_map/ppermute | solution.py:532
  59.2 1.5 %collective-permute-start.20 = (f32[8,128]{1,0:T(8,128)S(1)}, f32[8,128]{1,0:T(8,128)S(1)}, u32[]{:S(2)}, u32[]{:S(2)}) collective-permute-start(f32[8,128]{1,0:T(8,128)S(1)} %add.94), channel_id=1, source_target_pairs={{0,16},{8,24},{16,0},{24,8},{1,17},{9,25},{17,1},{25,9},{2,18},{10... | collective-permute-start | bytes 12296 | tf_op jit(solution)/shard_map/ppermute | solution.py:532
  60.8 5.0 %step1.1 = (f32[4,16,32,128]{3,2,1,0:T(8,128)S(1)}, f32[68,8,128]{2,1,0:T(8,128)S(1)}, f32[68,8,128]{2,1,0:T(8,128)S(1)}, f32[2,32,128]{2,1,0:T(8,128)S(1)}, f32[8,128]{1,0:T(8,128)S(1)}) custom-call(f32[4,16,32,128]{3,2,1,0:T(8,128)S(1)} %get-tuple-element.100.refs_0_, f32[68,8,128]{2,1,0:T(8,128)S(1)} %collective-permute-done.15.refs_1_, ...), custom_call_target="tpu_custom_call" | custom-call | flops 6000000000 | bytes 4000000 | tf_op jit(solution)/shard_map/step1/pallas_call | solution.py:608
  65.8 1.6 %collective-permute-start.21 = (f32[8,128]{1,0:T(8,128)S(1)}, f32[8,128]{1,0:T(8,128)S(1)}, u32[]{:S(2)}, u32[]{:S(2)}) collective-permute-start(f32[8,128]{1,0:T(8,128)S(1)} %get-tuple-element.113), channel_id=1, source_target_pairs={{0,8},{8,0},{16,24},{24,16},{1,9},{9,1},{17,25},{25,17},{2,10},{10... | collective-permute-start | bytes 12296 | tf_op jit(solution)/shard_map/ppermute | solution.py:532
  67.5 0.8 collective-permute-done.21
  68.3 2.8 %collective-permute-start.23 = (f32[68,8,128]{2,1,0:T(8,128)S(1)}, f32[68,8,128]{2,1,0:T(8,128)S(1)}, u32[]{:S(2)}, u32[]{:S(2)}) collective-permute-start(f32[68,8,128]{2,1,0:T(8,128)S(1)} %get-tuple-element.116), channel_id=1, source_target_pairs={{0,8},{8,16},{16,24},{24,25},{25,17},{17,9},{9,1},{1,2},{2,10},{10... | collective-permute-start | bytes 835592 | tf_op jit(solution)/shard_map/ppermute | solution.py:594
  71.1 2.8 %collective-permute-start.26 = (f32[8,128]{1,0:T(8,128)S(1)}, f32[8,128]{1,0:T(8,128)S(1)}, u32[]{:S(2)}, u32[]{:S(2)}) collective-permute-start(f32[8,128]{1,0:T(8,128)S(1)} %add.101), channel_id=1, source_target_pairs={{0,2},{1,3},{2,0},{3,1},{4,6},{5,7},{6,4},{7,5},{8,10},{9,11},{10,... | collective-permute-start | bytes 12296 | tf_op jit(solution)/shard_map/ppermute | solution.py:532
  73.9 1.0 collective-permute-start.27
  74.9 0.5 collective-permute-done.26
  75.4 2.2 %collective-permute-done.27 = f32[8,128]{1,0:T(8,128)S(1)} collective-permute-done((f32[8,128]{1,0:T(8,128)S(1)}, f32[8,128]{1,0:T(8,128)S(1)}, u32[]{:S(2)}, u32[]{:S(2)}) %collective-permute-start.27) | collective-permute-done | bytes 4128 | tf_op jit(solution)/shard_map/ppermute | solution.py:532
  77.6 0.6 collective-permute-done.22
  78.2 1.2 collective-permute-start.28
  79.4 5.0 %step2.1 = (f32[4,16,32,128]{3,2,1,0:T(8,128)S(1)}, f32[68,8,128]{2,1,0:T(8,128)S(1)}, f32[68,8,128]{2,1,0:T(8,128)S(1)}, f32[2,32,128]{2,1,0:T(8,128)S(1)}, f32[8,128]{1,0:T(8,128)S(1)}) custom-call(f32[4,16,32,128]{3,2,1,0:T(8,128)S(1)} %get-tuple-element.115.refs_0_, f32[68,8,128]{2,1,0:T(8,128)S(1)} %collective-permute-done.23.refs_1_, ...), custom_call_target="tpu_custom_call" | custom-call | flops 6000000000 | bytes 4000000 | tf_op jit(solution)/shard_map/step2/pallas_call | solution.py:608
  84.4 3.8 %collective-permute-start.29 = (f32[8,128]{1,0:T(8,128)S(1)}, f32[8,128]{1,0:T(8,128)S(1)}, u32[]{:S(2)}, u32[]{:S(2)}) collective-permute-start(f32[8,128]{1,0:T(8,128)S(1)} %get-tuple-element.127), channel_id=1, source_target_pairs={{0,8},{8,0},{16,24},{24,16},{1,9},{9,1},{17,25},{25,17},{2,10},{10... | collective-permute-start | bytes 12296 | tf_op jit(solution)/shard_map/ppermute | solution.py:532
  88.1 0.8 collective-permute-done.29
  89.0 1.5 %collective-permute-start.31 = (f32[68,8,128]{2,1,0:T(8,128)S(1)}, f32[68,8,128]{2,1,0:T(8,128)S(1)}, u32[]{:S(2)}, u32[]{:S(2)}) collective-permute-start(f32[68,8,128]{2,1,0:T(8,128)S(1)} %get-tuple-element.130), channel_id=1, source_target_pairs={{0,8},{8,16},{16,24},{24,25},{25,17},{17,9},{9,1},{1,2},{2,10},{10... | collective-permute-start | bytes 835592 | tf_op jit(solution)/shard_map/ppermute | solution.py:594
  90.5 0.4 collective-permute-start.33
  90.9 3.6 %collective-permute-start.34 = (f32[8,128]{1,0:T(8,128)S(1)}, f32[8,128]{1,0:T(8,128)S(1)}, u32[]{:S(2)}, u32[]{:S(2)}) collective-permute-start(f32[8,128]{1,0:T(8,128)S(1)} %add.107), channel_id=1, source_target_pairs={{0,2},{1,3},{2,0},{3,1},{4,6},{5,7},{6,4},{7,5},{8,10},{9,11},{10,... | collective-permute-start | bytes 12296 | tf_op jit(solution)/shard_map/ppermute | solution.py:532
  94.4 0.9 collective-permute-start.30
  95.3 0.4 collective-permute-done.34
  95.7 2.4 %collective-permute-done.35 = f32[8,128]{1,0:T(8,128)S(1)} collective-permute-done((f32[8,128]{1,0:T(8,128)S(1)}, f32[8,128]{1,0:T(8,128)S(1)}, u32[]{:S(2)}, u32[]{:S(2)}) %collective-permute-start.35) | collective-permute-done | bytes 4128 | tf_op jit(solution)/shard_map/ppermute | solution.py:532
  98.2 0.6 collective-permute-done.30
  98.7 0.3 collective-permute-start.36
  99.0 4.9 %step3.1.fields = f32[4,16,32,128]{3,2,1,0:T(8,128)S(1)} custom-call(f32[4,16,32,128]{3,2,1,0:T(8,128)S(1)} %get-tuple-element.132.refs_0_, f32[68,8,128]{2,1,0:T(8,128)S(1)} %collective-permute-done.31.refs_1_, f32[68,8,128]{2,1,0:T(8,128)S(1)} %collective-permute-done.32.refs_2_, f32[4,64,128]{2,1,0:T(8,128)S(1)} %maps.1.refs_3_, ...), custom_call_target="tpu_custom_call" | custom-call | flops 6000000000 | bytes 4000000 | tf_op jit(solution)/shard_map/step3/pallas_call | solution.py:608
  103.9 2.3 %send.1 = (f32[64,8,128]{2,1,0:T(8,128)S(1)}, f32[64,8,128]{2,1,0:T(8,128)S(1)}, f32[64,8,128]{2,1,0:T(8,128)S(1)}, f32[64,8,128]{2,1,0:T(8,128)S(1)}) custom-call(s32[135]{0:T(256)S(1)} %concatenate.3.scal.ints, f32[4,16,32,128]{3,2,1,0:T(8,128)S(1)} %step3.1.fields), custom_call_target="tpu_custom_call" | custom-call | flops 2000000000 | bytes 4000000 | tf_op jit(solution)/shard_map/send/pallas_call | solution.py:628
  106.2 3.5 %collective-permute-start.40 = (f32[64,8,128]{2,1,0:T(8,128)S(1)}, f32[64,8,128]{2,1,0:T(8,128)S(1)}, u32[]{:S(2)}, u32[]{:S(2)}) collective-permute-start(f32[64,8,128]{2,1,0:T(8,128)S(1)} %get-tuple-element.138), channel_id=1, source_target_pairs={{0,8},{8,0},{16,24},{24,16},{1,9},{9,1},{17,25},{25,17},{2,10},{10... | collective-permute-start | bytes 786440 | tf_op jit(solution)/shard_map/ppermute | solution.py:532
  109.7 2.6 %collective-permute-start.41 = (f32[64,8,128]{2,1,0:T(8,128)S(1)}, f32[64,8,128]{2,1,0:T(8,128)S(1)}, u32[]{:S(2)}, u32[]{:S(2)}) collective-permute-start(f32[64,8,128]{2,1,0:T(8,128)S(1)} %get-tuple-element.139), channel_id=1, source_target_pairs={{0,16},{8,24},{16,0},{24,8},{1,17},{9,25},{17,1},{25,9},{2,18},{10... | collective-permute-start | bytes 786440 | tf_op jit(solution)/shard_map/ppermute | solution.py:532
  112.3 0.6 collective-permute-start.42
  112.9 2.4 %collective-permute-start.38 = (f32[8,128]{1,0:T(8,128)S(1)}, f32[8,128]{1,0:T(8,128)S(1)}, u32[]{:S(2)}, u32[]{:S(2)}) collective-permute-start(f32[8,128]{1,0:T(8,128)S(1)} %add.111), channel_id=1, source_target_pairs={{0,2},{1,3},{2,0},{3,1},{4,6},{5,7},{6,4},{7,5},{8,10},{9,11},{10,... | collective-permute-start | bytes 12296 | tf_op jit(solution)/shard_map/ppermute | solution.py:532
  115.4 0.3 collective-permute-done.37
  115.7 1.2 collective-permute-start.39
  116.9 0.3 collective-permute-done.38
  117.2 2.5 %collective-permute-done.39 = f32[8,128]{1,0:T(8,128)S(1)} collective-permute-done((f32[8,128]{1,0:T(8,128)S(1)}, f32[8,128]{1,0:T(8,128)S(1)}, u32[]{:S(2)}, u32[]{:S(2)}) %collective-permute-start.39) | collective-permute-done | bytes 4128 | tf_op jit(solution)/shard_map/ppermute | solution.py:532
  119.7 5.2 %collective-permute-done.42.r3 = f32[64,8,128]{2,1,0:T(8,128)S(1)} collective-permute-done((f32[64,8,128]{2,1,0:T(8,128)S(1)}, f32[64,8,128]{2,1,0:T(8,128)S(1)}, u32[]{:S(2)}, u32[]{:S(2)}) %collective-permute-start.42) | collective-permute-done | bytes 262176 | tf_op jit(solution)/shard_map/ppermute | solution.py:532
  124.9 3.1 %final.1 = f32[4,16,32,128]{3,2,1,0:T(8,128)} custom-call(s32[135]{0:T(256)S(1)} %concatenate.3.scal.ints, f32[8,128]{1,0:T(8,128)S(1)} %add_add_fusion.mean, f32[64,8,128]{2,1,0:T(8,128)S(1)} %get-tuple-element.137.s0, f32[64,8,128]{2,1,0:T(8,128)S(1)} %collective-permute-done.40.r1, f32[64,8,128]{2,1,0:T(8,128)S(1)} %collective-permute-done.41.r2, ...), custom_call_target="tpu_custom_call" | custom-call | flops 2000000000 | bytes 4000000 | tf_op jit(solution)/shard_map/final/pallas_call | solution.py:636
  (62 shorter events, 0.4 us)
Async XLA Ops:
  0.0 6.3 %copy-start.1 = (f32[2,4,32,128]{3,2,1,0:T(8,128)S(1)}, f32[2,4,32,128]{3,2,1,0:T(8,128)}, u32[]{:S(2)}) copy-start(f32[2,4,32,128]{3,2,1,0:T(8,128)} %planes.1) | copy-start | bytes 393220
  0.9 5.4 %collective-permute-start = (f32[16,128]{1,0:T(8,128)S(1)}, f32[16,128]{1,0:T(8,128)S(1)}, u32[]{:S(2)}, u32[]{:S(2)}) collective-permute-start(f32[16,128]{1,0:T(8,128)S(1)} %get-tuple-element.142), channel_id=1, source_target_pairs={{0,1},{1,2},{2,3},{3,4},{4,5},{5,6},{6,7},{7,0},{8,9},{9,10},{10,1... | collective-permute-start | bytes 24584 | tf_op jit(solution)/shard_map/ppermute | solution.py:551
  2.9 3.3 %collective-permute-start.1 = (f32[16,128]{1,0:T(8,128)S(1)}, f32[16,128]{1,0:T(8,128)S(1)}, u32[]{:S(2)}, u32[]{:S(2)}) collective-permute-start(f32[16,128]{1,0:T(8,128)S(1)} %get-tuple-element.142), channel_id=1, source_target_pairs={{1,0},{2,1},{3,2},{4,3},{5,4},{6,5},{7,6},{0,7},{9,8},{10,9},{11,1... | collective-permute-start | bytes 24584 | tf_op jit(solution)/shard_map/ppermute | solution.py:551
  6.3 1.2 copy-start
  9.5 5.2 %collective-permute-start.2 = (f32[70,8,128]{2,1,0:T(8,128)S(1)}, f32[70,8,128]{2,1,0:T(8,128)S(1)}, u32[]{:S(2)}, u32[]{:S(2)}) collective-permute-start(f32[70,8,128]{2,1,0:T(8,128)S(1)} %get-tuple-element.74), channel_id=1, source_target_pairs={{0,8},{8,0},{16,24},{24,16},{1,9},{9,1},{17,25},{25,17},{2,10},{10... | collective-permute-start | bytes 860168 | tf_op jit(solution)/shard_map/ppermute | solution.py:532
  11.4 10.0 %collective-permute-start.3 = (f32[70,8,128]{2,1,0:T(8,128)S(1)}, f32[70,8,128]{2,1,0:T(8,128)S(1)}, u32[]{:S(2)}, u32[]{:S(2)}) collective-permute-start(f32[70,8,128]{2,1,0:T(8,128)S(1)} %get-tuple-element.77), channel_id=1, source_target_pairs={{0,16},{8,24},{16,0},{24,8},{1,17},{9,25},{17,1},{25,9},{2,18},{10... | collective-permute-start | bytes 860168 | tf_op jit(solution)/shard_map/ppermute | solution.py:532
  14.5 13.2 %collective-permute-start.4 = (f32[70,8,128]{2,1,0:T(8,128)S(1)}, f32[70,8,128]{2,1,0:T(8,128)S(1)}, u32[]{:S(2)}, u32[]{:S(2)}) collective-permute-start(f32[70,8,128]{2,1,0:T(8,128)S(1)} %get-tuple-element.78), channel_id=1, source_target_pairs={{0,24},{8,16},{16,8},{24,0},{1,25},{9,17},{17,9},{25,1},{2,26},{10... | collective-permute-start | bytes 860168 | tf_op jit(solution)/shard_map/ppermute | solution.py:532
  14.6 13.1 %collective-permute-start.5 = (f32[8,8,128]{2,1,0:T(8,128)S(1)}, f32[8,8,128]{2,1,0:T(8,128)S(1)}, u32[]{:S(2)}, u32[]{:S(2)}) collective-permute-start(f32[8,8,128]{2,1,0:T(8,128)S(1)} %get-tuple-element.79.p0), channel_id=1, source_target_pairs={{0,32},{32,0},{64,96},{96,64},{1,33},{33,1},{65,97},{97,65},{2,34}... | collective-permute-start | bytes 98312 | tf_op jit(solution)/shard_map/ppermute | solution.py:532
  16.4 11.3 %collective-permute-start.6 = (f32[8,8,128]{2,1,0:T(8,128)S(1)}, f32[8,8,128]{2,1,0:T(8,128)S(1)}, u32[]{:S(2)}, u32[]{:S(2)}) collective-permute-start(f32[8,8,128]{2,1,0:T(8,128)S(1)} %get-tuple-element.79.p0), channel_id=1, source_target_pairs={{0,64},{32,96},{64,0},{96,32},{1,65},{33,97},{65,1},{97,33},{2,66}... | collective-permute-start | bytes 98312 | tf_op jit(solution)/shard_map/ppermute | solution.py:532
  19.7 8.0 %collective-permute-start.7 = (f32[8,8,128]{2,1,0:T(8,128)S(1)}, f32[8,8,128]{2,1,0:T(8,128)S(1)}, u32[]{:S(2)}, u32[]{:S(2)}) collective-permute-start(f32[8,8,128]{2,1,0:T(8,128)S(1)} %get-tuple-element.79.p0), channel_id=1, source_target_pairs={{0,96},{32,64},{64,32},{96,0},{1,97},{33,65},{65,33},{97,1},{2,98}... | collective-permute-start | bytes 98312 | tf_op jit(solution)/shard_map/ppermute | solution.py:532
  29.5 1.2 collective-permute-start.8
  30.8 10.9 %collective-permute-start.10 = (f32[72,8,128]{2,1,0:T(8,128)S(1)}, f32[72,8,128]{2,1,0:T(8,128)S(1)}, u32[]{:S(2)}, u32[]{:S(2)}) collective-permute-start(f32[72,8,128]{2,1,0:T(8,128)S(1)} %get-tuple-element.86), channel_id=1, source_target_pairs={{0,8},{8,16},{16,24},{24,25},{25,17},{17,9},{9,1},{1,2},{2,10},{10... | collective-permute-start | bytes 884744 | tf_op jit(solution)/shard_map/ppermute | solution.py:594
  33.9 7.8 %collective-permute-start.11 = (f32[72,8,128]{2,1,0:T(8,128)S(1)}, f32[72,8,128]{2,1,0:T(8,128)S(1)}, u32[]{:S(2)}, u32[]{:S(2)}) collective-permute-start(f32[72,8,128]{2,1,0:T(8,128)S(1)} %get-tuple-element.87), channel_id=1, source_target_pairs={{8,0},{16,8},{24,16},{25,24},{17,25},{9,17},{1,9},{2,1},{10,2},{18... | collective-permute-start | bytes 884744 | tf_op jit(solution)/shard_map/ppermute | solution.py:595
  33.9 7.7 %collective-permute-start.9 = (f32[8,128]{1,0:T(8,128)S(1)}, f32[8,128]{1,0:T(8,128)S(1)}, u32[]{:S(2)}, u32[]{:S(2)}) collective-permute-start(f32[8,128]{1,0:T(8,128)S(1)} %add.91), channel_id=1, source_target_pairs={{0,4},{1,5},{2,6},{3,7},{4,0},{5,1},{6,2},{7,3},{8,12},{9,13},{10,... | collective-permute-start | bytes 12296 | tf_op jit(solution)/shard_map/ppermute | solution.py:532
  41.6 6.4 %collective-permute-start.12 = (f32[8,128]{1,0:T(8,128)S(1)}, f32[8,128]{1,0:T(8,128)S(1)}, u32[]{:S(2)}, u32[]{:S(2)}) collective-permute-start(f32[8,128]{1,0:T(8,128)S(1)} %add.92), channel_id=1, source_target_pairs={{0,16},{8,24},{16,0},{24,8},{1,17},{9,25},{17,1},{25,9},{2,18},{10... | collective-permute-start | bytes 12296 | tf_op jit(solution)/shard_map/ppermute | solution.py:532
  46.0 2.8 %collective-permute-start.13 = (f32[8,128]{1,0:T(8,128)S(1)}, f32[8,128]{1,0:T(8,128)S(1)}, u32[]{:S(2)}, u32[]{:S(2)}) collective-permute-start(f32[8,128]{1,0:T(8,128)S(1)} %get-tuple-element.98), channel_id=1, source_target_pairs={{0,8},{8,0},{16,24},{24,16},{1,9},{9,1},{17,25},{25,17},{2,10},{10... | collective-permute-start | bytes 12296 | tf_op jit(solution)/shard_map/ppermute | solution.py:532
  48.9 11.9 %collective-permute-start.15 = (f32[68,8,128]{2,1,0:T(8,128)S(1)}, f32[68,8,128]{2,1,0:T(8,128)S(1)}, u32[]{:S(2)}, u32[]{:S(2)}) collective-permute-start(f32[68,8,128]{2,1,0:T(8,128)S(1)} %get-tuple-element.101), channel_id=1, source_target_pairs={{0,8},{8,16},{16,24},{24,25},{25,17},{17,9},{9,1},{1,2},{2,10},{10... | collective-permute-start | bytes 835592 | tf_op jit(solution)/shard_map/ppermute | solution.py:594
  50.4 10.4 %collective-permute-start.16 = (f32[68,8,128]{2,1,0:T(8,128)S(1)}, f32[68,8,128]{2,1,0:T(8,128)S(1)}, u32[]{:S(2)}, u32[]{:S(2)}) collective-permute-start(f32[68,8,128]{2,1,0:T(8,128)S(1)} %get-tuple-element.102), channel_id=1, source_target_pairs={{8,0},{16,8},{24,16},{25,24},{17,25},{9,17},{1,9},{2,1},{10,2},{18... | collective-permute-start | bytes 835592 | tf_op jit(solution)/shard_map/ppermute | solution.py:595
  50.4 5.1 %collective-permute-start.17 = (f32[8,128]{1,0:T(8,128)S(1)}, f32[8,128]{1,0:T(8,128)S(1)}, u32[]{:S(2)}, u32[]{:S(2)}) collective-permute-start(f32[8,128]{1,0:T(8,128)S(1)} %add.95), channel_id=1, source_target_pairs={{0,1},{1,0},{2,3},{3,2},{4,5},{5,4},{6,7},{7,6},{8,9},{9,8},{10,11... | collective-permute-start | bytes 12296 | tf_op jit(solution)/shard_map/ppermute | solution.py:532
  50.6 6.3 %collective-permute-start.18 = (f32[8,128]{1,0:T(8,128)S(1)}, f32[8,128]{1,0:T(8,128)S(1)}, u32[]{:S(2)}, u32[]{:S(2)}) collective-permute-start(f32[8,128]{1,0:T(8,128)S(1)} %add.95), channel_id=1, source_target_pairs={{0,2},{1,3},{2,0},{3,1},{4,6},{5,7},{6,4},{7,5},{8,10},{9,11},{10,... | collective-permute-start | bytes 12296 | tf_op jit(solution)/shard_map/ppermute | solution.py:532
  55.5 3.7 %collective-permute-start.19 = (f32[8,128]{1,0:T(8,128)S(1)}, f32[8,128]{1,0:T(8,128)S(1)}, u32[]{:S(2)}, u32[]{:S(2)}) collective-permute-start(f32[8,128]{1,0:T(8,128)S(1)} %add.95), channel_id=1, source_target_pairs={{0,3},{1,2},{2,1},{3,0},{4,7},{5,6},{6,5},{7,4},{8,11},{9,10},{10,... | collective-permute-start | bytes 12296 | tf_op jit(solution)/shard_map/ppermute | solution.py:532
  55.5 3.7 %collective-permute-start.14 = (f32[8,128]{1,0:T(8,128)S(1)}, f32[8,128]{1,0:T(8,128)S(1)}, u32[]{:S(2)}, u32[]{:S(2)}) collective-permute-start(f32[8,128]{1,0:T(8,128)S(1)} %add.93), channel_id=1, source_target_pairs={{0,4},{1,5},{2,6},{3,7},{4,0},{5,1},{6,2},{7,3},{8,12},{9,13},{10,... | collective-permute-start | bytes 12296 | tf_op jit(solution)/shard_map/ppermute | solution.py:532
  59.2 8.2 %collective-permute-start.20 = (f32[8,128]{1,0:T(8,128)S(1)}, f32[8,128]{1,0:T(8,128)S(1)}, u32[]{:S(2)}, u32[]{:S(2)}) collective-permute-start(f32[8,128]{1,0:T(8,128)S(1)} %add.94), channel_id=1, source_target_pairs={{0,16},{8,24},{16,0},{24,8},{1,17},{9,25},{17,1},{25,9},{2,18},{10... | collective-permute-start | bytes 12296 | tf_op jit(solution)/shard_map/ppermute | solution.py:532
  65.8 2.5 %collective-permute-start.21 = (f32[8,128]{1,0:T(8,128)S(1)}, f32[8,128]{1,0:T(8,128)S(1)}, u32[]{:S(2)}, u32[]{:S(2)}) collective-permute-start(f32[8,128]{1,0:T(8,128)S(1)} %get-tuple-element.113), channel_id=1, source_target_pairs={{0,8},{8,0},{16,24},{24,16},{1,9},{9,1},{17,25},{25,17},{2,10},{10... | collective-permute-start | bytes 12296 | tf_op jit(solution)/shard_map/ppermute | solution.py:532
  68.3 11.1 %collective-permute-start.23 = (f32[68,8,128]{2,1,0:T(8,128)S(1)}, f32[68,8,128]{2,1,0:T(8,128)S(1)}, u32[]{:S(2)}, u32[]{:S(2)}) collective-permute-start(f32[68,8,128]{2,1,0:T(8,128)S(1)} %get-tuple-element.116), channel_id=1, source_target_pairs={{0,8},{8,16},{16,24},{24,25},{25,17},{17,9},{9,1},{1,2},{2,10},{10... | collective-permute-start | bytes 835592 | tf_op jit(solution)/shard_map/ppermute | solution.py:594
  71.1 8.3 %collective-permute-start.24 = (f32[68,8,128]{2,1,0:T(8,128)S(1)}, f32[68,8,128]{2,1,0:T(8,128)S(1)}, u32[]{:S(2)}, u32[]{:S(2)}) collective-permute-start(f32[68,8,128]{2,1,0:T(8,128)S(1)} %get-tuple-element.117), channel_id=1, source_target_pairs={{8,0},{16,8},{24,16},{25,24},{17,25},{9,17},{1,9},{2,1},{10,2},{18... | collective-permute-start | bytes 835592 | tf_op jit(solution)/shard_map/ppermute | solution.py:595
  71.1 3.9 %collective-permute-start.25 = (f32[8,128]{1,0:T(8,128)S(1)}, f32[8,128]{1,0:T(8,128)S(1)}, u32[]{:S(2)}, u32[]{:S(2)}) collective-permute-start(f32[8,128]{1,0:T(8,128)S(1)} %add.101), channel_id=1, source_target_pairs={{0,1},{1,0},{2,3},{3,2},{4,5},{5,4},{6,7},{7,6},{8,9},{9,8},{10,11... | collective-permute-start | bytes 12296 | tf_op jit(solution)/shard_map/ppermute | solution.py:532
  71.1 4.3 %collective-permute-start.26 = (f32[8,128]{1,0:T(8,128)S(1)}, f32[8,128]{1,0:T(8,128)S(1)}, u32[]{:S(2)}, u32[]{:S(2)}) collective-permute-start(f32[8,128]{1,0:T(8,128)S(1)} %add.101), channel_id=1, source_target_pairs={{0,2},{1,3},{2,0},{3,1},{4,6},{5,7},{6,4},{7,5},{8,10},{9,11},{10,... | collective-permute-start | bytes 12296 | tf_op jit(solution)/shard_map/ppermute | solution.py:532
  73.9 3.7 %collective-permute-start.27 = (f32[8,128]{1,0:T(8,128)S(1)}, f32[8,128]{1,0:T(8,128)S(1)}, u32[]{:S(2)}, u32[]{:S(2)}) collective-permute-start(f32[8,128]{1,0:T(8,128)S(1)} %add.101), channel_id=1, source_target_pairs={{0,3},{1,2},{2,1},{3,0},{4,7},{5,6},{6,5},{7,4},{8,11},{9,10},{10,... | collective-permute-start | bytes 12296 | tf_op jit(solution)/shard_map/ppermute | solution.py:532
  74.9 3.2 %collective-permute-start.22 = (f32[8,128]{1,0:T(8,128)S(1)}, f32[8,128]{1,0:T(8,128)S(1)}, u32[]{:S(2)}, u32[]{:S(2)}) collective-permute-start(f32[8,128]{1,0:T(8,128)S(1)} %add.99), channel_id=1, source_target_pairs={{0,4},{1,5},{2,6},{3,7},{4,0},{5,1},{6,2},{7,3},{8,12},{9,13},{10,... | collective-permute-start | bytes 12296 | tf_op jit(solution)/shard_map/ppermute | solution.py:532
  78.2 9.9 %collective-permute-start.28 = (f32[8,128]{1,0:T(8,128)S(1)}, f32[8,128]{1,0:T(8,128)S(1)}, u32[]{:S(2)}, u32[]{:S(2)}) collective-permute-start(f32[8,128]{1,0:T(8,128)S(1)} %add.100), channel_id=1, source_target_pairs={{0,16},{8,24},{16,0},{24,8},{1,17},{9,25},{17,1},{25,9},{2,18},{10... | collective-permute-start | bytes 12296 | tf_op jit(solution)/shard_map/ppermute | solution.py:532
  84.4 4.6 %collective-permute-start.29 = (f32[8,128]{1,0:T(8,128)S(1)}, f32[8,128]{1,0:T(8,128)S(1)}, u32[]{:S(2)}, u32[]{:S(2)}) collective-permute-start(f32[8,128]{1,0:T(8,128)S(1)} %get-tuple-element.127), channel_id=1, source_target_pairs={{0,8},{8,0},{16,24},{24,16},{1,9},{9,1},{17,25},{25,17},{2,10},{10... | collective-permute-start | bytes 12296 | tf_op jit(solution)/shard_map/ppermute | solution.py:532
  89.0 10.0 %collective-permute-start.31 = (f32[68,8,128]{2,1,0:T(8,128)S(1)}, f32[68,8,128]{2,1,0:T(8,128)S(1)}, u32[]{:S(2)}, u32[]{:S(2)}) collective-permute-start(f32[68,8,128]{2,1,0:T(8,128)S(1)} %get-tuple-element.130), channel_id=1, source_target_pairs={{0,8},{8,16},{16,24},{24,25},{25,17},{17,9},{9,1},{1,2},{2,10},{10... | collective-permute-start | bytes 835592 | tf_op jit(solution)/shard_map/ppermute | solution.py:594
  90.5 8.5 %collective-permute-start.32 = (f32[68,8,128]{2,1,0:T(8,128)S(1)}, f32[68,8,128]{2,1,0:T(8,128)S(1)}, u32[]{:S(2)}, u32[]{:S(2)}) collective-permute-start(f32[68,8,128]{2,1,0:T(8,128)S(1)} %get-tuple-element.131), channel_id=1, source_target_pairs={{8,0},{16,8},{24,16},{25,24},{17,25},{9,17},{1,9},{2,1},{10,2},{18... | collective-permute-start | bytes 835592 | tf_op jit(solution)/shard_map/ppermute | solution.py:595
  90.5 3.9 %collective-permute-start.33 = (f32[8,128]{1,0:T(8,128)S(1)}, f32[8,128]{1,0:T(8,128)S(1)}, u32[]{:S(2)}, u32[]{:S(2)}) collective-permute-start(f32[8,128]{1,0:T(8,128)S(1)} %add.107), channel_id=1, source_target_pairs={{0,1},{1,0},{2,3},{3,2},{4,5},{5,4},{6,7},{7,6},{8,9},{9,8},{10,11... | collective-permute-start | bytes 12296 | tf_op jit(solution)/shard_map/ppermute | solution.py:532
  90.9 4.9 %collective-permute-start.34 = (f32[8,128]{1,0:T(8,128)S(1)}, f32[8,128]{1,0:T(8,128)S(1)}, u32[]{:S(2)}, u32[]{:S(2)}) collective-permute-start(f32[8,128]{1,0:T(8,128)S(1)} %add.107), channel_id=1, source_target_pairs={{0,2},{1,3},{2,0},{3,1},{4,6},{5,7},{6,4},{7,5},{8,10},{9,11},{10,... | collective-permute-start | bytes 12296 | tf_op jit(solution)/shard_map/ppermute | solution.py:532
  94.4 3.7 %collective-permute-start.35 = (f32[8,128]{1,0:T(8,128)S(1)}, f32[8,128]{1,0:T(8,128)S(1)}, u32[]{:S(2)}, u32[]{:S(2)}) collective-permute-start(f32[8,128]{1,0:T(8,128)S(1)} %add.107), channel_id=1, source_target_pairs={{0,3},{1,2},{2,1},{3,0},{4,7},{5,6},{6,5},{7,4},{8,11},{9,10},{10,... | collective-permute-start | bytes 12296 | tf_op jit(solution)/shard_map/ppermute | solution.py:532
  94.4 4.3 %collective-permute-start.30 = (f32[8,128]{1,0:T(8,128)S(1)}, f32[8,128]{1,0:T(8,128)S(1)}, u32[]{:S(2)}, u32[]{:S(2)}) collective-permute-start(f32[8,128]{1,0:T(8,128)S(1)} %add.105), channel_id=1, source_target_pairs={{0,4},{1,5},{2,6},{3,7},{4,0},{5,1},{6,2},{7,3},{8,12},{9,13},{10,... | collective-permute-start | bytes 12296 | tf_op jit(solution)/shard_map/ppermute | solution.py:532
  98.7 5.2 %collective-permute-start.36 = (f32[8,128]{1,0:T(8,128)S(1)}, f32[8,128]{1,0:T(8,128)S(1)}, u32[]{:S(2)}, u32[]{:S(2)}) collective-permute-start(f32[8,128]{1,0:T(8,128)S(1)} %add.106), channel_id=1, source_target_pairs={{0,16},{8,24},{16,0},{24,8},{1,17},{9,25},{17,1},{25,9},{2,18},{10... | collective-permute-start | bytes 12296 | tf_op jit(solution)/shard_map/ppermute | solution.py:532
  106.2 13.5 %collective-permute-start.40 = (f32[64,8,128]{2,1,0:T(8,128)S(1)}, f32[64,8,128]{2,1,0:T(8,128)S(1)}, u32[]{:S(2)}, u32[]{:S(2)}) collective-permute-start(f32[64,8,128]{2,1,0:T(8,128)S(1)} %get-tuple-element.138), channel_id=1, source_target_pairs={{0,8},{8,0},{16,24},{24,16},{1,9},{9,1},{17,25},{25,17},{2,10},{10... | collective-permute-start | bytes 786440 | tf_op jit(solution)/shard_map/ppermute | solution.py:532
  109.7 10.0 %collective-permute-start.41 = (f32[64,8,128]{2,1,0:T(8,128)S(1)}, f32[64,8,128]{2,1,0:T(8,128)S(1)}, u32[]{:S(2)}, u32[]{:S(2)}) collective-permute-start(f32[64,8,128]{2,1,0:T(8,128)S(1)} %get-tuple-element.139), channel_id=1, source_target_pairs={{0,16},{8,24},{16,0},{24,8},{1,17},{9,25},{17,1},{25,9},{2,18},{10... | collective-permute-start | bytes 786440 | tf_op jit(solution)/shard_map/ppermute | solution.py:532
  112.3 12.6 %collective-permute-start.42 = (f32[64,8,128]{2,1,0:T(8,128)S(1)}, f32[64,8,128]{2,1,0:T(8,128)S(1)}, u32[]{:S(2)}, u32[]{:S(2)}) collective-permute-start(f32[64,8,128]{2,1,0:T(8,128)S(1)} %get-tuple-element.140), channel_id=1, source_target_pairs={{0,24},{8,16},{16,8},{24,0},{1,25},{9,17},{17,9},{25,1},{2,26},{10... | collective-permute-start | bytes 786440 | tf_op jit(solution)/shard_map/ppermute | solution.py:532
  112.9 2.8 %collective-permute-start.37 = (f32[8,128]{1,0:T(8,128)S(1)}, f32[8,128]{1,0:T(8,128)S(1)}, u32[]{:S(2)}, u32[]{:S(2)}) collective-permute-start(f32[8,128]{1,0:T(8,128)S(1)} %add.111), channel_id=1, source_target_pairs={{0,1},{1,0},{2,3},{3,2},{4,5},{5,4},{6,7},{7,6},{8,9},{9,8},{10,11... | collective-permute-start | bytes 12296 | tf_op jit(solution)/shard_map/ppermute | solution.py:532
  112.9 4.3 %collective-permute-start.38 = (f32[8,128]{1,0:T(8,128)S(1)}, f32[8,128]{1,0:T(8,128)S(1)}, u32[]{:S(2)}, u32[]{:S(2)}) collective-permute-start(f32[8,128]{1,0:T(8,128)S(1)} %add.111), channel_id=1, source_target_pairs={{0,2},{1,3},{2,0},{3,1},{4,6},{5,7},{6,4},{7,5},{8,10},{9,11},{10,... | collective-permute-start | bytes 12296 | tf_op jit(solution)/shard_map/ppermute | solution.py:532
  115.7 4.0 %collective-permute-start.39 = (f32[8,128]{1,0:T(8,128)S(1)}, f32[8,128]{1,0:T(8,128)S(1)}, u32[]{:S(2)}, u32[]{:S(2)}) collective-permute-start(f32[8,128]{1,0:T(8,128)S(1)} %add.111), channel_id=1, source_target_pairs={{0,3},{1,2},{2,1},{3,0},{4,7},{5,6},{6,5},{7,4},{8,11},{9,10},{10,... | collective-permute-start | bytes 12296 | tf_op jit(solution)/shard_map/ppermute | solution.py:532

commit v5 on v4

--- a/solution.py
+++ b/solution.py
@@ -15,14 +15,14 @@
 XI = 16
 GX = 4
 OWN = 32
-HALO = 8
-EXT = OWN + 2 * HALO
-PAD = EXT + 16
+WIDE, NARROW = 24, 8
+DEEP = WIDE // 8
 LANES = 128
 WIDTH = 2 * RADIUS + 1
 LOWEST = NZ // 2 - RADIUS
-TILES = 4 * XI
-MORE = 4
+TILES = 4 * XI * DEEP
+MORE = 2 * OWN // 8
+CHUNK = 4 * XI
 UNROLL = {"fill": 4, "tend": 4, "div": 16, "relax": 16, "correct": 16}
 
 TIME_STEP = 0.25
@@ -98,18 +98,26 @@
     return jnp.dot(a, b, precision=lax.Precision.HIGHEST, preferred_element_type=F32)
 
 
-def band_sums(fields, su, sd, sums):
+def band_sums(fields, sums, sent=()):
     matrix = group_matrix("row")
-    level = lanes(OWN) & (NZ - 1)
+    count = sums.shape[1]
+    level = lanes(count) & (NZ - 1)
     for c in range(2):
-        total = exact_dot(fields[c].reshape(XI * OWN, LANES), matrix)
-        packed = jnp.zeros((OWN, LANES), F32)
+        total = exact_dot(fields[c].reshape(XI * count, LANES), matrix)
+        packed = jnp.zeros((count, LANES), F32)
         for xi in range(XI):
-            packed = jnp.where(level == xi, total[xi * OWN : (xi + 1) * OWN], packed)
+            packed = jnp.where(level == xi, total[xi * count : (xi + 1) * count], packed)
         sums[c] = packed
-        for t in range(2):
-            sd[TILES + 2 * c + t] = packed[t * 8 : t * 8 + 8]
-            su[TILES + 2 * c + t] = packed[16 + t * 8 : 24 + t * 8]
+        for t in range(OWN // 8):
+            for out in sent:
+                out[TILES + c * (OWN // 8) + t] = packed[t * 8 : t * 8 + 8]
+
+
+def send_tile(su, sd, index, tile, value):
+    if tile < DEEP:
+        sd[index * DEEP + tile] = value
+    if tile >= OWN // 8 - DEEP:
+        su[index * DEEP + tile - (OWN // 8 - DEEP)] = value
 
 
 def block_transposed(sources, group, masks):
@@ -135,7 +143,7 @@
     rows("fill", per_row)
     for half in range(6):
         for out in (s0, s1, s2, s3):
-            out[TILES + half] = ids[half // 2, (half % 2) * 8 : (half % 2) * 8 + 8]
+            out[CHUNK + half] = ids[half // 2, (half % 2) * 8 : (half % 2) * 8 + 8]
     for plane in range(planes.shape[0]):
         for kt in range(4):
             sources = [planes[plane, c, kt * 8 : kt * 8 + 8, :] for c in range(4)]
@@ -147,11 +155,11 @@
     lane = lanes(NZ)
     pieces = []
     for g in range(GX):
-        moved_mid = pltpu.roll(ids[0, g], (16 - 32 * slab) & (LANES - 1), axis=1)
-        moved_left = pltpu.roll(ids[1, g], 16, axis=1)
-        moved_right = pltpu.roll(ids[2, g], OWN + 16, axis=1)
-        here = jnp.where((lane[:XI] < 16) & (slab == 0), moved_left, moved_mid)
-        here = jnp.where((lane[:XI] >= OWN + 16) & (slab == 3), moved_right, here)
+        moved_mid = pltpu.roll(ids[0, g], (32 - 32 * slab) & (LANES - 1), axis=1)
+        moved_left = pltpu.roll(ids[1, g], OWN, axis=1)
+        moved_right = pltpu.roll(ids[2, g], 2 * OWN, axis=1)
+        here = jnp.where((lane[:XI] < OWN) & (slab == 0), moved_left, moved_mid)
+        here = jnp.where((lane[:XI] >= 2 * OWN) & (slab == 3), moved_right, here)
         pieces += [here, jnp.full((XI, LANES), -1.0, F32)]
     here = jnp.concatenate(pieces, axis=0)
     turbines = (ints.shape[0] - INTS) // 2
@@ -174,11 +182,8 @@
         cosine = jnp.where(sector == value, F32(math.cos(angle)), cosine)
         sine = jnp.where(sector == value, F32(math.sin(angle)), sine)
     thrust = running * F32(-0.5 * THRUST_COEFF * TIME_STEP / float(WIDTH**2) ** 2)
-    low = lanes(LANES) < 64
-    first = jnp.where(low, here, pltpu.roll(thrust, 64, axis=1)).T
-    second = jnp.where(low, cosine, pltpu.roll(sine, 64, axis=1)).T
-    maps[0], maps[3] = first[:64], first[64:]
-    maps[1], maps[2] = second[:64], second[64:]
+    for which, value in enumerate((here, cosine, sine, thrust)):
+        maps[which] = value.T[: 3 * OWN]
 
 
 def over_groups(row):
@@ -193,9 +198,9 @@
     fields, inflow, su, sd, bands, sums, ids, held, planes = rest[layouts - 1 :]
     own, here = scal[0], scal[2]
     for s, source in enumerate((s0, r1, r2, r3)):
-        held[own ^ s] = source[:TILES]
+        held[own ^ s] = source[:CHUNK]
         for half in range(6):
-            ids[half // 2, own ^ s, (half % 2) * 8 : (half % 2) * 8 + 8, :] = source[TILES + half]
+            ids[half // 2, own ^ s, (half % 2) * 8 : (half % 2) * 8 + 8, :] = source[CHUNK + half]
     for s, source in enumerate(plane_refs):
         planes[here ^ s] = source[...]
 
@@ -205,8 +210,8 @@
         for c in range(4):
             value = turned[c * 32 : c * 32 + 32] + profile[c : c + 1, :]
             fields[c, xi] = value
-            sd[c * XI + xi] = value[:HALO]
-            su[c * XI + xi] = value[OWN - HALO :]
+            for t in range(OWN // 8):
+                send_tile(su, sd, c * XI + xi, t, value[t * 8 : t * 8 + 8])
             if c == 3:
                 total = total + jnp.sum(value, axis=0, keepdims=True)
         return total
@@ -223,9 +228,9 @@
     for c in range(4):
         value = turned[c * 32 : c * 32 + 32] + profile[c : c + 1, :]
         inflow[c] = value
-        sd[TILES + MORE + c] = value[:HALO]
-        su[TILES + MORE + c] = value[OWN - HALO :]
-    band_sums(fields, su, sd, bands)
+        for t in range(OWN // 8):
+            send_tile(su, sd, 4 * XI + MORE // DEEP + 1 + c, t, value[t * 8 : t * 8 + 8])
+    band_sums(fields, bands, (su, sd))
 
 
 def mean_response(mean):
@@ -257,44 +262,68 @@
 
 def step_kernel(*refs, step, cells):
     refs = list(refs)
-    fields_in, lo, hi, maps, bands_in, inflow_in = refs[:6]
-    del refs[:6]
-    mean = None
+    wide = step % 2 == 0
+    halo = WIDE if wide else NARROW
+    kept = NARROW if wide else 0
+    ext = OWN + 2 * halo
+    pad = ext + 16
+    tiles = ext // 8
+    own_tiles = range(halo // 8, halo // 8 + OWN // 8)
+    kept_tiles = range((halo - kept) // 8, (halo + OWN + kept) // 8)
+    band_tiles = range(1, tiles - 1) if wide else kept_tiles
+    fields_in, maps, bands_in, inflow_in = refs[:4]
+    del refs[:4]
+    lo = hi = mean = None
+    if wide:
+        lo, hi = refs[:2]
+        del refs[:2]
     if step > 0:
         mean = refs.pop(0)
     out = refs.pop(0)
-    su = sd = bands = sums = inflow_out = None
+    su = sd = bands = sums = inflow_out = wind = None
     if step < STEPS - 1:
-        su, sd, bands, sums = refs[:4]
-        del refs[:4]
+        bands, sums = refs[:2]
+        del refs[:2]
+        if not wide:
+            su, sd = refs[:2]
+            del refs[:2]
     if step == 0:
         inflow_out = refs.pop(0)
-    f, v, r, pa, pb, ns, change, inflow = refs
+    f, v, r, pa, pb, ns, change, inflow = refs[:8]
+    if wide:
+        wind = refs[8]
     first, last = level_masks()
-    lane_ext = lanes(EXT)
-    body = slice(8, 8 + EXT)
+    lane_ext = lanes(ext)
+    body = slice(8, 8 + ext)
 
     if step > 0:
-        du, dw = mean_response(mean[0:1, :] * F32(1.0 / cells))
+        row = 1 if step == STEPS - 1 else 0
+        du, dw = mean_response(mean[row : row + 1, :] * F32(1.0 / cells))
         change[0] = du
         change[1] = dw
-        inflow[...] = inflow_in[...]
+        inflow[...] = inflow_in[...] if wide else inflow_in[:, WIDE - NARROW : WIDE + OWN + NARROW]
     else:
         for c in range(4):
-            inflow[c, 0:8] = lo[TILES + MORE + c]
-            inflow[c, 8 : 8 + OWN] = inflow_in[c]
-            inflow[c, 8 + OWN : EXT] = hi[TILES + MORE + c]
+            for t in range(DEEP):
+                base = TILES + MORE + 1 + c * DEEP
+                inflow[c, t * 8 : t * 8 + 8] = lo[base + t]
+                inflow[c, WIDE + OWN + t * 8 : WIDE + OWN + t * 8 + 8] = hi[base + t]
+            inflow[c, WIDE : WIDE + OWN] = inflow_in[c]
         inflow_out[...] = inflow[...]
 
     def fill(xi, carry):
         for c in range(4):
-            low, mid, high = lo[c * XI + xi], fields_in[c, xi], hi[c * XI + xi]
-            if step > 0 and c in (0, 2):
-                d = change[c // 2, pl.ds(xi, 1), :]
-                low, mid, high = low + d, mid + d, high + d
-            f[c, xi + 1, 8:16] = low
-            f[c, xi + 1, 16 : 16 + OWN] = mid
-            f[c, xi + 1, 16 + OWN : 8 + EXT] = high
+            d = change[c // 2, pl.ds(xi, 1), :] if step > 0 and c in (0, 2) else None
+            if wide:
+                index = (c * XI + xi) * DEEP
+                parts = [lo[pl.ds(index, DEEP)].reshape(WIDE, LANES), fields_in[c, xi]]
+                parts.append(hi[pl.ds(index, DEEP)].reshape(WIDE, LANES))
+            else:
+                parts = [fields_in[c, xi]]
+            at = 8
+            for part in parts:
+                f[c, xi + 1, at : at + part.shape[0]] = part if d is None else part + d
+                at += part.shape[0]
         return carry
 
     rows("fill", fill)
@@ -314,18 +343,22 @@
 
     packed = []
     for c in range(2):
-        parts = [lo[TILES + 2 * c + t] for t in range(2)] + [bands_in[c]]
-        parts += [hi[TILES + 2 * c + t] for t in range(2)]
-        packed.append(jnp.concatenate(parts, axis=0))
+        if wide:
+            near = slice(TILES + c * (OWN // 8), TILES + (c + 1) * (OWN // 8))
+            parts = [lo[near].reshape(OWN, LANES), bands_in[c], hi[near].reshape(OWN, LANES)]
+            packed.append(jnp.concatenate(parts, axis=0))
+        else:
+            packed.append(bands_in[c])
     if step > 0:
         level = lanes(XI) & (NZ - 1)
         row = lax.broadcasted_iota(jnp.int32, (XI, LANES), 0)
         shift_u = jnp.where(level == row, exact_dot(change[0], group_matrix("row")), 0.0)
         packed[0] = packed[0] + jnp.sum(shift_u, axis=0, keepdims=True)
-    ident, cosine, sine = maps[0], maps[1], maps[2]
+    size = ext + 16
+    span = slice(OWN - halo - 8, OWN - halo - 8 + size)
+    ident, cosine, sine, factor = (maps[which, span, :] for which in range(4))
     speed = cosine * packed[0] + sine * packed[1]
     forward = backward = speed
-    size = ident.shape[0]
     row = lax.broadcasted_iota(jnp.int32, ident.shape, 0)
     for d in (1, 2, 4, 8):
         same = (ident == pltpu.roll(ident, d, axis=0)) & (row >= d)
@@ -333,22 +366,25 @@
         same = (ident == pltpu.roll(ident, size - d, axis=0)) & (row < size - d)
         backward = backward + jnp.where(same, pltpu.roll(backward, size - d, axis=0), 0.0)
     total = forward + backward - speed
-    thrust = maps[3] * total * jnp.abs(total)
-    level = lanes(EXT) & (NZ - 1)
+    thrust = factor * total * jnp.abs(total)
+    level = lanes(ext) & (NZ - 1)
     matrix = group_matrix("column")
     for c, direction in enumerate((cosine, sine)):
-        pushed = (thrust * direction)[8 : 8 + EXT]
+        pushed = (thrust * direction)[8 : 8 + ext]
         for part in range(0, XI, 4):
             spread = [jnp.where(level == xi, pushed, 0.0) for xi in range(part, part + 4)]
             result = exact_dot(jnp.concatenate(spread, axis=0), matrix)
-            ns[c, part : part + 4] = result.reshape(4, EXT, LANES)
+            ns[c, part : part + 4] = result.reshape(4, ext, LANES)
 
     def tendencies(xi, total):
-        for tile in range(EXT // 8):
+        for tile in range(tiles):
             base = 8 + tile * 8
             centre, gx, gy, gz, lap = [], [], [], [], []
             for c in range(4):
                 mid = f[c, xi + 1, base : base + 8, :]
+                if c == 3 and tile not in kept_tiles:
+                    centre.append(mid)
+                    continue
                 xm = f[c, xi, base : base + 8, :]
                 xp = f[c, xi + 2, base : base + 8, :]
                 ym = f[c, xi + 1, base - 1 : base + 7, :]
@@ -373,7 +409,7 @@
             nu = F32(TIME_STEP * VISCOSITY) + F32(0.5 * TIME_STEP * SMAGORINSKY) * strain
             half = F32(0.5 * TIME_STEP)
             au, av, aw = half * centre[0], half * centre[1], half * centre[2]
-            for c in range(4):
+            for c in range(4 if tile in kept_tiles else 3):
                 scale = nu * F32(DIFFUSIVITY_RATIO) if c == 3 else nu
                 new = centre[c] + (scale * lap[c] - (au * gx[c] + av * gy[c] + aw * gz[c]))
                 if c < 2:
@@ -382,14 +418,13 @@
                     new = new + F32(TIME_STEP * BUOYANCY) * centre[3]
                 if c < 3:
                     v[c, xi + 1, base : base + 8, :] = new
-                elif 1 <= tile <= 4:
-                    out[3, xi, tile * 8 - 8 : tile * 8, :] = new
-                    if sums is not None:
+                else:
+                    at = (tile - kept_tiles[0]) * 8
+                    out[3, xi, at : at + 8, :] = new
+                    if sums is not None and tile in own_tiles:
                         total = total + new
-                        if tile == 1:
-                            sd[3 * XI + xi] = new
-                        if tile == 4:
-                            su[3 * XI + xi] = new
+                        if su is not None:
+                            send_tile(su, sd, 3 * XI + xi, tile - own_tiles[0], new)
         return total
 
     total = rows("tend", tendencies, jnp.zeros((8, LANES), F32))
@@ -403,7 +438,7 @@
     )
 
     def divergence(xi, carry):
-        for tile in range(EXT // 8):
+        for tile in range(tiles):
             base = 8 + tile * 8
             here = slice(base, base + 8)
             w = v[2, xi + 1, here, :]
@@ -429,7 +464,7 @@
         ends(p)
 
         def relax(xi, carry, p=p, q=q):
-            for tile in range(EXT // 8):
+            for tile in range(tiles):
                 base = 8 + tile * 8
                 here = slice(base, base + 8)
                 mid = p[xi + 1, here, :]
@@ -445,41 +480,46 @@
     ends(p)
 
     def correct(xi, carry):
-        for tile in range(1, 5):
+        for tile in band_tiles:
             base = 8 + tile * 8
             here = slice(base, base + 8)
             mid = p[xi + 1, here, :]
             slopes = (
                 p[xi + 2, here, :] - p[xi, here, :],
                 p[xi + 1, base + 1 : base + 9, :] - p[xi + 1, base - 1 : base + 7, :],
-                above(mid, last) - below(mid, first),
+                above(mid, last) - below(mid, first) if tile in kept_tiles else None,
             )
-            for c in range(3):
+            for c in range(3 if tile in kept_tiles else 2):
                 new = v[c, xi + 1, here, :] - 0.5 * slopes[c]
-                out[c, xi, tile * 8 - 8 : tile * 8, :] = new
-                if sums is not None:
-                    if tile == 1:
-                        sd[c * XI + xi] = new
-                    if tile == 4:
-                        su[c * XI + xi] = new
+                if wide and c < 2:
+                    wind[c, xi, tile * 8 - 8 : tile * 8, :] = new
+                if tile in kept_tiles:
+                    at = (tile - kept_tiles[0]) * 8
+                    out[c, xi, at : at + 8, :] = new
+                if su is not None and tile in own_tiles:
+                    send_tile(su, sd, c * XI + xi, tile - own_tiles[0], new)
         return carry
 
     rows("correct", correct)
-    if sums is not None:
-        band_sums(out, su, sd, bands)
-
-
-def step_scratch():
-    return [
-        pltpu.VMEM((4, XI + 2, PAD, LANES), F32),
-        pltpu.VMEM((3, XI + 2, PAD, LANES), F32),
-        pltpu.VMEM((XI, EXT, LANES), F32),
-        pltpu.VMEM((XI + 2, PAD, LANES), F32),
-        pltpu.VMEM((XI + 2, PAD, LANES), F32),
-        pltpu.VMEM((2, XI, EXT, LANES), F32),
+    if bands is not None:
+        band_sums(wind if wide else out, bands, () if wide else (su, sd))
+
+
+def step_scratch(step):
+    wide = step % 2 == 0
+    ext = OWN + 2 * (WIDE if wide else NARROW)
+    pad = ext + 16
+    scratch = [
+        pltpu.VMEM((4, XI + 2, pad, LANES), F32),
+        pltpu.VMEM((3, XI + 2, pad, LANES), F32),
+        pltpu.VMEM((XI, ext, LANES), F32),
+        pltpu.VMEM((XI + 2, pad, LANES), F32),
+        pltpu.VMEM((XI + 2, pad, LANES), F32),
+        pltpu.VMEM((2, XI, ext, LANES), F32),
         pltpu.VMEM((2, XI, LANES), F32),
-        pltpu.VMEM((4, EXT, LANES), F32),
+        pltpu.VMEM((4, ext, LANES), F32),
     ]
+    return scratch + ([pltpu.VMEM((2, XI, ext - 16, LANES), F32)] if wide else [])
 
 
 def send_kernel(scal, fields, s0, s1, s2, s3, turned):
@@ -549,7 +589,7 @@
 
     ids = turbine_cell[0, :, NZ // 2, :].astype(F32)
     ids = jnp.stack([ids, lax.ppermute(ids, "gy", gy_up), lax.ppermute(ids, "gy", gy_down)])
-    chunk = shape(TILES + 6, 8, LANES)
+    chunk = shape(CHUNK + 6, 8, LANES)
     s0, s1, s2, s3, plane = call(
         pack_kernel,
         (chunk, chunk, chunk, chunk, shape(per_layout * 4, 8, LANES)),
@@ -560,7 +600,7 @@
     received[0], plane = lax.optimization_barrier((received[0], plane))
     plane_received = [swapped(plane, "layout", layouts, s) for s in range(1, layouts)]
 
-    first_payload = shape(TILES + MORE + 4, 8, LANES)
+    first_payload = shape(TILES + MORE + 1 + 4 * DEEP, 8, LANES)
     fields, inflow, su, sd, bands, sums, ids = call(
         functools.partial(unpack_kernel, layouts=layouts, per_layout=per_layout),
         (
@@ -574,57 +614,65 @@
         ),
         [SMEM, VMEM] + [VMEM] * (4 + layouts),
         [
-            pltpu.VMEM((GX, TILES, 8, LANES), F32),
+            pltpu.VMEM((GX, CHUNK, 8, LANES), F32),
             pltpu.VMEM((layouts, per_layout * 4, 8, LANES), F32),
         ],
         name="unpack",
     )(scal, profile, s0, *received, plane, *plane_received)
 
-    maps = call(maps_kernel, shape(4, 2 * OWN, LANES), [SMEM, VMEM], name="maps")(scal, ids)
+    maps = call(maps_kernel, shape(4, 3 * OWN, LANES), [SMEM, VMEM], name="maps")(scal, ids)
 
     half = groups // 2
 
-    def last_round(value):
+    def among_x(value):
         return sum([swapped(value, "gy", groups, d) for d in range(1, half)], value)
 
-    mean = pending = None
-    for step in range(STEPS):
-        partial = sums + swapped(sums, "gx", GX, 1)
-        su, sd, partial = lax.optimization_barrier((su, sd, partial))
-        lo = lax.ppermute(su, ("gx", "gy"), up)
-        hi = lax.ppermute(sd, ("gx", "gy"), down)
-        if pending is not None:
-            mean = last_round(pending)
-        partial = partial + swapped(partial, "gy", groups, half)
-        fields, partial = lax.optimization_barrier((fields, partial))
-        arriving = swapped(partial, "gx", GX, 2)
-        outs = [shape(4, XI, OWN, LANES)]
+    def run(step, operands):
+        wide = step % 2 == 0
+        outs = [shape(4, XI, OWN + 2 * (NARROW if wide else 0), LANES)]
         if step < STEPS - 1:
-            payload = shape(TILES + MORE, 8, LANES)
-            outs += [payload, payload, shape(2, OWN, LANES), shape(8, LANES)]
+            outs += [shape(2, 2 * OWN if wide else OWN, LANES), shape(8, LANES)]
+            if not wide:
+                outs += [shape(TILES + MORE, 8, LANES), shape(TILES + MORE, 8, LANES)]
         if step == 0:
-            outs += [shape(4, EXT, LANES)]
-        operands = [fields, lo, hi, maps, bands, inflow] + ([mean] if step > 0 else [])
-        results = call(
+            outs += [shape(4, OWN + 2 * WIDE, LANES)]
+        return call(
             functools.partial(step_kernel, step=step, cells=cells),
-            tuple(outs),
+            tuple(outs) if len(outs) > 1 else outs[0],
             [VMEM] * len(operands),
-            step_scratch(),
+            step_scratch(step),
             flops=6_000_000_000,
             name="step%d" % step,
         )(*operands)
-        results = list(results)
-        fields = results.pop(0)
-        if step < STEPS - 1:
-            su, sd, bands, sums = results[:4]
-            del results[:4]
-        if step == 0:
-            inflow = results.pop(0)
-        su, sd, fields, arriving = lax.optimization_barrier((su, sd, fields, arriving))
-        pending = partial + arriving
-    mean = last_round(pending)
-
-    chunk = shape(TILES, 8, LANES)
+
+    def exchange(su, sd, fields, value):
+        value = value + swapped(value, "gx", GX, 1)
+        su, sd, value = lax.optimization_barrier((su, sd, value))
+        lo = lax.ppermute(su, ("gx", "gy"), up)
+        hi = lax.ppermute(sd, ("gx", "gy"), down)
+        value = among_x(value + swapped(value, "gy", groups, half))
+        fields, value = lax.optimization_barrier((fields, value))
+        return lo, hi, fields, value, swapped(value, "gx", GX, 2)
+
+    lo, hi, fields, partial, arriving = exchange(su, sd, fields, sums)
+    fields, bands, sums, inflow = run(0, [fields, maps, bands, inflow, lo, hi])
+    fields, arriving = lax.optimization_barrier((fields, arriving))
+    early = swapped(sums, "gx", GX, 2)
+    fields, bands, late, su, sd = run(1, [fields, maps, bands, inflow, partial + arriving])
+    su, sd, fields, early = lax.optimization_barrier((su, sd, fields, early))
+    is_early = lax.broadcasted_iota(jnp.int32, (8, LANES), 0) == 0
+    both = jnp.where(is_early, sums + early, late)
+    lo, hi, fields, partial, arriving = exchange(su, sd, fields, both)
+    fields, bands, sums = run(2, [fields, maps, bands, inflow, lo, hi, partial])
+    fields, arriving = lax.optimization_barrier((fields, arriving))
+    early = swapped(sums, "gx", GX, 2)
+    fields = run(3, [fields, maps, bands, inflow, partial + arriving])
+    fields, early = lax.optimization_barrier((fields, early))
+    mean = sums + early
+    mean = among_x(mean + swapped(mean, "gx", GX, 1))
+    mean = mean + swapped(mean, "gy", groups, half)
+
+    chunk = shape(CHUNK, 8, LANES)
     s0, s1, s2, s3 = call(
         send_kernel,
         (chunk, chunk, chunk, chunk),

time: 128 us -> 146 us (1.14)
  waiting for transfers between devices: 34.5 us -> 62.2 us
  starting transfers between devices: 60.1 us -> 43.4 us
  Pallas kernels: 30.1 us -> 35.1 us
    ppermute x33 -> x28, waiting for transfers between devices: 34.2 us -> 62 us  [swapped(): return lax.ppermute(value, axis, [(i, i ^ distance) for i in range(size)])]
    ppermute x33 -> x28, starting transfers between devices: 46.7 us -> 35.4 us  [swapped(): return lax.ppermute(value, axis, [(i, i ^ distance) for i in range(size)])]
    ppermute x8 -> x4, starting transfers between devices: 8.97 us -> 3.64 us  [the longest x2 3.2 us: exchange(): lo = lax.ppermute(su, ('gx', 'gy'), up)]
    pallas_call x5, Pallas kernels: 21 us -> 26 us  [the longest x4 24.4 us: run(): call(functools.partial(step_kernel, step=step, cells=cells), tuple(outs)...]
  transfers between devices with their start and end apart: 43 -> 34, of which waited for: 20 -> 16; matrix products, arithmetic and copies ran while one was open for 1% -> 1% of each run, Pallas kernels for 16% -> 18%
where the time goes in v5:
time: 146 us; the launch traced here: 145 us
  waiting for transfers between devices  62.2 us (43%)
  starting transfers between devices  43.4 us (30%)
  Pallas kernels  35.1 us (24%)
  local copies, waits for them, and re-layouts  3.91 us (3%)
    ppermute x28, waiting for transfers between devices, swapped(): return lax.ppermute(value, axis, [(i, i ^ distance) for i in range(size)])  62 us
    ppermute x28, starting transfers between devices, swapped(): return lax.ppermute(value, axis, [(i, i ^ distance) for i in range(size)])  35.4 us
    pallas_call x4, Pallas kernels, run(): call(functools.partial(step_kernel, step=step, cells=cells), tuple(outs)...  24.4 us
    ppermute x2, starting transfers between devices, exchange(): lo = lax.ppermute(su, ('gx', 'gy'), up)  3.2 us
    pallas_call x1, Pallas kernels, local(): call(functools.partial(final_kernel, cells=cells), shape(4, XI, NZ, LANES...  3.11 us
  transfers between devices with their start and end apart: 34, of which 16 were waited for; matrix products, arithmetic and copies ran while one was open for 1% of the time, Pallas kernels for 18%

profile of v5, /device:TPU:1, one launch (start us, length us, event | category | flops | bytes accessed | tf_op | source)
XLA Modules:
  0.0 145.1 jit_solution(13983140161162917167)
XLA Ops:
  0.0 0.8 slice.3
  0.9 2.0 %collective-permute-start = (f32[16,128]{1,0:T(8,128)S(1)}, f32[16,128]{1,0:T(8,128)S(1)}, u32[]{:S(2)}, u32[]{:S(2)}) collective-permute-start(f32[16,128]{1,0:T(8,128)S(1)} %get-tuple-element.106), channel_id=1, source_target_pairs={{0,1},{1,2},{2,3},{3,4},{4,5},{5,6},{6,7},{7,0},{8,9},{9,10},{10,1... | collective-permute-start | bytes 24584 | tf_op jit(solution)/shard_map/ppermute | solution.py:591
  2.9 2.4 %collective-permute-start.1 = (f32[16,128]{1,0:T(8,128)S(1)}, f32[16,128]{1,0:T(8,128)S(1)}, u32[]{:S(2)}, u32[]{:S(2)}) collective-permute-start(f32[16,128]{1,0:T(8,128)S(1)} %get-tuple-element.106), channel_id=1, source_target_pairs={{1,0},{2,1},{3,2},{4,3},{5,4},{6,5},{7,6},{0,7},{9,8},{10,9},{11,1... | collective-permute-start | bytes 24584 | tf_op jit(solution)/shard_map/ppermute | solution.py:591
  5.2 0.8 concatenate.3.scal.ints
  6.0 0.2 collective-permute-done
  6.2 0.0 collective-permute-done.1
  6.2 1.2 copy-done
  7.4 0.9 copy-done.1
  8.3 2.0 %pack.1 = (f32[70,8,128]{2,1,0:T(8,128)S(1)}, f32[70,8,128]{2,1,0:T(8,128)S(1)}, f32[70,8,128]{2,1,0:T(8,128)S(1)}, f32[70,8,128]{2,1,0:T(8,128)S(1)}, f32[8,8,128]{2,1,0:T(8,128)S(1)}) custom-call(s32[135]{0:T(256)S(1)} %concatenate.3.scal.ints, f32[4,16,32,128]{3,2,1,0:T(8,128)S(1)} %bitcast.14, f32[2,4,32,128]{3,2,1,0:T(8,128)S(1)} %copy-done.1, ...), custom_call_target="tpu_custom_call" | custom-call | flops 2000000000 | bytes 4000000 | tf_op jit(solution)/shard_map/pack/pallas_call | solution.py:593
  10.3 1.9 %collective-permute-start.2 = (f32[70,8,128]{2,1,0:T(8,128)S(1)}, f32[70,8,128]{2,1,0:T(8,128)S(1)}, u32[]{:S(2)}, u32[]{:S(2)}) collective-permute-start(f32[70,8,128]{2,1,0:T(8,128)S(1)} %get-tuple-element.56), channel_id=1, source_target_pairs={{0,8},{8,0},{16,24},{24,16},{1,9},{9,1},{17,25},{25,17},{2,10},{10... | collective-permute-start | bytes 860168 | tf_op jit(solution)/shard_map/ppermute | solution.py:572
  12.2 0.1 pad.9.clone
  12.3 3.0 %collective-permute-start.3 = (f32[70,8,128]{2,1,0:T(8,128)S(1)}, f32[70,8,128]{2,1,0:T(8,128)S(1)}, u32[]{:S(2)}, u32[]{:S(2)}) collective-permute-start(f32[70,8,128]{2,1,0:T(8,128)S(1)} %get-tuple-element.59), channel_id=1, source_target_pairs={{0,16},{8,24},{16,0},{24,8},{1,17},{9,25},{17,1},{25,9},{2,18},{10... | collective-permute-start | bytes 860168 | tf_op jit(solution)/shard_map/ppermute | solution.py:572
  15.3 0.2 collective-permute-start.4
  15.5 0.0 collective-permute-done.2.r1
  15.5 1.8 %collective-permute-start.5 = (f32[8,8,128]{2,1,0:T(8,128)S(1)}, f32[8,8,128]{2,1,0:T(8,128)S(1)}, u32[]{:S(2)}, u32[]{:S(2)}) collective-permute-start(f32[8,8,128]{2,1,0:T(8,128)S(1)} %get-tuple-element.61.p0), channel_id=1, source_target_pairs={{0,32},{32,0},{64,96},{96,64},{1,33},{33,1},{65,97},{97,65},{2,34}... | collective-permute-start | bytes 98312 | tf_op jit(solution)/shard_map/ppermute | solution.py:572
  17.3 3.3 %collective-permute-start.6 = (f32[8,8,128]{2,1,0:T(8,128)S(1)}, f32[8,8,128]{2,1,0:T(8,128)S(1)}, u32[]{:S(2)}, u32[]{:S(2)}) collective-permute-start(f32[8,8,128]{2,1,0:T(8,128)S(1)} %get-tuple-element.61.p0), channel_id=1, source_target_pairs={{0,64},{32,96},{64,0},{96,32},{1,65},{33,97},{65,1},{97,33},{2,66}... | collective-permute-start | bytes 98312 | tf_op jit(solution)/shard_map/ppermute | solution.py:572
  20.6 0.1 pad_maximum_fusion.1
  20.7 0.1 tile.10
  20.8 1.5 %collective-permute-done.3.r2 = f32[70,8,128]{2,1,0:T(8,128)S(1)} collective-permute-done((f32[70,8,128]{2,1,0:T(8,128)S(1)}, f32[70,8,128]{2,1,0:T(8,128)S(1)}, u32[]{:S(2)}, u32[]{:S(2)}) %collective-permute-start.3) | collective-permute-done | bytes 286752 | tf_op jit(solution)/shard_map/ppermute | solution.py:572
  22.3 6.2 %collective-permute-done.4.r3 = f32[70,8,128]{2,1,0:T(8,128)S(1)} collective-permute-done((f32[70,8,128]{2,1,0:T(8,128)S(1)}, f32[70,8,128]{2,1,0:T(8,128)S(1)}, u32[]{:S(2)}, u32[]{:S(2)}) %collective-permute-start.4) | collective-permute-done | bytes 286752 | tf_op jit(solution)/shard_map/ppermute | solution.py:572
  28.6 0.0 collective-permute-done.5.rest_0_
  28.6 0.0 collective-permute-done.6.rest_1_
  28.6 0.0 collective-permute-done.7.rest_2_
  28.6 1.8 %unpack.1 = (f32[4,16,32,128]{3,2,1,0:T(8,128)S(1)}, f32[4,32,128]{2,1,0:T(8,128)S(1)}, f32[213,8,128]{2,1,0:T(8,128)S(1)}, f32[213,8,128]{2,1,0:T(8,128)S(1)}, ...) custom-call(s32[135]{0:T(256)S(1)} %concatenate.3.scal.ints, ...), custom_call_target="tpu_custom_call" | custom-call | flops 2000000000 | bytes 4000000 | tf_op jit(solution)/shard_map/unpack/pallas_call | solution.py:604
  30.4 0.4 collective-permute-start.8
  30.8 0.9 collective-permute-done.8
  31.6 3.1 %collective-permute-start.13 = (f32[213,8,128]{2,1,0:T(8,128)S(1)}, f32[213,8,128]{2,1,0:T(8,128)S(1)}, u32[]{:S(2)}, u32[]{:S(2)}) collective-permute-start(f32[213,8,128]{2,1,0:T(8,128)S(1)} %get-tuple-element.71), channel_id=1, source_target_pairs={{0,8},{8,16},{16,24},{24,25},{25,17},{17,9},{9,1},{1,2},{2,10},{10... | collective-permute-start | bytes 2617352 | tf_op jit(solution)/shard_map/ppermute | solution.py:651
  34.7 0.0 collective-permute-start.14
  34.7 0.4 collective-permute-start.9
  35.1 19.7 %collective-permute-done.9 = f32[8,128]{1,0:T(8,128)S(1)} collective-permute-done((f32[8,128]{1,0:T(8,128)S(1)}, f32[8,128]{1,0:T(8,128)S(1)}, u32[]{:S(2)}, u32[]{:S(2)}) %collective-permute-start.9) | collective-permute-done | bytes 4128 | tf_op jit(solution)/shard_map/ppermute | solution.py:572
  54.9 0.0 collective-permute-start.10
  54.9 5.0 %collective-permute-start.11 = (f32[8,128]{1,0:T(8,128)S(1)}, f32[8,128]{1,0:T(8,128)S(1)}, u32[]{:S(2)}, u32[]{:S(2)}) collective-permute-start(f32[8,128]{1,0:T(8,128)S(1)} %add.77), channel_id=1, source_target_pairs={{0,2},{1,3},{2,0},{3,1},{4,6},{5,7},{6,4},{7,5},{8,10},{9,11},{10,... | collective-permute-start | bytes 12296 | tf_op jit(solution)/shard_map/ppermute | solution.py:572
  59.8 1.6 %maps.1.refs_1_ = f32[4,96,128]{2,1,0:T(8,128)S(1)} custom-call(s32[135]{0:T(256)S(1)} %concatenate.3.scal.ints, f32[3,4,16,128]{3,2,1,0:T(8,128)S(1)} %get-tuple-element.68.ids), custom_call_target="tpu_custom_call" | custom-call | flops 2000000000 | bytes 4000000 | tf_op jit(solution)/shard_map/maps/pallas_call | solution.py:623
  61.5 2.0 %collective-permute-done.12 = f32[8,128]{1,0:T(8,128)S(1)} collective-permute-done((f32[8,128]{1,0:T(8,128)S(1)}, f32[8,128]{1,0:T(8,128)S(1)}, u32[]{:S(2)}, u32[]{:S(2)}) %collective-permute-start.12) | collective-permute-done | bytes 4128 | tf_op jit(solution)/shard_map/ppermute | solution.py:572
  63.5 6.9 %step0.1 = (f32[4,16,48,128]{3,2,1,0:T(8,128)S(1)}, f32[2,64,128]{2,1,0:T(8,128)S(1)}, f32[8,128]{1,0:T(8,128)S(1)}, f32[4,80,128]{2,1,0:T(8,128)S(1)}) custom-call(f32[4,16,32,128]{3,2,1,0:T(8,128)S(1)} %get-tuple-element.67.refs_0_, f32[4,96,128]{2,1,0:T(8,128)S(1)} %maps.1.refs_1_, f32[2,32,128]{2,1,0:T(8,128)S(1)} %get-tuple-element.69.refs_2_, ...), custom_call_target="tpu_custom_call" | custom-call | flops 6000000000 | bytes 4000000 | tf_op jit(solution)/shard_map/step0/pallas_call | solution.py:639
  70.5 3.2 %collective-permute-start.16 = (f32[8,128]{1,0:T(8,128)S(1)}, f32[8,128]{1,0:T(8,128)S(1)}, u32[]{:S(2)}, u32[]{:S(2)}) collective-permute-start(f32[8,128]{1,0:T(8,128)S(1)} %get-tuple-element.82), channel_id=1, source_target_pairs={{0,16},{8,24},{16,0},{24,8},{1,17},{9,25},{17,1},{25,9},{2,18},{10... | collective-permute-start | bytes 12296 | tf_op jit(solution)/shard_map/ppermute | solution.py:572
  73.7 5.0 %step1.1 = (f32[4,16,32,128]{3,2,1,0:T(8,128)S(1)}, f32[2,32,128]{2,1,0:T(8,128)S(1)}, f32[8,128]{1,0:T(8,128)S(1)}, f32[200,8,128]{2,1,0:T(8,128)S(1)}, f32[200,8,128]{2,1,0:T(8,128)S(1)}) custom-call(f32[4,16,48,128]{3,2,1,0:T(8,128)S(1)} %get-tuple-element.75.refs_0_, f32[4,96,128]{2,1,0:T(8,128)S(1)} %maps.1.refs_1_, ...), custom_call_target="tpu_custom_call" | custom-call | flops 6000000000 | bytes 4000000 | tf_op jit(solution)/shard_map/step1/pallas_call | solution.py:639
  78.7 0.1 add_select_fusion
  78.8 0.0 collective-permute-start.17
  78.8 1.2 collective-permute-done.17
  80.0 0.1 collective-permute-start.22
  80.1 0.4 collective-permute-start.23
  80.5 1.1 collective-permute-start.18
  81.6 18.2 %collective-permute-done.18 = f32[8,128]{1,0:T(8,128)S(1)} collective-permute-done((f32[8,128]{1,0:T(8,128)S(1)}, f32[8,128]{1,0:T(8,128)S(1)}, u32[]{:S(2)}, u32[]{:S(2)}) %collective-permute-start.18) | collective-permute-done | bytes 4128 | tf_op jit(solution)/shard_map/ppermute | solution.py:572
  99.8 5.1 %collective-permute-start.20 = (f32[8,128]{1,0:T(8,128)S(1)}, f32[8,128]{1,0:T(8,128)S(1)}, u32[]{:S(2)}, u32[]{:S(2)}) collective-permute-start(f32[8,128]{1,0:T(8,128)S(1)} %add.84), channel_id=1, source_target_pairs={{0,2},{1,3},{2,0},{3,1},{4,6},{5,7},{6,4},{7,5},{8,10},{9,11},{10,... | collective-permute-start | bytes 12296 | tf_op jit(solution)/shard_map/ppermute | solution.py:572
  104.9 1.0 collective-permute-done.20
  105.9 2.6 %collective-permute-done.21 = f32[8,128]{1,0:T(8,128)S(1)} collective-permute-done((f32[8,128]{1,0:T(8,128)S(1)}, f32[8,128]{1,0:T(8,128)S(1)}, u32[]{:S(2)}, u32[]{:S(2)}) %collective-permute-start.21) | collective-permute-done | bytes 4128 | tf_op jit(solution)/shard_map/ppermute | solution.py:572
  108.6 7.6 %step2.1 = (f32[4,16,48,128]{3,2,1,0:T(8,128)S(1)}, f32[2,64,128]{2,1,0:T(8,128)S(1)}, f32[8,128]{1,0:T(8,128)S(1)}) custom-call(f32[4,16,32,128]{3,2,1,0:T(8,128)S(1)} %get-tuple-element.89.refs_0_, f32[4,96,128]{2,1,0:T(8,128)S(1)} %maps.1.refs_1_, f32[2,32,128]{2,1,0:T(8,128)S(1)} %get-tuple-element.90.refs_2_, ...), custom_call_target="tpu_custom_call" | custom-call | flops 6000000000 | bytes 4000000 | tf_op jit(solution)/shard_map/step2/pallas_call | solution.py:639
  116.2 3.2 %collective-permute-start.25 = (f32[8,128]{1,0:T(8,128)S(1)}, f32[8,128]{1,0:T(8,128)S(1)}, u32[]{:S(2)}, u32[]{:S(2)}) collective-permute-start(f32[8,128]{1,0:T(8,128)S(1)} %get-tuple-element.94), channel_id=1, source_target_pairs={{0,16},{8,24},{16,0},{24,8},{1,17},{9,25},{17,1},{25,9},{2,18},{10... | collective-permute-start | bytes 12296 | tf_op jit(solution)/shard_map/ppermute | solution.py:572
  119.5 4.9 %step3.1.fields = f32[4,16,32,128]{3,2,1,0:T(8,128)S(1)} custom-call(f32[4,16,48,128]{3,2,1,0:T(8,128)S(1)} %get-tuple-element.96.refs_0_, f32[4,96,128]{2,1,0:T(8,128)S(1)} %maps.1.refs_1_, f32[2,64,128]{2,1,0:T(8,128)S(1)} %get-tuple-element.97.refs_2_, f32[4,80,128]{2,1,0:T(8,128)S(1)} %get-tuple-element.77.refs_3_, f32[8,128]{1,0:T(8,128)S(1)} %add.88.refs_4_), custom_call_target="tpu_custom_call" | custom-call | flops 6000000000 | bytes 4000000 | tf_op jit(solution)/shard_map/step3/pallas_call | solution.py:639
  124.4 2.3 %send.1 = (f32[64,8,128]{2,1,0:T(8,128)S(1)}, f32[64,8,128]{2,1,0:T(8,128)S(1)}, f32[64,8,128]{2,1,0:T(8,128)S(1)}, f32[64,8,128]{2,1,0:T(8,128)S(1)}) custom-call(s32[135]{0:T(256)S(1)} %concatenate.3.scal.ints, f32[4,16,32,128]{3,2,1,0:T(8,128)S(1)} %step3.1.fields), custom_call_target="tpu_custom_call" | custom-call | flops 2000000000 | bytes 4000000 | tf_op jit(solution)/shard_map/send/pallas_call | solution.py:676
  126.6 0.1 collective-permute-start.31
  126.7 0.1 collective-permute-start.32
  126.9 3.5 %collective-permute-start.33 = (f32[64,8,128]{2,1,0:T(8,128)S(1)}, f32[64,8,128]{2,1,0:T(8,128)S(1)}, u32[]{:S(2)}, u32[]{:S(2)}) collective-permute-start(f32[64,8,128]{2,1,0:T(8,128)S(1)} %get-tuple-element.104), channel_id=1, source_target_pairs={{0,24},{8,16},{16,8},{24,0},{1,25},{9,17},{17,9},{25,1},{2,26},{10... | collective-permute-start | bytes 786440 | tf_op jit(solution)/shard_map/ppermute | solution.py:572
  130.4 1.2 collective-permute-done.26
  131.5 1.4 collective-permute-start.28
  133.0 1.3 collective-permute-done.27
  134.3 1.1 collective-permute-start.29
  135.4 0.4 collective-permute-done.28
  135.8 2.5 %collective-permute-done.29 = f32[8,128]{1,0:T(8,128)S(1)} collective-permute-done((f32[8,128]{1,0:T(8,128)S(1)}, f32[8,128]{1,0:T(8,128)S(1)}, u32[]{:S(2)}, u32[]{:S(2)}) %collective-permute-start.29) | collective-permute-done | bytes 4128 | tf_op jit(solution)/shard_map/ppermute | solution.py:572
  138.3 0.5 collective-permute-start.30
  138.7 2.3 %collective-permute-done.30 = f32[8,128]{1,0:T(8,128)S(1)} collective-permute-done((f32[8,128]{1,0:T(8,128)S(1)}, f32[8,128]{1,0:T(8,128)S(1)}, u32[]{:S(2)}, u32[]{:S(2)}) %collective-permute-start.30) | collective-permute-done | bytes 4128 | tf_op jit(solution)/shard_map/ppermute | solution.py:572
  141.0 1.0 collective-permute-done.33.r3
  142.0 3.1 %final.1 = f32[4,16,32,128]{3,2,1,0:T(8,128)} custom-call(s32[135]{0:T(256)S(1)} %concatenate.3.scal.ints, f32[8,128]{1,0:T(8,128)S(1)} %add.94.mean, f32[64,8,128]{2,1,0:T(8,128)S(1)} %get-tuple-element.101.s0, f32[64,8,128]{2,1,0:T(8,128)S(1)} %collective-permute-done.31.r1, f32[64,8,128]{2,1,0:T(8,128)S(1)} %collective-permute-done.32.r2, ...), custom_call_target="tpu_custom_call" | custom-call | flops 2000000000 | bytes 4000000 | tf_op jit(solution)/shard_map/final/pallas_call | solution.py:684
  (42 shorter events, 0.1 us)
Async XLA Ops:
  0.9 5.4 %collective-permute-start = (f32[16,128]{1,0:T(8,128)S(1)}, f32[16,128]{1,0:T(8,128)S(1)}, u32[]{:S(2)}, u32[]{:S(2)}) collective-permute-start(f32[16,128]{1,0:T(8,128)S(1)} %get-tuple-element.106), channel_id=1, source_target_pairs={{0,1},{1,2},{2,3},{3,4},{4,5},{5,6},{6,7},{7,0},{8,9},{9,10},{10,1... | collective-permute-start | bytes 24584 | tf_op jit(solution)/shard_map/ppermute | solution.py:591
  2.9 3.3 %collective-permute-start.1 = (f32[16,128]{1,0:T(8,128)S(1)}, f32[16,128]{1,0:T(8,128)S(1)}, u32[]{:S(2)}, u32[]{:S(2)}) collective-permute-start(f32[16,128]{1,0:T(8,128)S(1)} %get-tuple-element.106), channel_id=1, source_target_pairs={{1,0},{2,1},{3,2},{4,3},{5,4},{6,5},{7,6},{0,7},{9,8},{10,9},{11,1... | collective-permute-start | bytes 24584 | tf_op jit(solution)/shard_map/ppermute | solution.py:591
  6.2 1.2 copy-start
  7.4 0.9 copy-start.1
  10.3 5.2 %collective-permute-start.2 = (f32[70,8,128]{2,1,0:T(8,128)S(1)}, f32[70,8,128]{2,1,0:T(8,128)S(1)}, u32[]{:S(2)}, u32[]{:S(2)}) collective-permute-start(f32[70,8,128]{2,1,0:T(8,128)S(1)} %get-tuple-element.56), channel_id=1, source_target_pairs={{0,8},{8,0},{16,24},{24,16},{1,9},{9,1},{17,25},{25,17},{2,10},{10... | collective-permute-start | bytes 860168 | tf_op jit(solution)/shard_map/ppermute | solution.py:572
  12.3 10.0 %collective-permute-start.3 = (f32[70,8,128]{2,1,0:T(8,128)S(1)}, f32[70,8,128]{2,1,0:T(8,128)S(1)}, u32[]{:S(2)}, u32[]{:S(2)}) collective-permute-start(f32[70,8,128]{2,1,0:T(8,128)S(1)} %get-tuple-element.59), channel_id=1, source_target_pairs={{0,16},{8,24},{16,0},{24,8},{1,17},{9,25},{17,1},{25,9},{2,18},{10... | collective-permute-start | bytes 860168 | tf_op jit(solution)/shard_map/ppermute | solution.py:572
  15.3 13.2 %collective-permute-start.4 = (f32[70,8,128]{2,1,0:T(8,128)S(1)}, f32[70,8,128]{2,1,0:T(8,128)S(1)}, u32[]{:S(2)}, u32[]{:S(2)}) collective-permute-start(f32[70,8,128]{2,1,0:T(8,128)S(1)} %get-tuple-element.60), channel_id=1, source_target_pairs={{0,24},{8,16},{16,8},{24,0},{1,25},{9,17},{17,9},{25,1},{2,26},{10... | collective-permute-start | bytes 860168 | tf_op jit(solution)/shard_map/ppermute | solution.py:572
  15.5 13.1 %collective-permute-start.5 = (f32[8,8,128]{2,1,0:T(8,128)S(1)}, f32[8,8,128]{2,1,0:T(8,128)S(1)}, u32[]{:S(2)}, u32[]{:S(2)}) collective-permute-start(f32[8,8,128]{2,1,0:T(8,128)S(1)} %get-tuple-element.61.p0), channel_id=1, source_target_pairs={{0,32},{32,0},{64,96},{96,64},{1,33},{33,1},{65,97},{97,65},{2,34}... | collective-permute-start | bytes 98312 | tf_op jit(solution)/shard_map/ppermute | solution.py:572
  17.3 11.3 %collective-permute-start.6 = (f32[8,8,128]{2,1,0:T(8,128)S(1)}, f32[8,8,128]{2,1,0:T(8,128)S(1)}, u32[]{:S(2)}, u32[]{:S(2)}) collective-permute-start(f32[8,8,128]{2,1,0:T(8,128)S(1)} %get-tuple-element.61.p0), channel_id=1, source_target_pairs={{0,64},{32,96},{64,0},{96,32},{1,65},{33,97},{65,1},{97,33},{2,66}... | collective-permute-start | bytes 98312 | tf_op jit(solution)/shard_map/ppermute | solution.py:572
  20.6 8.0 %collective-permute-start.7 = (f32[8,8,128]{2,1,0:T(8,128)S(1)}, f32[8,8,128]{2,1,0:T(8,128)S(1)}, u32[]{:S(2)}, u32[]{:S(2)}) collective-permute-start(f32[8,8,128]{2,1,0:T(8,128)S(1)} %get-tuple-element.61.p0), channel_id=1, source_target_pairs={{0,96},{32,64},{64,32},{96,0},{1,97},{33,65},{65,33},{97,1},{2,98}... | collective-permute-start | bytes 98312 | tf_op jit(solution)/shard_map/ppermute | solution.py:572
  30.4 1.2 collective-permute-start.8
  31.6 31.9 %collective-permute-start.13 = (f32[213,8,128]{2,1,0:T(8,128)S(1)}, f32[213,8,128]{2,1,0:T(8,128)S(1)}, u32[]{:S(2)}, u32[]{:S(2)}) collective-permute-start(f32[213,8,128]{2,1,0:T(8,128)S(1)} %get-tuple-element.71), channel_id=1, source_target_pairs={{0,8},{8,16},{16,24},{24,25},{25,17},{17,9},{9,1},{1,2},{2,10},{10... | collective-permute-start | bytes 2617352 | tf_op jit(solution)/shard_map/ppermute | solution.py:651
  34.7 28.8 %collective-permute-start.14 = (f32[213,8,128]{2,1,0:T(8,128)S(1)}, f32[213,8,128]{2,1,0:T(8,128)S(1)}, u32[]{:S(2)}, u32[]{:S(2)}) collective-permute-start(f32[213,8,128]{2,1,0:T(8,128)S(1)} %get-tuple-element.72), channel_id=1, source_target_pairs={{8,0},{16,8},{24,16},{25,24},{17,25},{9,17},{1,9},{2,1},{10,2},{18... | collective-permute-start | bytes 2617352 | tf_op jit(solution)/shard_map/ppermute | solution.py:652
  34.7 20.1 %collective-permute-start.9 = (f32[8,128]{1,0:T(8,128)S(1)}, f32[8,128]{1,0:T(8,128)S(1)}, u32[]{:S(2)}, u32[]{:S(2)}) collective-permute-start(f32[8,128]{1,0:T(8,128)S(1)} %add.76), channel_id=1, source_target_pairs={{0,4},{1,5},{2,6},{3,7},{4,0},{5,1},{6,2},{7,3},{8,12},{9,13},{10,... | collective-permute-start | bytes 12296 | tf_op jit(solution)/shard_map/ppermute | solution.py:572
  54.9 6.6 %collective-permute-start.10 = (f32[8,128]{1,0:T(8,128)S(1)}, f32[8,128]{1,0:T(8,128)S(1)}, u32[]{:S(2)}, u32[]{:S(2)}) collective-permute-start(f32[8,128]{1,0:T(8,128)S(1)} %add.77), channel_id=1, source_target_pairs={{0,1},{1,0},{2,3},{3,2},{4,5},{5,4},{6,7},{7,6},{8,9},{9,8},{10,11... | collective-permute-start | bytes 12296 | tf_op jit(solution)/shard_map/ppermute | solution.py:572
  54.9 6.6 %collective-permute-start.11 = (f32[8,128]{1,0:T(8,128)S(1)}, f32[8,128]{1,0:T(8,128)S(1)}, u32[]{:S(2)}, u32[]{:S(2)}) collective-permute-start(f32[8,128]{1,0:T(8,128)S(1)} %add.77), channel_id=1, source_target_pairs={{0,2},{1,3},{2,0},{3,1},{4,6},{5,7},{6,4},{7,5},{8,10},{9,11},{10,... | collective-permute-start | bytes 12296 | tf_op jit(solution)/shard_map/ppermute | solution.py:572
  59.8 3.7 %collective-permute-start.12 = (f32[8,128]{1,0:T(8,128)S(1)}, f32[8,128]{1,0:T(8,128)S(1)}, u32[]{:S(2)}, u32[]{:S(2)}) collective-permute-start(f32[8,128]{1,0:T(8,128)S(1)} %add.77), channel_id=1, source_target_pairs={{0,3},{1,2},{2,1},{3,0},{4,7},{5,6},{6,5},{7,4},{8,11},{9,10},{10,... | collective-permute-start | bytes 12296 | tf_op jit(solution)/shard_map/ppermute | solution.py:572
  63.5 7.0 %collective-permute-start.15 = (f32[8,128]{1,0:T(8,128)S(1)}, f32[8,128]{1,0:T(8,128)S(1)}, u32[]{:S(2)}, u32[]{:S(2)}) collective-permute-start(f32[8,128]{1,0:T(8,128)S(1)} %add_add_fusion.2), channel_id=1, source_target_pairs={{0,16},{8,24},{16,0},{24,8},{1,17},{9,25},{17,1},{25,9},{2,18},{10... | collective-permute-start | bytes 12296 | tf_op jit(solution)/shard_map/ppermute | solution.py:572
  70.5 8.2 %collective-permute-start.16 = (f32[8,128]{1,0:T(8,128)S(1)}, f32[8,128]{1,0:T(8,128)S(1)}, u32[]{:S(2)}, u32[]{:S(2)}) collective-permute-start(f32[8,128]{1,0:T(8,128)S(1)} %get-tuple-element.82), channel_id=1, source_target_pairs={{0,16},{8,24},{16,0},{24,8},{1,17},{9,25},{17,1},{25,9},{2,18},{10... | collective-permute-start | bytes 12296 | tf_op jit(solution)/shard_map/ppermute | solution.py:572
  78.8 1.2 collective-permute-start.17
  80.0 28.6 %collective-permute-start.22 = (f32[200,8,128]{2,1,0:T(8,128)S(1)}, f32[200,8,128]{2,1,0:T(8,128)S(1)}, u32[]{:S(2)}, u32[]{:S(2)}) collective-permute-start(f32[200,8,128]{2,1,0:T(8,128)S(1)} %get-tuple-element.91), channel_id=1, source_target_pairs={{0,8},{8,16},{16,24},{24,25},{25,17},{17,9},{9,1},{1,2},{2,10},{10... | collective-permute-start | bytes 2457608 | tf_op jit(solution)/shard_map/ppermute | solution.py:651
  80.1 28.5 %collective-permute-start.23 = (f32[200,8,128]{2,1,0:T(8,128)S(1)}, f32[200,8,128]{2,1,0:T(8,128)S(1)}, u32[]{:S(2)}, u32[]{:S(2)}) collective-permute-start(f32[200,8,128]{2,1,0:T(8,128)S(1)} %get-tuple-element.92), channel_id=1, source_target_pairs={{8,0},{16,8},{24,16},{25,24},{17,25},{9,17},{1,9},{2,1},{10,2},{18... | collective-permute-start | bytes 2457608 | tf_op jit(solution)/shard_map/ppermute | solution.py:652
  80.5 19.3 %collective-permute-start.18 = (f32[8,128]{1,0:T(8,128)S(1)}, f32[8,128]{1,0:T(8,128)S(1)}, u32[]{:S(2)}, u32[]{:S(2)}) collective-permute-start(f32[8,128]{1,0:T(8,128)S(1)} %add.83), channel_id=1, source_target_pairs={{0,4},{1,5},{2,6},{3,7},{4,0},{5,1},{6,2},{7,3},{8,12},{9,13},{10,... | collective-permute-start | bytes 12296 | tf_op jit(solution)/shard_map/ppermute | solution.py:572
  99.8 5.1 %collective-permute-start.19 = (f32[8,128]{1,0:T(8,128)S(1)}, f32[8,128]{1,0:T(8,128)S(1)}, u32[]{:S(2)}, u32[]{:S(2)}) collective-permute-start(f32[8,128]{1,0:T(8,128)S(1)} %add.84), channel_id=1, source_target_pairs={{0,1},{1,0},{2,3},{3,2},{4,5},{5,4},{6,7},{7,6},{8,9},{9,8},{10,11... | collective-permute-start | bytes 12296 | tf_op jit(solution)/shard_map/ppermute | solution.py:572
  99.8 6.1 %collective-permute-start.20 = (f32[8,128]{1,0:T(8,128)S(1)}, f32[8,128]{1,0:T(8,128)S(1)}, u32[]{:S(2)}, u32[]{:S(2)}) collective-permute-start(f32[8,128]{1,0:T(8,128)S(1)} %add.84), channel_id=1, source_target_pairs={{0,2},{1,3},{2,0},{3,1},{4,6},{5,7},{6,4},{7,5},{8,10},{9,11},{10,... | collective-permute-start | bytes 12296 | tf_op jit(solution)/shard_map/ppermute | solution.py:572
  104.9 3.7 %collective-permute-start.21 = (f32[8,128]{1,0:T(8,128)S(1)}, f32[8,128]{1,0:T(8,128)S(1)}, u32[]{:S(2)}, u32[]{:S(2)}) collective-permute-start(f32[8,128]{1,0:T(8,128)S(1)} %add.84), channel_id=1, source_target_pairs={{0,3},{1,2},{2,1},{3,0},{4,7},{5,6},{6,5},{7,4},{8,11},{9,10},{10,... | collective-permute-start | bytes 12296 | tf_op jit(solution)/shard_map/ppermute | solution.py:572
  108.6 7.6 %collective-permute-start.24 = (f32[8,128]{1,0:T(8,128)S(1)}, f32[8,128]{1,0:T(8,128)S(1)}, u32[]{:S(2)}, u32[]{:S(2)}) collective-permute-start(f32[8,128]{1,0:T(8,128)S(1)} %add_add_fusion.1.refs_6_), channel_id=1, source_target_pairs={{0,16},{8,24},{16,0},{24,8},{1,17},{9,25},{17,1},{25,9},{2,18},{10... | collective-permute-start | bytes 12296 | tf_op jit(solution)/shard_map/ppermute | solution.py:572
  116.2 8.2 %collective-permute-start.25 = (f32[8,128]{1,0:T(8,128)S(1)}, f32[8,128]{1,0:T(8,128)S(1)}, u32[]{:S(2)}, u32[]{:S(2)}) collective-permute-start(f32[8,128]{1,0:T(8,128)S(1)} %get-tuple-element.94), channel_id=1, source_target_pairs={{0,16},{8,24},{16,0},{24,8},{1,17},{9,25},{17,1},{25,9},{2,18},{10... | collective-permute-start | bytes 12296 | tf_op jit(solution)/shard_map/ppermute | solution.py:572
  126.6 14.4 %collective-permute-start.31 = (f32[64,8,128]{2,1,0:T(8,128)S(1)}, f32[64,8,128]{2,1,0:T(8,128)S(1)}, u32[]{:S(2)}, u32[]{:S(2)}) collective-permute-start(f32[64,8,128]{2,1,0:T(8,128)S(1)} %get-tuple-element.102), channel_id=1, source_target_pairs={{0,8},{8,0},{16,24},{24,16},{1,9},{9,1},{17,25},{25,17},{2,10},{10... | collective-permute-start | bytes 786440 | tf_op jit(solution)/shard_map/ppermute | solution.py:572
  126.7 14.3 %collective-permute-start.32 = (f32[64,8,128]{2,1,0:T(8,128)S(1)}, f32[64,8,128]{2,1,0:T(8,128)S(1)}, u32[]{:S(2)}, u32[]{:S(2)}) collective-permute-start(f32[64,8,128]{2,1,0:T(8,128)S(1)} %get-tuple-element.103), channel_id=1, source_target_pairs={{0,16},{8,24},{16,0},{24,8},{1,17},{9,25},{17,1},{25,9},{2,18},{10... | collective-permute-start | bytes 786440 | tf_op jit(solution)/shard_map/ppermute | solution.py:572
  126.9 15.1 %collective-permute-start.33 = (f32[64,8,128]{2,1,0:T(8,128)S(1)}, f32[64,8,128]{2,1,0:T(8,128)S(1)}, u32[]{:S(2)}, u32[]{:S(2)}) collective-permute-start(f32[64,8,128]{2,1,0:T(8,128)S(1)} %get-tuple-element.104), channel_id=1, source_target_pairs={{0,24},{8,16},{16,8},{24,0},{1,25},{9,17},{17,9},{25,1},{2,26},{10... | collective-permute-start | bytes 786440 | tf_op jit(solution)/shard_map/ppermute | solution.py:572
  130.4 1.2 collective-permute-start.26
  131.5 2.8 %collective-permute-start.27 = (f32[8,128]{1,0:T(8,128)S(1)}, f32[8,128]{1,0:T(8,128)S(1)}, u32[]{:S(2)}, u32[]{:S(2)}) collective-permute-start(f32[8,128]{1,0:T(8,128)S(1)} %add.90), channel_id=1, source_target_pairs={{0,1},{1,0},{2,3},{3,2},{4,5},{5,4},{6,7},{7,6},{8,9},{9,8},{10,11... | collective-permute-start | bytes 12296 | tf_op jit(solution)/shard_map/ppermute | solution.py:572
  131.5 4.3 %collective-permute-start.28 = (f32[8,128]{1,0:T(8,128)S(1)}, f32[8,128]{1,0:T(8,128)S(1)}, u32[]{:S(2)}, u32[]{:S(2)}) collective-permute-start(f32[8,128]{1,0:T(8,128)S(1)} %add.90), channel_id=1, source_target_pairs={{0,2},{1,3},{2,0},{3,1},{4,6},{5,7},{6,4},{7,5},{8,10},{9,11},{10,... | collective-permute-start | bytes 12296 | tf_op jit(solution)/shard_map/ppermute | solution.py:572
  134.3 4.0 %collective-permute-start.29 = (f32[8,128]{1,0:T(8,128)S(1)}, f32[8,128]{1,0:T(8,128)S(1)}, u32[]{:S(2)}, u32[]{:S(2)}) collective-permute-start(f32[8,128]{1,0:T(8,128)S(1)} %add.90), channel_id=1, source_target_pairs={{0,3},{1,2},{2,1},{3,0},{4,7},{5,6},{6,5},{7,4},{8,11},{9,10},{10,... | collective-permute-start | bytes 12296 | tf_op jit(solution)/shard_map/ppermute | solution.py:572
  138.3 2.8 %collective-permute-start.30 = (f32[8,128]{1,0:T(8,128)S(1)}, f32[8,128]{1,0:T(8,128)S(1)}, u32[]{:S(2)}, u32[]{:S(2)}) collective-permute-start(f32[8,128]{1,0:T(8,128)S(1)} %add_add_fusion), channel_id=1, source_target_pairs={{0,4},{1,5},{2,6},{3,7},{4,0},{5,1},{6,2},{7,3},{8,12},{9,13},{10,... | collective-permute-start | bytes 12296 | tf_op jit(solution)/shard_map/ppermute | solution.py:572

commit v6 on v4

--- a/solution.py
+++ b/solution.py
@@ -39,6 +39,7 @@
 
 VMEM = pl.BlockSpec(memory_space=pltpu.VMEM)
 SMEM = pl.BlockSpec(memory_space=pltpu.SMEM)
+HBM = pl.BlockSpec(memory_space=pltpu.HBM)
 
 
 def shape(*dims):
@@ -120,26 +121,40 @@
     return out
 
 
-def pack_kernel(scal, state, planes, ids, s0, s1, s2, s3, pl_out):
+def pack_kernel(
+    scal, state, planes_in, ids, s0, s1, s2, s3, pl_out, sums, tile, planes, state_sems, plane_sem
+):
     slab = scal[1]
     group = lanes() >> 5
     masks = [group == c for c in range(4)]
-
-    def per_row(x, carry):
-        for kt in range(4):
-            sources = [state[c, x, kt * 8 : kt * 8 + 8, :] for c in range(4)]
-            for s, out in enumerate((s0, s1, s2, s3)):
-                out[x * 4 + kt] = block_transposed(sources, slab ^ s, masks)
-        return carry
-
-    rows("fill", per_row)
+    copies = []
+    for part in range(4):
+        here = pl.ds(part * 4, 4)
+        copies.append(
+            pltpu.make_async_copy(state.at[:, here], tile.at[:, here], state_sems.at[part])
+        )
+        copies[-1].start()
+    plane_copy = pltpu.make_async_copy(planes_in, planes, plane_sem)
+    plane_copy.start()
     for half in range(6):
         for out in (s0, s1, s2, s3):
             out[TILES + half] = ids[half // 2, (half % 2) * 8 : (half % 2) * 8 + 8]
+    total = jnp.zeros((NZ, LANES), F32)
+    for part in range(4):
+        copies[part].wait()
+        for x in range(part * 4, part * 4 + 4):
+            total = total + tile[3, x]
+            for kt in range(4):
+                sources = [tile[c, x, kt * 8 : kt * 8 + 8, :] for c in range(4)]
+                for s, out in enumerate((s0, s1, s2, s3)):
+                    out[x * 4 + kt] = block_transposed(sources, slab ^ s, masks)
+    plane_copy.wait()
     for plane in range(planes.shape[0]):
         for kt in range(4):
             sources = [planes[plane, c, kt * 8 : kt * 8 + 8, :] for c in range(4)]
             pl_out[plane * 4 + kt] = block_transposed(sources, slab, masks)
+    levels = jnp.concatenate([total] * GX, axis=0).T
+    sums[...] = jnp.broadcast_to(jnp.sum(levels, axis=0, keepdims=True), (8, LANES))
 
 
 def maps_kernel(ints, ids, maps):
@@ -190,7 +205,7 @@
     scal, profile, s0, r1, r2, r3, p0, *rest, layouts, per_layout
 ):
     plane_refs = (p0,) + rest[: layouts - 1]
-    fields, inflow, su, sd, bands, sums, ids, held, planes = rest[layouts - 1 :]
+    fields, inflow, su, sd, bands, ids, held, planes = rest[layouts - 1 :]
     own, here = scal[0], scal[2]
     for s, source in enumerate((s0, r1, r2, r3)):
         held[own ^ s] = source[:TILES]
@@ -199,7 +214,7 @@
     for s, source in enumerate(plane_refs):
         planes[here ^ s] = source[...]
 
-    def per_row(xi, total):
+    def per_row(xi, carry):
         parts = [held[g, pl.ds(xi * 4, 4)].reshape(NZ, LANES) for g in range(GX)]
         turned = jnp.concatenate(parts, axis=0).T
         for c in range(4):
@@ -207,12 +222,9 @@
             fields[c, xi] = value
             sd[c * XI + xi] = value[:HALO]
             su[c * XI + xi] = value[OWN - HALO :]
-            if c == 3:
-                total = total + jnp.sum(value, axis=0, keepdims=True)
-        return total
-
-    total = rows("fill", per_row, jnp.zeros((1, LANES), F32))
-    sums[...] = jnp.broadcast_to(over_groups(total), (8, LANES))
+        return carry
+
+    rows("fill", per_row)
     parts = []
     for step in range(STEPS):
         plane = scal[3 + step]
@@ -487,12 +499,12 @@
 
     def per_row(xi, carry):
         stacked = jnp.concatenate([fields[c, xi] for c in range(4)], axis=0)
-        turned[...] = stacked.T.reshape(GX, 4, 8, LANES)
+        turned[xi] = stacked.T.reshape(GX, 4, 8, LANES)
         for s, out in enumerate((s0, s1, s2, s3)):
-            out[pl.ds(xi * 4, 4)] = turned[own ^ s]
+            out[pl.ds(xi * 4, 4)] = turned[xi, own ^ s]
         return carry
 
-    lax.fori_loop(0, XI, per_row, 0)
+    rows("fill", per_row)
 
 
 def final_kernel(scal, mean, s0, r1, r2, r3, out, columns, *, cells):
@@ -550,18 +562,35 @@
     ids = turbine_cell[0, :, NZ // 2, :].astype(F32)
     ids = jnp.stack([ids, lax.ppermute(ids, "gy", gy_up), lax.ppermute(ids, "gy", gy_down)])
     chunk = shape(TILES + 6, 8, LANES)
-    s0, s1, s2, s3, plane = call(
+    s0, s1, s2, s3, plane, sums = call(
         pack_kernel,
-        (chunk, chunk, chunk, chunk, shape(per_layout * 4, 8, LANES)),
-        [SMEM, VMEM, VMEM, VMEM],
+        (chunk, chunk, chunk, chunk, shape(per_layout * 4, 8, LANES), shape(8, LANES)),
+        [SMEM, HBM, HBM, VMEM],
+        [
+            pltpu.VMEM((4, XI, NZ, LANES), F32),
+            pltpu.VMEM((per_layout, 4, NZ, LANES), F32),
+            pltpu.SemaphoreType.DMA((4,)),
+            pltpu.SemaphoreType.DMA,
+        ],
         name="pack",
     )(scal, state[0], planes, ids)
     received = [swapped(value, "gx", GX, s) for s, value in ((1, s1), (2, s2), (3, s3))]
-    received[0], plane = lax.optimization_barrier((received[0], plane))
+    received[0], plane, sums = lax.optimization_barrier((received[0], plane, sums))
     plane_received = [swapped(plane, "layout", layouts, s) for s in range(1, layouts)]
 
+    half = groups // 2
+
+    def last_round(value):
+        return sum([swapped(value, "gy", groups, d) for d in range(1, half)], value)
+
+    partial = last_round(sums + swapped(sums, "gx", GX, 1))
+    partial = partial + swapped(partial, "gy", groups, half)
+    s0, partial = lax.optimization_barrier((s0, partial))
+    arriving = swapped(partial, "gx", GX, 2)
+    partial = partial + cells * profile[3:4]
+
     first_payload = shape(TILES + MORE + 4, 8, LANES)
-    fields, inflow, su, sd, bands, sums, ids = call(
+    fields, inflow, su, sd, bands, ids = call(
         functools.partial(unpack_kernel, layouts=layouts, per_layout=per_layout),
         (
             shape(4, XI, OWN, LANES),
@@ -569,7 +598,6 @@
             first_payload,
             first_payload,
             shape(2, OWN, LANES),
-            shape(8, LANES),
             shape(3, GX, XI, LANES),
         ),
         [SMEM, VMEM] + [VMEM] * (4 + layouts),
@@ -582,22 +610,18 @@
 
     maps = call(maps_kernel, shape(4, 2 * OWN, LANES), [SMEM, VMEM], name="maps")(scal, ids)
 
-    half = groups // 2
-
-    def last_round(value):
-        return sum([swapped(value, "gy", groups, d) for d in range(1, half)], value)
-
     mean = pending = None
     for step in range(STEPS):
-        partial = sums + swapped(sums, "gx", GX, 1)
-        su, sd, partial = lax.optimization_barrier((su, sd, partial))
+        if step > 0:
+            partial = sums + swapped(sums, "gx", GX, 1)
+            su, sd, partial = lax.optimization_barrier((su, sd, partial))
         lo = lax.ppermute(su, ("gx", "gy"), up)
         hi = lax.ppermute(sd, ("gx", "gy"), down)
-        if pending is not None:
-            mean = last_round(pending)
-        partial = partial + swapped(partial, "gy", groups, half)
-        fields, partial = lax.optimization_barrier((fields, partial))
-        arriving = swapped(partial, "gx", GX, 2)
+        if step > 0:
+            mean = last_round(pending) if step > 1 else pending
+            partial = partial + swapped(partial, "gy", groups, half)
+            fields, partial = lax.optimization_barrier((fields, partial))
+            arriving = swapped(partial, "gx", GX, 2)
         outs = [shape(4, XI, OWN, LANES)]
         if step < STEPS - 1:
             payload = shape(TILES + MORE, 8, LANES)
@@ -629,7 +653,7 @@
         send_kernel,
         (chunk, chunk, chunk, chunk),
         [SMEM, VMEM],
-        [pltpu.VMEM((GX, 4, 8, LANES), F32)],
+        [pltpu.VMEM((XI, GX, 4, 8, LANES), F32)],
         name="send",
     )(scal, fields)
     received = [swapped(value, "gx", GX, s) for s, value in ((1, s1), (2, s2), (3, s3))]

time: 128 us -> 135 us (1.055)
  starting transfers between devices: 60.1 us -> 64 us
  waiting for transfers between devices: 34.5 us -> 38.2 us
    ppermute x4, waiting for transfers between devices: 0.01 us -> 4.32 us  [local(): hi = lax.ppermute(sd, ('gx', 'gy'), down)]
    ppermute x4, starting transfers between devices: 8.96 us -> 11.4 us  [local(): lo = lax.ppermute(su, ('gx', 'gy'), up)]
    ppermute x33, waiting for transfers between devices: 34.2 us -> 31.8 us  [swapped(): return lax.ppermute(value, axis, [(i, i ^ distance) for i in range(size)])]
    ppermute x4, waiting for transfers between devices: 0.01 us -> 1.82 us  [local(): lo = lax.ppermute(su, ('gx', 'gy'), up)]
    ppermute x33, starting transfers between devices: 46.7 us -> 48.2 us  [swapped(): return lax.ppermute(value, axis, [(i, i ^ distance) for i in range(size)])]
  transfers between devices with their start and end apart: 43 -> 43, of which waited for: 20 -> 21; matrix products, arithmetic and copies ran while one was open for 1% -> 1% of each run, Pallas kernels for 16% -> 16%
where the time goes in v6:
time: 135 us
  starting transfers between devices  64 us (47%)
  waiting for transfers between devices  38.2 us (28%)
  Pallas kernels  29.3 us (22%)
  local copies, waits for them, and re-layouts  3.13 us (2%)
    ppermute x33, starting transfers between devices, swapped(): return lax.ppermute(value, axis, [(i, i ^ distance) for i in range(size)])  48.2 us
    ppermute x33, waiting for transfers between devices, swapped(): return lax.ppermute(value, axis, [(i, i ^ distance) for i in range(size)])  31.8 us
    pallas_call x4, Pallas kernels, local(): call(functools.partial(step_kernel, step=step, cells=cells), tuple(outs),...  19.3 us
    ppermute x4, starting transfers between devices, local(): lo = lax.ppermute(su, ('gx', 'gy'), up)  11.4 us
    ppermute x4, waiting for transfers between devices, local(): hi = lax.ppermute(sd, ('gx', 'gy'), down)  4.32 us
    pallas_call x1, Pallas kernels, local(): call(functools.partial(final_kernel, cells=cells), shape(4, XI, NZ, LANES...  3.11 us
  transfers between devices with their start and end apart: 43, of which 21 were waited for; matrix products, arithmetic and copies ran while one was open for 1% of the time, Pallas kernels for 16%

profile of v6, /device:TPU:1, one launch (start us, length us, event | category | flops | bytes accessed | tf_op | source)
XLA Modules:
  0.0 135.0 jit_solution(2401439204904816445)
XLA Ops:
  0.0 0.9 slice.7
  0.9 2.0 %collective-permute-start = (f32[16,128]{1,0:T(8,128)S(1)}, f32[16,128]{1,0:T(8,128)S(1)}, u32[]{:S(2)}, u32[]{:S(2)}) collective-permute-start(f32[16,128]{1,0:T(8,128)S(1)} %get-tuple-element.138), channel_id=1, source_target_pairs={{0,1},{1,2},{2,3},{3,4},{4,5},{5,6},{6,7},{7,0},{8,9},{9,10},{10,1... | collective-permute-start | bytes 24584 | tf_op jit(solution)/shard_map/ppermute | solution.py:563
  2.9 2.4 %collective-permute-start.1 = (f32[16,128]{1,0:T(8,128)S(1)}, f32[16,128]{1,0:T(8,128)S(1)}, u32[]{:S(2)}, u32[]{:S(2)}) collective-permute-start(f32[16,128]{1,0:T(8,128)S(1)} %get-tuple-element.138), channel_id=1, source_target_pairs={{1,0},{2,1},{3,2},{4,3},{5,4},{6,5},{7,6},{0,7},{9,8},{10,9},{11,1... | collective-permute-start | bytes 24584 | tf_op jit(solution)/shard_map/ppermute | solution.py:563
  5.3 0.8 concatenate.3.scal.ints
  6.3 1.2 copy-done
  7.5 2.3 %pack.1 = (f32[70,8,128]{2,1,0:T(8,128)S(1)}, f32[70,8,128]{2,1,0:T(8,128)S(1)}, f32[70,8,128]{2,1,0:T(8,128)S(1)}, f32[70,8,128]{2,1,0:T(8,128)S(1)}, f32[8,8,128]{2,1,0:T(8,128)S(1)}, /*index=5*/f32[8,128]{1,0:T(8,128)S(1)}) custom-call(s32[135]{0:T(256)S(1)} %concatenate.3.scal.ints, f32[4,16,32,128]{3,2,1,0:T(8,128)S(1)} %bitcast.14, ...), custom_call_target="tpu_custom_call" | custom-call | flops 2000000000 | bytes 4000000 | tf_op jit(solution)/shard_map/pack/pallas_call | solution.py:565
  9.8 1.9 %collective-permute-start.2 = (f32[70,8,128]{2,1,0:T(8,128)S(1)}, f32[70,8,128]{2,1,0:T(8,128)S(1)}, u32[]{:S(2)}, u32[]{:S(2)}) collective-permute-start(f32[70,8,128]{2,1,0:T(8,128)S(1)} %get-tuple-element.72), channel_id=1, source_target_pairs={{0,8},{8,0},{16,24},{24,16},{1,9},{9,1},{17,25},{25,17},{2,10},{10... | collective-permute-start | bytes 860168 | tf_op jit(solution)/shard_map/ppermute | solution.py:544
  11.7 1.2 collective-permute-done.2.r1
  12.9 0.4 collective-permute-start.3
  13.3 0.8 collective-permute-done.3
  14.1 0.7 collective-permute-start.4
  14.8 4.6 %collective-permute-start.5 = (f32[8,128]{1,0:T(8,128)S(1)}, f32[8,128]{1,0:T(8,128)S(1)}, u32[]{:S(2)}, u32[]{:S(2)}) collective-permute-start(f32[8,128]{1,0:T(8,128)S(1)} %add.102), channel_id=1, source_target_pairs={{0,2},{1,3},{2,0},{3,1},{4,6},{5,7},{6,4},{7,5},{8,10},{9,11},{10,... | collective-permute-start | bytes 12296 | tf_op jit(solution)/shard_map/ppermute | solution.py:544
  19.4 2.6 %collective-permute-start.8 = (f32[70,8,128]{2,1,0:T(8,128)S(1)}, f32[70,8,128]{2,1,0:T(8,128)S(1)}, u32[]{:S(2)}, u32[]{:S(2)}) collective-permute-start(f32[70,8,128]{2,1,0:T(8,128)S(1)} %get-tuple-element.78), channel_id=1, source_target_pairs={{0,16},{8,24},{16,0},{24,8},{1,17},{9,25},{17,1},{25,9},{2,18},{10... | collective-permute-start | bytes 860168 | tf_op jit(solution)/shard_map/ppermute | solution.py:544
  22.0 1.4 %collective-permute-start.9 = (f32[70,8,128]{2,1,0:T(8,128)S(1)}, f32[70,8,128]{2,1,0:T(8,128)S(1)}, u32[]{:S(2)}, u32[]{:S(2)}) collective-permute-start(f32[70,8,128]{2,1,0:T(8,128)S(1)} %get-tuple-element.79), channel_id=1, source_target_pairs={{0,24},{8,16},{16,8},{24,0},{1,25},{9,17},{17,9},{25,1},{2,26},{10... | collective-permute-start | bytes 860168 | tf_op jit(solution)/shard_map/ppermute | solution.py:544
  23.4 0.4 collective-permute-start.7
  23.9 1.7 %collective-permute-start.10 = (f32[8,8,128]{2,1,0:T(8,128)S(1)}, f32[8,8,128]{2,1,0:T(8,128)S(1)}, u32[]{:S(2)}, u32[]{:S(2)}) collective-permute-start(f32[8,8,128]{2,1,0:T(8,128)S(1)} %get-tuple-element.80.p0), channel_id=1, source_target_pairs={{0,32},{32,0},{64,96},{96,64},{1,33},{33,1},{65,97},{97,65},{2,34}... | collective-permute-start | bytes 98312 | tf_op jit(solution)/shard_map/ppermute | solution.py:544
  25.6 3.3 %collective-permute-start.11 = (f32[8,8,128]{2,1,0:T(8,128)S(1)}, f32[8,8,128]{2,1,0:T(8,128)S(1)}, u32[]{:S(2)}, u32[]{:S(2)}) collective-permute-start(f32[8,8,128]{2,1,0:T(8,128)S(1)} %get-tuple-element.80.p0), channel_id=1, source_target_pairs={{0,64},{32,96},{64,0},{96,32},{1,65},{33,97},{65,1},{97,33},{2,66}... | collective-permute-start | bytes 98312 | tf_op jit(solution)/shard_map/ppermute | solution.py:544
  28.9 5.2 %collective-permute-done.7 = f32[8,128]{1,0:T(8,128)S(1)} collective-permute-done((f32[8,128]{1,0:T(8,128)S(1)}, f32[8,128]{1,0:T(8,128)S(1)}, u32[]{:S(2)}, u32[]{:S(2)}) %collective-permute-start.7) | collective-permute-done | bytes 4128 | tf_op jit(solution)/shard_map/ppermute | solution.py:544
  34.1 3.8 %collective-permute-start.12 = (f32[8,8,128]{2,1,0:T(8,128)S(1)}, f32[8,8,128]{2,1,0:T(8,128)S(1)}, u32[]{:S(2)}, u32[]{:S(2)}) collective-permute-start(f32[8,8,128]{2,1,0:T(8,128)S(1)} %get-tuple-element.80.p0), channel_id=1, source_target_pairs={{0,96},{32,64},{64,32},{96,0},{1,97},{33,65},{65,33},{97,1},{2,98}... | collective-permute-start | bytes 98312 | tf_op jit(solution)/shard_map/ppermute | solution.py:544
  38.0 1.1 collective-permute-done.12.rest_2_
  39.1 1.7 %unpack.1 = (f32[4,16,32,128]{3,2,1,0:T(8,128)S(1)}, f32[4,32,128]{2,1,0:T(8,128)S(1)}, f32[72,8,128]{2,1,0:T(8,128)S(1)}, f32[72,8,128]{2,1,0:T(8,128)S(1)}, f3...) custom-call(s32[135]{0:T(256)S(1)} %concatenate.3.scal.ints, f32[8,128]{1,0:T(8,128)S(1)} %pad.4.profile, ...), custom_call_target="tpu_custom_call" | custom-call | flops 2000000000 | bytes 4000000 | tf_op jit(solution)/shard_map/unpack/pallas_call | solution.py:593
  40.9 3.9 %collective-permute-start.13 = (f32[72,8,128]{2,1,0:T(8,128)S(1)}, f32[72,8,128]{2,1,0:T(8,128)S(1)}, u32[]{:S(2)}, u32[]{:S(2)}) collective-permute-start(f32[72,8,128]{2,1,0:T(8,128)S(1)} %get-tuple-element.82), channel_id=1, source_target_pairs={{0,8},{8,16},{16,24},{24,25},{25,17},{17,9},{9,1},{1,2},{2,10},{10... | collective-permute-start | bytes 884744 | tf_op jit(solution)/shard_map/ppermute | solution.py:618
  44.8 0.2 collective-permute-start.15
  45.0 1.6 %maps.1.refs_3_ = f32[4,64,128]{2,1,0:T(8,128)S(1)} custom-call(s32[135]{0:T(256)S(1)} %concatenate.3.scal.ints, f32[3,4,16,128]{3,2,1,0:T(8,128)S(1)} %get-tuple-element.84.ids), custom_call_target="tpu_custom_call" | custom-call | flops 2000000000 | bytes 4000000 | tf_op jit(solution)/shard_map/maps/pallas_call | solution.py:611
  46.6 1.8 %collective-permute-done.13.refs_1_ = f32[72,8,128]{2,1,0:T(8,128)S(1)} collective-permute-done((f32[72,8,128]{2,1,0:T(8,128)S(1)}, f32[72,8,128]{2,1,0:T(8,128)S(1)}, u32[]{:S(2)}, u32[]{:S(2)}) %collective-permute-start.13) | collective-permute-done | bytes 294944 | tf_op jit(solution)/shard_map/ppermute | solution.py:618
  48.4 4.0 %collective-permute-done.14.refs_2_ = f32[72,8,128]{2,1,0:T(8,128)S(1)} collective-permute-done((f32[72,8,128]{2,1,0:T(8,128)S(1)}, f32[72,8,128]{2,1,0:T(8,128)S(1)}, u32[]{:S(2)}, u32[]{:S(2)}) %collective-permute-start.14) | collective-permute-done | bytes 294944 | tf_op jit(solution)/shard_map/ppermute | solution.py:619
  52.4 4.4 %step0.1 = (f32[4,16,32,128]{3,2,1,0:T(8,128)S(1)}, f32[68,8,128]{2,1,0:T(8,128)S(1)}, f32[68,8,128]{2,1,0:T(8,128)S(1)}, f32[2,32,128]{2,1,0:T(8,128)S(1)}, f32...) custom-call(f32[4,16,32,128]{3,2,1,0:T(8,128)S(1)} %get-tuple-element.81.refs_0_, ...), custom_call_target="tpu_custom_call" | custom-call | flops 6000000000 | bytes 4000000 | tf_op jit(solution)/shard_map/step0/pallas_call | solution.py:632
  56.8 0.4 collective-permute-start.16
  57.2 0.9 collective-permute-done.16
  58.1 3.2 %collective-permute-start.18 = (f32[68,8,128]{2,1,0:T(8,128)S(1)}, f32[68,8,128]{2,1,0:T(8,128)S(1)}, u32[]{:S(2)}, u32[]{:S(2)}) collective-permute-start(f32[68,8,128]{2,1,0:T(8,128)S(1)} %get-tuple-element.97), channel_id=1, source_target_pairs={{0,8},{8,16},{16,24},{24,25},{25,17},{17,9},{9,1},{1,2},{2,10},{10... | collective-permute-start | bytes 835592 | tf_op jit(solution)/shard_map/ppermute | solution.py:618
  61.3 0.3 collective-permute-start.17
  61.7 6.7 %collective-permute-done.17 = f32[8,128]{1,0:T(8,128)S(1)} collective-permute-done((f32[8,128]{1,0:T(8,128)S(1)}, f32[8,128]{1,0:T(8,128)S(1)}, u32[]{:S(2)}, u32[]{:S(2)}) %collective-permute-start.17) | collective-permute-done | bytes 4128 | tf_op jit(solution)/shard_map/ppermute | solution.py:544
  68.4 0.3 collective-permute-done.19.refs_2_
  68.7 5.0 %step1.1 = (f32[4,16,32,128]{3,2,1,0:T(8,128)S(1)}, f32[68,8,128]{2,1,0:T(8,128)S(1)}, f32[68,8,128]{2,1,0:T(8,128)S(1)}, f32[2,32,128]{2,1,0:T(8,128)S(1)}, f32[8,128]{1,0:T(8,128)S(1)}) custom-call(f32[4,16,32,128]{3,2,1,0:T(8,128)S(1)} %get-tuple-element.96.refs_0_, f32[68,8,128]{2,1,0:T(8,128)S(1)} %collective-permute-done.18.refs_1_, ...), custom_call_target="tpu_custom_call" | custom-call | flops 6000000000 | bytes 4000000 | tf_op jit(solution)/shard_map/step1/pallas_call | solution.py:632
  73.7 1.8 %collective-permute-start.21 = (f32[8,128]{1,0:T(8,128)S(1)}, f32[8,128]{1,0:T(8,128)S(1)}, u32[]{:S(2)}, u32[]{:S(2)}) collective-permute-start(f32[8,128]{1,0:T(8,128)S(1)} %get-tuple-element.109), channel_id=1, source_target_pairs={{0,8},{8,0},{16,24},{24,16},{1,9},{9,1},{17,25},{25,17},{2,10},{10... | collective-permute-start | bytes 12296 | tf_op jit(solution)/shard_map/ppermute | solution.py:544
  75.6 0.8 collective-permute-done.21
  76.4 1.6 %collective-permute-start.23 = (f32[68,8,128]{2,1,0:T(8,128)S(1)}, f32[68,8,128]{2,1,0:T(8,128)S(1)}, u32[]{:S(2)}, u32[]{:S(2)}) collective-permute-start(f32[68,8,128]{2,1,0:T(8,128)S(1)} %get-tuple-element.112), channel_id=1, source_target_pairs={{0,8},{8,16},{16,24},{24,25},{25,17},{17,9},{9,1},{1,2},{2,10},{10... | collective-permute-start | bytes 835592 | tf_op jit(solution)/shard_map/ppermute | solution.py:618
  78.0 5.3 %collective-permute-start.26 = (f32[8,128]{1,0:T(8,128)S(1)}, f32[8,128]{1,0:T(8,128)S(1)}, u32[]{:S(2)}, u32[]{:S(2)}) collective-permute-start(f32[8,128]{1,0:T(8,128)S(1)} %add.115), channel_id=1, source_target_pairs={{0,2},{1,3},{2,0},{3,1},{4,6},{5,7},{6,4},{7,5},{8,10},{9,11},{10,... | collective-permute-start | bytes 12296 | tf_op jit(solution)/shard_map/ppermute | solution.py:544
  83.3 1.0 collective-permute-start.22
  84.3 0.3 collective-permute-done.26
  84.6 2.3 %collective-permute-done.27 = f32[8,128]{1,0:T(8,128)S(1)} collective-permute-done((f32[8,128]{1,0:T(8,128)S(1)}, f32[8,128]{1,0:T(8,128)S(1)}, u32[]{:S(2)}, u32[]{:S(2)}) %collective-permute-start.27) | collective-permute-done | bytes 4128 | tf_op jit(solution)/shard_map/ppermute | solution.py:544
  87.0 1.3 collective-permute-start.28
  88.3 5.0 %step2.1 = (f32[4,16,32,128]{3,2,1,0:T(8,128)S(1)}, f32[68,8,128]{2,1,0:T(8,128)S(1)}, f32[68,8,128]{2,1,0:T(8,128)S(1)}, f32[2,32,128]{2,1,0:T(8,128)S(1)}, f32[8,128]{1,0:T(8,128)S(1)}) custom-call(f32[4,16,32,128]{3,2,1,0:T(8,128)S(1)} %get-tuple-element.111.refs_0_, f32[68,8,128]{2,1,0:T(8,128)S(1)} %collective-permute-done.23.refs_1_, ...), custom_call_target="tpu_custom_call" | custom-call | flops 6000000000 | bytes 4000000 | tf_op jit(solution)/shard_map/step2/pallas_call | solution.py:632
  93.3 1.8 %collective-permute-start.29 = (f32[8,128]{1,0:T(8,128)S(1)}, f32[8,128]{1,0:T(8,128)S(1)}, u32[]{:S(2)}, u32[]{:S(2)}) collective-permute-start(f32[8,128]{1,0:T(8,128)S(1)} %get-tuple-element.123), channel_id=1, source_target_pairs={{0,8},{8,0},{16,24},{24,16},{1,9},{9,1},{17,25},{25,17},{2,10},{10... | collective-permute-start | bytes 12296 | tf_op jit(solution)/shard_map/ppermute | solution.py:544
  95.1 0.8 collective-permute-done.29
  95.9 2.7 %collective-permute-start.31 = (f32[68,8,128]{2,1,0:T(8,128)S(1)}, f32[68,8,128]{2,1,0:T(8,128)S(1)}, u32[]{:S(2)}, u32[]{:S(2)}) collective-permute-start(f32[68,8,128]{2,1,0:T(8,128)S(1)} %get-tuple-element.126), channel_id=1, source_target_pairs={{0,8},{8,16},{16,24},{24,25},{25,17},{17,9},{9,1},{1,2},{2,10},{10... | collective-permute-start | bytes 835592 | tf_op jit(solution)/shard_map/ppermute | solution.py:618
  98.6 2.8 %collective-permute-start.34 = (f32[8,128]{1,0:T(8,128)S(1)}, f32[8,128]{1,0:T(8,128)S(1)}, u32[]{:S(2)}, u32[]{:S(2)}) collective-permute-start(f32[8,128]{1,0:T(8,128)S(1)} %add.121), channel_id=1, source_target_pairs={{0,2},{1,3},{2,0},{3,1},{4,6},{5,7},{6,4},{7,5},{8,10},{9,11},{10,... | collective-permute-start | bytes 12296 | tf_op jit(solution)/shard_map/ppermute | solution.py:544
  101.5 1.0 collective-permute-start.35
  102.6 0.4 collective-permute-done.34
  102.9 2.2 %collective-permute-done.35 = f32[8,128]{1,0:T(8,128)S(1)} collective-permute-done((f32[8,128]{1,0:T(8,128)S(1)}, f32[8,128]{1,0:T(8,128)S(1)}, u32[]{:S(2)}, u32[]{:S(2)}) %collective-permute-start.35) | collective-permute-done | bytes 4128 | tf_op jit(solution)/shard_map/ppermute | solution.py:544
  105.1 0.8 collective-permute-done.30
  106.0 1.0 collective-permute-start.36
  107.0 4.9 %step3.1.fields = f32[4,16,32,128]{3,2,1,0:T(8,128)S(1)} custom-call(f32[4,16,32,128]{3,2,1,0:T(8,128)S(1)} %get-tuple-element.128.refs_0_, f32[68,8,128]{2,1,0:T(8,128)S(1)} %collective-permute-done.31.refs_1_, f32[68,8,128]{2,1,0:T(8,128)S(1)} %collective-permute-done.32.refs_2_, f32[4,64,128]{2,1,0:T(8,128)S(1)} %maps.1.refs_3_, ...), custom_call_target="tpu_custom_call" | custom-call | flops 6000000000 | bytes 4000000 | tf_op jit(solution)/shard_map/step3/pallas_call | solution.py:632
  111.9 1.2 send.1
  113.1 3.7 %collective-permute-start.40 = (f32[64,8,128]{2,1,0:T(8,128)S(1)}, f32[64,8,128]{2,1,0:T(8,128)S(1)}, u32[]{:S(2)}, u32[]{:S(2)}) collective-permute-start(f32[64,8,128]{2,1,0:T(8,128)S(1)} %get-tuple-element.134), channel_id=1, source_target_pairs={{0,8},{8,0},{16,24},{24,16},{1,9},{9,1},{17,25},{25,17},{2,10},{10... | collective-permute-start | bytes 786440 | tf_op jit(solution)/shard_map/ppermute | solution.py:544
  116.7 1.4 %collective-permute-start.41 = (f32[64,8,128]{2,1,0:T(8,128)S(1)}, f32[64,8,128]{2,1,0:T(8,128)S(1)}, u32[]{:S(2)}, u32[]{:S(2)}) collective-permute-start(f32[64,8,128]{2,1,0:T(8,128)S(1)} %get-tuple-element.135), channel_id=1, source_target_pairs={{0,16},{8,24},{16,0},{24,8},{1,17},{9,25},{17,1},{25,9},{2,18},{10... | collective-permute-start | bytes 786440 | tf_op jit(solution)/shard_map/ppermute | solution.py:544
  118.1 1.8 %collective-permute-start.42 = (f32[64,8,128]{2,1,0:T(8,128)S(1)}, f32[64,8,128]{2,1,0:T(8,128)S(1)}, u32[]{:S(2)}, u32[]{:S(2)}) collective-permute-start(f32[64,8,128]{2,1,0:T(8,128)S(1)} %get-tuple-element.136), channel_id=1, source_target_pairs={{0,24},{8,16},{16,8},{24,0},{1,25},{9,17},{17,9},{25,1},{2,26},{10... | collective-permute-start | bytes 786440 | tf_op jit(solution)/shard_map/ppermute | solution.py:544
  120.0 2.4 %collective-permute-start.38 = (f32[8,128]{1,0:T(8,128)S(1)}, f32[8,128]{1,0:T(8,128)S(1)}, u32[]{:S(2)}, u32[]{:S(2)}) collective-permute-start(f32[8,128]{1,0:T(8,128)S(1)} %add.125), channel_id=1, source_target_pairs={{0,2},{1,3},{2,0},{3,1},{4,6},{5,7},{6,4},{7,5},{8,10},{9,11},{10,... | collective-permute-start | bytes 12296 | tf_op jit(solution)/shard_map/ppermute | solution.py:544
  122.4 0.3 collective-permute-done.37
  122.7 1.2 collective-permute-start.39
  124.0 0.3 collective-permute-done.38
  124.2 2.5 %collective-permute-done.39 = f32[8,128]{1,0:T(8,128)S(1)} collective-permute-done((f32[8,128]{1,0:T(8,128)S(1)}, f32[8,128]{1,0:T(8,128)S(1)}, u32[]{:S(2)}, u32[]{:S(2)}) %collective-permute-start.39) | collective-permute-done | bytes 4128 | tf_op jit(solution)/shard_map/ppermute | solution.py:544
  126.7 5.2 %collective-permute-done.42.r3 = f32[64,8,128]{2,1,0:T(8,128)S(1)} collective-permute-done((f32[64,8,128]{2,1,0:T(8,128)S(1)}, f32[64,8,128]{2,1,0:T(8,128)S(1)}, u32[]{:S(2)}, u32[]{:S(2)}) %collective-permute-start.42) | collective-permute-done | bytes 262176 | tf_op jit(solution)/shard_map/ppermute | solution.py:544
  131.9 3.1 %final.1 = f32[4,16,32,128]{3,2,1,0:T(8,128)} custom-call(s32[135]{0:T(256)S(1)} %concatenate.3.scal.ints, f32[8,128]{1,0:T(8,128)S(1)} %add_add_fusion.mean, f32[64,8,128]{2,1,0:T(8,128)S(1)} %get-tuple-element.133.s0, f32[64,8,128]{2,1,0:T(8,128)S(1)} %collective-permute-done.40.r1, f32[64,8,128]{2,1,0:T(8,128)S(1)} %collective-permute-done.41.r2, ...), custom_call_target="tpu_custom_call" | custom-call | flops 2000000000 | bytes 4000000 | tf_op jit(solution)/shard_map/final/pallas_call | solution.py:660
  (65 shorter events, 0.8 us)
Async XLA Ops:
  0.0 6.3 %copy-start.1 = (f32[2,4,32,128]{3,2,1,0:T(8,128)S(1)}, f32[2,4,32,128]{3,2,1,0:T(8,128)}, u32[]{:S(2)}) copy-start(f32[2,4,32,128]{3,2,1,0:T(8,128)} %planes_in.1) | copy-start | bytes 393220
  0.9 5.4 %collective-permute-start = (f32[16,128]{1,0:T(8,128)S(1)}, f32[16,128]{1,0:T(8,128)S(1)}, u32[]{:S(2)}, u32[]{:S(2)}) collective-permute-start(f32[16,128]{1,0:T(8,128)S(1)} %get-tuple-element.138), channel_id=1, source_target_pairs={{0,1},{1,2},{2,3},{3,4},{4,5},{5,6},{6,7},{7,0},{8,9},{9,10},{10,1... | collective-permute-start | bytes 24584 | tf_op jit(solution)/shard_map/ppermute | solution.py:563
  2.9 3.3 %collective-permute-start.1 = (f32[16,128]{1,0:T(8,128)S(1)}, f32[16,128]{1,0:T(8,128)S(1)}, u32[]{:S(2)}, u32[]{:S(2)}) collective-permute-start(f32[16,128]{1,0:T(8,128)S(1)} %get-tuple-element.138), channel_id=1, source_target_pairs={{1,0},{2,1},{3,2},{4,3},{5,4},{6,5},{7,6},{0,7},{9,8},{10,9},{11,1... | collective-permute-start | bytes 24584 | tf_op jit(solution)/shard_map/ppermute | solution.py:563
  6.3 1.2 copy-start
  9.8 3.1 %collective-permute-start.2 = (f32[70,8,128]{2,1,0:T(8,128)S(1)}, f32[70,8,128]{2,1,0:T(8,128)S(1)}, u32[]{:S(2)}, u32[]{:S(2)}) collective-permute-start(f32[70,8,128]{2,1,0:T(8,128)S(1)} %get-tuple-element.72), channel_id=1, source_target_pairs={{0,8},{8,0},{16,24},{24,16},{1,9},{9,1},{17,25},{25,17},{2,10},{10... | collective-permute-start | bytes 860168 | tf_op jit(solution)/shard_map/ppermute | solution.py:544
  12.9 1.2 collective-permute-start.3
  14.1 9.3 %collective-permute-start.4 = (f32[8,128]{1,0:T(8,128)S(1)}, f32[8,128]{1,0:T(8,128)S(1)}, u32[]{:S(2)}, u32[]{:S(2)}) collective-permute-start(f32[8,128]{1,0:T(8,128)S(1)} %add.102), channel_id=1, source_target_pairs={{0,1},{1,0},{2,3},{3,2},{4,5},{5,4},{6,7},{7,6},{8,9},{9,8},{10,11... | collective-permute-start | bytes 12296 | tf_op jit(solution)/shard_map/ppermute | solution.py:544
  14.8 8.6 %collective-permute-start.5 = (f32[8,128]{1,0:T(8,128)S(1)}, f32[8,128]{1,0:T(8,128)S(1)}, u32[]{:S(2)}, u32[]{:S(2)}) collective-permute-start(f32[8,128]{1,0:T(8,128)S(1)} %add.102), channel_id=1, source_target_pairs={{0,2},{1,3},{2,0},{3,1},{4,6},{5,7},{6,4},{7,5},{8,10},{9,11},{10,... | collective-permute-start | bytes 12296 | tf_op jit(solution)/shard_map/ppermute | solution.py:544
  19.4 4.1 %collective-permute-start.6 = (f32[8,128]{1,0:T(8,128)S(1)}, f32[8,128]{1,0:T(8,128)S(1)}, u32[]{:S(2)}, u32[]{:S(2)}) collective-permute-start(f32[8,128]{1,0:T(8,128)S(1)} %add.102), channel_id=1, source_target_pairs={{0,3},{1,2},{2,1},{3,0},{4,7},{5,6},{6,5},{7,4},{8,11},{9,10},{10,... | collective-permute-start | bytes 12296 | tf_op jit(solution)/shard_map/ppermute | solution.py:544
  19.4 18.6 %collective-permute-start.8 = (f32[70,8,128]{2,1,0:T(8,128)S(1)}, f32[70,8,128]{2,1,0:T(8,128)S(1)}, u32[]{:S(2)}, u32[]{:S(2)}) collective-permute-start(f32[70,8,128]{2,1,0:T(8,128)S(1)} %get-tuple-element.78), channel_id=1, source_target_pairs={{0,16},{8,24},{16,0},{24,8},{1,17},{9,25},{17,1},{25,9},{2,18},{10... | collective-permute-start | bytes 860168 | tf_op jit(solution)/shard_map/ppermute | solution.py:544
  22.0 16.0 %collective-permute-start.9 = (f32[70,8,128]{2,1,0:T(8,128)S(1)}, f32[70,8,128]{2,1,0:T(8,128)S(1)}, u32[]{:S(2)}, u32[]{:S(2)}) collective-permute-start(f32[70,8,128]{2,1,0:T(8,128)S(1)} %get-tuple-element.79), channel_id=1, source_target_pairs={{0,24},{8,16},{16,8},{24,0},{1,25},{9,17},{17,9},{25,1},{2,26},{10... | collective-permute-start | bytes 860168 | tf_op jit(solution)/shard_map/ppermute | solution.py:544
  23.4 10.6 %collective-permute-start.7 = (f32[8,128]{1,0:T(8,128)S(1)}, f32[8,128]{1,0:T(8,128)S(1)}, u32[]{:S(2)}, u32[]{:S(2)}) collective-permute-start(f32[8,128]{1,0:T(8,128)S(1)} %add_add_fusion.4), channel_id=1, source_target_pairs={{0,4},{1,5},{2,6},{3,7},{4,0},{5,1},{6,2},{7,3},{8,12},{9,13},{10,... | collective-permute-start | bytes 12296 | tf_op jit(solution)/shard_map/ppermute | solution.py:544
  23.9 14.1 %collective-permute-start.10 = (f32[8,8,128]{2,1,0:T(8,128)S(1)}, f32[8,8,128]{2,1,0:T(8,128)S(1)}, u32[]{:S(2)}, u32[]{:S(2)}) collective-permute-start(f32[8,8,128]{2,1,0:T(8,128)S(1)} %get-tuple-element.80.p0), channel_id=1, source_target_pairs={{0,32},{32,0},{64,96},{96,64},{1,33},{33,1},{65,97},{97,65},{2,34}... | collective-permute-start | bytes 98312 | tf_op jit(solution)/shard_map/ppermute | solution.py:544
  25.6 12.5 %collective-permute-start.11 = (f32[8,8,128]{2,1,0:T(8,128)S(1)}, f32[8,8,128]{2,1,0:T(8,128)S(1)}, u32[]{:S(2)}, u32[]{:S(2)}) collective-permute-start(f32[8,8,128]{2,1,0:T(8,128)S(1)} %get-tuple-element.80.p0), channel_id=1, source_target_pairs={{0,64},{32,96},{64,0},{96,32},{1,65},{33,97},{65,1},{97,33},{2,66}... | collective-permute-start | bytes 98312 | tf_op jit(solution)/shard_map/ppermute | solution.py:544
  34.1 5.1 %collective-permute-start.12 = (f32[8,8,128]{2,1,0:T(8,128)S(1)}, f32[8,8,128]{2,1,0:T(8,128)S(1)}, u32[]{:S(2)}, u32[]{:S(2)}) collective-permute-start(f32[8,8,128]{2,1,0:T(8,128)S(1)} %get-tuple-element.80.p0), channel_id=1, source_target_pairs={{0,96},{32,64},{64,32},{96,0},{1,97},{33,65},{65,33},{97,1},{2,98}... | collective-permute-start | bytes 98312 | tf_op jit(solution)/shard_map/ppermute | solution.py:544
  40.9 7.6 %collective-permute-start.13 = (f32[72,8,128]{2,1,0:T(8,128)S(1)}, f32[72,8,128]{2,1,0:T(8,128)S(1)}, u32[]{:S(2)}, u32[]{:S(2)}) collective-permute-start(f32[72,8,128]{2,1,0:T(8,128)S(1)} %get-tuple-element.82), channel_id=1, source_target_pairs={{0,8},{8,16},{16,24},{24,25},{25,17},{17,9},{9,1},{1,2},{2,10},{10... | collective-permute-start | bytes 884744 | tf_op jit(solution)/shard_map/ppermute | solution.py:618
  44.8 7.7 %collective-permute-start.14 = (f32[72,8,128]{2,1,0:T(8,128)S(1)}, f32[72,8,128]{2,1,0:T(8,128)S(1)}, u32[]{:S(2)}, u32[]{:S(2)}) collective-permute-start(f32[72,8,128]{2,1,0:T(8,128)S(1)} %get-tuple-element.83), channel_id=1, source_target_pairs={{8,0},{16,8},{24,16},{25,24},{17,25},{9,17},{1,9},{2,1},{10,2},{18... | collective-permute-start | bytes 884744 | tf_op jit(solution)/shard_map/ppermute | solution.py:619
  44.8 12.4 %collective-permute-start.15 = (f32[8,128]{1,0:T(8,128)S(1)}, f32[8,128]{1,0:T(8,128)S(1)}, u32[]{:S(2)}, u32[]{:S(2)}) collective-permute-start(f32[8,128]{1,0:T(8,128)S(1)} %add.106), channel_id=1, source_target_pairs={{0,16},{8,24},{16,0},{24,8},{1,17},{9,25},{17,1},{25,9},{2,18},{10... | collective-permute-start | bytes 12296 | tf_op jit(solution)/shard_map/ppermute | solution.py:544
  56.8 1.2 collective-permute-start.16
  58.1 10.3 %collective-permute-start.18 = (f32[68,8,128]{2,1,0:T(8,128)S(1)}, f32[68,8,128]{2,1,0:T(8,128)S(1)}, u32[]{:S(2)}, u32[]{:S(2)}) collective-permute-start(f32[68,8,128]{2,1,0:T(8,128)S(1)} %get-tuple-element.97), channel_id=1, source_target_pairs={{0,8},{8,16},{16,24},{24,25},{25,17},{17,9},{9,1},{1,2},{2,10},{10... | collective-permute-start | bytes 835592 | tf_op jit(solution)/shard_map/ppermute | solution.py:618
  61.2 7.5 %collective-permute-start.19 = (f32[68,8,128]{2,1,0:T(8,128)S(1)}, f32[68,8,128]{2,1,0:T(8,128)S(1)}, u32[]{:S(2)}, u32[]{:S(2)}) collective-permute-start(f32[68,8,128]{2,1,0:T(8,128)S(1)} %get-tuple-element.98), channel_id=1, source_target_pairs={{8,0},{16,8},{24,16},{25,24},{17,25},{9,17},{1,9},{2,1},{10,2},{18... | collective-permute-start | bytes 835592 | tf_op jit(solution)/shard_map/ppermute | solution.py:619
  61.3 7.0 %collective-permute-start.17 = (f32[8,128]{1,0:T(8,128)S(1)}, f32[8,128]{1,0:T(8,128)S(1)}, u32[]{:S(2)}, u32[]{:S(2)}) collective-permute-start(f32[8,128]{1,0:T(8,128)S(1)} %add.107), channel_id=1, source_target_pairs={{0,4},{1,5},{2,6},{3,7},{4,0},{5,1},{6,2},{7,3},{8,12},{9,13},{10,... | collective-permute-start | bytes 12296 | tf_op jit(solution)/shard_map/ppermute | solution.py:544
  68.4 7.2 %collective-permute-start.20 = (f32[8,128]{1,0:T(8,128)S(1)}, f32[8,128]{1,0:T(8,128)S(1)}, u32[]{:S(2)}, u32[]{:S(2)}) collective-permute-start(f32[8,128]{1,0:T(8,128)S(1)} %add.108), channel_id=1, source_target_pairs={{0,16},{8,24},{16,0},{24,8},{1,17},{9,25},{17,1},{25,9},{2,18},{10... | collective-permute-start | bytes 12296 | tf_op jit(solution)/shard_map/ppermute | solution.py:544
  73.7 2.7 %collective-permute-start.21 = (f32[8,128]{1,0:T(8,128)S(1)}, f32[8,128]{1,0:T(8,128)S(1)}, u32[]{:S(2)}, u32[]{:S(2)}) collective-permute-start(f32[8,128]{1,0:T(8,128)S(1)} %get-tuple-element.109), channel_id=1, source_target_pairs={{0,8},{8,0},{16,24},{24,16},{1,9},{9,1},{17,25},{25,17},{2,10},{10... | collective-permute-start | bytes 12296 | tf_op jit(solution)/shard_map/ppermute | solution.py:544
  76.4 11.9 %collective-permute-start.23 = (f32[68,8,128]{2,1,0:T(8,128)S(1)}, f32[68,8,128]{2,1,0:T(8,128)S(1)}, u32[]{:S(2)}, u32[]{:S(2)}) collective-permute-start(f32[68,8,128]{2,1,0:T(8,128)S(1)} %get-tuple-element.112), channel_id=1, source_target_pairs={{0,8},{8,16},{16,24},{24,25},{25,17},{17,9},{9,1},{1,2},{2,10},{10... | collective-permute-start | bytes 835592 | tf_op jit(solution)/shard_map/ppermute | solution.py:618
  78.0 10.3 %collective-permute-start.24 = (f32[68,8,128]{2,1,0:T(8,128)S(1)}, f32[68,8,128]{2,1,0:T(8,128)S(1)}, u32[]{:S(2)}, u32[]{:S(2)}) collective-permute-start(f32[68,8,128]{2,1,0:T(8,128)S(1)} %get-tuple-element.113), channel_id=1, source_target_pairs={{8,0},{16,8},{24,16},{25,24},{17,25},{9,17},{1,9},{2,1},{10,2},{18... | collective-permute-start | bytes 835592 | tf_op jit(solution)/shard_map/ppermute | solution.py:619
  78.0 5.3 %collective-permute-start.25 = (f32[8,128]{1,0:T(8,128)S(1)}, f32[8,128]{1,0:T(8,128)S(1)}, u32[]{:S(2)}, u32[]{:S(2)}) collective-permute-start(f32[8,128]{1,0:T(8,128)S(1)} %add.115), channel_id=1, source_target_pairs={{0,1},{1,0},{2,3},{3,2},{4,5},{5,4},{6,7},{7,6},{8,9},{9,8},{10,11... | collective-permute-start | bytes 12296 | tf_op jit(solution)/shard_map/ppermute | solution.py:544
  78.0 6.6 %collective-permute-start.26 = (f32[8,128]{1,0:T(8,128)S(1)}, f32[8,128]{1,0:T(8,128)S(1)}, u32[]{:S(2)}, u32[]{:S(2)}) collective-permute-start(f32[8,128]{1,0:T(8,128)S(1)} %add.115), channel_id=1, source_target_pairs={{0,2},{1,3},{2,0},{3,1},{4,6},{5,7},{6,4},{7,5},{8,10},{9,11},{10,... | collective-permute-start | bytes 12296 | tf_op jit(solution)/shard_map/ppermute | solution.py:544
  83.3 3.7 %collective-permute-start.27 = (f32[8,128]{1,0:T(8,128)S(1)}, f32[8,128]{1,0:T(8,128)S(1)}, u32[]{:S(2)}, u32[]{:S(2)}) collective-permute-start(f32[8,128]{1,0:T(8,128)S(1)} %add.115), channel_id=1, source_target_pairs={{0,3},{1,2},{2,1},{3,0},{4,7},{5,6},{6,5},{7,4},{8,11},{9,10},{10,... | collective-permute-start | bytes 12296 | tf_op jit(solution)/shard_map/ppermute | solution.py:544
  83.3 3.7 %collective-permute-start.22 = (f32[8,128]{1,0:T(8,128)S(1)}, f32[8,128]{1,0:T(8,128)S(1)}, u32[]{:S(2)}, u32[]{:S(2)}) collective-permute-start(f32[8,128]{1,0:T(8,128)S(1)} %add.113), channel_id=1, source_target_pairs={{0,4},{1,5},{2,6},{3,7},{4,0},{5,1},{6,2},{7,3},{8,12},{9,13},{10,... | collective-permute-start | bytes 12296 | tf_op jit(solution)/shard_map/ppermute | solution.py:544
  87.0 8.1 %collective-permute-start.28 = (f32[8,128]{1,0:T(8,128)S(1)}, f32[8,128]{1,0:T(8,128)S(1)}, u32[]{:S(2)}, u32[]{:S(2)}) collective-permute-start(f32[8,128]{1,0:T(8,128)S(1)} %add.114), channel_id=1, source_target_pairs={{0,16},{8,24},{16,0},{24,8},{1,17},{9,25},{17,1},{25,9},{2,18},{10... | collective-permute-start | bytes 12296 | tf_op jit(solution)/shard_map/ppermute | solution.py:544
  93.3 2.6 %collective-permute-start.29 = (f32[8,128]{1,0:T(8,128)S(1)}, f32[8,128]{1,0:T(8,128)S(1)}, u32[]{:S(2)}, u32[]{:S(2)}) collective-permute-start(f32[8,128]{1,0:T(8,128)S(1)} %get-tuple-element.123), channel_id=1, source_target_pairs={{0,8},{8,0},{16,24},{24,16},{1,9},{9,1},{17,25},{25,17},{2,10},{10... | collective-permute-start | bytes 12296 | tf_op jit(solution)/shard_map/ppermute | solution.py:544
  95.9 11.1 %collective-permute-start.31 = (f32[68,8,128]{2,1,0:T(8,128)S(1)}, f32[68,8,128]{2,1,0:T(8,128)S(1)}, u32[]{:S(2)}, u32[]{:S(2)}) collective-permute-start(f32[68,8,128]{2,1,0:T(8,128)S(1)} %get-tuple-element.126), channel_id=1, source_target_pairs={{0,8},{8,16},{16,24},{24,25},{25,17},{17,9},{9,1},{1,2},{2,10},{10... | collective-permute-start | bytes 835592 | tf_op jit(solution)/shard_map/ppermute | solution.py:618
  98.6 8.4 %collective-permute-start.32 = (f32[68,8,128]{2,1,0:T(8,128)S(1)}, f32[68,8,128]{2,1,0:T(8,128)S(1)}, u32[]{:S(2)}, u32[]{:S(2)}) collective-permute-start(f32[68,8,128]{2,1,0:T(8,128)S(1)} %get-tuple-element.127), channel_id=1, source_target_pairs={{8,0},{16,8},{24,16},{25,24},{17,25},{9,17},{1,9},{2,1},{10,2},{18... | collective-permute-start | bytes 835592 | tf_op jit(solution)/shard_map/ppermute | solution.py:619
  98.6 3.9 %collective-permute-start.33 = (f32[8,128]{1,0:T(8,128)S(1)}, f32[8,128]{1,0:T(8,128)S(1)}, u32[]{:S(2)}, u32[]{:S(2)}) collective-permute-start(f32[8,128]{1,0:T(8,128)S(1)} %add.121), channel_id=1, source_target_pairs={{0,1},{1,0},{2,3},{3,2},{4,5},{5,4},{6,7},{7,6},{8,9},{9,8},{10,11... | collective-permute-start | bytes 12296 | tf_op jit(solution)/shard_map/ppermute | solution.py:544
  98.6 4.3 %collective-permute-start.34 = (f32[8,128]{1,0:T(8,128)S(1)}, f32[8,128]{1,0:T(8,128)S(1)}, u32[]{:S(2)}, u32[]{:S(2)}) collective-permute-start(f32[8,128]{1,0:T(8,128)S(1)} %add.121), channel_id=1, source_target_pairs={{0,2},{1,3},{2,0},{3,1},{4,6},{5,7},{6,4},{7,5},{8,10},{9,11},{10,... | collective-permute-start | bytes 12296 | tf_op jit(solution)/shard_map/ppermute | solution.py:544
  101.5 3.7 %collective-permute-start.35 = (f32[8,128]{1,0:T(8,128)S(1)}, f32[8,128]{1,0:T(8,128)S(1)}, u32[]{:S(2)}, u32[]{:S(2)}) collective-permute-start(f32[8,128]{1,0:T(8,128)S(1)} %add.121), channel_id=1, source_target_pairs={{0,3},{1,2},{2,1},{3,0},{4,7},{5,6},{6,5},{7,4},{8,11},{9,10},{10,... | collective-permute-start | bytes 12296 | tf_op jit(solution)/shard_map/ppermute | solution.py:544
  102.5 3.5 %collective-permute-start.30 = (f32[8,128]{1,0:T(8,128)S(1)}, f32[8,128]{1,0:T(8,128)S(1)}, u32[]{:S(2)}, u32[]{:S(2)}) collective-permute-start(f32[8,128]{1,0:T(8,128)S(1)} %add.119), channel_id=1, source_target_pairs={{0,4},{1,5},{2,6},{3,7},{4,0},{5,1},{6,2},{7,3},{8,12},{9,13},{10,... | collective-permute-start | bytes 12296 | tf_op jit(solution)/shard_map/ppermute | solution.py:544
  106.0 5.9 %collective-permute-start.36 = (f32[8,128]{1,0:T(8,128)S(1)}, f32[8,128]{1,0:T(8,128)S(1)}, u32[]{:S(2)}, u32[]{:S(2)}) collective-permute-start(f32[8,128]{1,0:T(8,128)S(1)} %add.120), channel_id=1, source_target_pairs={{0,16},{8,24},{16,0},{24,8},{1,17},{9,25},{17,1},{25,9},{2,18},{10... | collective-permute-start | bytes 12296 | tf_op jit(solution)/shard_map/ppermute | solution.py:544
  113.1 13.6 %collective-permute-start.40 = (f32[64,8,128]{2,1,0:T(8,128)S(1)}, f32[64,8,128]{2,1,0:T(8,128)S(1)}, u32[]{:S(2)}, u32[]{:S(2)}) collective-permute-start(f32[64,8,128]{2,1,0:T(8,128)S(1)} %get-tuple-element.134), channel_id=1, source_target_pairs={{0,8},{8,0},{16,24},{24,16},{1,9},{9,1},{17,25},{25,17},{2,10},{10... | collective-permute-start | bytes 786440 | tf_op jit(solution)/shard_map/ppermute | solution.py:544
  116.7 10.0 %collective-permute-start.41 = (f32[64,8,128]{2,1,0:T(8,128)S(1)}, f32[64,8,128]{2,1,0:T(8,128)S(1)}, u32[]{:S(2)}, u32[]{:S(2)}) collective-permute-start(f32[64,8,128]{2,1,0:T(8,128)S(1)} %get-tuple-element.135), channel_id=1, source_target_pairs={{0,16},{8,24},{16,0},{24,8},{1,17},{9,25},{17,1},{25,9},{2,18},{10... | collective-permute-start | bytes 786440 | tf_op jit(solution)/shard_map/ppermute | solution.py:544
  118.1 13.8 %collective-permute-start.42 = (f32[64,8,128]{2,1,0:T(8,128)S(1)}, f32[64,8,128]{2,1,0:T(8,128)S(1)}, u32[]{:S(2)}, u32[]{:S(2)}) collective-permute-start(f32[64,8,128]{2,1,0:T(8,128)S(1)} %get-tuple-element.136), channel_id=1, source_target_pairs={{0,24},{8,16},{16,8},{24,0},{1,25},{9,17},{17,9},{25,1},{2,26},{10... | collective-permute-start | bytes 786440 | tf_op jit(solution)/shard_map/ppermute | solution.py:544
  120.0 2.8 %collective-permute-start.37 = (f32[8,128]{1,0:T(8,128)S(1)}, f32[8,128]{1,0:T(8,128)S(1)}, u32[]{:S(2)}, u32[]{:S(2)}) collective-permute-start(f32[8,128]{1,0:T(8,128)S(1)} %add.125), channel_id=1, source_target_pairs={{0,1},{1,0},{2,3},{3,2},{4,5},{5,4},{6,7},{7,6},{8,9},{9,8},{10,11... | collective-permute-start | bytes 12296 | tf_op jit(solution)/shard_map/ppermute | solution.py:544
  120.0 4.3 %collective-permute-start.38 = (f32[8,128]{1,0:T(8,128)S(1)}, f32[8,128]{1,0:T(8,128)S(1)}, u32[]{:S(2)}, u32[]{:S(2)}) collective-permute-start(f32[8,128]{1,0:T(8,128)S(1)} %add.125), channel_id=1, source_target_pairs={{0,2},{1,3},{2,0},{3,1},{4,6},{5,7},{6,4},{7,5},{8,10},{9,11},{10,... | collective-permute-start | bytes 12296 | tf_op jit(solution)/shard_map/ppermute | solution.py:544
  122.7 4.0 %collective-permute-start.39 = (f32[8,128]{1,0:T(8,128)S(1)}, f32[8,128]{1,0:T(8,128)S(1)}, u32[]{:S(2)}, u32[]{:S(2)}) collective-permute-start(f32[8,128]{1,0:T(8,128)S(1)} %add.125), channel_id=1, source_target_pairs={{0,3},{1,2},{2,1},{3,0},{4,7},{5,6},{6,5},{7,4},{8,11},{9,10},{10,... | collective-permute-start | bytes 12296 | tf_op jit(solution)/shard_map/ppermute | solution.py:544

commit v7 on v4

--- a/solution.py
+++ b/solution.py
@@ -124,18 +124,22 @@
     slab = scal[1]
     group = lanes() >> 5
     masks = [group == c for c in range(4)]
-
-    def per_row(x, carry):
+    outs = (s0, s1, s2, s3)
+
+    def per_row(x, total):
         for kt in range(4):
             sources = [state[c, x, kt * 8 : kt * 8 + 8, :] for c in range(4)]
-            for s, out in enumerate((s0, s1, s2, s3)):
+            for s, out in enumerate(outs):
                 out[x * 4 + kt] = block_transposed(sources, slab ^ s, masks)
-        return carry
-
-    rows("fill", per_row)
-    for half in range(6):
-        for out in (s0, s1, s2, s3):
+        return total + state[3, x]
+
+    total = rows("fill", per_row, jnp.zeros((NZ, LANES), F32))
+    levels = jnp.concatenate([total] * GX, axis=0).T
+    levels = jnp.broadcast_to(jnp.sum(levels, axis=0, keepdims=True), (8, LANES))
+    for out in outs:
+        for half in range(6):
             out[TILES + half] = ids[half // 2, (half % 2) * 8 : (half % 2) * 8 + 8]
+        out[TILES + 6] = levels
     for plane in range(planes.shape[0]):
         for kt in range(4):
             sources = [planes[plane, c, kt * 8 : kt * 8 + 8, :] for c in range(4)]
@@ -196,10 +200,11 @@
         held[own ^ s] = source[:TILES]
         for half in range(6):
             ids[half // 2, own ^ s, (half % 2) * 8 : (half % 2) * 8 + 8, :] = source[TILES + half]
+    sums[...] = s0[TILES + 6] + r1[TILES + 6] + r2[TILES + 6] + r3[TILES + 6]
     for s, source in enumerate(plane_refs):
         planes[here ^ s] = source[...]
 
-    def per_row(xi, total):
+    def per_row(xi, carry):
         parts = [held[g, pl.ds(xi * 4, 4)].reshape(NZ, LANES) for g in range(GX)]
         turned = jnp.concatenate(parts, axis=0).T
         for c in range(4):
@@ -207,12 +212,9 @@
             fields[c, xi] = value
             sd[c * XI + xi] = value[:HALO]
             su[c * XI + xi] = value[OWN - HALO :]
-            if c == 3:
-                total = total + jnp.sum(value, axis=0, keepdims=True)
-        return total
-
-    total = rows("fill", per_row, jnp.zeros((1, LANES), F32))
-    sums[...] = jnp.broadcast_to(over_groups(total), (8, LANES))
+        return carry
+
+    rows("fill", per_row)
     parts = []
     for step in range(STEPS):
         plane = scal[3 + step]
@@ -487,12 +489,12 @@
 
     def per_row(xi, carry):
         stacked = jnp.concatenate([fields[c, xi] for c in range(4)], axis=0)
-        turned[...] = stacked.T.reshape(GX, 4, 8, LANES)
+        turned[xi] = stacked.T.reshape(GX, 4, 8, LANES)
         for s, out in enumerate((s0, s1, s2, s3)):
-            out[pl.ds(xi * 4, 4)] = turned[own ^ s]
+            out[pl.ds(xi * 4, 4)] = turned[xi, own ^ s]
         return carry
 
-    lax.fori_loop(0, XI, per_row, 0)
+    rows("fill", per_row)
 
 
 def final_kernel(scal, mean, s0, r1, r2, r3, out, columns, *, cells):
@@ -549,7 +551,7 @@
 
     ids = turbine_cell[0, :, NZ // 2, :].astype(F32)
     ids = jnp.stack([ids, lax.ppermute(ids, "gy", gy_up), lax.ppermute(ids, "gy", gy_down)])
-    chunk = shape(TILES + 6, 8, LANES)
+    chunk = shape(TILES + 7, 8, LANES)
     s0, s1, s2, s3, plane = call(
         pack_kernel,
         (chunk, chunk, chunk, chunk, shape(per_layout * 4, 8, LANES)),
@@ -584,20 +586,25 @@
 
     half = groups // 2
 
-    def last_round(value):
+    def among_x(value):
         return sum([swapped(value, "gy", groups, d) for d in range(1, half)], value)
+
+    def last_swap(value):
+        return value + swapped(value, "gy", groups, half)
 
     mean = pending = None
     for step in range(STEPS):
-        partial = sums + swapped(sums, "gx", GX, 1)
-        su, sd, partial = lax.optimization_barrier((su, sd, partial))
+        partial = sums
+        if step > 0:
+            partial = partial + swapped(partial, "gx", GX, 1)
+            su, sd, partial = lax.optimization_barrier((su, sd, partial))
+            mean = last_swap(pending) if step > 1 else pending
         lo = lax.ppermute(su, ("gx", "gy"), up)
         hi = lax.ppermute(sd, ("gx", "gy"), down)
-        if pending is not None:
-            mean = last_round(pending)
-        partial = partial + swapped(partial, "gy", groups, half)
-        fields, partial = lax.optimization_barrier((fields, partial))
-        arriving = swapped(partial, "gx", GX, 2)
+        fields, partial = lax.optimization_barrier((fields, among_x(partial)))
+        arriving = swapped(partial, "gx", GX, 2) if step > 0 else swapped(partial, "gy", groups, half)
+        if step == 0:
+            partial = partial + cells * profile[3:4]
         outs = [shape(4, XI, OWN, LANES)]
         if step < STEPS - 1:
             payload = shape(TILES + MORE, 8, LANES)
@@ -622,14 +629,14 @@
             inflow = results.pop(0)
         su, sd, fields, arriving = lax.optimization_barrier((su, sd, fields, arriving))
         pending = partial + arriving
-    mean = last_round(pending)
+    mean = last_swap(pending)
 
     chunk = shape(TILES, 8, LANES)
     s0, s1, s2, s3 = call(
         send_kernel,
         (chunk, chunk, chunk, chunk),
         [SMEM, VMEM],
-        [pltpu.VMEM((GX, 4, 8, LANES), F32)],
+        [pltpu.VMEM((XI, GX, 4, 8, LANES), F32)],
         name="send",
     )(scal, fields)
     received = [swapped(value, "gx", GX, s) for s, value in ((1, s1), (2, s2), (3, s3))]

time: 128 us -> 137 us (1.070)
  waiting for transfers between devices: 34.5 us -> 41.5 us
  starting transfers between devices: 60.1 us -> 62.6 us
    ppermute x4, waiting for transfers between devices: 0.01 us -> 8.15 us  [local(): lo = lax.ppermute(su, ('gx', 'gy'), up)]
    ppermute x33 -> x31, waiting for transfers between devices: 34.2 us -> 30.7 us  [swapped(): return lax.ppermute(value, axis, [(i, i ^ distance) for i in range(size)])]
    ppermute x4, waiting for transfers between devices: 0.01 us -> 2.4 us  [local(): hi = lax.ppermute(sd, ('gx', 'gy'), down)]
    ppermute x4, starting transfers between devices: 8.96 us -> 10.3 us  [local(): lo = lax.ppermute(su, ('gx', 'gy'), up)]
    ppermute x33 -> x31, starting transfers between devices: 46.7 us -> 47.9 us  [swapped(): return lax.ppermute(value, axis, [(i, i ^ distance) for i in range(size)])]
  transfers between devices with their start and end apart: 43 -> 41, of which waited for: 20 -> 16; matrix products, arithmetic and copies ran while one was open for 1% -> 1% of each run, Pallas kernels for 16% -> 15%
where the time goes in v7:
time: 137 us
  starting transfers between devices  62.6 us (46%)
  waiting for transfers between devices  41.5 us (30%)
  Pallas kernels  29 us (21%)
  local copies, waits for them, and re-layouts  3.13 us (2%)
    ppermute x31, starting transfers between devices, swapped(): return lax.ppermute(value, axis, [(i, i ^ distance) for i in range(size)])  47.9 us
    ppermute x31, waiting for transfers between devices, swapped(): return lax.ppermute(value, axis, [(i, i ^ distance) for i in range(size)])  30.7 us
    pallas_call x4, Pallas kernels, local(): call(functools.partial(step_kernel, step=step, cells=cells), tuple(outs),...  19.3 us
    ppermute x4, starting transfers between devices, local(): lo = lax.ppermute(su, ('gx', 'gy'), up)  10.3 us
    ppermute x4, waiting for transfers between devices, local(): lo = lax.ppermute(su, ('gx', 'gy'), up)  8.15 us
    pallas_call x1, Pallas kernels, local(): call(functools.partial(final_kernel, cells=cells), shape(4, XI, NZ, LANES...  3.11 us
  transfers between devices with their start and end apart: 41, of which 16 were waited for; matrix products, arithmetic and copies ran while one was open for 1% of the time, Pallas kernels for 15%

profile of v7, /device:TPU:1, one launch (start us, length us, event | category | flops | bytes accessed | tf_op | source)
XLA Modules:
  0.0 136.6 jit_solution(7557798881103596327)
XLA Ops:
  0.0 0.9 slice.7
  0.9 2.0 %collective-permute-start = (f32[16,128]{1,0:T(8,128)S(1)}, f32[16,128]{1,0:T(8,128)S(1)}, u32[]{:S(2)}, u32[]{:S(2)}) collective-permute-start(f32[16,128]{1,0:T(8,128)S(1)} %get-tuple-element.136), channel_id=1, source_target_pairs={{0,1},{1,2},{2,3},{3,4},{4,5},{5,6},{6,7},{7,0},{8,9},{9,10},{10,1... | collective-permute-start | bytes 24584 | tf_op jit(solution)/shard_map/ppermute | solution.py:553
  2.9 2.4 %collective-permute-start.1 = (f32[16,128]{1,0:T(8,128)S(1)}, f32[16,128]{1,0:T(8,128)S(1)}, u32[]{:S(2)}, u32[]{:S(2)}) collective-permute-start(f32[16,128]{1,0:T(8,128)S(1)} %get-tuple-element.136), channel_id=1, source_target_pairs={{1,0},{2,1},{3,2},{4,3},{5,4},{6,5},{7,6},{0,7},{9,8},{10,9},{11,1... | collective-permute-start | bytes 24584 | tf_op jit(solution)/shard_map/ppermute | solution.py:553
  5.3 0.8 concatenate.3.scal.ints
  6.0 0.2 collective-permute-done
  6.2 0.0 collective-permute-done.1
  6.3 0.0 copy-start
  6.3 1.2 copy-done
  7.5 2.0 %pack.1 = (f32[71,8,128]{2,1,0:T(8,128)S(1)}, f32[71,8,128]{2,1,0:T(8,128)S(1)}, f32[71,8,128]{2,1,0:T(8,128)S(1)}, f32[71,8,128]{2,1,0:T(8,128)S(1)}, f32[8,8,128]{2,1,0:T(8,128)S(1)}) custom-call(s32[135]{0:T(256)S(1)} %concatenate.3.scal.ints, f32[4,16,32,128]{3,2,1,0:T(8,128)S(1)} %bitcast.14, f32[2,4,32,128]{3,2,1,0:T(8,128)S(1)} %copy-done.1, ...), custom_call_target="tpu_custom_call" | custom-call | flops 2000000000 | bytes 4000000 | tf_op jit(solution)/shard_map/pack/pallas_call | solution.py:555
  9.5 1.9 %collective-permute-start.2 = (f32[71,8,128]{2,1,0:T(8,128)S(1)}, f32[71,8,128]{2,1,0:T(8,128)S(1)}, u32[]{:S(2)}, u32[]{:S(2)}) collective-permute-start(f32[71,8,128]{2,1,0:T(8,128)S(1)} %get-tuple-element.71), channel_id=1, source_target_pairs={{0,8},{8,0},{16,24},{24,16},{1,9},{9,1},{17,25},{25,17},{2,10},{10... | collective-permute-start | bytes 872456 | tf_op jit(solution)/shard_map/ppermute | solution.py:534
  11.4 0.1 pad.9.clone
  11.5 3.0 %collective-permute-start.3 = (f32[71,8,128]{2,1,0:T(8,128)S(1)}, f32[71,8,128]{2,1,0:T(8,128)S(1)}, u32[]{:S(2)}, u32[]{:S(2)}) collective-permute-start(f32[71,8,128]{2,1,0:T(8,128)S(1)} %get-tuple-element.74), channel_id=1, source_target_pairs={{0,16},{8,24},{16,0},{24,8},{1,17},{9,25},{17,1},{25,9},{2,18},{10... | collective-permute-start | bytes 872456 | tf_op jit(solution)/shard_map/ppermute | solution.py:534
  14.5 0.2 collective-permute-start.4
  14.7 1.8 %collective-permute-start.5 = (f32[8,8,128]{2,1,0:T(8,128)S(1)}, f32[8,8,128]{2,1,0:T(8,128)S(1)}, u32[]{:S(2)}, u32[]{:S(2)}) collective-permute-start(f32[8,8,128]{2,1,0:T(8,128)S(1)} %get-tuple-element.76.p0), channel_id=1, source_target_pairs={{0,32},{32,0},{64,96},{96,64},{1,33},{33,1},{65,97},{97,65},{2,34}... | collective-permute-start | bytes 98312 | tf_op jit(solution)/shard_map/ppermute | solution.py:534
  16.5 3.3 %collective-permute-start.6 = (f32[8,8,128]{2,1,0:T(8,128)S(1)}, f32[8,8,128]{2,1,0:T(8,128)S(1)}, u32[]{:S(2)}, u32[]{:S(2)}) collective-permute-start(f32[8,8,128]{2,1,0:T(8,128)S(1)} %get-tuple-element.76.p0), channel_id=1, source_target_pairs={{0,64},{32,96},{64,0},{96,32},{1,65},{33,97},{65,1},{97,33},{2,66}... | collective-permute-start | bytes 98312 | tf_op jit(solution)/shard_map/ppermute | solution.py:534
  19.8 0.1 pad_maximum_fusion.1
  19.9 0.1 tile.12
  20.0 1.6 %collective-permute-done.3.r2 = f32[71,8,128]{2,1,0:T(8,128)S(1)} collective-permute-done((f32[71,8,128]{2,1,0:T(8,128)S(1)}, f32[71,8,128]{2,1,0:T(8,128)S(1)}, u32[]{:S(2)}, u32[]{:S(2)}) %collective-permute-start.3) | collective-permute-done | bytes 290848 | tf_op jit(solution)/shard_map/ppermute | solution.py:534
  21.6 6.3 %collective-permute-done.4.r3 = f32[71,8,128]{2,1,0:T(8,128)S(1)} collective-permute-done((f32[71,8,128]{2,1,0:T(8,128)S(1)}, f32[71,8,128]{2,1,0:T(8,128)S(1)}, u32[]{:S(2)}, u32[]{:S(2)}) %collective-permute-start.4) | collective-permute-done | bytes 290848 | tf_op jit(solution)/shard_map/ppermute | solution.py:534
  27.9 1.7 %unpack.1 = (f32[4,16,32,128]{3,2,1,0:T(8,128)S(1)}, f32[4,32,128]{2,1,0:T(8,128)S(1)}, f32[72,8,128]{2,1,0:T(8,128)S(1)}, f32[72,8,128]{2,1,0:T(8,128)S(1)}, f3...) custom-call(s32[135]{0:T(256)S(1)} %concatenate.3.scal.ints, ...), custom_call_target="tpu_custom_call" | custom-call | flops 2000000000 | bytes 4000000 | tf_op jit(solution)/shard_map/unpack/pallas_call | solution.py:566
  29.7 4.1 %collective-permute-start.10 = (f32[8,128]{1,0:T(8,128)S(1)}, f32[8,128]{1,0:T(8,128)S(1)}, u32[]{:S(2)}, u32[]{:S(2)}) collective-permute-start(f32[8,128]{1,0:T(8,128)S(1)} %get-tuple-element.78), channel_id=1, source_target_pairs={{0,3},{1,2},{2,1},{3,0},{4,7},{5,6},{6,5},{7,4},{8,11},{9,10},{10,... | collective-permute-start | bytes 12296 | tf_op jit(solution)/shard_map/ppermute | solution.py:534
  33.8 1.3 collective-permute-start.9
  35.0 3.3 %collective-permute-start.11 = (f32[72,8,128]{2,1,0:T(8,128)S(1)}, f32[72,8,128]{2,1,0:T(8,128)S(1)}, u32[]{:S(2)}, u32[]{:S(2)}) collective-permute-start(f32[72,8,128]{2,1,0:T(8,128)S(1)} %get-tuple-element.80), channel_id=1, source_target_pairs={{0,8},{8,16},{16,24},{24,25},{25,17},{17,9},{9,1},{1,2},{2,10},{10... | collective-permute-start | bytes 884744 | tf_op jit(solution)/shard_map/ppermute | solution.py:602
  38.4 1.6 %maps.1.refs_3_ = f32[4,64,128]{2,1,0:T(8,128)S(1)} custom-call(s32[135]{0:T(256)S(1)} %concatenate.3.scal.ints, f32[3,4,16,128]{3,2,1,0:T(8,128)S(1)} %get-tuple-element.82.ids), custom_call_target="tpu_custom_call" | custom-call | flops 2000000000 | bytes 4000000 | tf_op jit(solution)/shard_map/maps/pallas_call | solution.py:585
  40.1 0.1 collective-permute-start.13
  40.2 5.1 %collective-permute-done.11.refs_1_ = f32[72,8,128]{2,1,0:T(8,128)S(1)} collective-permute-done((f32[72,8,128]{2,1,0:T(8,128)S(1)}, f32[72,8,128]{2,1,0:T(8,128)S(1)}, u32[]{:S(2)}, u32[]{:S(2)}) %collective-permute-start.11) | collective-permute-done | bytes 294944 | tf_op jit(solution)/shard_map/ppermute | solution.py:602
  45.3 0.8 collective-permute-done.12.refs_2_
  46.0 4.4 %step0.1 = (f32[4,16,32,128]{3,2,1,0:T(8,128)S(1)}, f32[68,8,128]{2,1,0:T(8,128)S(1)}, f32[68,8,128]{2,1,0:T(8,128)S(1)}, f32[2,32,128]{2,1,0:T(8,128)S(1)}, f32...) custom-call(f32[4,16,32,128]{3,2,1,0:T(8,128)S(1)} %get-tuple-element.79.refs_0_, ...), custom_call_target="tpu_custom_call" | custom-call | flops 6000000000 | bytes 4000000 | tf_op jit(solution)/shard_map/step0/pallas_call | solution.py:615
  50.4 0.1 collective-permute-start.14
  50.5 0.1 mul.30
  50.6 1.0 collective-permute-done.14
  51.7 3.3 %collective-permute-start.16 = (f32[8,128]{1,0:T(8,128)S(1)}, f32[8,128]{1,0:T(8,128)S(1)}, u32[]{:S(2)}, u32[]{:S(2)}) collective-permute-start(f32[8,128]{1,0:T(8,128)S(1)} %add.99), channel_id=1, source_target_pairs={{0,2},{1,3},{2,0},{3,1},{4,6},{5,7},{6,4},{7,5},{8,10},{9,11},{10,... | collective-permute-start | bytes 12296 | tf_op jit(solution)/shard_map/ppermute | solution.py:534
  54.9 0.6 collective-permute-start.17
  55.5 4.0 %collective-permute-start.18 = (f32[68,8,128]{2,1,0:T(8,128)S(1)}, f32[68,8,128]{2,1,0:T(8,128)S(1)}, u32[]{:S(2)}, u32[]{:S(2)}) collective-permute-start(f32[68,8,128]{2,1,0:T(8,128)S(1)} %get-tuple-element.95), channel_id=1, source_target_pairs={{0,8},{8,16},{16,24},{24,25},{25,17},{17,9},{9,1},{1,2},{2,10},{10... | collective-permute-start | bytes 835592 | tf_op jit(solution)/shard_map/ppermute | solution.py:602
  59.6 2.7 %collective-permute-start.20 = (f32[8,128]{1,0:T(8,128)S(1)}, f32[8,128]{1,0:T(8,128)S(1)}, u32[]{:S(2)}, u32[]{:S(2)}) collective-permute-start(f32[8,128]{1,0:T(8,128)S(1)} %add_add_fusion.3), channel_id=1, source_target_pairs={{0,16},{8,24},{16,0},{24,8},{1,17},{9,25},{17,1},{25,9},{2,18},{10... | collective-permute-start | bytes 12296 | tf_op jit(solution)/shard_map/ppermute | solution.py:534
  62.4 3.1 %collective-permute-done.18.refs_1_ = f32[68,8,128]{2,1,0:T(8,128)S(1)} collective-permute-done((f32[68,8,128]{2,1,0:T(8,128)S(1)}, f32[68,8,128]{2,1,0:T(8,128)S(1)}, u32[]{:S(2)}, u32[]{:S(2)}) %collective-permute-start.18) | collective-permute-done | bytes 278560 | tf_op jit(solution)/shard_map/ppermute | solution.py:602
  65.4 1.6 %collective-permute-done.19.refs_2_ = f32[68,8,128]{2,1,0:T(8,128)S(1)} collective-permute-done((f32[68,8,128]{2,1,0:T(8,128)S(1)}, f32[68,8,128]{2,1,0:T(8,128)S(1)}, u32[]{:S(2)}, u32[]{:S(2)}) %collective-permute-start.19) | collective-permute-done | bytes 278560 | tf_op jit(solution)/shard_map/ppermute | solution.py:603
  67.1 5.0 %step1.1 = (f32[4,16,32,128]{3,2,1,0:T(8,128)S(1)}, f32[68,8,128]{2,1,0:T(8,128)S(1)}, f32[68,8,128]{2,1,0:T(8,128)S(1)}, f32[2,32,128]{2,1,0:T(8,128)S(1)}, f32[8,128]{1,0:T(8,128)S(1)}) custom-call(f32[4,16,32,128]{3,2,1,0:T(8,128)S(1)} %get-tuple-element.94.refs_0_, f32[68,8,128]{2,1,0:T(8,128)S(1)} %collective-permute-done.18.refs_1_, ...), custom_call_target="tpu_custom_call" | custom-call | flops 6000000000 | bytes 4000000 | tf_op jit(solution)/shard_map/step1/pallas_call | solution.py:615
  72.1 0.1 collective-permute-start.21
  72.2 1.1 collective-permute-done.21
  73.3 2.4 %collective-permute-start.25 = (f32[68,8,128]{2,1,0:T(8,128)S(1)}, f32[68,8,128]{2,1,0:T(8,128)S(1)}, u32[]{:S(2)}, u32[]{:S(2)}) collective-permute-start(f32[68,8,128]{2,1,0:T(8,128)S(1)} %get-tuple-element.110), channel_id=1, source_target_pairs={{0,8},{8,16},{16,24},{24,25},{25,17},{17,9},{9,1},{1,2},{2,10},{10... | collective-permute-start | bytes 835592 | tf_op jit(solution)/shard_map/ppermute | solution.py:602
  75.7 0.5 collective-permute-start.27
  76.2 4.2 %collective-permute-start.23 = (f32[8,128]{1,0:T(8,128)S(1)}, f32[8,128]{1,0:T(8,128)S(1)}, u32[]{:S(2)}, u32[]{:S(2)}) collective-permute-start(f32[8,128]{1,0:T(8,128)S(1)} %add.107), channel_id=1, source_target_pairs={{0,2},{1,3},{2,0},{3,1},{4,6},{5,7},{6,4},{7,5},{8,10},{9,11},{10,... | collective-permute-start | bytes 12296 | tf_op jit(solution)/shard_map/ppermute | solution.py:534
  80.4 2.8 %collective-permute-done.27 = f32[8,128]{1,0:T(8,128)S(1)} collective-permute-done((f32[8,128]{1,0:T(8,128)S(1)}, f32[8,128]{1,0:T(8,128)S(1)}, u32[]{:S(2)}, u32[]{:S(2)}) %collective-permute-start.27) | collective-permute-done | bytes 4128 | tf_op jit(solution)/shard_map/ppermute | solution.py:534
  83.2 3.1 %collective-permute-start.24 = (f32[8,128]{1,0:T(8,128)S(1)}, f32[8,128]{1,0:T(8,128)S(1)}, u32[]{:S(2)}, u32[]{:S(2)}) collective-permute-start(f32[8,128]{1,0:T(8,128)S(1)} %add.107), channel_id=1, source_target_pairs={{0,3},{1,2},{2,1},{3,0},{4,7},{5,6},{6,5},{7,4},{8,11},{9,10},{10,... | collective-permute-start | bytes 12296 | tf_op jit(solution)/shard_map/ppermute | solution.py:534
  86.3 1.0 collective-permute-done.24
  87.4 5.0 %step2.1 = (f32[4,16,32,128]{3,2,1,0:T(8,128)S(1)}, f32[68,8,128]{2,1,0:T(8,128)S(1)}, f32[68,8,128]{2,1,0:T(8,128)S(1)}, f32[2,32,128]{2,1,0:T(8,128)S(1)}, f32[8,128]{1,0:T(8,128)S(1)}) custom-call(f32[4,16,32,128]{3,2,1,0:T(8,128)S(1)} %get-tuple-element.109.refs_0_, f32[68,8,128]{2,1,0:T(8,128)S(1)} %collective-permute-done.25.refs_1_, ...), custom_call_target="tpu_custom_call" | custom-call | flops 6000000000 | bytes 4000000 | tf_op jit(solution)/shard_map/step2/pallas_call | solution.py:615
  92.4 2.9 %collective-permute-start.29 = (f32[8,128]{1,0:T(8,128)S(1)}, f32[8,128]{1,0:T(8,128)S(1)}, u32[]{:S(2)}, u32[]{:S(2)}) collective-permute-start(f32[8,128]{1,0:T(8,128)S(1)} %get-tuple-element.121), channel_id=1, source_target_pairs={{0,8},{8,0},{16,24},{24,16},{1,9},{9,1},{17,25},{25,17},{2,10},{10... | collective-permute-start | bytes 12296 | tf_op jit(solution)/shard_map/ppermute | solution.py:534
  95.2 0.8 collective-permute-done.29
  96.1 0.6 collective-permute-start.33
  96.6 1.6 %collective-permute-start.35 = (f32[8,128]{1,0:T(8,128)S(1)}, f32[8,128]{1,0:T(8,128)S(1)}, u32[]{:S(2)}, u32[]{:S(2)}) collective-permute-start(f32[8,128]{1,0:T(8,128)S(1)} %add.117), channel_id=1, source_target_pairs={{0,4},{1,5},{2,6},{3,7},{4,0},{5,1},{6,2},{7,3},{8,12},{9,13},{10,... | collective-permute-start | bytes 12296 | tf_op jit(solution)/shard_map/ppermute | solution.py:534
  98.2 4.1 %collective-permute-start.31 = (f32[8,128]{1,0:T(8,128)S(1)}, f32[8,128]{1,0:T(8,128)S(1)}, u32[]{:S(2)}, u32[]{:S(2)}) collective-permute-start(f32[8,128]{1,0:T(8,128)S(1)} %add.113), channel_id=1, source_target_pairs={{0,2},{1,3},{2,0},{3,1},{4,6},{5,7},{6,4},{7,5},{8,10},{9,11},{10,... | collective-permute-start | bytes 12296 | tf_op jit(solution)/shard_map/ppermute | solution.py:534
  102.3 3.0 %collective-permute-done.35 = f32[8,128]{1,0:T(8,128)S(1)} collective-permute-done((f32[8,128]{1,0:T(8,128)S(1)}, f32[8,128]{1,0:T(8,128)S(1)}, u32[]{:S(2)}, u32[]{:S(2)}) %collective-permute-start.35) | collective-permute-done | bytes 4128 | tf_op jit(solution)/shard_map/ppermute | solution.py:534
  105.3 2.8 %collective-permute-start.32 = (f32[8,128]{1,0:T(8,128)S(1)}, f32[8,128]{1,0:T(8,128)S(1)}, u32[]{:S(2)}, u32[]{:S(2)}) collective-permute-start(f32[8,128]{1,0:T(8,128)S(1)} %add.113), channel_id=1, source_target_pairs={{0,3},{1,2},{2,1},{3,0},{4,7},{5,6},{6,5},{7,4},{8,11},{9,10},{10,... | collective-permute-start | bytes 12296 | tf_op jit(solution)/shard_map/ppermute | solution.py:534
  108.1 1.0 collective-permute-done.32
  109.1 0.0 collective-permute-start.36
  109.1 4.9 %step3.1.fields = f32[4,16,32,128]{3,2,1,0:T(8,128)S(1)} custom-call(f32[4,16,32,128]{3,2,1,0:T(8,128)S(1)} %get-tuple-element.126.refs_0_, f32[68,8,128]{2,1,0:T(8,128)S(1)} %collective-permute-done.33.refs_1_, f32[68,8,128]{2,1,0:T(8,128)S(1)} %collective-permute-done.34.refs_2_, f32[4,64,128]{2,1,0:T(8,128)S(1)} %maps.1.refs_3_, ...), custom_call_target="tpu_custom_call" | custom-call | flops 6000000000 | bytes 4000000 | tf_op jit(solution)/shard_map/step3/pallas_call | solution.py:615
  114.1 1.2 send.1
  115.2 3.1 %collective-permute-start.38 = (f32[64,8,128]{2,1,0:T(8,128)S(1)}, f32[64,8,128]{2,1,0:T(8,128)S(1)}, u32[]{:S(2)}, u32[]{:S(2)}) collective-permute-start(f32[64,8,128]{2,1,0:T(8,128)S(1)} %get-tuple-element.132), channel_id=1, source_target_pairs={{0,8},{8,0},{16,24},{24,16},{1,9},{9,1},{17,25},{25,17},{2,10},{10... | collective-permute-start | bytes 786440 | tf_op jit(solution)/shard_map/ppermute | solution.py:534
  118.3 1.3 collective-permute-start.39
  119.6 2.0 %collective-permute-start.40 = (f32[64,8,128]{2,1,0:T(8,128)S(1)}, f32[64,8,128]{2,1,0:T(8,128)S(1)}, u32[]{:S(2)}, u32[]{:S(2)}) collective-permute-start(f32[64,8,128]{2,1,0:T(8,128)S(1)} %get-tuple-element.134), channel_id=1, source_target_pairs={{0,24},{8,16},{16,8},{24,0},{1,25},{9,17},{17,9},{25,1},{2,26},{10... | collective-permute-start | bytes 786440 | tf_op jit(solution)/shard_map/ppermute | solution.py:534
  121.6 9.8 %collective-permute-done.37 = f32[8,128]{1,0:T(8,128)S(1)} collective-permute-done((f32[8,128]{1,0:T(8,128)S(1)}, f32[8,128]{1,0:T(8,128)S(1)}, u32[]{:S(2)}, u32[]{:S(2)}) %collective-permute-start.37) | collective-permute-done | bytes 4128 | tf_op jit(solution)/shard_map/ppermute | solution.py:534
  131.4 2.1 %collective-permute-done.40.r3 = f32[64,8,128]{2,1,0:T(8,128)S(1)} collective-permute-done((f32[64,8,128]{2,1,0:T(8,128)S(1)}, f32[64,8,128]{2,1,0:T(8,128)S(1)}, u32[]{:S(2)}, u32[]{:S(2)}) %collective-permute-start.40) | collective-permute-done | bytes 262176 | tf_op jit(solution)/shard_map/ppermute | solution.py:534
  133.5 3.1 %final.1 = f32[4,16,32,128]{3,2,1,0:T(8,128)} custom-call(s32[135]{0:T(256)S(1)} %concatenate.3.scal.ints, f32[8,128]{1,0:T(8,128)S(1)} %add.120.mean, f32[64,8,128]{2,1,0:T(8,128)S(1)} %get-tuple-element.131.s0, f32[64,8,128]{2,1,0:T(8,128)S(1)} %collective-permute-done.38.r1, f32[64,8,128]{2,1,0:T(8,128)S(1)} %collective-permute-done.39.r2, ...), custom_call_target="tpu_custom_call" | custom-call | flops 2000000000 | bytes 4000000 | tf_op jit(solution)/shard_map/final/pallas_call | solution.py:643
  (59 shorter events, 0.2 us)
Async XLA Ops:
  0.0 6.3 %copy-start.1 = (f32[2,4,32,128]{3,2,1,0:T(8,128)S(1)}, f32[2,4,32,128]{3,2,1,0:T(8,128)}, u32[]{:S(2)}) copy-start(f32[2,4,32,128]{3,2,1,0:T(8,128)} %planes.1) | copy-start | bytes 393220
  0.9 5.4 %collective-permute-start = (f32[16,128]{1,0:T(8,128)S(1)}, f32[16,128]{1,0:T(8,128)S(1)}, u32[]{:S(2)}, u32[]{:S(2)}) collective-permute-start(f32[16,128]{1,0:T(8,128)S(1)} %get-tuple-element.136), channel_id=1, source_target_pairs={{0,1},{1,2},{2,3},{3,4},{4,5},{5,6},{6,7},{7,0},{8,9},{9,10},{10,1... | collective-permute-start | bytes 24584 | tf_op jit(solution)/shard_map/ppermute | solution.py:553
  2.9 3.3 %collective-permute-start.1 = (f32[16,128]{1,0:T(8,128)S(1)}, f32[16,128]{1,0:T(8,128)S(1)}, u32[]{:S(2)}, u32[]{:S(2)}) collective-permute-start(f32[16,128]{1,0:T(8,128)S(1)} %get-tuple-element.136), channel_id=1, source_target_pairs={{1,0},{2,1},{3,2},{4,3},{5,4},{6,5},{7,6},{0,7},{9,8},{10,9},{11,1... | collective-permute-start | bytes 24584 | tf_op jit(solution)/shard_map/ppermute | solution.py:553
  6.3 1.2 copy-start
  9.5 5.2 %collective-permute-start.2 = (f32[71,8,128]{2,1,0:T(8,128)S(1)}, f32[71,8,128]{2,1,0:T(8,128)S(1)}, u32[]{:S(2)}, u32[]{:S(2)}) collective-permute-start(f32[71,8,128]{2,1,0:T(8,128)S(1)} %get-tuple-element.71), channel_id=1, source_target_pairs={{0,8},{8,0},{16,24},{24,16},{1,9},{9,1},{17,25},{25,17},{2,10},{10... | collective-permute-start | bytes 872456 | tf_op jit(solution)/shard_map/ppermute | solution.py:534
  11.5 10.1 %collective-permute-start.3 = (f32[71,8,128]{2,1,0:T(8,128)S(1)}, f32[71,8,128]{2,1,0:T(8,128)S(1)}, u32[]{:S(2)}, u32[]{:S(2)}) collective-permute-start(f32[71,8,128]{2,1,0:T(8,128)S(1)} %get-tuple-element.74), channel_id=1, source_target_pairs={{0,16},{8,24},{16,0},{24,8},{1,17},{9,25},{17,1},{25,9},{2,18},{10... | collective-permute-start | bytes 872456 | tf_op jit(solution)/shard_map/ppermute | solution.py:534
  14.5 13.4 %collective-permute-start.4 = (f32[71,8,128]{2,1,0:T(8,128)S(1)}, f32[71,8,128]{2,1,0:T(8,128)S(1)}, u32[]{:S(2)}, u32[]{:S(2)}) collective-permute-start(f32[71,8,128]{2,1,0:T(8,128)S(1)} %get-tuple-element.75), channel_id=1, source_target_pairs={{0,24},{8,16},{16,8},{24,0},{1,25},{9,17},{17,9},{25,1},{2,26},{10... | collective-permute-start | bytes 872456 | tf_op jit(solution)/shard_map/ppermute | solution.py:534
  14.7 13.2 %collective-permute-start.5 = (f32[8,8,128]{2,1,0:T(8,128)S(1)}, f32[8,8,128]{2,1,0:T(8,128)S(1)}, u32[]{:S(2)}, u32[]{:S(2)}) collective-permute-start(f32[8,8,128]{2,1,0:T(8,128)S(1)} %get-tuple-element.76.p0), channel_id=1, source_target_pairs={{0,32},{32,0},{64,96},{96,64},{1,33},{33,1},{65,97},{97,65},{2,34}... | collective-permute-start | bytes 98312 | tf_op jit(solution)/shard_map/ppermute | solution.py:534
  16.5 11.4 %collective-permute-start.6 = (f32[8,8,128]{2,1,0:T(8,128)S(1)}, f32[8,8,128]{2,1,0:T(8,128)S(1)}, u32[]{:S(2)}, u32[]{:S(2)}) collective-permute-start(f32[8,8,128]{2,1,0:T(8,128)S(1)} %get-tuple-element.76.p0), channel_id=1, source_target_pairs={{0,64},{32,96},{64,0},{96,32},{1,65},{33,97},{65,1},{97,33},{2,66}... | collective-permute-start | bytes 98312 | tf_op jit(solution)/shard_map/ppermute | solution.py:534
  19.8 8.1 %collective-permute-start.7 = (f32[8,8,128]{2,1,0:T(8,128)S(1)}, f32[8,8,128]{2,1,0:T(8,128)S(1)}, u32[]{:S(2)}, u32[]{:S(2)}) collective-permute-start(f32[8,8,128]{2,1,0:T(8,128)S(1)} %get-tuple-element.76.p0), channel_id=1, source_target_pairs={{0,96},{32,64},{64,32},{96,0},{1,97},{33,65},{65,33},{97,1},{2,98}... | collective-permute-start | bytes 98312 | tf_op jit(solution)/shard_map/ppermute | solution.py:534
  29.7 10.4 %collective-permute-start.10 = (f32[8,128]{1,0:T(8,128)S(1)}, f32[8,128]{1,0:T(8,128)S(1)}, u32[]{:S(2)}, u32[]{:S(2)}) collective-permute-start(f32[8,128]{1,0:T(8,128)S(1)} %get-tuple-element.78), channel_id=1, source_target_pairs={{0,3},{1,2},{2,1},{3,0},{4,7},{5,6},{6,5},{7,4},{8,11},{9,10},{10,... | collective-permute-start | bytes 12296 | tf_op jit(solution)/shard_map/ppermute | solution.py:534
  33.8 6.3 %collective-permute-start.8 = (f32[8,128]{1,0:T(8,128)S(1)}, f32[8,128]{1,0:T(8,128)S(1)}, u32[]{:S(2)}, u32[]{:S(2)}) collective-permute-start(f32[8,128]{1,0:T(8,128)S(1)} %get-tuple-element.78), channel_id=1, source_target_pairs={{0,1},{1,0},{2,3},{3,2},{4,5},{5,4},{6,7},{7,6},{8,9},{9,8},{10,11... | collective-permute-start | bytes 12296 | tf_op jit(solution)/shard_map/ppermute | solution.py:534
  33.8 6.3 %collective-permute-start.9 = (f32[8,128]{1,0:T(8,128)S(1)}, f32[8,128]{1,0:T(8,128)S(1)}, u32[]{:S(2)}, u32[]{:S(2)}) collective-permute-start(f32[8,128]{1,0:T(8,128)S(1)} %get-tuple-element.78), channel_id=1, source_target_pairs={{0,2},{1,3},{2,0},{3,1},{4,6},{5,7},{6,4},{7,5},{8,10},{9,11},{10,... | collective-permute-start | bytes 12296 | tf_op jit(solution)/shard_map/ppermute | solution.py:534
  35.0 10.2 %collective-permute-start.11 = (f32[72,8,128]{2,1,0:T(8,128)S(1)}, f32[72,8,128]{2,1,0:T(8,128)S(1)}, u32[]{:S(2)}, u32[]{:S(2)}) collective-permute-start(f32[72,8,128]{2,1,0:T(8,128)S(1)} %get-tuple-element.80), channel_id=1, source_target_pairs={{0,8},{8,16},{16,24},{24,25},{25,17},{17,9},{9,1},{1,2},{2,10},{10... | collective-permute-start | bytes 884744 | tf_op jit(solution)/shard_map/ppermute | solution.py:602
  38.4 7.7 %collective-permute-start.12 = (f32[72,8,128]{2,1,0:T(8,128)S(1)}, f32[72,8,128]{2,1,0:T(8,128)S(1)}, u32[]{:S(2)}, u32[]{:S(2)}) collective-permute-start(f32[72,8,128]{2,1,0:T(8,128)S(1)} %get-tuple-element.81), channel_id=1, source_target_pairs={{8,0},{16,8},{24,16},{25,24},{17,25},{9,17},{1,9},{2,1},{10,2},{18... | collective-permute-start | bytes 884744 | tf_op jit(solution)/shard_map/ppermute | solution.py:603
  40.1 10.5 %collective-permute-start.13 = (f32[8,128]{1,0:T(8,128)S(1)}, f32[8,128]{1,0:T(8,128)S(1)}, u32[]{:S(2)}, u32[]{:S(2)}) collective-permute-start(f32[8,128]{1,0:T(8,128)S(1)} %add_add_fusion.4), channel_id=1, source_target_pairs={{0,4},{1,5},{2,6},{3,7},{4,0},{5,1},{6,2},{7,3},{8,12},{9,13},{10,... | collective-permute-start | bytes 12296 | tf_op jit(solution)/shard_map/ppermute | solution.py:534
  50.4 1.2 collective-permute-start.14
  51.7 7.9 %collective-permute-start.15 = (f32[8,128]{1,0:T(8,128)S(1)}, f32[8,128]{1,0:T(8,128)S(1)}, u32[]{:S(2)}, u32[]{:S(2)}) collective-permute-start(f32[8,128]{1,0:T(8,128)S(1)} %add.99), channel_id=1, source_target_pairs={{0,1},{1,0},{2,3},{3,2},{4,5},{5,4},{6,7},{7,6},{8,9},{9,8},{10,11... | collective-permute-start | bytes 12296 | tf_op jit(solution)/shard_map/ppermute | solution.py:534
  51.7 7.9 %collective-permute-start.16 = (f32[8,128]{1,0:T(8,128)S(1)}, f32[8,128]{1,0:T(8,128)S(1)}, u32[]{:S(2)}, u32[]{:S(2)}) collective-permute-start(f32[8,128]{1,0:T(8,128)S(1)} %add.99), channel_id=1, source_target_pairs={{0,2},{1,3},{2,0},{3,1},{4,6},{5,7},{6,4},{7,5},{8,10},{9,11},{10,... | collective-permute-start | bytes 12296 | tf_op jit(solution)/shard_map/ppermute | solution.py:534
  54.9 4.7 %collective-permute-start.17 = (f32[8,128]{1,0:T(8,128)S(1)}, f32[8,128]{1,0:T(8,128)S(1)}, u32[]{:S(2)}, u32[]{:S(2)}) collective-permute-start(f32[8,128]{1,0:T(8,128)S(1)} %add.99), channel_id=1, source_target_pairs={{0,3},{1,2},{2,1},{3,0},{4,7},{5,6},{6,5},{7,4},{8,11},{9,10},{10,... | collective-permute-start | bytes 12296 | tf_op jit(solution)/shard_map/ppermute | solution.py:534
  55.5 9.9 %collective-permute-start.18 = (f32[68,8,128]{2,1,0:T(8,128)S(1)}, f32[68,8,128]{2,1,0:T(8,128)S(1)}, u32[]{:S(2)}, u32[]{:S(2)}) collective-permute-start(f32[68,8,128]{2,1,0:T(8,128)S(1)} %get-tuple-element.95), channel_id=1, source_target_pairs={{0,8},{8,16},{16,24},{24,25},{25,17},{17,9},{9,1},{1,2},{2,10},{10... | collective-permute-start | bytes 835592 | tf_op jit(solution)/shard_map/ppermute | solution.py:602
  59.6 7.5 %collective-permute-start.19 = (f32[68,8,128]{2,1,0:T(8,128)S(1)}, f32[68,8,128]{2,1,0:T(8,128)S(1)}, u32[]{:S(2)}, u32[]{:S(2)}) collective-permute-start(f32[68,8,128]{2,1,0:T(8,128)S(1)} %get-tuple-element.96), channel_id=1, source_target_pairs={{8,0},{16,8},{24,16},{25,24},{17,25},{9,17},{1,9},{2,1},{10,2},{18... | collective-permute-start | bytes 835592 | tf_op jit(solution)/shard_map/ppermute | solution.py:603
  59.6 12.5 %collective-permute-start.20 = (f32[8,128]{1,0:T(8,128)S(1)}, f32[8,128]{1,0:T(8,128)S(1)}, u32[]{:S(2)}, u32[]{:S(2)}) collective-permute-start(f32[8,128]{1,0:T(8,128)S(1)} %add_add_fusion.3), channel_id=1, source_target_pairs={{0,16},{8,24},{16,0},{24,8},{1,17},{9,25},{17,1},{25,9},{2,18},{10... | collective-permute-start | bytes 12296 | tf_op jit(solution)/shard_map/ppermute | solution.py:534
  72.1 1.2 collective-permute-start.21
  73.3 14.0 %collective-permute-start.25 = (f32[68,8,128]{2,1,0:T(8,128)S(1)}, f32[68,8,128]{2,1,0:T(8,128)S(1)}, u32[]{:S(2)}, u32[]{:S(2)}) collective-permute-start(f32[68,8,128]{2,1,0:T(8,128)S(1)} %get-tuple-element.110), channel_id=1, source_target_pairs={{0,8},{8,16},{16,24},{24,25},{25,17},{17,9},{9,1},{1,2},{2,10},{10... | collective-permute-start | bytes 835592 | tf_op jit(solution)/shard_map/ppermute | solution.py:602
  75.7 11.7 %collective-permute-start.26 = (f32[68,8,128]{2,1,0:T(8,128)S(1)}, f32[68,8,128]{2,1,0:T(8,128)S(1)}, u32[]{:S(2)}, u32[]{:S(2)}) collective-permute-start(f32[68,8,128]{2,1,0:T(8,128)S(1)} %get-tuple-element.111), channel_id=1, source_target_pairs={{8,0},{16,8},{24,16},{25,24},{17,25},{9,17},{1,9},{2,1},{10,2},{18... | collective-permute-start | bytes 835592 | tf_op jit(solution)/shard_map/ppermute | solution.py:603
  75.7 7.5 %collective-permute-start.27 = (f32[8,128]{1,0:T(8,128)S(1)}, f32[8,128]{1,0:T(8,128)S(1)}, u32[]{:S(2)}, u32[]{:S(2)}) collective-permute-start(f32[8,128]{1,0:T(8,128)S(1)} %add.111), channel_id=1, source_target_pairs={{0,4},{1,5},{2,6},{3,7},{4,0},{5,1},{6,2},{7,3},{8,12},{9,13},{10,... | collective-permute-start | bytes 12296 | tf_op jit(solution)/shard_map/ppermute | solution.py:534
  76.2 10.1 %collective-permute-start.22 = (f32[8,128]{1,0:T(8,128)S(1)}, f32[8,128]{1,0:T(8,128)S(1)}, u32[]{:S(2)}, u32[]{:S(2)}) collective-permute-start(f32[8,128]{1,0:T(8,128)S(1)} %add.107), channel_id=1, source_target_pairs={{0,1},{1,0},{2,3},{3,2},{4,5},{5,4},{6,7},{7,6},{8,9},{9,8},{10,11... | collective-permute-start | bytes 12296 | tf_op jit(solution)/shard_map/ppermute | solution.py:534
  76.2 10.1 %collective-permute-start.23 = (f32[8,128]{1,0:T(8,128)S(1)}, f32[8,128]{1,0:T(8,128)S(1)}, u32[]{:S(2)}, u32[]{:S(2)}) collective-permute-start(f32[8,128]{1,0:T(8,128)S(1)} %add.107), channel_id=1, source_target_pairs={{0,2},{1,3},{2,0},{3,1},{4,6},{5,7},{6,4},{7,5},{8,10},{9,11},{10,... | collective-permute-start | bytes 12296 | tf_op jit(solution)/shard_map/ppermute | solution.py:534
  83.2 4.1 %collective-permute-start.24 = (f32[8,128]{1,0:T(8,128)S(1)}, f32[8,128]{1,0:T(8,128)S(1)}, u32[]{:S(2)}, u32[]{:S(2)}) collective-permute-start(f32[8,128]{1,0:T(8,128)S(1)} %add.107), channel_id=1, source_target_pairs={{0,3},{1,2},{2,1},{3,0},{4,7},{5,6},{6,5},{7,4},{8,11},{9,10},{10,... | collective-permute-start | bytes 12296 | tf_op jit(solution)/shard_map/ppermute | solution.py:534
  87.3 7.9 %collective-permute-start.28 = (f32[8,128]{1,0:T(8,128)S(1)}, f32[8,128]{1,0:T(8,128)S(1)}, u32[]{:S(2)}, u32[]{:S(2)}) collective-permute-start(f32[8,128]{1,0:T(8,128)S(1)} %add_add_fusion.1), channel_id=1, source_target_pairs={{0,16},{8,24},{16,0},{24,8},{1,17},{9,25},{17,1},{25,9},{2,18},{10... | collective-permute-start | bytes 12296 | tf_op jit(solution)/shard_map/ppermute | solution.py:534
  92.4 3.7 %collective-permute-start.29 = (f32[8,128]{1,0:T(8,128)S(1)}, f32[8,128]{1,0:T(8,128)S(1)}, u32[]{:S(2)}, u32[]{:S(2)}) collective-permute-start(f32[8,128]{1,0:T(8,128)S(1)} %get-tuple-element.121), channel_id=1, source_target_pairs={{0,8},{8,0},{16,24},{24,16},{1,9},{9,1},{17,25},{25,17},{2,10},{10... | collective-permute-start | bytes 12296 | tf_op jit(solution)/shard_map/ppermute | solution.py:534
  96.1 13.1 %collective-permute-start.33 = (f32[68,8,128]{2,1,0:T(8,128)S(1)}, f32[68,8,128]{2,1,0:T(8,128)S(1)}, u32[]{:S(2)}, u32[]{:S(2)}) collective-permute-start(f32[68,8,128]{2,1,0:T(8,128)S(1)} %get-tuple-element.124), channel_id=1, source_target_pairs={{0,8},{8,16},{16,24},{24,25},{25,17},{17,9},{9,1},{1,2},{2,10},{10... | collective-permute-start | bytes 835592 | tf_op jit(solution)/shard_map/ppermute | solution.py:602
  96.6 12.5 %collective-permute-start.34 = (f32[68,8,128]{2,1,0:T(8,128)S(1)}, f32[68,8,128]{2,1,0:T(8,128)S(1)}, u32[]{:S(2)}, u32[]{:S(2)}) collective-permute-start(f32[68,8,128]{2,1,0:T(8,128)S(1)} %get-tuple-element.125), channel_id=1, source_target_pairs={{8,0},{16,8},{24,16},{25,24},{17,25},{9,17},{1,9},{2,1},{10,2},{18... | collective-permute-start | bytes 835592 | tf_op jit(solution)/shard_map/ppermute | solution.py:603
  96.6 8.7 %collective-permute-start.35 = (f32[8,128]{1,0:T(8,128)S(1)}, f32[8,128]{1,0:T(8,128)S(1)}, u32[]{:S(2)}, u32[]{:S(2)}) collective-permute-start(f32[8,128]{1,0:T(8,128)S(1)} %add.117), channel_id=1, source_target_pairs={{0,4},{1,5},{2,6},{3,7},{4,0},{5,1},{6,2},{7,3},{8,12},{9,13},{10,... | collective-permute-start | bytes 12296 | tf_op jit(solution)/shard_map/ppermute | solution.py:534
  98.2 9.9 %collective-permute-start.30 = (f32[8,128]{1,0:T(8,128)S(1)}, f32[8,128]{1,0:T(8,128)S(1)}, u32[]{:S(2)}, u32[]{:S(2)}) collective-permute-start(f32[8,128]{1,0:T(8,128)S(1)} %add.113), channel_id=1, source_target_pairs={{0,1},{1,0},{2,3},{3,2},{4,5},{5,4},{6,7},{7,6},{8,9},{9,8},{10,11... | collective-permute-start | bytes 12296 | tf_op jit(solution)/shard_map/ppermute | solution.py:534
  98.2 9.9 %collective-permute-start.31 = (f32[8,128]{1,0:T(8,128)S(1)}, f32[8,128]{1,0:T(8,128)S(1)}, u32[]{:S(2)}, u32[]{:S(2)}) collective-permute-start(f32[8,128]{1,0:T(8,128)S(1)} %add.113), channel_id=1, source_target_pairs={{0,2},{1,3},{2,0},{3,1},{4,6},{5,7},{6,4},{7,5},{8,10},{9,11},{10,... | collective-permute-start | bytes 12296 | tf_op jit(solution)/shard_map/ppermute | solution.py:534
  105.3 3.8 %collective-permute-start.32 = (f32[8,128]{1,0:T(8,128)S(1)}, f32[8,128]{1,0:T(8,128)S(1)}, u32[]{:S(2)}, u32[]{:S(2)}) collective-permute-start(f32[8,128]{1,0:T(8,128)S(1)} %add.113), channel_id=1, source_target_pairs={{0,3},{1,2},{2,1},{3,0},{4,7},{5,6},{6,5},{7,4},{8,11},{9,10},{10,... | collective-permute-start | bytes 12296 | tf_op jit(solution)/shard_map/ppermute | solution.py:534
  109.1 4.9 %collective-permute-start.36 = (f32[8,128]{1,0:T(8,128)S(1)}, f32[8,128]{1,0:T(8,128)S(1)}, u32[]{:S(2)}, u32[]{:S(2)}) collective-permute-start(f32[8,128]{1,0:T(8,128)S(1)} %add_add_fusion), channel_id=1, source_target_pairs={{0,16},{8,24},{16,0},{24,8},{1,17},{9,25},{17,1},{25,9},{2,18},{10... | collective-permute-start | bytes 12296 | tf_op jit(solution)/shard_map/ppermute | solution.py:534
  115.2 16.2 %collective-permute-start.38 = (f32[64,8,128]{2,1,0:T(8,128)S(1)}, f32[64,8,128]{2,1,0:T(8,128)S(1)}, u32[]{:S(2)}, u32[]{:S(2)}) collective-permute-start(f32[64,8,128]{2,1,0:T(8,128)S(1)} %get-tuple-element.132), channel_id=1, source_target_pairs={{0,8},{8,0},{16,24},{24,16},{1,9},{9,1},{17,25},{25,17},{2,10},{10... | collective-permute-start | bytes 786440 | tf_op jit(solution)/shard_map/ppermute | solution.py:534
  118.3 13.1 %collective-permute-start.39 = (f32[64,8,128]{2,1,0:T(8,128)S(1)}, f32[64,8,128]{2,1,0:T(8,128)S(1)}, u32[]{:S(2)}, u32[]{:S(2)}) collective-permute-start(f32[64,8,128]{2,1,0:T(8,128)S(1)} %get-tuple-element.133), channel_id=1, source_target_pairs={{0,16},{8,24},{16,0},{24,8},{1,17},{9,25},{17,1},{25,9},{2,18},{10... | collective-permute-start | bytes 786440 | tf_op jit(solution)/shard_map/ppermute | solution.py:534
  119.6 14.0 %collective-permute-start.40 = (f32[64,8,128]{2,1,0:T(8,128)S(1)}, f32[64,8,128]{2,1,0:T(8,128)S(1)}, u32[]{:S(2)}, u32[]{:S(2)}) collective-permute-start(f32[64,8,128]{2,1,0:T(8,128)S(1)} %get-tuple-element.134), channel_id=1, source_target_pairs={{0,24},{8,16},{16,8},{24,0},{1,25},{9,17},{17,9},{25,1},{2,26},{10... | collective-permute-start | bytes 786440 | tf_op jit(solution)/shard_map/ppermute | solution.py:534
  121.6 9.8 %collective-permute-start.37 = (f32[8,128]{1,0:T(8,128)S(1)}, f32[8,128]{1,0:T(8,128)S(1)}, u32[]{:S(2)}, u32[]{:S(2)}) collective-permute-start(f32[8,128]{1,0:T(8,128)S(1)} %add.119), channel_id=1, source_target_pairs={{0,4},{1,5},{2,6},{3,7},{4,0},{5,1},{6,2},{7,3},{8,12},{9,13},{10,... | collective-permute-start | bytes 12296 | tf_op jit(solution)/shard_map/ppermute | solution.py:534

commit v8 on v7

--- a/solution.py
+++ b/solution.py
@@ -120,20 +120,36 @@
     return out
 
 
-def pack_kernel(scal, state, planes, ids, s0, s1, s2, s3, pl_out):
+def transposed4(a, odd, high):
+    b0 = jnp.where(odd, pltpu.roll(a[1], 32, axis=1), a[0])
+    b1 = jnp.where(odd, a[1], pltpu.roll(a[0], 96, axis=1))
+    b2 = jnp.where(odd, pltpu.roll(a[3], 32, axis=1), a[2])
+    b3 = jnp.where(odd, a[3], pltpu.roll(a[2], 96, axis=1))
+    return (
+        jnp.where(high, pltpu.roll(b2, 64, axis=1), b0),
+        jnp.where(high, pltpu.roll(b3, 64, axis=1), b1),
+        jnp.where(high, b2, pltpu.roll(b0, 64, axis=1)),
+        jnp.where(high, b3, pltpu.roll(b1, 64, axis=1)),
+    )
+
+
+def pack_kernel(scal, state, planes, ids, s0, s1, s2, s3, pl_out, stage):
     slab = scal[1]
     group = lanes() >> 5
     masks = [group == c for c in range(4)]
     outs = (s0, s1, s2, s3)
+    odd, high = (group & 1) == 1, group >= 2
 
     def per_row(x, total):
         for kt in range(4):
             sources = [state[c, x, kt * 8 : kt * 8 + 8, :] for c in range(4)]
-            for s, out in enumerate(outs):
-                out[x * 4 + kt] = block_transposed(sources, slab ^ s, masks)
+            for b, value in enumerate(transposed4(sources, odd, high)):
+                stage[b, x * 4 + kt] = value
         return total + state[3, x]
 
     total = rows("fill", per_row, jnp.zeros((NZ, LANES), F32))
+    for s, out in enumerate(outs):
+        out[:TILES] = stage[slab ^ s]
     levels = jnp.concatenate([total] * GX, axis=0).T
     levels = jnp.broadcast_to(jnp.sum(levels, axis=0, keepdims=True), (8, LANES))
     for out in outs:
@@ -497,22 +513,20 @@
     rows("fill", per_row)
 
 
-def final_kernel(scal, mean, s0, r1, r2, r3, out, columns, *, cells):
+def final_kernel(scal, mean, s0, r1, r2, r3, out, columns, stage, *, cells):
     own, slab = scal[0], scal[1]
+    for s, source in enumerate((s0, r1, r2, r3)):
+        stage[slab ^ s] = source[...]
     du, dw = mean_response(mean[0:1, :] * F32(1.0 / cells))
     pad = jnp.zeros((LANES - 2 * XI, LANES), F32)
     columns[...] = jnp.concatenate([du, dw, pad], axis=0).T
     own_columns = columns[pl.ds(pl.multiple_of(own * NZ, NZ), NZ), :]
     group = lanes() >> 5
-    masks = [group == (slab ^ s) for s in range(4)]
+    odd, high = (group & 1) == 1, group >= 2
     for x in range(XI):
         for kt in range(4):
-            sources = [ref[x * 4 + kt] for ref in (s0, r1, r2, r3)]
-            for c in range(4):
-                value = None
-                for s, source in enumerate(sources):
-                    moved = pltpu.roll(source, (((slab ^ s) - c) & 3) * 32, axis=1)
-                    value = moved if value is None else jnp.where(masks[s], moved, value)
+            sources = [stage[b, x * 4 + kt] for b in range(4)]
+            for c, value in enumerate(transposed4(sources, odd, high)):
                 if c in (0, 2):
                     column = (0 if c == 0 else XI) + x
                     value = value + own_columns[kt * 8 : kt * 8 + 8, column : column + 1]
@@ -556,6 +570,7 @@
         pack_kernel,
         (chunk, chunk, chunk, chunk, shape(per_layout * 4, 8, LANES)),
         [SMEM, VMEM, VMEM, VMEM],
+        [pltpu.VMEM((GX, TILES, 8, LANES), F32)],
         name="pack",
     )(scal, state[0], planes, ids)
     received = [swapped(value, "gx", GX, s) for s, value in ((1, s1), (2, s2), (3, s3))]
@@ -589,22 +604,21 @@
     def among_x(value):
         return sum([swapped(value, "gy", groups, d) for d in range(1, half)], value)
 
-    def last_swap(value):
-        return value + swapped(value, "gy", groups, half)
-
     mean = pending = None
     for step in range(STEPS):
         partial = sums
         if step > 0:
             partial = partial + swapped(partial, "gx", GX, 1)
             su, sd, partial = lax.optimization_barrier((su, sd, partial))
-            mean = last_swap(pending) if step > 1 else pending
+            mean = among_x(pending)
         lo = lax.ppermute(su, ("gx", "gy"), up)
         hi = lax.ppermute(sd, ("gx", "gy"), down)
-        fields, partial = lax.optimization_barrier((fields, among_x(partial)))
+        if step == 1:
+            mean = mean + cells * profile[3:4]
+        if step > 0:
+            partial = partial + swapped(partial, "gy", groups, half)
+            fields, partial = lax.optimization_barrier((fields, partial))
         arriving = swapped(partial, "gx", GX, 2) if step > 0 else swapped(partial, "gy", groups, half)
-        if step == 0:
-            partial = partial + cells * profile[3:4]
         outs = [shape(4, XI, OWN, LANES)]
         if step < STEPS - 1:
             payload = shape(TILES + MORE, 8, LANES)
@@ -629,7 +643,7 @@
             inflow = results.pop(0)
         su, sd, fields, arriving = lax.optimization_barrier((su, sd, fields, arriving))
         pending = partial + arriving
-    mean = last_swap(pending)
+    mean = among_x(pending)
 
     chunk = shape(TILES, 8, LANES)
     s0, s1, s2, s3 = call(
@@ -644,7 +658,7 @@
         functools.partial(final_kernel, cells=cells),
         shape(4, XI, NZ, LANES),
         [SMEM, VMEM] + [VMEM] * 4,
-        [pltpu.VMEM((LANES, LANES), F32)],
+        [pltpu.VMEM((LANES, LANES), F32), pltpu.VMEM((GX, TILES, 8, LANES), F32)],
         name="final",
     )(scal, mean, s0, *received)
     return fields[None]

time: 137 us -> 131 us (0.956)
  waiting for transfers between devices: 41.5 us -> 36.6 us
  starting transfers between devices: 62.6 us -> 58.9 us
  Pallas kernels: 29 us -> 31.8 us
    ppermute x31, starting transfers between devices: 47.9 us -> 42.4 us  [swapped(): return lax.ppermute(value, axis, [(i, i ^ distance) for i in range(size)])]
    ppermute x4, waiting for transfers between devices: 8.15 us -> 4.83 us  [local(): lo = lax.ppermute(su, ('gx', 'gy'), up)]
    pallas_call x1, Pallas kernels: 3.11 us -> 6.23 us  [local(): call(functools.partial(final_kernel, cells=cells), shape(4, XI, NZ, LANES...]
    ppermute x4, starting transfers between devices: 10.3 us -> 12.1 us  [local(): lo = lax.ppermute(su, ('gx', 'gy'), up)]
    ppermute x4, waiting for transfers between devices: 2.4 us -> 0.93 us  [local(): hi = lax.ppermute(sd, ('gx', 'gy'), down)]
  transfers between devices with their start and end apart: 41 -> 41, of which waited for: 16 -> 18; matrix products, arithmetic and copies ran while one was open for 1% -> 1% of each run, Pallas kernels for 15% -> 16%
where the time goes in v8:
time: 131 us
  starting transfers between devices  58.9 us (45%)
  waiting for transfers between devices  36.6 us (28%)
  Pallas kernels  31.8 us (24%)
  local copies, waits for them, and re-layouts  3.14 us (2%)
    ppermute x31, starting transfers between devices, swapped(): return lax.ppermute(value, axis, [(i, i ^ distance) for i in range(size)])  42.4 us
    ppermute x31, waiting for transfers between devices, swapped(): return lax.ppermute(value, axis, [(i, i ^ distance) for i in range(size)])  30.6 us
    pallas_call x4, Pallas kernels, local(): call(functools.partial(step_kernel, step=step, cells=cells), tuple(outs),...  19.3 us
    ppermute x4, starting transfers between devices, local(): lo = lax.ppermute(su, ('gx', 'gy'), up)  12.1 us
    pallas_call x1, Pallas kernels, local(): call(functools.partial(final_kernel, cells=cells), shape(4, XI, NZ, LANES...  6.23 us
    ppermute x4, waiting for transfers between devices, local(): lo = lax.ppermute(su, ('gx', 'gy'), up)  4.83 us
  transfers between devices with their start and end apart: 41, of which 18 were waited for; matrix products, arithmetic and copies ran while one was open for 1% of the time, Pallas kernels for 16%

profile of v8, /device:TPU:1, one launch (start us, length us, event | category | flops | bytes accessed | tf_op | source)
XLA Modules:
  0.0 130.9 jit_solution(1072197230663708093)
XLA Ops:
  0.0 0.9 slice.7
  0.9 2.0 %collective-permute-start = (f32[16,128]{1,0:T(8,128)S(1)}, f32[16,128]{1,0:T(8,128)S(1)}, u32[]{:S(2)}, u32[]{:S(2)}) collective-permute-start(f32[16,128]{1,0:T(8,128)S(1)} %get-tuple-element.132), channel_id=1, source_target_pairs={{0,1},{1,2},{2,3},{3,4},{4,5},{5,6},{6,7},{7,0},{8,9},{9,10},{10,1... | collective-permute-start | bytes 24584 | tf_op jit(solution)/shard_map/ppermute | solution.py:567
  2.9 2.4 %collective-permute-start.1 = (f32[16,128]{1,0:T(8,128)S(1)}, f32[16,128]{1,0:T(8,128)S(1)}, u32[]{:S(2)}, u32[]{:S(2)}) collective-permute-start(f32[16,128]{1,0:T(8,128)S(1)} %get-tuple-element.132), channel_id=1, source_target_pairs={{1,0},{2,1},{3,2},{4,3},{5,4},{6,5},{7,6},{0,7},{9,8},{10,9},{11,1... | collective-permute-start | bytes 24584 | tf_op jit(solution)/shard_map/ppermute | solution.py:567
  5.3 0.8 concatenate.3.scal.ints
  6.0 0.2 collective-permute-done
  6.3 0.0 copy-start
  6.3 1.2 copy-done
  7.5 1.7 %pack.1 = (f32[71,8,128]{2,1,0:T(8,128)S(1)}, f32[71,8,128]{2,1,0:T(8,128)S(1)}, f32[71,8,128]{2,1,0:T(8,128)S(1)}, f32[71,8,128]{2,1,0:T(8,128)S(1)}, f32[8,8,128]{2,1,0:T(8,128)S(1)}) custom-call(s32[135]{0:T(256)S(1)} %concatenate.3.scal.ints, f32[4,16,32,128]{3,2,1,0:T(8,128)S(1)} %bitcast.14, f32[2,4,32,128]{3,2,1,0:T(8,128)S(1)} %copy-done.1, ...), custom_call_target="tpu_custom_call" | custom-call | flops 2000000000 | bytes 4000000 | tf_op jit(solution)/shard_map/pack/pallas_call | solution.py:569
  9.2 1.9 %collective-permute-start.2 = (f32[71,8,128]{2,1,0:T(8,128)S(1)}, f32[71,8,128]{2,1,0:T(8,128)S(1)}, u32[]{:S(2)}, u32[]{:S(2)}) collective-permute-start(f32[71,8,128]{2,1,0:T(8,128)S(1)} %get-tuple-element.69), channel_id=1, source_target_pairs={{0,8},{8,0},{16,24},{24,16},{1,9},{9,1},{17,25},{25,17},{2,10},{10... | collective-permute-start | bytes 872456 | tf_op jit(solution)/shard_map/ppermute | solution.py:548
  11.1 0.1 pad.9.clone
  11.2 3.0 %collective-permute-start.3 = (f32[71,8,128]{2,1,0:T(8,128)S(1)}, f32[71,8,128]{2,1,0:T(8,128)S(1)}, u32[]{:S(2)}, u32[]{:S(2)}) collective-permute-start(f32[71,8,128]{2,1,0:T(8,128)S(1)} %get-tuple-element.72), channel_id=1, source_target_pairs={{0,16},{8,24},{16,0},{24,8},{1,17},{9,25},{17,1},{25,9},{2,18},{10... | collective-permute-start | bytes 872456 | tf_op jit(solution)/shard_map/ppermute | solution.py:548
  14.2 0.2 collective-permute-start.4
  14.4 1.8 %collective-permute-start.5 = (f32[8,8,128]{2,1,0:T(8,128)S(1)}, f32[8,8,128]{2,1,0:T(8,128)S(1)}, u32[]{:S(2)}, u32[]{:S(2)}) collective-permute-start(f32[8,8,128]{2,1,0:T(8,128)S(1)} %get-tuple-element.74.p0), channel_id=1, source_target_pairs={{0,32},{32,0},{64,96},{96,64},{1,33},{33,1},{65,97},{97,65},{2,34}... | collective-permute-start | bytes 98312 | tf_op jit(solution)/shard_map/ppermute | solution.py:548
  16.2 3.3 %collective-permute-start.6 = (f32[8,8,128]{2,1,0:T(8,128)S(1)}, f32[8,8,128]{2,1,0:T(8,128)S(1)}, u32[]{:S(2)}, u32[]{:S(2)}) collective-permute-start(f32[8,8,128]{2,1,0:T(8,128)S(1)} %get-tuple-element.74.p0), channel_id=1, source_target_pairs={{0,64},{32,96},{64,0},{96,32},{1,65},{33,97},{65,1},{97,33},{2,66}... | collective-permute-start | bytes 98312 | tf_op jit(solution)/shard_map/ppermute | solution.py:548
  19.5 0.1 pad_maximum_fusion.1
  19.6 0.1 tile.12
  19.7 1.6 %collective-permute-done.3.r2 = f32[71,8,128]{2,1,0:T(8,128)S(1)} collective-permute-done((f32[71,8,128]{2,1,0:T(8,128)S(1)}, f32[71,8,128]{2,1,0:T(8,128)S(1)}, u32[]{:S(2)}, u32[]{:S(2)}) %collective-permute-start.3) | collective-permute-done | bytes 290848 | tf_op jit(solution)/shard_map/ppermute | solution.py:548
  21.3 6.3 %collective-permute-done.4.r3 = f32[71,8,128]{2,1,0:T(8,128)S(1)} collective-permute-done((f32[71,8,128]{2,1,0:T(8,128)S(1)}, f32[71,8,128]{2,1,0:T(8,128)S(1)}, u32[]{:S(2)}, u32[]{:S(2)}) %collective-permute-start.4) | collective-permute-done | bytes 290848 | tf_op jit(solution)/shard_map/ppermute | solution.py:548
  27.7 1.7 %unpack.1 = (f32[4,16,32,128]{3,2,1,0:T(8,128)S(1)}, f32[4,32,128]{2,1,0:T(8,128)S(1)}, f32[72,8,128]{2,1,0:T(8,128)S(1)}, f32[72,8,128]{2,1,0:T(8,128)S(1)}, f3...) custom-call(s32[135]{0:T(256)S(1)} %concatenate.3.scal.ints, ...), custom_call_target="tpu_custom_call" | custom-call | flops 2000000000 | bytes 4000000 | tf_op jit(solution)/shard_map/unpack/pallas_call | solution.py:581
  29.4 3.2 %collective-permute-start.8 = (f32[72,8,128]{2,1,0:T(8,128)S(1)}, f32[72,8,128]{2,1,0:T(8,128)S(1)}, u32[]{:S(2)}, u32[]{:S(2)}) collective-permute-start(f32[72,8,128]{2,1,0:T(8,128)S(1)} %get-tuple-element.76), channel_id=1, source_target_pairs={{0,8},{8,16},{16,24},{24,25},{25,17},{17,9},{9,1},{1,2},{2,10},{10... | collective-permute-start | bytes 884744 | tf_op jit(solution)/shard_map/ppermute | solution.py:614
  32.6 0.4 collective-permute-start.10
  33.0 1.6 %maps.1.refs_3_ = f32[4,64,128]{2,1,0:T(8,128)S(1)} custom-call(s32[135]{0:T(256)S(1)} %concatenate.3.scal.ints, f32[3,4,16,128]{3,2,1,0:T(8,128)S(1)} %get-tuple-element.78.ids), custom_call_target="tpu_custom_call" | custom-call | flops 2000000000 | bytes 4000000 | tf_op jit(solution)/shard_map/maps/pallas_call | solution.py:600
  34.7 4.8 %collective-permute-done.8.refs_1_ = f32[72,8,128]{2,1,0:T(8,128)S(1)} collective-permute-done((f32[72,8,128]{2,1,0:T(8,128)S(1)}, f32[72,8,128]{2,1,0:T(8,128)S(1)}, u32[]{:S(2)}, u32[]{:S(2)}) %collective-permute-start.8) | collective-permute-done | bytes 294944 | tf_op jit(solution)/shard_map/ppermute | solution.py:614
  39.5 0.8 collective-permute-done.9.refs_2_
  40.3 4.4 %step0.1 = (f32[4,16,32,128]{3,2,1,0:T(8,128)S(1)}, f32[68,8,128]{2,1,0:T(8,128)S(1)}, f32[68,8,128]{2,1,0:T(8,128)S(1)}, f32[2,32,128]{2,1,0:T(8,128)S(1)}, f32...) custom-call(f32[4,16,32,128]{3,2,1,0:T(8,128)S(1)} %get-tuple-element.75.refs_0_, ...), custom_call_target="tpu_custom_call" | custom-call | flops 6000000000 | bytes 4000000 | tf_op jit(solution)/shard_map/step0/pallas_call | solution.py:629
  44.7 0.1 collective-permute-start.11
  44.8 0.1 collective-permute-start.15
  44.9 4.3 %collective-permute-start.16 = (f32[8,128]{1,0:T(8,128)S(1)}, f32[8,128]{1,0:T(8,128)S(1)}, u32[]{:S(2)}, u32[]{:S(2)}) collective-permute-start(f32[8,128]{1,0:T(8,128)S(1)} %add.98), channel_id=1, source_target_pairs={{0,2},{1,3},{2,0},{3,1},{4,6},{5,7},{6,4},{7,5},{8,10},{9,11},{10,... | collective-permute-start | bytes 12296 | tf_op jit(solution)/shard_map/ppermute | solution.py:548
  49.2 4.6 %collective-permute-start.13 = (f32[68,8,128]{2,1,0:T(8,128)S(1)}, f32[68,8,128]{2,1,0:T(8,128)S(1)}, u32[]{:S(2)}, u32[]{:S(2)}) collective-permute-start(f32[68,8,128]{2,1,0:T(8,128)S(1)} %get-tuple-element.91), channel_id=1, source_target_pairs={{0,8},{8,16},{16,24},{24,25},{25,17},{17,9},{9,1},{1,2},{2,10},{10... | collective-permute-start | bytes 835592 | tf_op jit(solution)/shard_map/ppermute | solution.py:614
  53.8 0.1 mul.30
  53.9 0.3 collective-permute-start.12
  54.2 6.9 %collective-permute-done.12 = f32[8,128]{1,0:T(8,128)S(1)} collective-permute-done((f32[8,128]{1,0:T(8,128)S(1)}, f32[8,128]{1,0:T(8,128)S(1)}, u32[]{:S(2)}, u32[]{:S(2)}) %collective-permute-start.12) | collective-permute-done | bytes 4128 | tf_op jit(solution)/shard_map/ppermute | solution.py:548
  61.1 0.1 collective-permute-done.14.refs_2_
  61.3 5.0 %step1.1 = (f32[4,16,32,128]{3,2,1,0:T(8,128)S(1)}, f32[68,8,128]{2,1,0:T(8,128)S(1)}, f32[68,8,128]{2,1,0:T(8,128)S(1)}, f32[2,32,128]{2,1,0:T(8,128)S(1)}, f32[8,128]{1,0:T(8,128)S(1)}) custom-call(f32[4,16,32,128]{3,2,1,0:T(8,128)S(1)} %get-tuple-element.90.refs_0_, f32[68,8,128]{2,1,0:T(8,128)S(1)} %collective-permute-done.13.refs_1_, ...), custom_call_target="tpu_custom_call" | custom-call | flops 6000000000 | bytes 4000000 | tf_op jit(solution)/shard_map/step1/pallas_call | solution.py:629
  66.3 2.0 %collective-permute-start.19 = (f32[8,128]{1,0:T(8,128)S(1)}, f32[8,128]{1,0:T(8,128)S(1)}, u32[]{:S(2)}, u32[]{:S(2)}) collective-permute-start(f32[8,128]{1,0:T(8,128)S(1)} %get-tuple-element.103), channel_id=1, source_target_pairs={{0,8},{8,0},{16,24},{24,16},{1,9},{9,1},{17,25},{25,17},{2,10},{10... | collective-permute-start | bytes 12296 | tf_op jit(solution)/shard_map/ppermute | solution.py:548
  68.3 0.8 collective-permute-done.19
  69.1 1.3 collective-permute-start.21
  70.4 4.4 %collective-permute-start.24 = (f32[8,128]{1,0:T(8,128)S(1)}, f32[8,128]{1,0:T(8,128)S(1)}, u32[]{:S(2)}, u32[]{:S(2)}) collective-permute-start(f32[8,128]{1,0:T(8,128)S(1)} %add.107), channel_id=1, source_target_pairs={{0,2},{1,3},{2,0},{3,1},{4,6},{5,7},{6,4},{7,5},{8,10},{9,11},{10,... | collective-permute-start | bytes 12296 | tf_op jit(solution)/shard_map/ppermute | solution.py:548
  74.8 1.1 collective-permute-start.20
  75.9 0.2 collective-permute-done.24
  76.1 2.3 %collective-permute-done.25 = f32[8,128]{1,0:T(8,128)S(1)} collective-permute-done((f32[8,128]{1,0:T(8,128)S(1)}, f32[8,128]{1,0:T(8,128)S(1)}, u32[]{:S(2)}, u32[]{:S(2)}) %collective-permute-start.25) | collective-permute-done | bytes 4128 | tf_op jit(solution)/shard_map/ppermute | solution.py:548
  78.5 1.4 %collective-permute-start.26 = (f32[8,128]{1,0:T(8,128)S(1)}, f32[8,128]{1,0:T(8,128)S(1)}, u32[]{:S(2)}, u32[]{:S(2)}) collective-permute-start(f32[8,128]{1,0:T(8,128)S(1)} %add.106), channel_id=1, source_target_pairs={{0,16},{8,24},{16,0},{24,8},{1,17},{9,25},{17,1},{25,9},{2,18},{10... | collective-permute-start | bytes 12296 | tf_op jit(solution)/shard_map/ppermute | solution.py:548
  79.9 5.0 %step2.1 = (f32[4,16,32,128]{3,2,1,0:T(8,128)S(1)}, f32[68,8,128]{2,1,0:T(8,128)S(1)}, f32[68,8,128]{2,1,0:T(8,128)S(1)}, f32[2,32,128]{2,1,0:T(8,128)S(1)}, f32[8,128]{1,0:T(8,128)S(1)}) custom-call(f32[4,16,32,128]{3,2,1,0:T(8,128)S(1)} %get-tuple-element.105.refs_0_, f32[68,8,128]{2,1,0:T(8,128)S(1)} %collective-permute-done.21.refs_1_, ...), custom_call_target="tpu_custom_call" | custom-call | flops 6000000000 | bytes 4000000 | tf_op jit(solution)/shard_map/step2/pallas_call | solution.py:629
  84.9 2.6 %collective-permute-start.27 = (f32[8,128]{1,0:T(8,128)S(1)}, f32[8,128]{1,0:T(8,128)S(1)}, u32[]{:S(2)}, u32[]{:S(2)}) collective-permute-start(f32[8,128]{1,0:T(8,128)S(1)} %get-tuple-element.117), channel_id=1, source_target_pairs={{0,8},{8,0},{16,24},{24,16},{1,9},{9,1},{17,25},{25,17},{2,10},{10... | collective-permute-start | bytes 12296 | tf_op jit(solution)/shard_map/ppermute | solution.py:548
  87.5 0.8 collective-permute-done.27
  88.3 3.0 %collective-permute-start.29 = (f32[68,8,128]{2,1,0:T(8,128)S(1)}, f32[68,8,128]{2,1,0:T(8,128)S(1)}, u32[]{:S(2)}, u32[]{:S(2)}) collective-permute-start(f32[68,8,128]{2,1,0:T(8,128)S(1)} %get-tuple-element.120), channel_id=1, source_target_pairs={{0,8},{8,16},{16,24},{24,25},{25,17},{17,9},{9,1},{1,2},{2,10},{10... | collective-permute-start | bytes 835592 | tf_op jit(solution)/shard_map/ppermute | solution.py:614
  91.3 2.4 %collective-permute-start.32 = (f32[8,128]{1,0:T(8,128)S(1)}, f32[8,128]{1,0:T(8,128)S(1)}, u32[]{:S(2)}, u32[]{:S(2)}) collective-permute-start(f32[8,128]{1,0:T(8,128)S(1)} %add.113), channel_id=1, source_target_pairs={{0,2},{1,3},{2,0},{3,1},{4,6},{5,7},{6,4},{7,5},{8,10},{9,11},{10,... | collective-permute-start | bytes 12296 | tf_op jit(solution)/shard_map/ppermute | solution.py:548
  93.7 1.4 %collective-permute-start.33 = (f32[8,128]{1,0:T(8,128)S(1)}, f32[8,128]{1,0:T(8,128)S(1)}, u32[]{:S(2)}, u32[]{:S(2)}) collective-permute-start(f32[8,128]{1,0:T(8,128)S(1)} %add.113), channel_id=1, source_target_pairs={{0,3},{1,2},{2,1},{3,0},{4,7},{5,6},{6,5},{7,4},{8,11},{9,10},{10,... | collective-permute-start | bytes 12296 | tf_op jit(solution)/shard_map/ppermute | solution.py:548
  95.2 0.5 collective-permute-done.32
  95.7 1.8 %collective-permute-done.33 = f32[8,128]{1,0:T(8,128)S(1)} collective-permute-done((f32[8,128]{1,0:T(8,128)S(1)}, f32[8,128]{1,0:T(8,128)S(1)}, u32[]{:S(2)}, u32[]{:S(2)}) %collective-permute-start.33) | collective-permute-done | bytes 4128 | tf_op jit(solution)/shard_map/ppermute | solution.py:548
  97.5 1.0 collective-permute-done.28
  98.5 1.2 collective-permute-start.34
  99.7 4.9 %step3.1.fields = f32[4,16,32,128]{3,2,1,0:T(8,128)S(1)} custom-call(f32[4,16,32,128]{3,2,1,0:T(8,128)S(1)} %get-tuple-element.122.refs_0_, f32[68,8,128]{2,1,0:T(8,128)S(1)} %collective-permute-done.29.refs_1_, f32[68,8,128]{2,1,0:T(8,128)S(1)} %collective-permute-done.30.refs_2_, f32[4,64,128]{2,1,0:T(8,128)S(1)} %maps.1.refs_3_, ...), custom_call_target="tpu_custom_call" | custom-call | flops 6000000000 | bytes 4000000 | tf_op jit(solution)/shard_map/step3/pallas_call | solution.py:629
  104.6 1.2 send.1
  105.8 3.7 %collective-permute-start.38 = (f32[64,8,128]{2,1,0:T(8,128)S(1)}, f32[64,8,128]{2,1,0:T(8,128)S(1)}, u32[]{:S(2)}, u32[]{:S(2)}) collective-permute-start(f32[64,8,128]{2,1,0:T(8,128)S(1)} %get-tuple-element.128), channel_id=1, source_target_pairs={{0,8},{8,0},{16,24},{24,16},{1,9},{9,1},{17,25},{25,17},{2,10},{10... | collective-permute-start | bytes 786440 | tf_op jit(solution)/shard_map/ppermute | solution.py:548
  109.5 1.1 collective-permute-start.39
  110.5 2.2 %collective-permute-start.40 = (f32[64,8,128]{2,1,0:T(8,128)S(1)}, f32[64,8,128]{2,1,0:T(8,128)S(1)}, u32[]{:S(2)}, u32[]{:S(2)}) collective-permute-start(f32[64,8,128]{2,1,0:T(8,128)S(1)} %get-tuple-element.130), channel_id=1, source_target_pairs={{0,24},{8,16},{16,8},{24,0},{1,25},{9,17},{17,9},{25,1},{2,26},{10... | collective-permute-start | bytes 786440 | tf_op jit(solution)/shard_map/ppermute | solution.py:548
  112.7 2.4 %collective-permute-start.36 = (f32[8,128]{1,0:T(8,128)S(1)}, f32[8,128]{1,0:T(8,128)S(1)}, u32[]{:S(2)}, u32[]{:S(2)}) collective-permute-start(f32[8,128]{1,0:T(8,128)S(1)} %add.117), channel_id=1, source_target_pairs={{0,2},{1,3},{2,0},{3,1},{4,6},{5,7},{6,4},{7,5},{8,10},{9,11},{10,... | collective-permute-start | bytes 12296 | tf_op jit(solution)/shard_map/ppermute | solution.py:548
  115.1 0.3 collective-permute-done.35
  115.4 1.2 collective-permute-start.37
  116.7 0.3 collective-permute-done.36
  116.9 2.5 %collective-permute-done.37 = f32[8,128]{1,0:T(8,128)S(1)} collective-permute-done((f32[8,128]{1,0:T(8,128)S(1)}, f32[8,128]{1,0:T(8,128)S(1)}, u32[]{:S(2)}, u32[]{:S(2)}) %collective-permute-start.37) | collective-permute-done | bytes 4128 | tf_op jit(solution)/shard_map/ppermute | solution.py:548
  119.4 5.2 %collective-permute-done.40.r3 = f32[64,8,128]{2,1,0:T(8,128)S(1)} collective-permute-done((f32[64,8,128]{2,1,0:T(8,128)S(1)}, f32[64,8,128]{2,1,0:T(8,128)S(1)}, u32[]{:S(2)}, u32[]{:S(2)}) %collective-permute-start.40) | collective-permute-done | bytes 262176 | tf_op jit(solution)/shard_map/ppermute | solution.py:548
  124.6 6.2 %final.1 = f32[4,16,32,128]{3,2,1,0:T(8,128)} custom-call(s32[135]{0:T(256)S(1)} %concatenate.3.scal.ints, f32[8,128]{1,0:T(8,128)S(1)} %add_add_fusion.mean, f32[64,8,128]{2,1,0:T(8,128)S(1)} %get-tuple-element.127.s0, f32[64,8,128]{2,1,0:T(8,128)S(1)} %collective-permute-done.38.r1, f32[64,8,128]{2,1,0:T(8,128)S(1)} %collective-permute-done.39.r2, ...), custom_call_target="tpu_custom_call" | custom-call | flops 2000000000 | bytes 4000000 | tf_op jit(solution)/shard_map/final/pallas_call | solution.py:657
  (59 shorter events, 0.2 us)
Async XLA Ops:
  0.0 6.3 %copy-start.1 = (f32[2,4,32,128]{3,2,1,0:T(8,128)S(1)}, f32[2,4,32,128]{3,2,1,0:T(8,128)}, u32[]{:S(2)}) copy-start(f32[2,4,32,128]{3,2,1,0:T(8,128)} %planes.1) | copy-start | bytes 393220
  0.9 5.4 %collective-permute-start = (f32[16,128]{1,0:T(8,128)S(1)}, f32[16,128]{1,0:T(8,128)S(1)}, u32[]{:S(2)}, u32[]{:S(2)}) collective-permute-start(f32[16,128]{1,0:T(8,128)S(1)} %get-tuple-element.132), channel_id=1, source_target_pairs={{0,1},{1,2},{2,3},{3,4},{4,5},{5,6},{6,7},{7,0},{8,9},{9,10},{10,1... | collective-permute-start | bytes 24584 | tf_op jit(solution)/shard_map/ppermute | solution.py:567
  2.9 3.3 %collective-permute-start.1 = (f32[16,128]{1,0:T(8,128)S(1)}, f32[16,128]{1,0:T(8,128)S(1)}, u32[]{:S(2)}, u32[]{:S(2)}) collective-permute-start(f32[16,128]{1,0:T(8,128)S(1)} %get-tuple-element.132), channel_id=1, source_target_pairs={{1,0},{2,1},{3,2},{4,3},{5,4},{6,5},{7,6},{0,7},{9,8},{10,9},{11,1... | collective-permute-start | bytes 24584 | tf_op jit(solution)/shard_map/ppermute | solution.py:567
  6.3 1.2 copy-start
  9.2 5.2 %collective-permute-start.2 = (f32[71,8,128]{2,1,0:T(8,128)S(1)}, f32[71,8,128]{2,1,0:T(8,128)S(1)}, u32[]{:S(2)}, u32[]{:S(2)}) collective-permute-start(f32[71,8,128]{2,1,0:T(8,128)S(1)} %get-tuple-element.69), channel_id=1, source_target_pairs={{0,8},{8,0},{16,24},{24,16},{1,9},{9,1},{17,25},{25,17},{2,10},{10... | collective-permute-start | bytes 872456 | tf_op jit(solution)/shard_map/ppermute | solution.py:548
  11.2 10.1 %collective-permute-start.3 = (f32[71,8,128]{2,1,0:T(8,128)S(1)}, f32[71,8,128]{2,1,0:T(8,128)S(1)}, u32[]{:S(2)}, u32[]{:S(2)}) collective-permute-start(f32[71,8,128]{2,1,0:T(8,128)S(1)} %get-tuple-element.72), channel_id=1, source_target_pairs={{0,16},{8,24},{16,0},{24,8},{1,17},{9,25},{17,1},{25,9},{2,18},{10... | collective-permute-start | bytes 872456 | tf_op jit(solution)/shard_map/ppermute | solution.py:548
  14.2 13.4 %collective-permute-start.4 = (f32[71,8,128]{2,1,0:T(8,128)S(1)}, f32[71,8,128]{2,1,0:T(8,128)S(1)}, u32[]{:S(2)}, u32[]{:S(2)}) collective-permute-start(f32[71,8,128]{2,1,0:T(8,128)S(1)} %get-tuple-element.73), channel_id=1, source_target_pairs={{0,24},{8,16},{16,8},{24,0},{1,25},{9,17},{17,9},{25,1},{2,26},{10... | collective-permute-start | bytes 872456 | tf_op jit(solution)/shard_map/ppermute | solution.py:548
  14.4 13.2 %collective-permute-start.5 = (f32[8,8,128]{2,1,0:T(8,128)S(1)}, f32[8,8,128]{2,1,0:T(8,128)S(1)}, u32[]{:S(2)}, u32[]{:S(2)}) collective-permute-start(f32[8,8,128]{2,1,0:T(8,128)S(1)} %get-tuple-element.74.p0), channel_id=1, source_target_pairs={{0,32},{32,0},{64,96},{96,64},{1,33},{33,1},{65,97},{97,65},{2,34}... | collective-permute-start | bytes 98312 | tf_op jit(solution)/shard_map/ppermute | solution.py:548
  16.2 11.4 %collective-permute-start.6 = (f32[8,8,128]{2,1,0:T(8,128)S(1)}, f32[8,8,128]{2,1,0:T(8,128)S(1)}, u32[]{:S(2)}, u32[]{:S(2)}) collective-permute-start(f32[8,8,128]{2,1,0:T(8,128)S(1)} %get-tuple-element.74.p0), channel_id=1, source_target_pairs={{0,64},{32,96},{64,0},{96,32},{1,65},{33,97},{65,1},{97,33},{2,66}... | collective-permute-start | bytes 98312 | tf_op jit(solution)/shard_map/ppermute | solution.py:548
  19.5 8.1 %collective-permute-start.7 = (f32[8,8,128]{2,1,0:T(8,128)S(1)}, f32[8,8,128]{2,1,0:T(8,128)S(1)}, u32[]{:S(2)}, u32[]{:S(2)}) collective-permute-start(f32[8,8,128]{2,1,0:T(8,128)S(1)} %get-tuple-element.74.p0), channel_id=1, source_target_pairs={{0,96},{32,64},{64,32},{96,0},{1,97},{33,65},{65,33},{97,1},{2,98}... | collective-permute-start | bytes 98312 | tf_op jit(solution)/shard_map/ppermute | solution.py:548
  29.4 10.1 %collective-permute-start.8 = (f32[72,8,128]{2,1,0:T(8,128)S(1)}, f32[72,8,128]{2,1,0:T(8,128)S(1)}, u32[]{:S(2)}, u32[]{:S(2)}) collective-permute-start(f32[72,8,128]{2,1,0:T(8,128)S(1)} %get-tuple-element.76), channel_id=1, source_target_pairs={{0,8},{8,16},{16,24},{24,25},{25,17},{17,9},{9,1},{1,2},{2,10},{10... | collective-permute-start | bytes 884744 | tf_op jit(solution)/shard_map/ppermute | solution.py:614
  32.6 7.7 %collective-permute-start.9 = (f32[72,8,128]{2,1,0:T(8,128)S(1)}, f32[72,8,128]{2,1,0:T(8,128)S(1)}, u32[]{:S(2)}, u32[]{:S(2)}) collective-permute-start(f32[72,8,128]{2,1,0:T(8,128)S(1)} %get-tuple-element.77), channel_id=1, source_target_pairs={{8,0},{16,8},{24,16},{25,24},{17,25},{9,17},{1,9},{2,1},{10,2},{18... | collective-permute-start | bytes 884744 | tf_op jit(solution)/shard_map/ppermute | solution.py:615
  32.6 12.2 %collective-permute-start.10 = (f32[8,128]{1,0:T(8,128)S(1)}, f32[8,128]{1,0:T(8,128)S(1)}, u32[]{:S(2)}, u32[]{:S(2)}) collective-permute-start(f32[8,128]{1,0:T(8,128)S(1)} %get-tuple-element.84), channel_id=1, source_target_pairs={{0,4},{1,5},{2,6},{3,7},{4,0},{5,1},{6,2},{7,3},{8,12},{9,13},{10,... | collective-permute-start | bytes 12296 | tf_op jit(solution)/shard_map/ppermute | solution.py:548
  44.7 4.5 %collective-permute-start.11 = (f32[8,128]{1,0:T(8,128)S(1)}, f32[8,128]{1,0:T(8,128)S(1)}, u32[]{:S(2)}, u32[]{:S(2)}) collective-permute-start(f32[8,128]{1,0:T(8,128)S(1)} %get-tuple-element.88), channel_id=1, source_target_pairs={{0,8},{8,0},{16,24},{24,16},{1,9},{9,1},{17,25},{25,17},{2,10},{10... | collective-permute-start | bytes 12296 | tf_op jit(solution)/shard_map/ppermute | solution.py:548
  44.8 9.1 %collective-permute-start.15 = (f32[8,128]{1,0:T(8,128)S(1)}, f32[8,128]{1,0:T(8,128)S(1)}, u32[]{:S(2)}, u32[]{:S(2)}) collective-permute-start(f32[8,128]{1,0:T(8,128)S(1)} %add.98), channel_id=1, source_target_pairs={{0,1},{1,0},{2,3},{3,2},{4,5},{5,4},{6,7},{7,6},{8,9},{9,8},{10,11... | collective-permute-start | bytes 12296 | tf_op jit(solution)/shard_map/ppermute | solution.py:548
  44.9 9.3 %collective-permute-start.16 = (f32[8,128]{1,0:T(8,128)S(1)}, f32[8,128]{1,0:T(8,128)S(1)}, u32[]{:S(2)}, u32[]{:S(2)}) collective-permute-start(f32[8,128]{1,0:T(8,128)S(1)} %add.98), channel_id=1, source_target_pairs={{0,2},{1,3},{2,0},{3,1},{4,6},{5,7},{6,4},{7,5},{8,10},{9,11},{10,... | collective-permute-start | bytes 12296 | tf_op jit(solution)/shard_map/ppermute | solution.py:548
  49.1 5.1 %collective-permute-start.17 = (f32[8,128]{1,0:T(8,128)S(1)}, f32[8,128]{1,0:T(8,128)S(1)}, u32[]{:S(2)}, u32[]{:S(2)}) collective-permute-start(f32[8,128]{1,0:T(8,128)S(1)} %add.98), channel_id=1, source_target_pairs={{0,3},{1,2},{2,1},{3,0},{4,7},{5,6},{6,5},{7,4},{8,11},{9,10},{10,... | collective-permute-start | bytes 12296 | tf_op jit(solution)/shard_map/ppermute | solution.py:548
  49.2 11.9 %collective-permute-start.13 = (f32[68,8,128]{2,1,0:T(8,128)S(1)}, f32[68,8,128]{2,1,0:T(8,128)S(1)}, u32[]{:S(2)}, u32[]{:S(2)}) collective-permute-start(f32[68,8,128]{2,1,0:T(8,128)S(1)} %get-tuple-element.91), channel_id=1, source_target_pairs={{0,8},{8,16},{16,24},{24,25},{25,17},{17,9},{9,1},{1,2},{2,10},{10... | collective-permute-start | bytes 835592 | tf_op jit(solution)/shard_map/ppermute | solution.py:614
  53.8 7.5 %collective-permute-start.14 = (f32[68,8,128]{2,1,0:T(8,128)S(1)}, f32[68,8,128]{2,1,0:T(8,128)S(1)}, u32[]{:S(2)}, u32[]{:S(2)}) collective-permute-start(f32[68,8,128]{2,1,0:T(8,128)S(1)} %get-tuple-element.92), channel_id=1, source_target_pairs={{8,0},{16,8},{24,16},{25,24},{17,25},{9,17},{1,9},{2,1},{10,2},{18... | collective-permute-start | bytes 835592 | tf_op jit(solution)/shard_map/ppermute | solution.py:615
  53.9 7.2 %collective-permute-start.12 = (f32[8,128]{1,0:T(8,128)S(1)}, f32[8,128]{1,0:T(8,128)S(1)}, u32[]{:S(2)}, u32[]{:S(2)}) collective-permute-start(f32[8,128]{1,0:T(8,128)S(1)} %add.96), channel_id=1, source_target_pairs={{0,4},{1,5},{2,6},{3,7},{4,0},{5,1},{6,2},{7,3},{8,12},{9,13},{10,... | collective-permute-start | bytes 12296 | tf_op jit(solution)/shard_map/ppermute | solution.py:548
  61.1 7.2 %collective-permute-start.18 = (f32[8,128]{1,0:T(8,128)S(1)}, f32[8,128]{1,0:T(8,128)S(1)}, u32[]{:S(2)}, u32[]{:S(2)}) collective-permute-start(f32[8,128]{1,0:T(8,128)S(1)} %add.97), channel_id=1, source_target_pairs={{0,16},{8,24},{16,0},{24,8},{1,17},{9,25},{17,1},{25,9},{2,18},{10... | collective-permute-start | bytes 12296 | tf_op jit(solution)/shard_map/ppermute | solution.py:548
  66.3 2.8 %collective-permute-start.19 = (f32[8,128]{1,0:T(8,128)S(1)}, f32[8,128]{1,0:T(8,128)S(1)}, u32[]{:S(2)}, u32[]{:S(2)}) collective-permute-start(f32[8,128]{1,0:T(8,128)S(1)} %get-tuple-element.103), channel_id=1, source_target_pairs={{0,8},{8,0},{16,24},{24,16},{1,9},{9,1},{17,25},{25,17},{2,10},{10... | collective-permute-start | bytes 12296 | tf_op jit(solution)/shard_map/ppermute | solution.py:548
  69.1 10.7 %collective-permute-start.21 = (f32[68,8,128]{2,1,0:T(8,128)S(1)}, f32[68,8,128]{2,1,0:T(8,128)S(1)}, u32[]{:S(2)}, u32[]{:S(2)}) collective-permute-start(f32[68,8,128]{2,1,0:T(8,128)S(1)} %get-tuple-element.106), channel_id=1, source_target_pairs={{0,8},{8,16},{16,24},{24,25},{25,17},{17,9},{9,1},{1,2},{2,10},{10... | collective-permute-start | bytes 835592 | tf_op jit(solution)/shard_map/ppermute | solution.py:614
  70.4 9.5 %collective-permute-start.22 = (f32[68,8,128]{2,1,0:T(8,128)S(1)}, f32[68,8,128]{2,1,0:T(8,128)S(1)}, u32[]{:S(2)}, u32[]{:S(2)}) collective-permute-start(f32[68,8,128]{2,1,0:T(8,128)S(1)} %get-tuple-element.107), channel_id=1, source_target_pairs={{8,0},{16,8},{24,16},{25,24},{17,25},{9,17},{1,9},{2,1},{10,2},{18... | collective-permute-start | bytes 835592 | tf_op jit(solution)/shard_map/ppermute | solution.py:615
  70.4 4.4 %collective-permute-start.23 = (f32[8,128]{1,0:T(8,128)S(1)}, f32[8,128]{1,0:T(8,128)S(1)}, u32[]{:S(2)}, u32[]{:S(2)}) collective-permute-start(f32[8,128]{1,0:T(8,128)S(1)} %add.107), channel_id=1, source_target_pairs={{0,1},{1,0},{2,3},{3,2},{4,5},{5,4},{6,7},{7,6},{8,9},{9,8},{10,11... | collective-permute-start | bytes 12296 | tf_op jit(solution)/shard_map/ppermute | solution.py:548
  70.4 5.7 %collective-permute-start.24 = (f32[8,128]{1,0:T(8,128)S(1)}, f32[8,128]{1,0:T(8,128)S(1)}, u32[]{:S(2)}, u32[]{:S(2)}) collective-permute-start(f32[8,128]{1,0:T(8,128)S(1)} %add.107), channel_id=1, source_target_pairs={{0,2},{1,3},{2,0},{3,1},{4,6},{5,7},{6,4},{7,5},{8,10},{9,11},{10,... | collective-permute-start | bytes 12296 | tf_op jit(solution)/shard_map/ppermute | solution.py:548
  74.8 3.7 %collective-permute-start.25 = (f32[8,128]{1,0:T(8,128)S(1)}, f32[8,128]{1,0:T(8,128)S(1)}, u32[]{:S(2)}, u32[]{:S(2)}) collective-permute-start(f32[8,128]{1,0:T(8,128)S(1)} %add.107), channel_id=1, source_target_pairs={{0,3},{1,2},{2,1},{3,0},{4,7},{5,6},{6,5},{7,4},{8,11},{9,10},{10,... | collective-permute-start | bytes 12296 | tf_op jit(solution)/shard_map/ppermute | solution.py:548
  74.8 3.7 %collective-permute-start.20 = (f32[8,128]{1,0:T(8,128)S(1)}, f32[8,128]{1,0:T(8,128)S(1)}, u32[]{:S(2)}, u32[]{:S(2)}) collective-permute-start(f32[8,128]{1,0:T(8,128)S(1)} %add.105), channel_id=1, source_target_pairs={{0,4},{1,5},{2,6},{3,7},{4,0},{5,1},{6,2},{7,3},{8,12},{9,13},{10,... | collective-permute-start | bytes 12296 | tf_op jit(solution)/shard_map/ppermute | solution.py:548
  78.5 9.0 %collective-permute-start.26 = (f32[8,128]{1,0:T(8,128)S(1)}, f32[8,128]{1,0:T(8,128)S(1)}, u32[]{:S(2)}, u32[]{:S(2)}) collective-permute-start(f32[8,128]{1,0:T(8,128)S(1)} %add.106), channel_id=1, source_target_pairs={{0,16},{8,24},{16,0},{24,8},{1,17},{9,25},{17,1},{25,9},{2,18},{10... | collective-permute-start | bytes 12296 | tf_op jit(solution)/shard_map/ppermute | solution.py:548
  84.9 3.4 %collective-permute-start.27 = (f32[8,128]{1,0:T(8,128)S(1)}, f32[8,128]{1,0:T(8,128)S(1)}, u32[]{:S(2)}, u32[]{:S(2)}) collective-permute-start(f32[8,128]{1,0:T(8,128)S(1)} %get-tuple-element.117), channel_id=1, source_target_pairs={{0,8},{8,0},{16,24},{24,16},{1,9},{9,1},{17,25},{25,17},{2,10},{10... | collective-permute-start | bytes 12296 | tf_op jit(solution)/shard_map/ppermute | solution.py:548
  88.3 11.4 %collective-permute-start.29 = (f32[68,8,128]{2,1,0:T(8,128)S(1)}, f32[68,8,128]{2,1,0:T(8,128)S(1)}, u32[]{:S(2)}, u32[]{:S(2)}) collective-permute-start(f32[68,8,128]{2,1,0:T(8,128)S(1)} %get-tuple-element.120), channel_id=1, source_target_pairs={{0,8},{8,16},{16,24},{24,25},{25,17},{17,9},{9,1},{1,2},{2,10},{10... | collective-permute-start | bytes 835592 | tf_op jit(solution)/shard_map/ppermute | solution.py:614
  91.3 8.4 %collective-permute-start.30 = (f32[68,8,128]{2,1,0:T(8,128)S(1)}, f32[68,8,128]{2,1,0:T(8,128)S(1)}, u32[]{:S(2)}, u32[]{:S(2)}) collective-permute-start(f32[68,8,128]{2,1,0:T(8,128)S(1)} %get-tuple-element.121), channel_id=1, source_target_pairs={{8,0},{16,8},{24,16},{25,24},{17,25},{9,17},{1,9},{2,1},{10,2},{18... | collective-permute-start | bytes 835592 | tf_op jit(solution)/shard_map/ppermute | solution.py:615
  91.3 3.9 %collective-permute-start.31 = (f32[8,128]{1,0:T(8,128)S(1)}, f32[8,128]{1,0:T(8,128)S(1)}, u32[]{:S(2)}, u32[]{:S(2)}) collective-permute-start(f32[8,128]{1,0:T(8,128)S(1)} %add.113), channel_id=1, source_target_pairs={{0,1},{1,0},{2,3},{3,2},{4,5},{5,4},{6,7},{7,6},{8,9},{9,8},{10,11... | collective-permute-start | bytes 12296 | tf_op jit(solution)/shard_map/ppermute | solution.py:548
  91.3 4.3 %collective-permute-start.32 = (f32[8,128]{1,0:T(8,128)S(1)}, f32[8,128]{1,0:T(8,128)S(1)}, u32[]{:S(2)}, u32[]{:S(2)}) collective-permute-start(f32[8,128]{1,0:T(8,128)S(1)} %add.113), channel_id=1, source_target_pairs={{0,2},{1,3},{2,0},{3,1},{4,6},{5,7},{6,4},{7,5},{8,10},{9,11},{10,... | collective-permute-start | bytes 12296 | tf_op jit(solution)/shard_map/ppermute | solution.py:548
  93.7 3.7 %collective-permute-start.33 = (f32[8,128]{1,0:T(8,128)S(1)}, f32[8,128]{1,0:T(8,128)S(1)}, u32[]{:S(2)}, u32[]{:S(2)}) collective-permute-start(f32[8,128]{1,0:T(8,128)S(1)} %add.113), channel_id=1, source_target_pairs={{0,3},{1,2},{2,1},{3,0},{4,7},{5,6},{6,5},{7,4},{8,11},{9,10},{10,... | collective-permute-start | bytes 12296 | tf_op jit(solution)/shard_map/ppermute | solution.py:548
  95.2 3.3 %collective-permute-start.28 = (f32[8,128]{1,0:T(8,128)S(1)}, f32[8,128]{1,0:T(8,128)S(1)}, u32[]{:S(2)}, u32[]{:S(2)}) collective-permute-start(f32[8,128]{1,0:T(8,128)S(1)} %add.111), channel_id=1, source_target_pairs={{0,4},{1,5},{2,6},{3,7},{4,0},{5,1},{6,2},{7,3},{8,12},{9,13},{10,... | collective-permute-start | bytes 12296 | tf_op jit(solution)/shard_map/ppermute | solution.py:548
  98.5 6.1 %collective-permute-start.34 = (f32[8,128]{1,0:T(8,128)S(1)}, f32[8,128]{1,0:T(8,128)S(1)}, u32[]{:S(2)}, u32[]{:S(2)}) collective-permute-start(f32[8,128]{1,0:T(8,128)S(1)} %add.112), channel_id=1, source_target_pairs={{0,16},{8,24},{16,0},{24,8},{1,17},{9,25},{17,1},{25,9},{2,18},{10... | collective-permute-start | bytes 12296 | tf_op jit(solution)/shard_map/ppermute | solution.py:548
  105.8 13.6 %collective-permute-start.38 = (f32[64,8,128]{2,1,0:T(8,128)S(1)}, f32[64,8,128]{2,1,0:T(8,128)S(1)}, u32[]{:S(2)}, u32[]{:S(2)}) collective-permute-start(f32[64,8,128]{2,1,0:T(8,128)S(1)} %get-tuple-element.128), channel_id=1, source_target_pairs={{0,8},{8,0},{16,24},{24,16},{1,9},{9,1},{17,25},{25,17},{2,10},{10... | collective-permute-start | bytes 786440 | tf_op jit(solution)/shard_map/ppermute | solution.py:548
  109.5 10.0 %collective-permute-start.39 = (f32[64,8,128]{2,1,0:T(8,128)S(1)}, f32[64,8,128]{2,1,0:T(8,128)S(1)}, u32[]{:S(2)}, u32[]{:S(2)}) collective-permute-start(f32[64,8,128]{2,1,0:T(8,128)S(1)} %get-tuple-element.129), channel_id=1, source_target_pairs={{0,16},{8,24},{16,0},{24,8},{1,17},{9,25},{17,1},{25,9},{2,18},{10... | collective-permute-start | bytes 786440 | tf_op jit(solution)/shard_map/ppermute | solution.py:548
  110.5 14.1 %collective-permute-start.40 = (f32[64,8,128]{2,1,0:T(8,128)S(1)}, f32[64,8,128]{2,1,0:T(8,128)S(1)}, u32[]{:S(2)}, u32[]{:S(2)}) collective-permute-start(f32[64,8,128]{2,1,0:T(8,128)S(1)} %get-tuple-element.130), channel_id=1, source_target_pairs={{0,24},{8,16},{16,8},{24,0},{1,25},{9,17},{17,9},{25,1},{2,26},{10... | collective-permute-start | bytes 786440 | tf_op jit(solution)/shard_map/ppermute | solution.py:548
  112.7 2.8 %collective-permute-start.35 = (f32[8,128]{1,0:T(8,128)S(1)}, f32[8,128]{1,0:T(8,128)S(1)}, u32[]{:S(2)}, u32[]{:S(2)}) collective-permute-start(f32[8,128]{1,0:T(8,128)S(1)} %add.117), channel_id=1, source_target_pairs={{0,1},{1,0},{2,3},{3,2},{4,5},{5,4},{6,7},{7,6},{8,9},{9,8},{10,11... | collective-permute-start | bytes 12296 | tf_op jit(solution)/shard_map/ppermute | solution.py:548
  112.7 4.3 %collective-permute-start.36 = (f32[8,128]{1,0:T(8,128)S(1)}, f32[8,128]{1,0:T(8,128)S(1)}, u32[]{:S(2)}, u32[]{:S(2)}) collective-permute-start(f32[8,128]{1,0:T(8,128)S(1)} %add.117), channel_id=1, source_target_pairs={{0,2},{1,3},{2,0},{3,1},{4,6},{5,7},{6,4},{7,5},{8,10},{9,11},{10,... | collective-permute-start | bytes 12296 | tf_op jit(solution)/shard_map/ppermute | solution.py:548
  115.4 4.0 %collective-permute-start.37 = (f32[8,128]{1,0:T(8,128)S(1)}, f32[8,128]{1,0:T(8,128)S(1)}, u32[]{:S(2)}, u32[]{:S(2)}) collective-permute-start(f32[8,128]{1,0:T(8,128)S(1)} %add.117), channel_id=1, source_target_pairs={{0,3},{1,2},{2,1},{3,0},{4,7},{5,6},{6,5},{7,4},{8,11},{9,10},{10,... | collective-permute-start | bytes 12296 | tf_op jit(solution)/shard_map/ppermute | solution.py:548

commit v9 on v8

--- a/solution.py
+++ b/solution.py
@@ -513,20 +513,22 @@
     rows("fill", per_row)
 
 
-def final_kernel(scal, mean, s0, r1, r2, r3, out, columns, stage, *, cells):
+def final_kernel(scal, mean, s0, r1, r2, r3, out, columns, *, cells):
     own, slab = scal[0], scal[1]
-    for s, source in enumerate((s0, r1, r2, r3)):
-        stage[slab ^ s] = source[...]
     du, dw = mean_response(mean[0:1, :] * F32(1.0 / cells))
     pad = jnp.zeros((LANES - 2 * XI, LANES), F32)
     columns[...] = jnp.concatenate([du, dw, pad], axis=0).T
     own_columns = columns[pl.ds(pl.multiple_of(own * NZ, NZ), NZ), :]
     group = lanes() >> 5
-    odd, high = (group & 1) == 1, group >= 2
+    masks = [group == (slab ^ s) for s in range(4)]
     for x in range(XI):
         for kt in range(4):
-            sources = [stage[b, x * 4 + kt] for b in range(4)]
-            for c, value in enumerate(transposed4(sources, odd, high)):
+            sources = [ref[x * 4 + kt] for ref in (s0, r1, r2, r3)]
+            for c in range(4):
+                value = None
+                for s, source in enumerate(sources):
+                    moved = pltpu.roll(source, (((slab ^ s) - c) & 3) * 32, axis=1)
+                    value = moved if value is None else jnp.where(masks[s], moved, value)
                 if c in (0, 2):
                     column = (0 if c == 0 else XI) + x
                     value = value + own_columns[kt * 8 : kt * 8 + 8, column : column + 1]
@@ -609,7 +611,7 @@
         partial = sums
         if step > 0:
             partial = partial + swapped(partial, "gx", GX, 1)
-            su, sd, partial = lax.optimization_barrier((su, sd, partial))
+            su, sd, partial, pending = lax.optimization_barrier((su, sd, partial, pending))
             mean = among_x(pending)
         lo = lax.ppermute(su, ("gx", "gy"), up)
         hi = lax.ppermute(sd, ("gx", "gy"), down)
@@ -658,7 +660,7 @@
         functools.partial(final_kernel, cells=cells),
         shape(4, XI, NZ, LANES),
         [SMEM, VMEM] + [VMEM] * 4,
-        [pltpu.VMEM((LANES, LANES), F32), pltpu.VMEM((GX, TILES, 8, LANES), F32)],
+        [pltpu.VMEM((LANES, LANES), F32)],
         name="final",
     )(scal, mean, s0, *received)
     return fields[None]

time: 131 us -> 130 us (level)
  Pallas kernels: 31.8 us -> 28.7 us
    ppermute x31, waiting for transfers between devices: 30.6 us -> 24.2 us  [swapped(): return lax.ppermute(value, axis, [(i, i ^ distance) for i in range(size)])]
    ppermute x4, waiting for transfers between devices: 4.83 us -> 10.1 us  [local(): lo = lax.ppermute(su, ('gx', 'gy'), up)]
    pallas_call x1, Pallas kernels: 6.23 us -> 3.11 us  [local(): call(functools.partial(final_kernel, cells=cells), shape(4, XI, NZ, LANES...]
    ppermute x4, waiting for transfers between devices: 0.93 us -> 2.44 us  [local(): hi = lax.ppermute(sd, ('gx', 'gy'), down)]
  transfers between devices with their start and end apart: 41 -> 41, of which waited for: 18 -> 16; matrix products, arithmetic and copies ran while one was open for 1% -> 1% of each run, Pallas kernels for 16% -> 16%
where the time goes in v9:
time: 130 us; the launch traced here: 129 us
  starting transfers between devices  60.2 us (46%)
  waiting for transfers between devices  36.9 us (28%)
  Pallas kernels  28.7 us (22%)
  local copies, waits for them, and re-layouts  3.13 us (2%)
    ppermute x31, starting transfers between devices, swapped(): return lax.ppermute(value, axis, [(i, i ^ distance) for i in range(size)])  42.8 us
    ppermute x31, waiting for transfers between devices, swapped(): return lax.ppermute(value, axis, [(i, i ^ distance) for i in range(size)])  24.2 us
    pallas_call x4, Pallas kernels, local(): call(functools.partial(step_kernel, step=step, cells=cells), tuple(outs),...  19.3 us
    ppermute x4, starting transfers between devices, local(): lo = lax.ppermute(su, ('gx', 'gy'), up)  13 us
    ppermute x4, waiting for transfers between devices, local(): lo = lax.ppermute(su, ('gx', 'gy'), up)  10.1 us
    pallas_call x1, Pallas kernels, local(): call(functools.partial(final_kernel, cells=cells), shape(4, XI, NZ, LANES...  3.11 us
  transfers between devices with their start and end apart: 41, of which 16 were waited for; matrix products, arithmetic and copies ran while one was open for 1% of the time, Pallas kernels for 16%

profile of v9, /device:TPU:1, one launch (start us, length us, event | category | flops | bytes accessed | tf_op | source)
XLA Modules:
  0.0 129.4 jit_solution(12936125966579983786)
XLA Ops:
  0.0 0.9 slice.7
  0.9 2.0 %collective-permute-start = (f32[16,128]{1,0:T(8,128)S(1)}, f32[16,128]{1,0:T(8,128)S(1)}, u32[]{:S(2)}, u32[]{:S(2)}) collective-permute-start(f32[16,128]{1,0:T(8,128)S(1)} %get-tuple-element.138), channel_id=1, source_target_pairs={{0,1},{1,2},{2,3},{3,4},{4,5},{5,6},{6,7},{7,0},{8,9},{9,10},{10,1... | collective-permute-start | bytes 24584 | tf_op jit(solution)/shard_map/ppermute | solution.py:569
  2.9 2.4 %collective-permute-start.1 = (f32[16,128]{1,0:T(8,128)S(1)}, f32[16,128]{1,0:T(8,128)S(1)}, u32[]{:S(2)}, u32[]{:S(2)}) collective-permute-start(f32[16,128]{1,0:T(8,128)S(1)} %get-tuple-element.138), channel_id=1, source_target_pairs={{1,0},{2,1},{3,2},{4,3},{5,4},{6,5},{7,6},{0,7},{9,8},{10,9},{11,1... | collective-permute-start | bytes 24584 | tf_op jit(solution)/shard_map/ppermute | solution.py:569
  5.3 0.8 concatenate.3.scal.ints
  6.0 0.2 collective-permute-done
  6.2 0.0 collective-permute-done.1
  6.3 0.0 copy-start
  6.3 1.2 copy-done
  7.5 1.7 %pack.1 = (f32[71,8,128]{2,1,0:T(8,128)S(1)}, f32[71,8,128]{2,1,0:T(8,128)S(1)}, f32[71,8,128]{2,1,0:T(8,128)S(1)}, f32[71,8,128]{2,1,0:T(8,128)S(1)}, f32[8,8,128]{2,1,0:T(8,128)S(1)}) custom-call(s32[135]{0:T(256)S(1)} %concatenate.3.scal.ints, f32[4,16,32,128]{3,2,1,0:T(8,128)S(1)} %bitcast.14, f32[2,4,32,128]{3,2,1,0:T(8,128)S(1)} %copy-done.1, ...), custom_call_target="tpu_custom_call" | custom-call | flops 2000000000 | bytes 4000000 | tf_op jit(solution)/shard_map/pack/pallas_call | solution.py:571
  9.2 1.9 %collective-permute-start.2 = (f32[71,8,128]{2,1,0:T(8,128)S(1)}, f32[71,8,128]{2,1,0:T(8,128)S(1)}, u32[]{:S(2)}, u32[]{:S(2)}) collective-permute-start(f32[71,8,128]{2,1,0:T(8,128)S(1)} %get-tuple-element.72), channel_id=1, source_target_pairs={{0,8},{8,0},{16,24},{24,16},{1,9},{9,1},{17,25},{25,17},{2,10},{10... | collective-permute-start | bytes 872456 | tf_op jit(solution)/shard_map/ppermute | solution.py:550
  11.1 0.1 pad.9.clone
  11.2 3.0 %collective-permute-start.3 = (f32[71,8,128]{2,1,0:T(8,128)S(1)}, f32[71,8,128]{2,1,0:T(8,128)S(1)}, u32[]{:S(2)}, u32[]{:S(2)}) collective-permute-start(f32[71,8,128]{2,1,0:T(8,128)S(1)} %get-tuple-element.75), channel_id=1, source_target_pairs={{0,16},{8,24},{16,0},{24,8},{1,17},{9,25},{17,1},{25,9},{2,18},{10... | collective-permute-start | bytes 872456 | tf_op jit(solution)/shard_map/ppermute | solution.py:550
  14.2 0.2 collective-permute-start.4
  14.4 1.8 %collective-permute-start.5 = (f32[8,8,128]{2,1,0:T(8,128)S(1)}, f32[8,8,128]{2,1,0:T(8,128)S(1)}, u32[]{:S(2)}, u32[]{:S(2)}) collective-permute-start(f32[8,8,128]{2,1,0:T(8,128)S(1)} %get-tuple-element.77.p0), channel_id=1, source_target_pairs={{0,32},{32,0},{64,96},{96,64},{1,33},{33,1},{65,97},{97,65},{2,34}... | collective-permute-start | bytes 98312 | tf_op jit(solution)/shard_map/ppermute | solution.py:550
  16.2 3.3 %collective-permute-start.6 = (f32[8,8,128]{2,1,0:T(8,128)S(1)}, f32[8,8,128]{2,1,0:T(8,128)S(1)}, u32[]{:S(2)}, u32[]{:S(2)}) collective-permute-start(f32[8,8,128]{2,1,0:T(8,128)S(1)} %get-tuple-element.77.p0), channel_id=1, source_target_pairs={{0,64},{32,96},{64,0},{96,32},{1,65},{33,97},{65,1},{97,33},{2,66}... | collective-permute-start | bytes 98312 | tf_op jit(solution)/shard_map/ppermute | solution.py:550
  19.5 0.1 pad_maximum_fusion.1
  19.6 0.1 tile.12
  19.7 1.6 %collective-permute-done.3.r2 = f32[71,8,128]{2,1,0:T(8,128)S(1)} collective-permute-done((f32[71,8,128]{2,1,0:T(8,128)S(1)}, f32[71,8,128]{2,1,0:T(8,128)S(1)}, u32[]{:S(2)}, u32[]{:S(2)}) %collective-permute-start.3) | collective-permute-done | bytes 290848 | tf_op jit(solution)/shard_map/ppermute | solution.py:550
  21.3 6.3 %collective-permute-done.4.r3 = f32[71,8,128]{2,1,0:T(8,128)S(1)} collective-permute-done((f32[71,8,128]{2,1,0:T(8,128)S(1)}, f32[71,8,128]{2,1,0:T(8,128)S(1)}, u32[]{:S(2)}, u32[]{:S(2)}) %collective-permute-start.4) | collective-permute-done | bytes 290848 | tf_op jit(solution)/shard_map/ppermute | solution.py:550
  27.7 1.7 %unpack.1 = (f32[4,16,32,128]{3,2,1,0:T(8,128)S(1)}, f32[4,32,128]{2,1,0:T(8,128)S(1)}, f32[72,8,128]{2,1,0:T(8,128)S(1)}, f32[72,8,128]{2,1,0:T(8,128)S(1)}, f3...) custom-call(s32[135]{0:T(256)S(1)} %concatenate.3.scal.ints, ...), custom_call_target="tpu_custom_call" | custom-call | flops 2000000000 | bytes 4000000 | tf_op jit(solution)/shard_map/unpack/pallas_call | solution.py:583
  29.4 3.2 %collective-permute-start.8 = (f32[72,8,128]{2,1,0:T(8,128)S(1)}, f32[72,8,128]{2,1,0:T(8,128)S(1)}, u32[]{:S(2)}, u32[]{:S(2)}) collective-permute-start(f32[72,8,128]{2,1,0:T(8,128)S(1)} %get-tuple-element.79), channel_id=1, source_target_pairs={{0,8},{8,16},{16,24},{24,25},{25,17},{17,9},{9,1},{1,2},{2,10},{10... | collective-permute-start | bytes 884744 | tf_op jit(solution)/shard_map/ppermute | solution.py:616
  32.6 0.4 collective-permute-start.10
  33.0 1.6 %maps.1.refs_3_ = f32[4,64,128]{2,1,0:T(8,128)S(1)} custom-call(s32[135]{0:T(256)S(1)} %concatenate.3.scal.ints, f32[3,4,16,128]{3,2,1,0:T(8,128)S(1)} %get-tuple-element.81.ids), custom_call_target="tpu_custom_call" | custom-call | flops 2000000000 | bytes 4000000 | tf_op jit(solution)/shard_map/maps/pallas_call | solution.py:602
  34.7 4.8 %collective-permute-done.8.refs_1_ = f32[72,8,128]{2,1,0:T(8,128)S(1)} collective-permute-done((f32[72,8,128]{2,1,0:T(8,128)S(1)}, f32[72,8,128]{2,1,0:T(8,128)S(1)}, u32[]{:S(2)}, u32[]{:S(2)}) %collective-permute-start.8) | collective-permute-done | bytes 294944 | tf_op jit(solution)/shard_map/ppermute | solution.py:616
  39.5 0.8 collective-permute-done.9.refs_2_
  40.3 4.4 %step0.1 = (f32[4,16,32,128]{3,2,1,0:T(8,128)S(1)}, f32[68,8,128]{2,1,0:T(8,128)S(1)}, f32[68,8,128]{2,1,0:T(8,128)S(1)}, f32[2,32,128]{2,1,0:T(8,128)S(1)}, f32...) custom-call(f32[4,16,32,128]{3,2,1,0:T(8,128)S(1)} %get-tuple-element.78.refs_0_, ...), custom_call_target="tpu_custom_call" | custom-call | flops 6000000000 | bytes 4000000 | tf_op jit(solution)/shard_map/step0/pallas_call | solution.py:631
  44.7 0.1 collective-permute-start.11
  44.8 1.1 collective-permute-done.11
  45.9 0.4 collective-permute-start.12
  46.3 4.2 %collective-permute-start.16 = (f32[8,128]{1,0:T(8,128)S(1)}, f32[8,128]{1,0:T(8,128)S(1)}, u32[]{:S(2)}, u32[]{:S(2)}) collective-permute-start(f32[8,128]{1,0:T(8,128)S(1)} %add.97), channel_id=1, source_target_pairs={{0,2},{1,3},{2,0},{3,1},{4,6},{5,7},{6,4},{7,5},{8,10},{9,11},{10,... | collective-permute-start | bytes 12296 | tf_op jit(solution)/shard_map/ppermute | solution.py:550
  50.5 5.4 %collective-permute-start.13 = (f32[68,8,128]{2,1,0:T(8,128)S(1)}, f32[68,8,128]{2,1,0:T(8,128)S(1)}, u32[]{:S(2)}, u32[]{:S(2)}) collective-permute-start(f32[68,8,128]{2,1,0:T(8,128)S(1)} %get-tuple-element.95), channel_id=1, source_target_pairs={{0,8},{8,16},{16,24},{24,25},{25,17},{17,9},{9,1},{1,2},{2,10},{10... | collective-permute-start | bytes 835592 | tf_op jit(solution)/shard_map/ppermute | solution.py:616
  56.0 0.1 mul.30
  56.1 0.5 collective-permute-start.18
  56.5 5.2 %collective-permute-done.13.refs_1_ = f32[68,8,128]{2,1,0:T(8,128)S(1)} collective-permute-done((f32[68,8,128]{2,1,0:T(8,128)S(1)}, f32[68,8,128]{2,1,0:T(8,128)S(1)}, u32[]{:S(2)}, u32[]{:S(2)}) %collective-permute-start.13) | collective-permute-done | bytes 278560 | tf_op jit(solution)/shard_map/ppermute | solution.py:616
  61.8 1.7 %collective-permute-done.14.refs_2_ = f32[68,8,128]{2,1,0:T(8,128)S(1)} collective-permute-done((f32[68,8,128]{2,1,0:T(8,128)S(1)}, f32[68,8,128]{2,1,0:T(8,128)S(1)}, u32[]{:S(2)}, u32[]{:S(2)}) %collective-permute-start.14) | collective-permute-done | bytes 278560 | tf_op jit(solution)/shard_map/ppermute | solution.py:617
  63.4 5.0 %step1.1 = (f32[4,16,32,128]{3,2,1,0:T(8,128)S(1)}, f32[68,8,128]{2,1,0:T(8,128)S(1)}, f32[68,8,128]{2,1,0:T(8,128)S(1)}, f32[2,32,128]{2,1,0:T(8,128)S(1)}, f32[8,128]{1,0:T(8,128)S(1)}) custom-call(f32[4,16,32,128]{3,2,1,0:T(8,128)S(1)} %get-tuple-element.94.refs_0_, f32[68,8,128]{2,1,0:T(8,128)S(1)} %collective-permute-done.13.refs_1_, ...), custom_call_target="tpu_custom_call" | custom-call | flops 6000000000 | bytes 4000000 | tf_op jit(solution)/shard_map/step1/pallas_call | solution.py:631
  68.4 0.1 collective-permute-start.19
  68.6 1.1 collective-permute-done.19
  69.7 2.3 %collective-permute-start.21 = (f32[68,8,128]{2,1,0:T(8,128)S(1)}, f32[68,8,128]{2,1,0:T(8,128)S(1)}, u32[]{:S(2)}, u32[]{:S(2)}) collective-permute-start(f32[68,8,128]{2,1,0:T(8,128)S(1)} %get-tuple-element.111), channel_id=1, source_target_pairs={{0,8},{8,16},{16,24},{24,25},{25,17},{17,9},{9,1},{1,2},{2,10},{10... | collective-permute-start | bytes 835592 | tf_op jit(solution)/shard_map/ppermute | solution.py:616
  72.0 0.3 collective-permute-start.20
  72.3 4.5 %collective-permute-start.24 = (f32[8,128]{1,0:T(8,128)S(1)}, f32[8,128]{1,0:T(8,128)S(1)}, u32[]{:S(2)}, u32[]{:S(2)}) collective-permute-start(f32[8,128]{1,0:T(8,128)S(1)} %add.106), channel_id=1, source_target_pairs={{0,2},{1,3},{2,0},{3,1},{4,6},{5,7},{6,4},{7,5},{8,10},{9,11},{10,... | collective-permute-start | bytes 12296 | tf_op jit(solution)/shard_map/ppermute | solution.py:550
  76.8 2.5 %collective-permute-done.20 = f32[8,128]{1,0:T(8,128)S(1)} collective-permute-done((f32[8,128]{1,0:T(8,128)S(1)}, f32[8,128]{1,0:T(8,128)S(1)}, u32[]{:S(2)}, u32[]{:S(2)}) %collective-permute-start.20) | collective-permute-done | bytes 4128 | tf_op jit(solution)/shard_map/ppermute | solution.py:550
  79.3 3.5 %collective-permute-start.25 = (f32[8,128]{1,0:T(8,128)S(1)}, f32[8,128]{1,0:T(8,128)S(1)}, u32[]{:S(2)}, u32[]{:S(2)}) collective-permute-start(f32[8,128]{1,0:T(8,128)S(1)} %add.106), channel_id=1, source_target_pairs={{0,3},{1,2},{2,1},{3,0},{4,7},{5,6},{6,5},{7,4},{8,11},{9,10},{10,... | collective-permute-start | bytes 12296 | tf_op jit(solution)/shard_map/ppermute | solution.py:550
  82.9 1.0 collective-permute-done.25
  83.9 5.0 %step2.1 = (f32[4,16,32,128]{3,2,1,0:T(8,128)S(1)}, f32[68,8,128]{2,1,0:T(8,128)S(1)}, f32[68,8,128]{2,1,0:T(8,128)S(1)}, f32[2,32,128]{2,1,0:T(8,128)S(1)}, f32[8,128]{1,0:T(8,128)S(1)}) custom-call(f32[4,16,32,128]{3,2,1,0:T(8,128)S(1)} %get-tuple-element.110.refs_0_, f32[68,8,128]{2,1,0:T(8,128)S(1)} %collective-permute-done.21.refs_1_, ...), custom_call_target="tpu_custom_call" | custom-call | flops 6000000000 | bytes 4000000 | tf_op jit(solution)/shard_map/step2/pallas_call | solution.py:631
  88.9 0.1 collective-permute-start.27
  89.0 1.1 collective-permute-done.27
  90.2 2.0 %collective-permute-start.29 = (f32[68,8,128]{2,1,0:T(8,128)S(1)}, f32[68,8,128]{2,1,0:T(8,128)S(1)}, u32[]{:S(2)}, u32[]{:S(2)}) collective-permute-start(f32[68,8,128]{2,1,0:T(8,128)S(1)} %get-tuple-element.126), channel_id=1, source_target_pairs={{0,8},{8,16},{16,24},{24,25},{25,17},{17,9},{9,1},{1,2},{2,10},{10... | collective-permute-start | bytes 835592 | tf_op jit(solution)/shard_map/ppermute | solution.py:616
  92.2 0.6 collective-permute-start.28
  92.8 5.1 %collective-permute-start.32 = (f32[8,128]{1,0:T(8,128)S(1)}, f32[8,128]{1,0:T(8,128)S(1)}, u32[]{:S(2)}, u32[]{:S(2)}) collective-permute-start(f32[8,128]{1,0:T(8,128)S(1)} %add.112), channel_id=1, source_target_pairs={{0,2},{1,3},{2,0},{3,1},{4,6},{5,7},{6,4},{7,5},{8,10},{9,11},{10,... | collective-permute-start | bytes 12296 | tf_op jit(solution)/shard_map/ppermute | solution.py:550
  97.8 2.2 %collective-permute-done.28 = f32[8,128]{1,0:T(8,128)S(1)} collective-permute-done((f32[8,128]{1,0:T(8,128)S(1)}, f32[8,128]{1,0:T(8,128)S(1)}, u32[]{:S(2)}, u32[]{:S(2)}) %collective-permute-start.28) | collective-permute-done | bytes 4128 | tf_op jit(solution)/shard_map/ppermute | solution.py:550
  100.0 3.9 %collective-permute-start.33 = (f32[8,128]{1,0:T(8,128)S(1)}, f32[8,128]{1,0:T(8,128)S(1)}, u32[]{:S(2)}, u32[]{:S(2)}) collective-permute-start(f32[8,128]{1,0:T(8,128)S(1)} %add.112), channel_id=1, source_target_pairs={{0,3},{1,2},{2,1},{3,0},{4,7},{5,6},{6,5},{7,4},{8,11},{9,10},{10,... | collective-permute-start | bytes 12296 | tf_op jit(solution)/shard_map/ppermute | solution.py:550
  103.9 0.0 collective-permute-start.34
  103.9 1.0 collective-permute-done.33
  104.9 4.9 %step3.1.fields = f32[4,16,32,128]{3,2,1,0:T(8,128)S(1)} custom-call(f32[4,16,32,128]{3,2,1,0:T(8,128)S(1)} %get-tuple-element.128.refs_0_, f32[68,8,128]{2,1,0:T(8,128)S(1)} %collective-permute-done.29.refs_1_, f32[68,8,128]{2,1,0:T(8,128)S(1)} %collective-permute-done.30.refs_2_, f32[4,64,128]{2,1,0:T(8,128)S(1)} %maps.1.refs_3_, ...), custom_call_target="tpu_custom_call" | custom-call | flops 6000000000 | bytes 4000000 | tf_op jit(solution)/shard_map/step3/pallas_call | solution.py:631
  109.8 1.2 send.1
  111.0 0.1 collective-permute-start.38
  111.1 2.1 %collective-permute-start.39 = (f32[64,8,128]{2,1,0:T(8,128)S(1)}, f32[64,8,128]{2,1,0:T(8,128)S(1)}, u32[]{:S(2)}, u32[]{:S(2)}) collective-permute-start(f32[64,8,128]{2,1,0:T(8,128)S(1)} %get-tuple-element.135), channel_id=1, source_target_pairs={{0,16},{8,24},{16,0},{24,8},{1,17},{9,25},{17,1},{25,9},{2,18},{10... | collective-permute-start | bytes 786440 | tf_op jit(solution)/shard_map/ppermute | solution.py:550
  113.2 1.5 %collective-permute-start.40 = (f32[64,8,128]{2,1,0:T(8,128)S(1)}, f32[64,8,128]{2,1,0:T(8,128)S(1)}, u32[]{:S(2)}, u32[]{:S(2)}) collective-permute-start(f32[64,8,128]{2,1,0:T(8,128)S(1)} %get-tuple-element.136), channel_id=1, source_target_pairs={{0,24},{8,16},{16,8},{24,0},{1,25},{9,17},{17,9},{25,1},{2,26},{10... | collective-permute-start | bytes 786440 | tf_op jit(solution)/shard_map/ppermute | solution.py:550
  114.7 3.9 %collective-permute-start.36 = (f32[8,128]{1,0:T(8,128)S(1)}, f32[8,128]{1,0:T(8,128)S(1)}, u32[]{:S(2)}, u32[]{:S(2)}) collective-permute-start(f32[8,128]{1,0:T(8,128)S(1)} %add.117), channel_id=1, source_target_pairs={{0,2},{1,3},{2,0},{3,1},{4,6},{5,7},{6,4},{7,5},{8,10},{9,11},{10,... | collective-permute-start | bytes 12296 | tf_op jit(solution)/shard_map/ppermute | solution.py:550
  118.6 1.6 %collective-permute-start.37 = (f32[8,128]{1,0:T(8,128)S(1)}, f32[8,128]{1,0:T(8,128)S(1)}, u32[]{:S(2)}, u32[]{:S(2)}) collective-permute-start(f32[8,128]{1,0:T(8,128)S(1)} %add.117), channel_id=1, source_target_pairs={{0,3},{1,2},{2,1},{3,0},{4,7},{5,6},{6,5},{7,4},{8,11},{9,10},{10,... | collective-permute-start | bytes 12296 | tf_op jit(solution)/shard_map/ppermute | solution.py:550
  120.2 2.4 %collective-permute-done.37 = f32[8,128]{1,0:T(8,128)S(1)} collective-permute-done((f32[8,128]{1,0:T(8,128)S(1)}, f32[8,128]{1,0:T(8,128)S(1)}, u32[]{:S(2)}, u32[]{:S(2)}) %collective-permute-start.37) | collective-permute-done | bytes 4128 | tf_op jit(solution)/shard_map/ppermute | solution.py:550
  122.6 3.7 %collective-permute-done.40.r3 = f32[64,8,128]{2,1,0:T(8,128)S(1)} collective-permute-done((f32[64,8,128]{2,1,0:T(8,128)S(1)}, f32[64,8,128]{2,1,0:T(8,128)S(1)}, u32[]{:S(2)}, u32[]{:S(2)}) %collective-permute-start.40) | collective-permute-done | bytes 262176 | tf_op jit(solution)/shard_map/ppermute | solution.py:550
  126.3 3.1 %final.1 = f32[4,16,32,128]{3,2,1,0:T(8,128)} custom-call(s32[135]{0:T(256)S(1)} %concatenate.3.scal.ints, f32[8,128]{1,0:T(8,128)S(1)} %add_add_fusion.mean, f32[64,8,128]{2,1,0:T(8,128)S(1)} %get-tuple-element.133.s0, f32[64,8,128]{2,1,0:T(8,128)S(1)} %collective-permute-done.38.r1, f32[64,8,128]{2,1,0:T(8,128)S(1)} %collective-permute-done.39.r2, ...), custom_call_target="tpu_custom_call" | custom-call | flops 2000000000 | bytes 4000000 | tf_op jit(solution)/shard_map/final/pallas_call | solution.py:659
  (59 shorter events, 0.2 us)
Async XLA Ops:
  0.0 6.3 %copy-start.1 = (f32[2,4,32,128]{3,2,1,0:T(8,128)S(1)}, f32[2,4,32,128]{3,2,1,0:T(8,128)}, u32[]{:S(2)}) copy-start(f32[2,4,32,128]{3,2,1,0:T(8,128)} %planes.1) | copy-start | bytes 393220
  0.9 5.4 %collective-permute-start = (f32[16,128]{1,0:T(8,128)S(1)}, f32[16,128]{1,0:T(8,128)S(1)}, u32[]{:S(2)}, u32[]{:S(2)}) collective-permute-start(f32[16,128]{1,0:T(8,128)S(1)} %get-tuple-element.138), channel_id=1, source_target_pairs={{0,1},{1,2},{2,3},{3,4},{4,5},{5,6},{6,7},{7,0},{8,9},{9,10},{10,1... | collective-permute-start | bytes 24584 | tf_op jit(solution)/shard_map/ppermute | solution.py:569
  2.9 3.3 %collective-permute-start.1 = (f32[16,128]{1,0:T(8,128)S(1)}, f32[16,128]{1,0:T(8,128)S(1)}, u32[]{:S(2)}, u32[]{:S(2)}) collective-permute-start(f32[16,128]{1,0:T(8,128)S(1)} %get-tuple-element.138), channel_id=1, source_target_pairs={{1,0},{2,1},{3,2},{4,3},{5,4},{6,5},{7,6},{0,7},{9,8},{10,9},{11,1... | collective-permute-start | bytes 24584 | tf_op jit(solution)/shard_map/ppermute | solution.py:569
  6.3 1.2 copy-start
  9.2 5.2 %collective-permute-start.2 = (f32[71,8,128]{2,1,0:T(8,128)S(1)}, f32[71,8,128]{2,1,0:T(8,128)S(1)}, u32[]{:S(2)}, u32[]{:S(2)}) collective-permute-start(f32[71,8,128]{2,1,0:T(8,128)S(1)} %get-tuple-element.72), channel_id=1, source_target_pairs={{0,8},{8,0},{16,24},{24,16},{1,9},{9,1},{17,25},{25,17},{2,10},{10... | collective-permute-start | bytes 872456 | tf_op jit(solution)/shard_map/ppermute | solution.py:550
  11.2 10.1 %collective-permute-start.3 = (f32[71,8,128]{2,1,0:T(8,128)S(1)}, f32[71,8,128]{2,1,0:T(8,128)S(1)}, u32[]{:S(2)}, u32[]{:S(2)}) collective-permute-start(f32[71,8,128]{2,1,0:T(8,128)S(1)} %get-tuple-element.75), channel_id=1, source_target_pairs={{0,16},{8,24},{16,0},{24,8},{1,17},{9,25},{17,1},{25,9},{2,18},{10... | collective-permute-start | bytes 872456 | tf_op jit(solution)/shard_map/ppermute | solution.py:550
  14.2 13.4 %collective-permute-start.4 = (f32[71,8,128]{2,1,0:T(8,128)S(1)}, f32[71,8,128]{2,1,0:T(8,128)S(1)}, u32[]{:S(2)}, u32[]{:S(2)}) collective-permute-start(f32[71,8,128]{2,1,0:T(8,128)S(1)} %get-tuple-element.76), channel_id=1, source_target_pairs={{0,24},{8,16},{16,8},{24,0},{1,25},{9,17},{17,9},{25,1},{2,26},{10... | collective-permute-start | bytes 872456 | tf_op jit(solution)/shard_map/ppermute | solution.py:550
  14.4 13.2 %collective-permute-start.5 = (f32[8,8,128]{2,1,0:T(8,128)S(1)}, f32[8,8,128]{2,1,0:T(8,128)S(1)}, u32[]{:S(2)}, u32[]{:S(2)}) collective-permute-start(f32[8,8,128]{2,1,0:T(8,128)S(1)} %get-tuple-element.77.p0), channel_id=1, source_target_pairs={{0,32},{32,0},{64,96},{96,64},{1,33},{33,1},{65,97},{97,65},{2,34}... | collective-permute-start | bytes 98312 | tf_op jit(solution)/shard_map/ppermute | solution.py:550
  16.2 11.4 %collective-permute-start.6 = (f32[8,8,128]{2,1,0:T(8,128)S(1)}, f32[8,8,128]{2,1,0:T(8,128)S(1)}, u32[]{:S(2)}, u32[]{:S(2)}) collective-permute-start(f32[8,8,128]{2,1,0:T(8,128)S(1)} %get-tuple-element.77.p0), channel_id=1, source_target_pairs={{0,64},{32,96},{64,0},{96,32},{1,65},{33,97},{65,1},{97,33},{2,66}... | collective-permute-start | bytes 98312 | tf_op jit(solution)/shard_map/ppermute | solution.py:550
  19.5 8.1 %collective-permute-start.7 = (f32[8,8,128]{2,1,0:T(8,128)S(1)}, f32[8,8,128]{2,1,0:T(8,128)S(1)}, u32[]{:S(2)}, u32[]{:S(2)}) collective-permute-start(f32[8,8,128]{2,1,0:T(8,128)S(1)} %get-tuple-element.77.p0), channel_id=1, source_target_pairs={{0,96},{32,64},{64,32},{96,0},{1,97},{33,65},{65,33},{97,1},{2,98}... | collective-permute-start | bytes 98312 | tf_op jit(solution)/shard_map/ppermute | solution.py:550
  29.4 10.1 %collective-permute-start.8 = (f32[72,8,128]{2,1,0:T(8,128)S(1)}, f32[72,8,128]{2,1,0:T(8,128)S(1)}, u32[]{:S(2)}, u32[]{:S(2)}) collective-permute-start(f32[72,8,128]{2,1,0:T(8,128)S(1)} %get-tuple-element.79), channel_id=1, source_target_pairs={{0,8},{8,16},{16,24},{24,25},{25,17},{17,9},{9,1},{1,2},{2,10},{10... | collective-permute-start | bytes 884744 | tf_op jit(solution)/shard_map/ppermute | solution.py:616
  32.6 7.7 %collective-permute-start.9 = (f32[72,8,128]{2,1,0:T(8,128)S(1)}, f32[72,8,128]{2,1,0:T(8,128)S(1)}, u32[]{:S(2)}, u32[]{:S(2)}) collective-permute-start(f32[72,8,128]{2,1,0:T(8,128)S(1)} %get-tuple-element.80), channel_id=1, source_target_pairs={{8,0},{16,8},{24,16},{25,24},{17,25},{9,17},{1,9},{2,1},{10,2},{18... | collective-permute-start | bytes 884744 | tf_op jit(solution)/shard_map/ppermute | solution.py:617
  32.6 12.2 %collective-permute-start.10 = (f32[8,128]{1,0:T(8,128)S(1)}, f32[8,128]{1,0:T(8,128)S(1)}, u32[]{:S(2)}, u32[]{:S(2)}) collective-permute-start(f32[8,128]{1,0:T(8,128)S(1)} %get-tuple-element.87), channel_id=1, source_target_pairs={{0,4},{1,5},{2,6},{3,7},{4,0},{5,1},{6,2},{7,3},{8,12},{9,13},{10,... | collective-permute-start | bytes 12296 | tf_op jit(solution)/shard_map/ppermute | solution.py:550
  44.7 1.2 collective-permute-start.11
  45.9 10.0 %collective-permute-start.12 = (f32[8,128]{1,0:T(8,128)S(1)}, f32[8,128]{1,0:T(8,128)S(1)}, u32[]{:S(2)}, u32[]{:S(2)}) collective-permute-start(f32[8,128]{1,0:T(8,128)S(1)} %add.96), channel_id=1, source_target_pairs={{0,4},{1,5},{2,6},{3,7},{4,0},{5,1},{6,2},{7,3},{8,12},{9,13},{10,... | collective-permute-start | bytes 12296 | tf_op jit(solution)/shard_map/ppermute | solution.py:550
  46.3 9.7 %collective-permute-start.15 = (f32[8,128]{1,0:T(8,128)S(1)}, f32[8,128]{1,0:T(8,128)S(1)}, u32[]{:S(2)}, u32[]{:S(2)}) collective-permute-start(f32[8,128]{1,0:T(8,128)S(1)} %add.97), channel_id=1, source_target_pairs={{0,1},{1,0},{2,3},{3,2},{4,5},{5,4},{6,7},{7,6},{8,9},{9,8},{10,11... | collective-permute-start | bytes 12296 | tf_op jit(solution)/shard_map/ppermute | solution.py:550
  46.3 10.2 %collective-permute-start.16 = (f32[8,128]{1,0:T(8,128)S(1)}, f32[8,128]{1,0:T(8,128)S(1)}, u32[]{:S(2)}, u32[]{:S(2)}) collective-permute-start(f32[8,128]{1,0:T(8,128)S(1)} %add.97), channel_id=1, source_target_pairs={{0,2},{1,3},{2,0},{3,1},{4,6},{5,7},{6,4},{7,5},{8,10},{9,11},{10,... | collective-permute-start | bytes 12296 | tf_op jit(solution)/shard_map/ppermute | solution.py:550
  50.5 6.0 %collective-permute-start.17 = (f32[8,128]{1,0:T(8,128)S(1)}, f32[8,128]{1,0:T(8,128)S(1)}, u32[]{:S(2)}, u32[]{:S(2)}) collective-permute-start(f32[8,128]{1,0:T(8,128)S(1)} %add.97), channel_id=1, source_target_pairs={{0,3},{1,2},{2,1},{3,0},{4,7},{5,6},{6,5},{7,4},{8,11},{9,10},{10,... | collective-permute-start | bytes 12296 | tf_op jit(solution)/shard_map/ppermute | solution.py:550
  50.5 11.3 %collective-permute-start.13 = (f32[68,8,128]{2,1,0:T(8,128)S(1)}, f32[68,8,128]{2,1,0:T(8,128)S(1)}, u32[]{:S(2)}, u32[]{:S(2)}) collective-permute-start(f32[68,8,128]{2,1,0:T(8,128)S(1)} %get-tuple-element.95), channel_id=1, source_target_pairs={{0,8},{8,16},{16,24},{24,25},{25,17},{17,9},{9,1},{1,2},{2,10},{10... | collective-permute-start | bytes 835592 | tf_op jit(solution)/shard_map/ppermute | solution.py:616
  56.0 7.5 %collective-permute-start.14 = (f32[68,8,128]{2,1,0:T(8,128)S(1)}, f32[68,8,128]{2,1,0:T(8,128)S(1)}, u32[]{:S(2)}, u32[]{:S(2)}) collective-permute-start(f32[68,8,128]{2,1,0:T(8,128)S(1)} %get-tuple-element.96), channel_id=1, source_target_pairs={{8,0},{16,8},{24,16},{25,24},{17,25},{9,17},{1,9},{2,1},{10,2},{18... | collective-permute-start | bytes 835592 | tf_op jit(solution)/shard_map/ppermute | solution.py:617
  56.1 12.5 %collective-permute-start.18 = (f32[8,128]{1,0:T(8,128)S(1)}, f32[8,128]{1,0:T(8,128)S(1)}, u32[]{:S(2)}, u32[]{:S(2)}) collective-permute-start(f32[8,128]{1,0:T(8,128)S(1)} %add.98), channel_id=1, source_target_pairs={{0,16},{8,24},{16,0},{24,8},{1,17},{9,25},{17,1},{25,9},{2,18},{10... | collective-permute-start | bytes 12296 | tf_op jit(solution)/shard_map/ppermute | solution.py:550
  68.4 1.2 collective-permute-start.19
  69.7 14.2 %collective-permute-start.21 = (f32[68,8,128]{2,1,0:T(8,128)S(1)}, f32[68,8,128]{2,1,0:T(8,128)S(1)}, u32[]{:S(2)}, u32[]{:S(2)}) collective-permute-start(f32[68,8,128]{2,1,0:T(8,128)S(1)} %get-tuple-element.111), channel_id=1, source_target_pairs={{0,8},{8,16},{16,24},{24,25},{25,17},{17,9},{9,1},{1,2},{2,10},{10... | collective-permute-start | bytes 835592 | tf_op jit(solution)/shard_map/ppermute | solution.py:616
  72.0 11.9 %collective-permute-start.22 = (f32[68,8,128]{2,1,0:T(8,128)S(1)}, f32[68,8,128]{2,1,0:T(8,128)S(1)}, u32[]{:S(2)}, u32[]{:S(2)}) collective-permute-start(f32[68,8,128]{2,1,0:T(8,128)S(1)} %get-tuple-element.112), channel_id=1, source_target_pairs={{8,0},{16,8},{24,16},{25,24},{17,25},{9,17},{1,9},{2,1},{10,2},{18... | collective-permute-start | bytes 835592 | tf_op jit(solution)/shard_map/ppermute | solution.py:617
  72.0 7.3 %collective-permute-start.20 = (f32[8,128]{1,0:T(8,128)S(1)}, f32[8,128]{1,0:T(8,128)S(1)}, u32[]{:S(2)}, u32[]{:S(2)}) collective-permute-start(f32[8,128]{1,0:T(8,128)S(1)} %add.105), channel_id=1, source_target_pairs={{0,4},{1,5},{2,6},{3,7},{4,0},{5,1},{6,2},{7,3},{8,12},{9,13},{10,... | collective-permute-start | bytes 12296 | tf_op jit(solution)/shard_map/ppermute | solution.py:550
  72.3 10.5 %collective-permute-start.23 = (f32[8,128]{1,0:T(8,128)S(1)}, f32[8,128]{1,0:T(8,128)S(1)}, u32[]{:S(2)}, u32[]{:S(2)}) collective-permute-start(f32[8,128]{1,0:T(8,128)S(1)} %add.106), channel_id=1, source_target_pairs={{0,1},{1,0},{2,3},{3,2},{4,5},{5,4},{6,7},{7,6},{8,9},{9,8},{10,11... | collective-permute-start | bytes 12296 | tf_op jit(solution)/shard_map/ppermute | solution.py:550
  72.3 10.5 %collective-permute-start.24 = (f32[8,128]{1,0:T(8,128)S(1)}, f32[8,128]{1,0:T(8,128)S(1)}, u32[]{:S(2)}, u32[]{:S(2)}) collective-permute-start(f32[8,128]{1,0:T(8,128)S(1)} %add.106), channel_id=1, source_target_pairs={{0,2},{1,3},{2,0},{3,1},{4,6},{5,7},{6,4},{7,5},{8,10},{9,11},{10,... | collective-permute-start | bytes 12296 | tf_op jit(solution)/shard_map/ppermute | solution.py:550
  79.3 4.5 %collective-permute-start.25 = (f32[8,128]{1,0:T(8,128)S(1)}, f32[8,128]{1,0:T(8,128)S(1)}, u32[]{:S(2)}, u32[]{:S(2)}) collective-permute-start(f32[8,128]{1,0:T(8,128)S(1)} %add.106), channel_id=1, source_target_pairs={{0,3},{1,2},{2,1},{3,0},{4,7},{5,6},{6,5},{7,4},{8,11},{9,10},{10,... | collective-permute-start | bytes 12296 | tf_op jit(solution)/shard_map/ppermute | solution.py:550
  82.9 6.1 %collective-permute-start.26 = (f32[8,128]{1,0:T(8,128)S(1)}, f32[8,128]{1,0:T(8,128)S(1)}, u32[]{:S(2)}, u32[]{:S(2)}) collective-permute-start(f32[8,128]{1,0:T(8,128)S(1)} %add.107), channel_id=1, source_target_pairs={{0,16},{8,24},{16,0},{24,8},{1,17},{9,25},{17,1},{25,9},{2,18},{10... | collective-permute-start | bytes 12296 | tf_op jit(solution)/shard_map/ppermute | solution.py:550
  88.9 1.2 collective-permute-start.27
  90.2 14.7 %collective-permute-start.29 = (f32[68,8,128]{2,1,0:T(8,128)S(1)}, f32[68,8,128]{2,1,0:T(8,128)S(1)}, u32[]{:S(2)}, u32[]{:S(2)}) collective-permute-start(f32[68,8,128]{2,1,0:T(8,128)S(1)} %get-tuple-element.126), channel_id=1, source_target_pairs={{0,8},{8,16},{16,24},{24,25},{25,17},{17,9},{9,1},{1,2},{2,10},{10... | collective-permute-start | bytes 835592 | tf_op jit(solution)/shard_map/ppermute | solution.py:616
  92.2 12.7 %collective-permute-start.30 = (f32[68,8,128]{2,1,0:T(8,128)S(1)}, f32[68,8,128]{2,1,0:T(8,128)S(1)}, u32[]{:S(2)}, u32[]{:S(2)}) collective-permute-start(f32[68,8,128]{2,1,0:T(8,128)S(1)} %get-tuple-element.127), channel_id=1, source_target_pairs={{8,0},{16,8},{24,16},{25,24},{17,25},{9,17},{1,9},{2,1},{10,2},{18... | collective-permute-start | bytes 835592 | tf_op jit(solution)/shard_map/ppermute | solution.py:617
  92.2 7.8 %collective-permute-start.28 = (f32[8,128]{1,0:T(8,128)S(1)}, f32[8,128]{1,0:T(8,128)S(1)}, u32[]{:S(2)}, u32[]{:S(2)}) collective-permute-start(f32[8,128]{1,0:T(8,128)S(1)} %add.111), channel_id=1, source_target_pairs={{0,4},{1,5},{2,6},{3,7},{4,0},{5,1},{6,2},{7,3},{8,12},{9,13},{10,... | collective-permute-start | bytes 12296 | tf_op jit(solution)/shard_map/ppermute | solution.py:550
  92.8 11.1 %collective-permute-start.31 = (f32[8,128]{1,0:T(8,128)S(1)}, f32[8,128]{1,0:T(8,128)S(1)}, u32[]{:S(2)}, u32[]{:S(2)}) collective-permute-start(f32[8,128]{1,0:T(8,128)S(1)} %add.112), channel_id=1, source_target_pairs={{0,1},{1,0},{2,3},{3,2},{4,5},{5,4},{6,7},{7,6},{8,9},{9,8},{10,11... | collective-permute-start | bytes 12296 | tf_op jit(solution)/shard_map/ppermute | solution.py:550
  92.8 11.1 %collective-permute-start.32 = (f32[8,128]{1,0:T(8,128)S(1)}, f32[8,128]{1,0:T(8,128)S(1)}, u32[]{:S(2)}, u32[]{:S(2)}) collective-permute-start(f32[8,128]{1,0:T(8,128)S(1)} %add.112), channel_id=1, source_target_pairs={{0,2},{1,3},{2,0},{3,1},{4,6},{5,7},{6,4},{7,5},{8,10},{9,11},{10,... | collective-permute-start | bytes 12296 | tf_op jit(solution)/shard_map/ppermute | solution.py:550
  100.0 4.9 %collective-permute-start.33 = (f32[8,128]{1,0:T(8,128)S(1)}, f32[8,128]{1,0:T(8,128)S(1)}, u32[]{:S(2)}, u32[]{:S(2)}) collective-permute-start(f32[8,128]{1,0:T(8,128)S(1)} %add.112), channel_id=1, source_target_pairs={{0,3},{1,2},{2,1},{3,0},{4,7},{5,6},{6,5},{7,4},{8,11},{9,10},{10,... | collective-permute-start | bytes 12296 | tf_op jit(solution)/shard_map/ppermute | solution.py:550
  103.9 5.9 %collective-permute-start.34 = (f32[8,128]{1,0:T(8,128)S(1)}, f32[8,128]{1,0:T(8,128)S(1)}, u32[]{:S(2)}, u32[]{:S(2)}) collective-permute-start(f32[8,128]{1,0:T(8,128)S(1)} %add.113), channel_id=1, source_target_pairs={{0,16},{8,24},{16,0},{24,8},{1,17},{9,25},{17,1},{25,9},{2,18},{10... | collective-permute-start | bytes 12296 | tf_op jit(solution)/shard_map/ppermute | solution.py:550
  111.0 11.6 %collective-permute-start.38 = (f32[64,8,128]{2,1,0:T(8,128)S(1)}, f32[64,8,128]{2,1,0:T(8,128)S(1)}, u32[]{:S(2)}, u32[]{:S(2)}) collective-permute-start(f32[64,8,128]{2,1,0:T(8,128)S(1)} %get-tuple-element.134), channel_id=1, source_target_pairs={{0,8},{8,0},{16,24},{24,16},{1,9},{9,1},{17,25},{25,17},{2,10},{10... | collective-permute-start | bytes 786440 | tf_op jit(solution)/shard_map/ppermute | solution.py:550
  111.1 11.5 %collective-permute-start.39 = (f32[64,8,128]{2,1,0:T(8,128)S(1)}, f32[64,8,128]{2,1,0:T(8,128)S(1)}, u32[]{:S(2)}, u32[]{:S(2)}) collective-permute-start(f32[64,8,128]{2,1,0:T(8,128)S(1)} %get-tuple-element.135), channel_id=1, source_target_pairs={{0,16},{8,24},{16,0},{24,8},{1,17},{9,25},{17,1},{25,9},{2,18},{10... | collective-permute-start | bytes 786440 | tf_op jit(solution)/shard_map/ppermute | solution.py:550
  113.2 13.1 %collective-permute-start.40 = (f32[64,8,128]{2,1,0:T(8,128)S(1)}, f32[64,8,128]{2,1,0:T(8,128)S(1)}, u32[]{:S(2)}, u32[]{:S(2)}) collective-permute-start(f32[64,8,128]{2,1,0:T(8,128)S(1)} %get-tuple-element.136), channel_id=1, source_target_pairs={{0,24},{8,16},{16,8},{24,0},{1,25},{9,17},{17,9},{25,1},{2,26},{10... | collective-permute-start | bytes 786440 | tf_op jit(solution)/shard_map/ppermute | solution.py:550
  114.7 3.9 %collective-permute-start.35 = (f32[8,128]{1,0:T(8,128)S(1)}, f32[8,128]{1,0:T(8,128)S(1)}, u32[]{:S(2)}, u32[]{:S(2)}) collective-permute-start(f32[8,128]{1,0:T(8,128)S(1)} %add.117), channel_id=1, source_target_pairs={{0,1},{1,0},{2,3},{3,2},{4,5},{5,4},{6,7},{7,6},{8,9},{9,8},{10,11... | collective-permute-start | bytes 12296 | tf_op jit(solution)/shard_map/ppermute | solution.py:550
  114.7 5.4 %collective-permute-start.36 = (f32[8,128]{1,0:T(8,128)S(1)}, f32[8,128]{1,0:T(8,128)S(1)}, u32[]{:S(2)}, u32[]{:S(2)}) collective-permute-start(f32[8,128]{1,0:T(8,128)S(1)} %add.117), channel_id=1, source_target_pairs={{0,2},{1,3},{2,0},{3,1},{4,6},{5,7},{6,4},{7,5},{8,10},{9,11},{10,... | collective-permute-start | bytes 12296 | tf_op jit(solution)/shard_map/ppermute | solution.py:550
  118.6 4.0 %collective-permute-start.37 = (f32[8,128]{1,0:T(8,128)S(1)}, f32[8,128]{1,0:T(8,128)S(1)}, u32[]{:S(2)}, u32[]{:S(2)}) collective-permute-start(f32[8,128]{1,0:T(8,128)S(1)} %add.117), channel_id=1, source_target_pairs={{0,3},{1,2},{2,1},{3,0},{4,7},{5,6},{6,5},{7,4},{8,11},{9,10},{10,... | collective-permute-start | bytes 12296 | tf_op jit(solution)/shard_map/ppermute | solution.py:550

commit v10 on v4

--- a/solution.py
+++ b/solution.py
@@ -23,7 +23,7 @@
 LOWEST = NZ // 2 - RADIUS
 TILES = 4 * XI
 MORE = 4
-UNROLL = {"fill": 4, "tend": 4, "div": 16, "relax": 16, "correct": 16}
+UNROLL = {"fill": 4, "tend": 8, "div": 16, "relax": 16, "correct": 16}
 
 TIME_STEP = 0.25
 VISCOSITY = 0.02
@@ -120,19 +120,35 @@
     return out
 
 
-def pack_kernel(scal, state, planes, ids, s0, s1, s2, s3, pl_out):
+def transposed4(a, odd, high):
+    b0 = jnp.where(odd, pltpu.roll(a[1], 32, axis=1), a[0])
+    b1 = jnp.where(odd, a[1], pltpu.roll(a[0], 96, axis=1))
+    b2 = jnp.where(odd, pltpu.roll(a[3], 32, axis=1), a[2])
+    b3 = jnp.where(odd, a[3], pltpu.roll(a[2], 96, axis=1))
+    return (
+        jnp.where(high, pltpu.roll(b2, 64, axis=1), b0),
+        jnp.where(high, pltpu.roll(b3, 64, axis=1), b1),
+        jnp.where(high, b2, pltpu.roll(b0, 64, axis=1)),
+        jnp.where(high, b3, pltpu.roll(b1, 64, axis=1)),
+    )
+
+
+def pack_kernel(scal, state, planes, ids, s0, s1, s2, s3, pl_out, stage):
     slab = scal[1]
     group = lanes() >> 5
     masks = [group == c for c in range(4)]
+    odd, high = (group & 1) == 1, group >= 2
 
     def per_row(x, carry):
         for kt in range(4):
             sources = [state[c, x, kt * 8 : kt * 8 + 8, :] for c in range(4)]
-            for s, out in enumerate((s0, s1, s2, s3)):
-                out[x * 4 + kt] = block_transposed(sources, slab ^ s, masks)
+            for b, value in enumerate(transposed4(sources, odd, high)):
+                stage[b, x * 4 + kt] = value
         return carry
 
     rows("fill", per_row)
+    for s, out in enumerate((s0, s1, s2, s3)):
+        out[:TILES] = stage[slab ^ s]
     for half in range(6):
         for out in (s0, s1, s2, s3):
             out[TILES + half] = ids[half // 2, (half % 2) * 8 : (half % 2) * 8 + 8]
@@ -487,12 +503,12 @@
 
     def per_row(xi, carry):
         stacked = jnp.concatenate([fields[c, xi] for c in range(4)], axis=0)
-        turned[...] = stacked.T.reshape(GX, 4, 8, LANES)
+        turned[xi] = stacked.T.reshape(GX, 4, 8, LANES)
         for s, out in enumerate((s0, s1, s2, s3)):
-            out[pl.ds(xi * 4, 4)] = turned[own ^ s]
+            out[pl.ds(xi * 4, 4)] = turned[xi, own ^ s]
         return carry
 
-    lax.fori_loop(0, XI, per_row, 0)
+    rows("fill", per_row)
 
 
 def final_kernel(scal, mean, s0, r1, r2, r3, out, columns, *, cells):
@@ -554,6 +570,7 @@
         pack_kernel,
         (chunk, chunk, chunk, chunk, shape(per_layout * 4, 8, LANES)),
         [SMEM, VMEM, VMEM, VMEM],
+        [pltpu.VMEM((GX, TILES, 8, LANES), F32)],
         name="pack",
     )(scal, state[0], planes, ids)
     received = [swapped(value, "gx", GX, s) for s, value in ((1, s1), (2, s2), (3, s3))]
@@ -629,7 +646,7 @@
         send_kernel,
         (chunk, chunk, chunk, chunk),
         [SMEM, VMEM],
-        [pltpu.VMEM((GX, 4, 8, LANES), F32)],
+        [pltpu.VMEM((XI, GX, 4, 8, LANES), F32)],
         name="send",
     )(scal, fields)
     received = [swapped(value, "gx", GX, s) for s, value in ((1, s1), (2, s2), (3, s3))]

time: 128 us -> 126 us (0.984)
  Pallas kernels: 30.1 us -> 28.4 us
where the time goes in v10:
time: 126 us
  starting transfers between devices  60.1 us (48%)
  waiting for transfers between devices  34.5 us (27%)
  Pallas kernels  28.4 us (23%)
  local copies, waits for them, and re-layouts  3.05 us (2%)
    ppermute x33, starting transfers between devices, swapped(): return lax.ppermute(value, axis, [(i, i ^ distance) for i in range(size)])  46.7 us
    ppermute x33, waiting for transfers between devices, swapped(): return lax.ppermute(value, axis, [(i, i ^ distance) for i in range(size)])  34.2 us
    pallas_call x4, Pallas kernels, local(): call(functools.partial(step_kernel, step=step, cells=cells), tuple(outs),...  19 us
    ppermute x4, starting transfers between devices, local(): lo = lax.ppermute(su, ('gx', 'gy'), up)  8.96 us
    pallas_call x1, Pallas kernels, local(): call(functools.partial(final_kernel, cells=cells), shape(4, XI, NZ, LANES...  3.11 us
  transfers between devices with their start and end apart: 43, of which 20 were waited for; matrix products, arithmetic and copies ran while one was open for 1% of the time, Pallas kernels for 16%

profile of v10, /device:TPU:1, one launch (start us, length us, event | category | flops | bytes accessed | tf_op | source)
XLA Modules:
  0.0 126.3 jit_solution(9948431522742134871)
XLA Ops:
  0.0 0.9 slice.3
  0.9 2.0 %collective-permute-start = (f32[16,128]{1,0:T(8,128)S(1)}, f32[16,128]{1,0:T(8,128)S(1)}, u32[]{:S(2)}, u32[]{:S(2)}) collective-permute-start(f32[16,128]{1,0:T(8,128)S(1)} %get-tuple-element.142), channel_id=1, source_target_pairs={{0,1},{1,2},{2,3},{3,4},{4,5},{5,6},{6,7},{7,0},{8,9},{9,10},{10,1... | collective-permute-start | bytes 24584 | tf_op jit(solution)/shard_map/ppermute | solution.py:567
  2.9 2.4 %collective-permute-start.1 = (f32[16,128]{1,0:T(8,128)S(1)}, f32[16,128]{1,0:T(8,128)S(1)}, u32[]{:S(2)}, u32[]{:S(2)}) collective-permute-start(f32[16,128]{1,0:T(8,128)S(1)} %get-tuple-element.142), channel_id=1, source_target_pairs={{1,0},{2,1},{3,2},{4,3},{5,4},{6,5},{7,6},{0,7},{9,8},{10,9},{11,1... | collective-permute-start | bytes 24584 | tf_op jit(solution)/shard_map/ppermute | solution.py:567
  5.3 0.8 concatenate.3.scal.ints
  6.0 0.2 collective-permute-done
  6.3 1.2 copy-done
  7.5 1.7 %pack.1 = (f32[70,8,128]{2,1,0:T(8,128)S(1)}, f32[70,8,128]{2,1,0:T(8,128)S(1)}, f32[70,8,128]{2,1,0:T(8,128)S(1)}, f32[70,8,128]{2,1,0:T(8,128)S(1)}, f32[8,8,128]{2,1,0:T(8,128)S(1)}) custom-call(s32[135]{0:T(256)S(1)} %concatenate.3.scal.ints, f32[4,16,32,128]{3,2,1,0:T(8,128)S(1)} %bitcast.14, f32[2,4,32,128]{3,2,1,0:T(8,128)S(1)} %copy-done.1, ...), custom_call_target="tpu_custom_call" | custom-call | flops 2000000000 | bytes 4000000 | tf_op jit(solution)/shard_map/pack/pallas_call | solution.py:569
  9.2 1.9 %collective-permute-start.2 = (f32[70,8,128]{2,1,0:T(8,128)S(1)}, f32[70,8,128]{2,1,0:T(8,128)S(1)}, u32[]{:S(2)}, u32[]{:S(2)}) collective-permute-start(f32[70,8,128]{2,1,0:T(8,128)S(1)} %get-tuple-element.74), channel_id=1, source_target_pairs={{0,8},{8,0},{16,24},{24,16},{1,9},{9,1},{17,25},{25,17},{2,10},{10... | collective-permute-start | bytes 860168 | tf_op jit(solution)/shard_map/ppermute | solution.py:548
  11.2 3.0 %collective-permute-start.3 = (f32[70,8,128]{2,1,0:T(8,128)S(1)}, f32[70,8,128]{2,1,0:T(8,128)S(1)}, u32[]{:S(2)}, u32[]{:S(2)}) collective-permute-start(f32[70,8,128]{2,1,0:T(8,128)S(1)} %get-tuple-element.77), channel_id=1, source_target_pairs={{0,16},{8,24},{16,0},{24,8},{1,17},{9,25},{17,1},{25,9},{2,18},{10... | collective-permute-start | bytes 860168 | tf_op jit(solution)/shard_map/ppermute | solution.py:548
  14.2 0.2 collective-permute-start.4
  14.4 1.8 %collective-permute-start.5 = (f32[8,8,128]{2,1,0:T(8,128)S(1)}, f32[8,8,128]{2,1,0:T(8,128)S(1)}, u32[]{:S(2)}, u32[]{:S(2)}) collective-permute-start(f32[8,8,128]{2,1,0:T(8,128)S(1)} %get-tuple-element.79.p0), channel_id=1, source_target_pairs={{0,32},{32,0},{64,96},{96,64},{1,33},{33,1},{65,97},{97,65},{2,34}... | collective-permute-start | bytes 98312 | tf_op jit(solution)/shard_map/ppermute | solution.py:548
  16.2 3.3 %collective-permute-start.6 = (f32[8,8,128]{2,1,0:T(8,128)S(1)}, f32[8,8,128]{2,1,0:T(8,128)S(1)}, u32[]{:S(2)}, u32[]{:S(2)}) collective-permute-start(f32[8,8,128]{2,1,0:T(8,128)S(1)} %get-tuple-element.79.p0), channel_id=1, source_target_pairs={{0,64},{32,96},{64,0},{96,32},{1,65},{33,97},{65,1},{97,33},{2,66}... | collective-permute-start | bytes 98312 | tf_op jit(solution)/shard_map/ppermute | solution.py:548
  19.7 1.5 %collective-permute-done.3.r2 = f32[70,8,128]{2,1,0:T(8,128)S(1)} collective-permute-done((f32[70,8,128]{2,1,0:T(8,128)S(1)}, f32[70,8,128]{2,1,0:T(8,128)S(1)}, u32[]{:S(2)}, u32[]{:S(2)}) %collective-permute-start.3) | collective-permute-done | bytes 286752 | tf_op jit(solution)/shard_map/ppermute | solution.py:548
  21.2 6.2 %collective-permute-done.4.r3 = f32[70,8,128]{2,1,0:T(8,128)S(1)} collective-permute-done((f32[70,8,128]{2,1,0:T(8,128)S(1)}, f32[70,8,128]{2,1,0:T(8,128)S(1)}, u32[]{:S(2)}, u32[]{:S(2)}) %collective-permute-start.4) | collective-permute-done | bytes 286752 | tf_op jit(solution)/shard_map/ppermute | solution.py:548
  27.5 1.8 %unpack.1 = (f32[4,16,32,128]{3,2,1,0:T(8,128)S(1)}, f32[4,32,128]{2,1,0:T(8,128)S(1)}, f32[72,8,128]{2,1,0:T(8,128)S(1)}, f32[72,8,128]{2,1,0:T(8,128)S(1)}, f3...) custom-call(s32[135]{0:T(256)S(1)} %concatenate.3.scal.ints, ...), custom_call_target="tpu_custom_call" | custom-call | flops 2000000000 | bytes 4000000 | tf_op jit(solution)/shard_map/unpack/pallas_call | solution.py:581
  29.3 0.4 collective-permute-start.8
  29.6 0.9 collective-permute-done.8
  30.5 3.1 %collective-permute-start.10 = (f32[72,8,128]{2,1,0:T(8,128)S(1)}, f32[72,8,128]{2,1,0:T(8,128)S(1)}, u32[]{:S(2)}, u32[]{:S(2)}) collective-permute-start(f32[72,8,128]{2,1,0:T(8,128)S(1)} %get-tuple-element.86), channel_id=1, source_target_pairs={{0,8},{8,16},{16,24},{24,25},{25,17},{17,9},{9,1},{1,2},{2,10},{10... | collective-permute-start | bytes 884744 | tf_op jit(solution)/shard_map/ppermute | solution.py:611
  33.6 0.4 collective-permute-start.9
  34.0 1.6 %maps.1.refs_3_ = f32[4,64,128]{2,1,0:T(8,128)S(1)} custom-call(s32[135]{0:T(256)S(1)} %concatenate.3.scal.ints, f32[3,4,16,128]{3,2,1,0:T(8,128)S(1)} %get-tuple-element.88.ids), custom_call_target="tpu_custom_call" | custom-call | flops 2000000000 | bytes 4000000 | tf_op jit(solution)/shard_map/maps/pallas_call | solution.py:600
  35.7 5.7 %collective-permute-done.9 = f32[8,128]{1,0:T(8,128)S(1)} collective-permute-done((f32[8,128]{1,0:T(8,128)S(1)}, f32[8,128]{1,0:T(8,128)S(1)}, u32[]{:S(2)}, u32[]{:S(2)}) %collective-permute-start.9) | collective-permute-done | bytes 4128 | tf_op jit(solution)/shard_map/ppermute | solution.py:548
  41.4 4.3 %step0.1 = (f32[4,16,32,128]{3,2,1,0:T(8,128)S(1)}, f32[68,8,128]{2,1,0:T(8,128)S(1)}, f32[68,8,128]{2,1,0:T(8,128)S(1)}, f32[2,32,128]{2,1,0:T(8,128)S(1)}, f32...) custom-call(f32[4,16,32,128]{3,2,1,0:T(8,128)S(1)} %get-tuple-element.85.refs_0_, ...), custom_call_target="tpu_custom_call" | custom-call | flops 6000000000 | bytes 4000000 | tf_op jit(solution)/shard_map/step0/pallas_call | solution.py:625
  45.7 2.0 %collective-permute-start.13 = (f32[8,128]{1,0:T(8,128)S(1)}, f32[8,128]{1,0:T(8,128)S(1)}, u32[]{:S(2)}, u32[]{:S(2)}) collective-permute-start(f32[8,128]{1,0:T(8,128)S(1)} %get-tuple-element.98), channel_id=1, source_target_pairs={{0,8},{8,0},{16,24},{24,16},{1,9},{9,1},{17,25},{25,17},{2,10},{10... | collective-permute-start | bytes 12296 | tf_op jit(solution)/shard_map/ppermute | solution.py:548
  47.7 0.8 collective-permute-done.13
  48.5 1.5 %collective-permute-start.15 = (f32[68,8,128]{2,1,0:T(8,128)S(1)}, f32[68,8,128]{2,1,0:T(8,128)S(1)}, u32[]{:S(2)}, u32[]{:S(2)}) collective-permute-start(f32[68,8,128]{2,1,0:T(8,128)S(1)} %get-tuple-element.101), channel_id=1, source_target_pairs={{0,8},{8,16},{16,24},{24,25},{25,17},{17,9},{9,1},{1,2},{2,10},{10... | collective-permute-start | bytes 835592 | tf_op jit(solution)/shard_map/ppermute | solution.py:611
  50.1 0.2 collective-permute-start.17
  50.2 5.0 %collective-permute-start.18 = (f32[8,128]{1,0:T(8,128)S(1)}, f32[8,128]{1,0:T(8,128)S(1)}, u32[]{:S(2)}, u32[]{:S(2)}) collective-permute-start(f32[8,128]{1,0:T(8,128)S(1)} %add.95), channel_id=1, source_target_pairs={{0,2},{1,3},{2,0},{3,1},{4,6},{5,7},{6,4},{7,5},{8,10},{9,11},{10,... | collective-permute-start | bytes 12296 | tf_op jit(solution)/shard_map/ppermute | solution.py:548
  55.2 1.1 collective-permute-start.14
  56.3 0.2 collective-permute-done.18
  56.5 2.4 %collective-permute-done.19 = f32[8,128]{1,0:T(8,128)S(1)} collective-permute-done((f32[8,128]{1,0:T(8,128)S(1)}, f32[8,128]{1,0:T(8,128)S(1)}, u32[]{:S(2)}, u32[]{:S(2)}) %collective-permute-start.19) | collective-permute-done | bytes 4128 | tf_op jit(solution)/shard_map/ppermute | solution.py:548
  58.9 1.5 %collective-permute-start.20 = (f32[8,128]{1,0:T(8,128)S(1)}, f32[8,128]{1,0:T(8,128)S(1)}, u32[]{:S(2)}, u32[]{:S(2)}) collective-permute-start(f32[8,128]{1,0:T(8,128)S(1)} %add.94), channel_id=1, source_target_pairs={{0,16},{8,24},{16,0},{24,8},{1,17},{9,25},{17,1},{25,9},{2,18},{10... | collective-permute-start | bytes 12296 | tf_op jit(solution)/shard_map/ppermute | solution.py:548
  60.4 4.9 %step1.1 = (f32[4,16,32,128]{3,2,1,0:T(8,128)S(1)}, f32[68,8,128]{2,1,0:T(8,128)S(1)}, f32[68,8,128]{2,1,0:T(8,128)S(1)}, f32[2,32,128]{2,1,0:T(8,128)S(1)}, f32[8,128]{1,0:T(8,128)S(1)}) custom-call(f32[4,16,32,128]{3,2,1,0:T(8,128)S(1)} %get-tuple-element.100.refs_0_, f32[68,8,128]{2,1,0:T(8,128)S(1)} %collective-permute-done.15.refs_1_, ...), custom_call_target="tpu_custom_call" | custom-call | flops 6000000000 | bytes 4000000 | tf_op jit(solution)/shard_map/step1/pallas_call | solution.py:625
  65.4 1.6 %collective-permute-start.21 = (f32[8,128]{1,0:T(8,128)S(1)}, f32[8,128]{1,0:T(8,128)S(1)}, u32[]{:S(2)}, u32[]{:S(2)}) collective-permute-start(f32[8,128]{1,0:T(8,128)S(1)} %get-tuple-element.113), channel_id=1, source_target_pairs={{0,8},{8,0},{16,24},{24,16},{1,9},{9,1},{17,25},{25,17},{2,10},{10... | collective-permute-start | bytes 12296 | tf_op jit(solution)/shard_map/ppermute | solution.py:548
  67.0 0.8 collective-permute-done.21
  67.9 2.8 %collective-permute-start.23 = (f32[68,8,128]{2,1,0:T(8,128)S(1)}, f32[68,8,128]{2,1,0:T(8,128)S(1)}, u32[]{:S(2)}, u32[]{:S(2)}) collective-permute-start(f32[68,8,128]{2,1,0:T(8,128)S(1)} %get-tuple-element.116), channel_id=1, source_target_pairs={{0,8},{8,16},{16,24},{24,25},{25,17},{17,9},{9,1},{1,2},{2,10},{10... | collective-permute-start | bytes 835592 | tf_op jit(solution)/shard_map/ppermute | solution.py:611
  70.7 2.8 %collective-permute-start.26 = (f32[8,128]{1,0:T(8,128)S(1)}, f32[8,128]{1,0:T(8,128)S(1)}, u32[]{:S(2)}, u32[]{:S(2)}) collective-permute-start(f32[8,128]{1,0:T(8,128)S(1)} %add.101), channel_id=1, source_target_pairs={{0,2},{1,3},{2,0},{3,1},{4,6},{5,7},{6,4},{7,5},{8,10},{9,11},{10,... | collective-permute-start | bytes 12296 | tf_op jit(solution)/shard_map/ppermute | solution.py:548
  73.5 1.0 collective-permute-start.27
  74.5 0.5 collective-permute-done.26
  75.0 2.2 %collective-permute-done.27 = f32[8,128]{1,0:T(8,128)S(1)} collective-permute-done((f32[8,128]{1,0:T(8,128)S(1)}, f32[8,128]{1,0:T(8,128)S(1)}, u32[]{:S(2)}, u32[]{:S(2)}) %collective-permute-start.27) | collective-permute-done | bytes 4128 | tf_op jit(solution)/shard_map/ppermute | solution.py:548
  77.2 0.6 collective-permute-done.22
  77.8 1.2 collective-permute-start.28
  78.9 4.9 %step2.1 = (f32[4,16,32,128]{3,2,1,0:T(8,128)S(1)}, f32[68,8,128]{2,1,0:T(8,128)S(1)}, f32[68,8,128]{2,1,0:T(8,128)S(1)}, f32[2,32,128]{2,1,0:T(8,128)S(1)}, f32[8,128]{1,0:T(8,128)S(1)}) custom-call(f32[4,16,32,128]{3,2,1,0:T(8,128)S(1)} %get-tuple-element.115.refs_0_, f32[68,8,128]{2,1,0:T(8,128)S(1)} %collective-permute-done.23.refs_1_, ...), custom_call_target="tpu_custom_call" | custom-call | flops 6000000000 | bytes 4000000 | tf_op jit(solution)/shard_map/step2/pallas_call | solution.py:625
  83.9 3.8 %collective-permute-start.29 = (f32[8,128]{1,0:T(8,128)S(1)}, f32[8,128]{1,0:T(8,128)S(1)}, u32[]{:S(2)}, u32[]{:S(2)}) collective-permute-start(f32[8,128]{1,0:T(8,128)S(1)} %get-tuple-element.127), channel_id=1, source_target_pairs={{0,8},{8,0},{16,24},{24,16},{1,9},{9,1},{17,25},{25,17},{2,10},{10... | collective-permute-start | bytes 12296 | tf_op jit(solution)/shard_map/ppermute | solution.py:548
  87.6 0.8 collective-permute-done.29
  88.5 1.5 %collective-permute-start.31 = (f32[68,8,128]{2,1,0:T(8,128)S(1)}, f32[68,8,128]{2,1,0:T(8,128)S(1)}, u32[]{:S(2)}, u32[]{:S(2)}) collective-permute-start(f32[68,8,128]{2,1,0:T(8,128)S(1)} %get-tuple-element.130), channel_id=1, source_target_pairs={{0,8},{8,16},{16,24},{24,25},{25,17},{17,9},{9,1},{1,2},{2,10},{10... | collective-permute-start | bytes 835592 | tf_op jit(solution)/shard_map/ppermute | solution.py:611
  90.0 0.4 collective-permute-start.33
  90.4 3.6 %collective-permute-start.34 = (f32[8,128]{1,0:T(8,128)S(1)}, f32[8,128]{1,0:T(8,128)S(1)}, u32[]{:S(2)}, u32[]{:S(2)}) collective-permute-start(f32[8,128]{1,0:T(8,128)S(1)} %add.107), channel_id=1, source_target_pairs={{0,2},{1,3},{2,0},{3,1},{4,6},{5,7},{6,4},{7,5},{8,10},{9,11},{10,... | collective-permute-start | bytes 12296 | tf_op jit(solution)/shard_map/ppermute | solution.py:548
  93.9 0.9 collective-permute-start.30
  94.8 0.4 collective-permute-done.34
  95.3 2.4 %collective-permute-done.35 = f32[8,128]{1,0:T(8,128)S(1)} collective-permute-done((f32[8,128]{1,0:T(8,128)S(1)}, f32[8,128]{1,0:T(8,128)S(1)}, u32[]{:S(2)}, u32[]{:S(2)}) %collective-permute-start.35) | collective-permute-done | bytes 4128 | tf_op jit(solution)/shard_map/ppermute | solution.py:548
  97.7 0.6 collective-permute-done.30
  98.2 0.3 collective-permute-start.36
  98.5 4.8 %step3.1.fields = f32[4,16,32,128]{3,2,1,0:T(8,128)S(1)} custom-call(f32[4,16,32,128]{3,2,1,0:T(8,128)S(1)} %get-tuple-element.132.refs_0_, f32[68,8,128]{2,1,0:T(8,128)S(1)} %collective-permute-done.31.refs_1_, f32[68,8,128]{2,1,0:T(8,128)S(1)} %collective-permute-done.32.refs_2_, f32[4,64,128]{2,1,0:T(8,128)S(1)} %maps.1.refs_3_, ...), custom_call_target="tpu_custom_call" | custom-call | flops 6000000000 | bytes 4000000 | tf_op jit(solution)/shard_map/step3/pallas_call | solution.py:625
  103.3 1.2 send.1
  104.5 3.5 %collective-permute-start.40 = (f32[64,8,128]{2,1,0:T(8,128)S(1)}, f32[64,8,128]{2,1,0:T(8,128)S(1)}, u32[]{:S(2)}, u32[]{:S(2)}) collective-permute-start(f32[64,8,128]{2,1,0:T(8,128)S(1)} %get-tuple-element.138), channel_id=1, source_target_pairs={{0,8},{8,0},{16,24},{24,16},{1,9},{9,1},{17,25},{25,17},{2,10},{10... | collective-permute-start | bytes 786440 | tf_op jit(solution)/shard_map/ppermute | solution.py:548
  108.0 2.6 %collective-permute-start.41 = (f32[64,8,128]{2,1,0:T(8,128)S(1)}, f32[64,8,128]{2,1,0:T(8,128)S(1)}, u32[]{:S(2)}, u32[]{:S(2)}) collective-permute-start(f32[64,8,128]{2,1,0:T(8,128)S(1)} %get-tuple-element.139), channel_id=1, source_target_pairs={{0,16},{8,24},{16,0},{24,8},{1,17},{9,25},{17,1},{25,9},{2,18},{10... | collective-permute-start | bytes 786440 | tf_op jit(solution)/shard_map/ppermute | solution.py:548
  110.6 0.6 collective-permute-start.42
  111.3 2.4 %collective-permute-start.38 = (f32[8,128]{1,0:T(8,128)S(1)}, f32[8,128]{1,0:T(8,128)S(1)}, u32[]{:S(2)}, u32[]{:S(2)}) collective-permute-start(f32[8,128]{1,0:T(8,128)S(1)} %add.111), channel_id=1, source_target_pairs={{0,2},{1,3},{2,0},{3,1},{4,6},{5,7},{6,4},{7,5},{8,10},{9,11},{10,... | collective-permute-start | bytes 12296 | tf_op jit(solution)/shard_map/ppermute | solution.py:548
  113.7 0.3 collective-permute-done.37
  114.0 1.2 collective-permute-start.39
  115.3 0.3 collective-permute-done.38
  115.5 2.5 %collective-permute-done.39 = f32[8,128]{1,0:T(8,128)S(1)} collective-permute-done((f32[8,128]{1,0:T(8,128)S(1)}, f32[8,128]{1,0:T(8,128)S(1)}, u32[]{:S(2)}, u32[]{:S(2)}) %collective-permute-start.39) | collective-permute-done | bytes 4128 | tf_op jit(solution)/shard_map/ppermute | solution.py:548
  118.0 5.2 %collective-permute-done.42.r3 = f32[64,8,128]{2,1,0:T(8,128)S(1)} collective-permute-done((f32[64,8,128]{2,1,0:T(8,128)S(1)}, f32[64,8,128]{2,1,0:T(8,128)S(1)}, u32[]{:S(2)}, u32[]{:S(2)}) %collective-permute-start.42) | collective-permute-done | bytes 262176 | tf_op jit(solution)/shard_map/ppermute | solution.py:548
  123.2 3.1 %final.1 = f32[4,16,32,128]{3,2,1,0:T(8,128)} custom-call(s32[135]{0:T(256)S(1)} %concatenate.3.scal.ints, f32[8,128]{1,0:T(8,128)S(1)} %add_add_fusion.mean, f32[64,8,128]{2,1,0:T(8,128)S(1)} %get-tuple-element.137.s0, f32[64,8,128]{2,1,0:T(8,128)S(1)} %collective-permute-done.40.r1, f32[64,8,128]{2,1,0:T(8,128)S(1)} %collective-permute-done.41.r2, ...), custom_call_target="tpu_custom_call" | custom-call | flops 2000000000 | bytes 4000000 | tf_op jit(solution)/shard_map/final/pallas_call | solution.py:653
  (62 shorter events, 0.4 us)
Async XLA Ops:
  0.0 6.3 %copy-start.1 = (f32[2,4,32,128]{3,2,1,0:T(8,128)S(1)}, f32[2,4,32,128]{3,2,1,0:T(8,128)}, u32[]{:S(2)}) copy-start(f32[2,4,32,128]{3,2,1,0:T(8,128)} %planes.1) | copy-start | bytes 393220
  0.9 5.4 %collective-permute-start = (f32[16,128]{1,0:T(8,128)S(1)}, f32[16,128]{1,0:T(8,128)S(1)}, u32[]{:S(2)}, u32[]{:S(2)}) collective-permute-start(f32[16,128]{1,0:T(8,128)S(1)} %get-tuple-element.142), channel_id=1, source_target_pairs={{0,1},{1,2},{2,3},{3,4},{4,5},{5,6},{6,7},{7,0},{8,9},{9,10},{10,1... | collective-permute-start | bytes 24584 | tf_op jit(solution)/shard_map/ppermute | solution.py:567
  2.9 3.3 %collective-permute-start.1 = (f32[16,128]{1,0:T(8,128)S(1)}, f32[16,128]{1,0:T(8,128)S(1)}, u32[]{:S(2)}, u32[]{:S(2)}) collective-permute-start(f32[16,128]{1,0:T(8,128)S(1)} %get-tuple-element.142), channel_id=1, source_target_pairs={{1,0},{2,1},{3,2},{4,3},{5,4},{6,5},{7,6},{0,7},{9,8},{10,9},{11,1... | collective-permute-start | bytes 24584 | tf_op jit(solution)/shard_map/ppermute | solution.py:567
  6.3 1.2 copy-start
  9.2 5.2 %collective-permute-start.2 = (f32[70,8,128]{2,1,0:T(8,128)S(1)}, f32[70,8,128]{2,1,0:T(8,128)S(1)}, u32[]{:S(2)}, u32[]{:S(2)}) collective-permute-start(f32[70,8,128]{2,1,0:T(8,128)S(1)} %get-tuple-element.74), channel_id=1, source_target_pairs={{0,8},{8,0},{16,24},{24,16},{1,9},{9,1},{17,25},{25,17},{2,10},{10... | collective-permute-start | bytes 860168 | tf_op jit(solution)/shard_map/ppermute | solution.py:548
  11.2 10.0 %collective-permute-start.3 = (f32[70,8,128]{2,1,0:T(8,128)S(1)}, f32[70,8,128]{2,1,0:T(8,128)S(1)}, u32[]{:S(2)}, u32[]{:S(2)}) collective-permute-start(f32[70,8,128]{2,1,0:T(8,128)S(1)} %get-tuple-element.77), channel_id=1, source_target_pairs={{0,16},{8,24},{16,0},{24,8},{1,17},{9,25},{17,1},{25,9},{2,18},{10... | collective-permute-start | bytes 860168 | tf_op jit(solution)/shard_map/ppermute | solution.py:548
  14.2 13.2 %collective-permute-start.4 = (f32[70,8,128]{2,1,0:T(8,128)S(1)}, f32[70,8,128]{2,1,0:T(8,128)S(1)}, u32[]{:S(2)}, u32[]{:S(2)}) collective-permute-start(f32[70,8,128]{2,1,0:T(8,128)S(1)} %get-tuple-element.78), channel_id=1, source_target_pairs={{0,24},{8,16},{16,8},{24,0},{1,25},{9,17},{17,9},{25,1},{2,26},{10... | collective-permute-start | bytes 860168 | tf_op jit(solution)/shard_map/ppermute | solution.py:548
  14.4 13.1 %collective-permute-start.5 = (f32[8,8,128]{2,1,0:T(8,128)S(1)}, f32[8,8,128]{2,1,0:T(8,128)S(1)}, u32[]{:S(2)}, u32[]{:S(2)}) collective-permute-start(f32[8,8,128]{2,1,0:T(8,128)S(1)} %get-tuple-element.79.p0), channel_id=1, source_target_pairs={{0,32},{32,0},{64,96},{96,64},{1,33},{33,1},{65,97},{97,65},{2,34}... | collective-permute-start | bytes 98312 | tf_op jit(solution)/shard_map/ppermute | solution.py:548
  16.2 11.3 %collective-permute-start.6 = (f32[8,8,128]{2,1,0:T(8,128)S(1)}, f32[8,8,128]{2,1,0:T(8,128)S(1)}, u32[]{:S(2)}, u32[]{:S(2)}) collective-permute-start(f32[8,8,128]{2,1,0:T(8,128)S(1)} %get-tuple-element.79.p0), channel_id=1, source_target_pairs={{0,64},{32,96},{64,0},{96,32},{1,65},{33,97},{65,1},{97,33},{2,66}... | collective-permute-start | bytes 98312 | tf_op jit(solution)/shard_map/ppermute | solution.py:548
  19.5 8.0 %collective-permute-start.7 = (f32[8,8,128]{2,1,0:T(8,128)S(1)}, f32[8,8,128]{2,1,0:T(8,128)S(1)}, u32[]{:S(2)}, u32[]{:S(2)}) collective-permute-start(f32[8,8,128]{2,1,0:T(8,128)S(1)} %get-tuple-element.79.p0), channel_id=1, source_target_pairs={{0,96},{32,64},{64,32},{96,0},{1,97},{33,65},{65,33},{97,1},{2,98}... | collective-permute-start | bytes 98312 | tf_op jit(solution)/shard_map/ppermute | solution.py:548
  29.3 1.2 collective-permute-start.8
  30.5 10.9 %collective-permute-start.10 = (f32[72,8,128]{2,1,0:T(8,128)S(1)}, f32[72,8,128]{2,1,0:T(8,128)S(1)}, u32[]{:S(2)}, u32[]{:S(2)}) collective-permute-start(f32[72,8,128]{2,1,0:T(8,128)S(1)} %get-tuple-element.86), channel_id=1, source_target_pairs={{0,8},{8,16},{16,24},{24,25},{25,17},{17,9},{9,1},{1,2},{2,10},{10... | collective-permute-start | bytes 884744 | tf_op jit(solution)/shard_map/ppermute | solution.py:611
  33.6 7.8 %collective-permute-start.11 = (f32[72,8,128]{2,1,0:T(8,128)S(1)}, f32[72,8,128]{2,1,0:T(8,128)S(1)}, u32[]{:S(2)}, u32[]{:S(2)}) collective-permute-start(f32[72,8,128]{2,1,0:T(8,128)S(1)} %get-tuple-element.87), channel_id=1, source_target_pairs={{8,0},{16,8},{24,16},{25,24},{17,25},{9,17},{1,9},{2,1},{10,2},{18... | collective-permute-start | bytes 884744 | tf_op jit(solution)/shard_map/ppermute | solution.py:612
  33.6 7.7 %collective-permute-start.9 = (f32[8,128]{1,0:T(8,128)S(1)}, f32[8,128]{1,0:T(8,128)S(1)}, u32[]{:S(2)}, u32[]{:S(2)}) collective-permute-start(f32[8,128]{1,0:T(8,128)S(1)} %add.91), channel_id=1, source_target_pairs={{0,4},{1,5},{2,6},{3,7},{4,0},{5,1},{6,2},{7,3},{8,12},{9,13},{10,... | collective-permute-start | bytes 12296 | tf_op jit(solution)/shard_map/ppermute | solution.py:548
  41.4 6.3 %collective-permute-start.12 = (f32[8,128]{1,0:T(8,128)S(1)}, f32[8,128]{1,0:T(8,128)S(1)}, u32[]{:S(2)}, u32[]{:S(2)}) collective-permute-start(f32[8,128]{1,0:T(8,128)S(1)} %add.92), channel_id=1, source_target_pairs={{0,16},{8,24},{16,0},{24,8},{1,17},{9,25},{17,1},{25,9},{2,18},{10... | collective-permute-start | bytes 12296 | tf_op jit(solution)/shard_map/ppermute | solution.py:548
  45.7 2.8 %collective-permute-start.13 = (f32[8,128]{1,0:T(8,128)S(1)}, f32[8,128]{1,0:T(8,128)S(1)}, u32[]{:S(2)}, u32[]{:S(2)}) collective-permute-start(f32[8,128]{1,0:T(8,128)S(1)} %get-tuple-element.98), channel_id=1, source_target_pairs={{0,8},{8,0},{16,24},{24,16},{1,9},{9,1},{17,25},{25,17},{2,10},{10... | collective-permute-start | bytes 12296 | tf_op jit(solution)/shard_map/ppermute | solution.py:548
  48.5 11.9 %collective-permute-start.15 = (f32[68,8,128]{2,1,0:T(8,128)S(1)}, f32[68,8,128]{2,1,0:T(8,128)S(1)}, u32[]{:S(2)}, u32[]{:S(2)}) collective-permute-start(f32[68,8,128]{2,1,0:T(8,128)S(1)} %get-tuple-element.101), channel_id=1, source_target_pairs={{0,8},{8,16},{16,24},{24,25},{25,17},{17,9},{9,1},{1,2},{2,10},{10... | collective-permute-start | bytes 835592 | tf_op jit(solution)/shard_map/ppermute | solution.py:611
  50.0 10.4 %collective-permute-start.16 = (f32[68,8,128]{2,1,0:T(8,128)S(1)}, f32[68,8,128]{2,1,0:T(8,128)S(1)}, u32[]{:S(2)}, u32[]{:S(2)}) collective-permute-start(f32[68,8,128]{2,1,0:T(8,128)S(1)} %get-tuple-element.102), channel_id=1, source_target_pairs={{8,0},{16,8},{24,16},{25,24},{17,25},{9,17},{1,9},{2,1},{10,2},{18... | collective-permute-start | bytes 835592 | tf_op jit(solution)/shard_map/ppermute | solution.py:612
  50.1 5.1 %collective-permute-start.17 = (f32[8,128]{1,0:T(8,128)S(1)}, f32[8,128]{1,0:T(8,128)S(1)}, u32[]{:S(2)}, u32[]{:S(2)}) collective-permute-start(f32[8,128]{1,0:T(8,128)S(1)} %add.95), channel_id=1, source_target_pairs={{0,1},{1,0},{2,3},{3,2},{4,5},{5,4},{6,7},{7,6},{8,9},{9,8},{10,11... | collective-permute-start | bytes 12296 | tf_op jit(solution)/shard_map/ppermute | solution.py:548
  50.2 6.3 %collective-permute-start.18 = (f32[8,128]{1,0:T(8,128)S(1)}, f32[8,128]{1,0:T(8,128)S(1)}, u32[]{:S(2)}, u32[]{:S(2)}) collective-permute-start(f32[8,128]{1,0:T(8,128)S(1)} %add.95), channel_id=1, source_target_pairs={{0,2},{1,3},{2,0},{3,1},{4,6},{5,7},{6,4},{7,5},{8,10},{9,11},{10,... | collective-permute-start | bytes 12296 | tf_op jit(solution)/shard_map/ppermute | solution.py:548
  55.2 3.7 %collective-permute-start.19 = (f32[8,128]{1,0:T(8,128)S(1)}, f32[8,128]{1,0:T(8,128)S(1)}, u32[]{:S(2)}, u32[]{:S(2)}) collective-permute-start(f32[8,128]{1,0:T(8,128)S(1)} %add.95), channel_id=1, source_target_pairs={{0,3},{1,2},{2,1},{3,0},{4,7},{5,6},{6,5},{7,4},{8,11},{9,10},{10,... | collective-permute-start | bytes 12296 | tf_op jit(solution)/shard_map/ppermute | solution.py:548
  55.2 3.7 %collective-permute-start.14 = (f32[8,128]{1,0:T(8,128)S(1)}, f32[8,128]{1,0:T(8,128)S(1)}, u32[]{:S(2)}, u32[]{:S(2)}) collective-permute-start(f32[8,128]{1,0:T(8,128)S(1)} %add.93), channel_id=1, source_target_pairs={{0,4},{1,5},{2,6},{3,7},{4,0},{5,1},{6,2},{7,3},{8,12},{9,13},{10,... | collective-permute-start | bytes 12296 | tf_op jit(solution)/shard_map/ppermute | solution.py:548
  58.9 8.1 %collective-permute-start.20 = (f32[8,128]{1,0:T(8,128)S(1)}, f32[8,128]{1,0:T(8,128)S(1)}, u32[]{:S(2)}, u32[]{:S(2)}) collective-permute-start(f32[8,128]{1,0:T(8,128)S(1)} %add.94), channel_id=1, source_target_pairs={{0,16},{8,24},{16,0},{24,8},{1,17},{9,25},{17,1},{25,9},{2,18},{10... | collective-permute-start | bytes 12296 | tf_op jit(solution)/shard_map/ppermute | solution.py:548
  65.4 2.5 %collective-permute-start.21 = (f32[8,128]{1,0:T(8,128)S(1)}, f32[8,128]{1,0:T(8,128)S(1)}, u32[]{:S(2)}, u32[]{:S(2)}) collective-permute-start(f32[8,128]{1,0:T(8,128)S(1)} %get-tuple-element.113), channel_id=1, source_target_pairs={{0,8},{8,0},{16,24},{24,16},{1,9},{9,1},{17,25},{25,17},{2,10},{10... | collective-permute-start | bytes 12296 | tf_op jit(solution)/shard_map/ppermute | solution.py:548
  67.9 11.1 %collective-permute-start.23 = (f32[68,8,128]{2,1,0:T(8,128)S(1)}, f32[68,8,128]{2,1,0:T(8,128)S(1)}, u32[]{:S(2)}, u32[]{:S(2)}) collective-permute-start(f32[68,8,128]{2,1,0:T(8,128)S(1)} %get-tuple-element.116), channel_id=1, source_target_pairs={{0,8},{8,16},{16,24},{24,25},{25,17},{17,9},{9,1},{1,2},{2,10},{10... | collective-permute-start | bytes 835592 | tf_op jit(solution)/shard_map/ppermute | solution.py:611
  70.7 8.3 %collective-permute-start.24 = (f32[68,8,128]{2,1,0:T(8,128)S(1)}, f32[68,8,128]{2,1,0:T(8,128)S(1)}, u32[]{:S(2)}, u32[]{:S(2)}) collective-permute-start(f32[68,8,128]{2,1,0:T(8,128)S(1)} %get-tuple-element.117), channel_id=1, source_target_pairs={{8,0},{16,8},{24,16},{25,24},{17,25},{9,17},{1,9},{2,1},{10,2},{18... | collective-permute-start | bytes 835592 | tf_op jit(solution)/shard_map/ppermute | solution.py:612
  70.7 3.9 %collective-permute-start.25 = (f32[8,128]{1,0:T(8,128)S(1)}, f32[8,128]{1,0:T(8,128)S(1)}, u32[]{:S(2)}, u32[]{:S(2)}) collective-permute-start(f32[8,128]{1,0:T(8,128)S(1)} %add.101), channel_id=1, source_target_pairs={{0,1},{1,0},{2,3},{3,2},{4,5},{5,4},{6,7},{7,6},{8,9},{9,8},{10,11... | collective-permute-start | bytes 12296 | tf_op jit(solution)/shard_map/ppermute | solution.py:548
  70.7 4.3 %collective-permute-start.26 = (f32[8,128]{1,0:T(8,128)S(1)}, f32[8,128]{1,0:T(8,128)S(1)}, u32[]{:S(2)}, u32[]{:S(2)}) collective-permute-start(f32[8,128]{1,0:T(8,128)S(1)} %add.101), channel_id=1, source_target_pairs={{0,2},{1,3},{2,0},{3,1},{4,6},{5,7},{6,4},{7,5},{8,10},{9,11},{10,... | collective-permute-start | bytes 12296 | tf_op jit(solution)/shard_map/ppermute | solution.py:548
  73.5 3.7 %collective-permute-start.27 = (f32[8,128]{1,0:T(8,128)S(1)}, f32[8,128]{1,0:T(8,128)S(1)}, u32[]{:S(2)}, u32[]{:S(2)}) collective-permute-start(f32[8,128]{1,0:T(8,128)S(1)} %add.101), channel_id=1, source_target_pairs={{0,3},{1,2},{2,1},{3,0},{4,7},{5,6},{6,5},{7,4},{8,11},{9,10},{10,... | collective-permute-start | bytes 12296 | tf_op jit(solution)/shard_map/ppermute | solution.py:548
  74.5 3.2 %collective-permute-start.22 = (f32[8,128]{1,0:T(8,128)S(1)}, f32[8,128]{1,0:T(8,128)S(1)}, u32[]{:S(2)}, u32[]{:S(2)}) collective-permute-start(f32[8,128]{1,0:T(8,128)S(1)} %add.99), channel_id=1, source_target_pairs={{0,4},{1,5},{2,6},{3,7},{4,0},{5,1},{6,2},{7,3},{8,12},{9,13},{10,... | collective-permute-start | bytes 12296 | tf_op jit(solution)/shard_map/ppermute | solution.py:548
  77.8 9.9 %collective-permute-start.28 = (f32[8,128]{1,0:T(8,128)S(1)}, f32[8,128]{1,0:T(8,128)S(1)}, u32[]{:S(2)}, u32[]{:S(2)}) collective-permute-start(f32[8,128]{1,0:T(8,128)S(1)} %add.100), channel_id=1, source_target_pairs={{0,16},{8,24},{16,0},{24,8},{1,17},{9,25},{17,1},{25,9},{2,18},{10... | collective-permute-start | bytes 12296 | tf_op jit(solution)/shard_map/ppermute | solution.py:548
  83.9 4.6 %collective-permute-start.29 = (f32[8,128]{1,0:T(8,128)S(1)}, f32[8,128]{1,0:T(8,128)S(1)}, u32[]{:S(2)}, u32[]{:S(2)}) collective-permute-start(f32[8,128]{1,0:T(8,128)S(1)} %get-tuple-element.127), channel_id=1, source_target_pairs={{0,8},{8,0},{16,24},{24,16},{1,9},{9,1},{17,25},{25,17},{2,10},{10... | collective-permute-start | bytes 12296 | tf_op jit(solution)/shard_map/ppermute | solution.py:548
  88.5 10.0 %collective-permute-start.31 = (f32[68,8,128]{2,1,0:T(8,128)S(1)}, f32[68,8,128]{2,1,0:T(8,128)S(1)}, u32[]{:S(2)}, u32[]{:S(2)}) collective-permute-start(f32[68,8,128]{2,1,0:T(8,128)S(1)} %get-tuple-element.130), channel_id=1, source_target_pairs={{0,8},{8,16},{16,24},{24,25},{25,17},{17,9},{9,1},{1,2},{2,10},{10... | collective-permute-start | bytes 835592 | tf_op jit(solution)/shard_map/ppermute | solution.py:611
  90.0 8.5 %collective-permute-start.32 = (f32[68,8,128]{2,1,0:T(8,128)S(1)}, f32[68,8,128]{2,1,0:T(8,128)S(1)}, u32[]{:S(2)}, u32[]{:S(2)}) collective-permute-start(f32[68,8,128]{2,1,0:T(8,128)S(1)} %get-tuple-element.131), channel_id=1, source_target_pairs={{8,0},{16,8},{24,16},{25,24},{17,25},{9,17},{1,9},{2,1},{10,2},{18... | collective-permute-start | bytes 835592 | tf_op jit(solution)/shard_map/ppermute | solution.py:612
  90.0 3.9 %collective-permute-start.33 = (f32[8,128]{1,0:T(8,128)S(1)}, f32[8,128]{1,0:T(8,128)S(1)}, u32[]{:S(2)}, u32[]{:S(2)}) collective-permute-start(f32[8,128]{1,0:T(8,128)S(1)} %add.107), channel_id=1, source_target_pairs={{0,1},{1,0},{2,3},{3,2},{4,5},{5,4},{6,7},{7,6},{8,9},{9,8},{10,11... | collective-permute-start | bytes 12296 | tf_op jit(solution)/shard_map/ppermute | solution.py:548
  90.4 4.9 %collective-permute-start.34 = (f32[8,128]{1,0:T(8,128)S(1)}, f32[8,128]{1,0:T(8,128)S(1)}, u32[]{:S(2)}, u32[]{:S(2)}) collective-permute-start(f32[8,128]{1,0:T(8,128)S(1)} %add.107), channel_id=1, source_target_pairs={{0,2},{1,3},{2,0},{3,1},{4,6},{5,7},{6,4},{7,5},{8,10},{9,11},{10,... | collective-permute-start | bytes 12296 | tf_op jit(solution)/shard_map/ppermute | solution.py:548
  93.9 3.7 %collective-permute-start.35 = (f32[8,128]{1,0:T(8,128)S(1)}, f32[8,128]{1,0:T(8,128)S(1)}, u32[]{:S(2)}, u32[]{:S(2)}) collective-permute-start(f32[8,128]{1,0:T(8,128)S(1)} %add.107), channel_id=1, source_target_pairs={{0,3},{1,2},{2,1},{3,0},{4,7},{5,6},{6,5},{7,4},{8,11},{9,10},{10,... | collective-permute-start | bytes 12296 | tf_op jit(solution)/shard_map/ppermute | solution.py:548
  93.9 4.3 %collective-permute-start.30 = (f32[8,128]{1,0:T(8,128)S(1)}, f32[8,128]{1,0:T(8,128)S(1)}, u32[]{:S(2)}, u32[]{:S(2)}) collective-permute-start(f32[8,128]{1,0:T(8,128)S(1)} %add.105), channel_id=1, source_target_pairs={{0,4},{1,5},{2,6},{3,7},{4,0},{5,1},{6,2},{7,3},{8,12},{9,13},{10,... | collective-permute-start | bytes 12296 | tf_op jit(solution)/shard_map/ppermute | solution.py:548
  98.2 5.1 %collective-permute-start.36 = (f32[8,128]{1,0:T(8,128)S(1)}, f32[8,128]{1,0:T(8,128)S(1)}, u32[]{:S(2)}, u32[]{:S(2)}) collective-permute-start(f32[8,128]{1,0:T(8,128)S(1)} %add.106), channel_id=1, source_target_pairs={{0,16},{8,24},{16,0},{24,8},{1,17},{9,25},{17,1},{25,9},{2,18},{10... | collective-permute-start | bytes 12296 | tf_op jit(solution)/shard_map/ppermute | solution.py:548
  104.5 13.5 %collective-permute-start.40 = (f32[64,8,128]{2,1,0:T(8,128)S(1)}, f32[64,8,128]{2,1,0:T(8,128)S(1)}, u32[]{:S(2)}, u32[]{:S(2)}) collective-permute-start(f32[64,8,128]{2,1,0:T(8,128)S(1)} %get-tuple-element.138), channel_id=1, source_target_pairs={{0,8},{8,0},{16,24},{24,16},{1,9},{9,1},{17,25},{25,17},{2,10},{10... | collective-permute-start | bytes 786440 | tf_op jit(solution)/shard_map/ppermute | solution.py:548
  108.0 10.0 %collective-permute-start.41 = (f32[64,8,128]{2,1,0:T(8,128)S(1)}, f32[64,8,128]{2,1,0:T(8,128)S(1)}, u32[]{:S(2)}, u32[]{:S(2)}) collective-permute-start(f32[64,8,128]{2,1,0:T(8,128)S(1)} %get-tuple-element.139), channel_id=1, source_target_pairs={{0,16},{8,24},{16,0},{24,8},{1,17},{9,25},{17,1},{25,9},{2,18},{10... | collective-permute-start | bytes 786440 | tf_op jit(solution)/shard_map/ppermute | solution.py:548
  110.6 12.6 %collective-permute-start.42 = (f32[64,8,128]{2,1,0:T(8,128)S(1)}, f32[64,8,128]{2,1,0:T(8,128)S(1)}, u32[]{:S(2)}, u32[]{:S(2)}) collective-permute-start(f32[64,8,128]{2,1,0:T(8,128)S(1)} %get-tuple-element.140), channel_id=1, source_target_pairs={{0,24},{8,16},{16,8},{24,0},{1,25},{9,17},{17,9},{25,1},{2,26},{10... | collective-permute-start | bytes 786440 | tf_op jit(solution)/shard_map/ppermute | solution.py:548
  111.3 2.8 %collective-permute-start.37 = (f32[8,128]{1,0:T(8,128)S(1)}, f32[8,128]{1,0:T(8,128)S(1)}, u32[]{:S(2)}, u32[]{:S(2)}) collective-permute-start(f32[8,128]{1,0:T(8,128)S(1)} %add.111), channel_id=1, source_target_pairs={{0,1},{1,0},{2,3},{3,2},{4,5},{5,4},{6,7},{7,6},{8,9},{9,8},{10,11... | collective-permute-start | bytes 12296 | tf_op jit(solution)/shard_map/ppermute | solution.py:548
  111.3 4.3 %collective-permute-start.38 = (f32[8,128]{1,0:T(8,128)S(1)}, f32[8,128]{1,0:T(8,128)S(1)}, u32[]{:S(2)}, u32[]{:S(2)}) collective-permute-start(f32[8,128]{1,0:T(8,128)S(1)} %add.111), channel_id=1, source_target_pairs={{0,2},{1,3},{2,0},{3,1},{4,6},{5,7},{6,4},{7,5},{8,10},{9,11},{10,... | collective-permute-start | bytes 12296 | tf_op jit(solution)/shard_map/ppermute | solution.py:548
  114.0 4.0 %collective-permute-start.39 = (f32[8,128]{1,0:T(8,128)S(1)}, f32[8,128]{1,0:T(8,128)S(1)}, u32[]{:S(2)}, u32[]{:S(2)}) collective-permute-start(f32[8,128]{1,0:T(8,128)S(1)} %add.111), channel_id=1, source_target_pairs={{0,3},{1,2},{2,1},{3,0},{4,7},{5,6},{6,5},{7,4},{8,11},{9,10},{10,... | collective-permute-start | bytes 12296 | tf_op jit(solution)/shard_map/ppermute | solution.py:548
